TPU v7x, 256 devices: a whole 4x4x8 slice. The times are simulated.
256 devices in a mesh: cfg: 2 (over core), vocab: 64 (over y, x, z_lo), rows: 2 (over z_hi).
Axes of the slice: x: 4, y: 4, z: 8 (z_hi: 2, z_lo: 4; z = z_hi * 4 + z_lo), core: 2. Of those that a mesh axis runs over, the one named last changes fastest.
Arguments:
- hidden: bfloat16 [2, 1024, 8192], P('cfg', None, ('rows', 'vocab')), may hold values from -72 to 72, as said below
- head: bfloat16 [8192, 65536], P('rows', 'vocab'), may hold values from -0.0625 to 0.0625
- scale_index: int32 [1024], P('rows'), may hold values from 0 to 8
- threshold: int32 [1024], P('rows'), may hold values from 2 to 33
Outputs:
- logprob: bfloat16 [1024, 65536], P(('rows', 'cfg'), 'vocab')
- typical: bfloat16 [1024, 65536], P(('rows', 'cfg'), 'vocab')
- entropy: float32 [1024], P(('rows', 'cfg'))
Inputs may be any that keep to these rules, and one draw needn't show every extreme that they name: `hidden`: each entry is a normal value clipped to 6 scales and multiplied by a per-row factor between 1 and 12 (1 in some draws).
All inputs are finite; a program needn't handle non-finite values.
Results may differ from a plain program's by a relative error of at most 0.001.
Values may be sent and summed in bfloat16 or wider, within the bound.
No kernel may reach another device: no remote copies, remote signals or barrier semaphores. Data moves between devices by JAX's collectives and lax.ppermute only.
A program may use at most 64 MiB of HBM per device.

v0:
```python
import jax
import jax.numpy as jnp
from jax import lax
from jax.sharding import PartitionSpec as P


def swapped(block, axis, stride):
    count = lax.axis_size(axis)
    route = []
    for low in range(count):
        high = low | 1 << stride
        if high != low and high < count:
            route += [(low, high), (high, low)]
    return lax.ppermute(block, axis, route)


def finish(guided, limits):
    local_peak = jnp.max(guided, axis=1)
    peak = lax.pmax(local_peak, "vocab")
    expo = jnp.exp(guided - peak[:, None])
    total, moment = lax.psum((jnp.sum(expo, axis=1), jnp.sum(expo * guided, axis=1)), "vocab")
    lse = peak + jnp.log(total)
    entropy = lse - moment / total
    shifted = guided - lse[:, None]
    deviation = -shifted - entropy[:, None]
    typical = jax.nn.sigmoid(2.0 * (limits[:, None] - jnp.abs(deviation)))
    return (shifted.astype(jnp.bfloat16), typical.astype(jnp.bfloat16), entropy)


def local(hidden, head, scale_index, threshold):
    rows_input = hidden[0]
    partial_sums = jnp.dot(
        lax.all_gather(rows_input, "vocab", axis=1, tiled=True),
        head,
        preferred_element_type=jnp.float32,
    )
    own_logits = lax.psum_scatter(partial_sums, "rows", scatter_dimension=0, tiled=True)
    branch = lax.axis_index("cfg")
    guide = 1.0 + 0.5 * scale_index.astype(jnp.float32)
    limits = threshold.astype(jnp.float32) / 8.0
    half_count = own_logits.shape[0] // 2
    offset = branch * half_count
    part_guide = lax.dynamic_slice_in_dim(guide, offset, half_count, 0)
    part_limits = lax.dynamic_slice_in_dim(limits, offset, half_count, 0)
    partner = swapped(own_logits, "cfg", 0)
    own_part = lax.dynamic_slice_in_dim(own_logits, offset, half_count, 0)
    other_part = lax.dynamic_slice_in_dim(partner, offset, half_count, 0)
    conditional = jnp.where(branch == 0, own_part, other_part)
    unconditional = jnp.where(branch == 0, other_part, own_part)
    guided = unconditional + part_guide[:, None] * (conditional - unconditional)
    return finish(guided, part_limits)


def solution(mesh):
    return jax.shard_map(
        local,
        mesh=mesh,
        in_specs=(P("cfg", None, ("rows", "vocab")), P("rows", "vocab"), P("rows"), P("rows")),
        out_specs=(P(("rows", "cfg"), "vocab"), P(("rows", "cfg"), "vocab"), P(("rows", "cfg"))),
        check_vma=False,
    )
```

profile of v0, /device:TPU:2, one launch (start us, length us, event | category | flops | bytes accessed | tf_op | source)
XLA Modules:
  0.0 882.3 jit_solution(11604314925678496638)
XLA Ops:
  7.2 0.0 all-gather.3.cloned.1.call-start
  7.2 0.7 all-gather.3.cloned.1.call-update
  7.9 0.0 copy-start.1
  7.9 0.0 copy-start.2
  7.9 0.0 reduce-scatter.2.cloned.1.call-start
  8.0 376.6 %all-gather.3.cloned.1.call-done = bf16[1,1024,4096]{1,2,0:T(8,128)(2,1)} async-done(((bf16[1,1024,64]{1,2,0:T(8,128)(2,1)}), bf16[1,1024,4096]{1,2,0:T(8,128)(2,1)}) %all-gather.3.cloned.1.call-update) | async-done | bytes 8388624 | tf_op jit(solution)/shard_map/all_gather | solution.py:33
  384.6 15.1 %fusion = f32[1024,1024]{1,0:T(8,128)} fusion(bf16[4096,1024]{1,0:T(8,128)(2,1)} %param.5, bf16[1,1024,4096]{1,2,0:T(8,128)(2,1)} %all-gather.3.cloned.1.call-done), kind=kOutput, calls=%fused_computation | convolution fusion | flops 8589934592 | bytes 20971520 | tf_op jit(solution)/shard_map/dot_general | solution.py:32
  399.7 0.0 reduce-scatter.2.cloned.1.call-update
  399.7 113.6 %reduce-scatter.2.cloned.1.call-done = f32[512,1024]{1,0:T(8,128)} async-done(((f32[1024,1024]{1,0:T(8,128)}), f32[512,1024]{1,0:T(8,128)}) %reduce-scatter.2.cloned.1.call-update) | async-done | bytes 2097168 | tf_op jit(solution)/shard_map/reduce_scatter | solution.py:37
  513.3 0.0 collective-permute-start
  513.3 0.0 copy-done.1
  513.3 0.1 dynamic_slice.14
  513.4 0.0 copy-done.2
  513.4 0.1 dynamic_slice.15
  513.5 4.2 collective-permute-done
  517.7 1.6 fusion.3
  519.3 170.6 %pmax.7 = f32[256]{0:T(256)S(1)} all-reduce(f32[256]{0:T(256)S(1)} %get-tuple-element.7), channel_id=1, replica_groups=mesh['cfg'=2,'vocab'=64,'rows'=2] {'vocab'}, use_global_device_ids=true, to_apply=%region_2.3 | all-reduce | flops 256 | bytes 2048 | tf_op jit(solution)/shard_map/pmax | solution.py:19
  689.9 0.4 multiply_reduce_fusion
  690.3 183.9 %all-reduce = (f32[256]{0:T(256)S(1)}, f32[256]{0:T(256)S(1)}) all-reduce(f32[256]{0:T(256)S(1)} %get-tuple-element.4, f32[256]{0:T(256)S(1)} %get-tuple-element.3), channel_id=1, replica_groups=mesh['cfg'=2,'vocab'=64,'rows'=2] {'vocab'}, use_global_device_ids=true, to_apply=%region_4.5 | all-reduce | flops 512 | bytes 4096 | tf_op jit(solution)/shard_map/psum | solution.py:21
  874.1 0.0 copy-start
  874.1 1.3 divide_convert_fusion
  875.4 0.0 copy-done
  (3 shorter events, 0.0 us)
Async XLA Ops:
  7.2 377.4 %all-gather.3.cloned.1.call-start = ((), (), s32[]{:S(2)}) async-start(), calls=%async_computation.2 | async-start | bytes 8519680 | tf_op jit(solution)/shard_map/all_gather | solution.py:33
  7.9 505.4 %copy-start.1 = (s32[512]{0:T(512)S(1)}, s32[512]{0:T(512)}, u32[]{:S(2)}) copy-start(s32[512]{0:T(512)} %param.6) | copy-start | bytes 6148
  7.9 505.5 %copy-start.2 = (s32[512]{0:T(512)S(1)}, s32[512]{0:T(512)}, u32[]{:S(2)}) copy-start(s32[512]{0:T(512)} %param.7) | copy-start | bytes 6148
  7.9 505.4 %reduce-scatter.2.cloned.1.call-start = ((), (), s32[]{:S(2)}) async-start(), calls=%async_computation.1 | async-start | bytes 6291456 | tf_op jit(solution)/shard_map/reduce_scatter | solution.py:37
  513.3 4.4 collective-permute-start
  874.1 1.3 copy-start
Sparse Core Ops, SparseCore 0:
  9.8 374.7 all-gather.2
  399.8 113.4 reduce-scatter.1
where the time goes:
time: 892 us; the launch traced here: 882 us
  waiting for transfers between devices  495 us (55%)
  blocking collectives  354 us (40%)
  matrix products  15.1 us (2%)
  between operations  14.1 us (2%)
    all_gather x1, waiting for transfers between devices, local(): lax.all_gather(rows_input, 'vocab', axis=1, tiled=True)  377 us
    psum x1, blocking collectives, finish(): lax.psum((jnp.sum(expo, axis=1), jnp.sum(expo * guided, axis=1)), 'vocab')  184 us
    pmax x1, blocking collectives, finish(): peak = lax.pmax(local_peak, 'vocab')  171 us
    reduce_scatter x1, waiting for transfers between devices, local(): lax.psum_scatter(partial_sums, 'rows', scatter_dimension=0, tiled=True)  114 us
  transfers between devices with their start and end apart: 3, of which 3 were waited for; matrix products, arithmetic and copies ran while one was open for 0% of the time, Pallas kernels for 0%

commit v1 on v0

v1 whole, which is shorter than its diff:
```python
import math

import jax
import jax.numpy as jnp
from jax import lax
from jax.experimental import pallas as pl
from jax.experimental.pallas import tpu as pltpu
from jax.sharding import Mesh, PartitionSpec as P

AXES = ("cfg", "y", "x", "zl", "zh")
SIZES = (2, 4, 4, 4, 2)
TOP = 32767.0
STEP = math.log(2.0) / 256.0


def pairs(axes, move):
    dims = [SIZES[AXES.index(a)] for a in axes]
    route = []
    for i in range(math.prod(dims)):
        rest, at = i, {}
        for a, n in reversed(list(zip(axes, dims))):
            at[a], rest = rest % n, rest // n
        to = move(dict(at))
        j = 0
        for a, n in zip(axes, dims):
            j = j * n + to[a] % n
        route.append((i, j))
    return route


def shifted(block, axis, k):
    return lax.ppermute(block, axis, pairs((axis,), lambda at: {axis: at[axis] + k}))


def crossed(block, first, second, k):
    def move(at):
        along = first if at["cfg"] == 0 else second
        at[along] += k
        return at

    axes = ("cfg", "y", "x")
    return lax.ppermute(block, axes, pairs(axes, move))


def code_of(largest):
    return jnp.ceil(jnp.log(jnp.maximum(largest, 1e-30)) * (1.0 / STEP)) + 1.0


def scale_of(code):
    return jnp.exp(code * STEP) * (1.0 / TOP)


def coded(values, scale):
    return jnp.clip(jnp.round(values / scale), -TOP, TOP).astype(jnp.int32).astype(jnp.int16)


def mix_kernel(core_ref, own_ref, other_ref, guide_ref, out_ref):
    own = own_ref[...].astype(jnp.float32)
    other = other_ref[...].astype(jnp.float32)
    first = core_ref[0] == 0
    cond = jnp.where(first, own, other)
    uncond = jnp.where(first, other, own)
    mixed = uncond + guide_ref[...] * (cond - uncond)
    code = code_of(jnp.max(jnp.abs(mixed), axis=0, keepdims=True))
    out_ref[:64] = coded(mixed, scale_of(code))
    out_ref[64:] = jnp.broadcast_to(code, (16, code.shape[1])).astype(jnp.int32).astype(jnp.int16)


def mix(core, own, other, guide):
    width = own.shape[1]
    return pl.pallas_call(
        mix_kernel,
        out_shape=jax.ShapeDtypeStruct((80, width), jnp.int16),
        in_specs=[pl.BlockSpec(memory_space=pltpu.SMEM)] + [pl.BlockSpec(memory_space=pltpu.VMEM)] * 3,
        out_specs=pl.BlockSpec(memory_space=pltpu.VMEM),
        name="mix",
    )(core, own, other, guide)


def stack_kernel(place_ref, a_ref, b_ref, c_ref, d_ref, out_ref):
    width = a_ref.shape[1]
    row = lax.broadcasted_iota(jnp.int32, (16, width), 0)
    codes = jnp.zeros((16, width), jnp.int32)
    for k, ref in enumerate((a_ref, b_ref, c_ref, d_ref)):
        place = place_ref[k]
        out_ref[pl.ds(pl.multiple_of(place * 64, 64), 64), :] = ref[:64]
        codes = jnp.where(row == place, ref[64:].astype(jnp.int32), codes)
    out_ref[256:] = codes.astype(jnp.int16)


def stack(place, parts):
    width = parts[0].shape[1]
    return pl.pallas_call(
        stack_kernel,
        out_shape=jax.ShapeDtypeStruct((272, width), jnp.int16),
        in_specs=[pl.BlockSpec(memory_space=pltpu.SMEM)] + [pl.BlockSpec(memory_space=pltpu.VMEM)] * 4,
        out_specs=pl.BlockSpec(memory_space=pltpu.VMEM),
        name="stack",
    )(place, *parts)


def product_kernel(index_ref, head_ref, *refs):
    parts, out_ref, total_ref = refs[:4], refs[4], refs[5]
    step = pl.program_id(0)

    @pl.when(step == 0)
    def _():
        total_ref[...] = jnp.zeros_like(total_ref)

    for k, part in enumerate(parts):

        @pl.when(step // 4 == k)
        def _(part=part):
            scale = scale_of(part[256:].astype(jnp.float32))
            high, low = [], []
            for j in range(4):
                value = part[64 * j : 64 * j + 64].astype(jnp.float32) * scale[j : j + 1]
                top = value.astype(jnp.bfloat16)
                high.append(top)
                low.append((value - top.astype(jnp.float32)).astype(jnp.bfloat16))
            weight = head_ref[...]
            dims = (((0,), (0,)), ((), ()))
            total_ref[...] += lax.dot_general(
                jnp.concatenate(high, 0), weight, dims, preferred_element_type=jnp.float32
            ) + lax.dot_general(jnp.concatenate(low, 0), weight, dims, preferred_element_type=jnp.float32)

    @pl.when(step == 15)
    def _():
        if out_ref.dtype == jnp.float32:
            out_ref[...] = total_ref[...]
        else:
            total = total_ref[...]
            count = total.shape[0]
            code = code_of(jnp.max(jnp.abs(total), axis=1, keepdims=True))
            out_ref[:count] = coded(total, scale_of(code))
            across = jnp.transpose(jnp.broadcast_to(code, (count, 128)))[:16]
            out_ref[count:, :count] = across.astype(jnp.int32).astype(jnp.int16)


def product(index, head, parts, keep):
    tokens, width = parts[0].shape[1], head.shape[1]

    def block(k):
        return lambda s, index: (jnp.clip(s - 4 * k, 0, 3), 0)

    out = (
        jax.ShapeDtypeStruct((tokens, width), jnp.float32)
        if keep
        else jax.ShapeDtypeStruct((tokens + 16, width), jnp.int16)
    )
    return pl.pallas_call(
        product_kernel,
        out_shape=out,
        grid_spec=pltpu.PrefetchScalarGridSpec(
            num_scalar_prefetch=1,
            grid=(16,),
            in_specs=[pl.BlockSpec((256, width), lambda s, index: (index[s], 0))]
            + [pl.BlockSpec((272, tokens), block(k)) for k in range(4)],
            out_specs=pl.BlockSpec(out.shape, lambda s, index: (0, 0)),
            scratch_shapes=[pltpu.VMEM((tokens, width), jnp.float32)],
        ),
        compiler_params=pltpu.CompilerParams(vmem_limit_bytes=24 << 20),
        cost_estimate=pl.CostEstimate(
            flops=4 * tokens * 4096 * width, bytes_accessed=10 << 20, transcendentals=0
        ),
        name="product",
    )(index, head, *parts)


def merged(stats):
    peak = stats[0][0]
    for s in stats[1:]:
        peak = jnp.maximum(peak, s[0])
    total = moment = 0.0
    for s in stats:
        weight = jnp.exp(s[0] - peak)
        total += s[1] * weight
        moment += s[2] * weight
    return jnp.stack([peak, total, moment])


def local(hidden, head, scale_index, threshold):
    core, far = lax.axis_index("cfg"), lax.axis_index("zh")
    y, x, zl = lax.axis_index("y"), lax.axis_index("x"), lax.axis_index("zl")
    features = hidden[0].T

    def tokens_of(which):
        cut = [
            lax.dynamic_slice_in_dim(features, half * 512 + which * 256, 256, 1) for half in (1 - far, far)
        ]
        return jnp.concatenate(cut, 1)

    other = lax.ppermute(tokens_of(1 - core), "cfg", [(0, 1), (1, 0)])
    guide = 1.0 + 0.5 * lax.dynamic_slice_in_dim(scale_index, core * 256, 256, 0).astype(jnp.float32)
    limits = lax.dynamic_slice_in_dim(threshold, core * 256, 256, 0).astype(jnp.float32) / 8.0
    away_guide = lax.ppermute(guide, "zh", [(0, 1), (1, 0)])
    guides = jnp.concatenate([away_guide, guide])[None]

    mixed = mix(core[None], tokens_of(core), other, guides)
    near = [mixed] + [shifted(mixed, "zl", k) for k in (1, 2, 3)]
    place = jnp.stack([(zl - k) % 4 for k in range(4)])
    column = stack(place, near)

    line = [column] + [crossed(column, "x", "y", k) for k in (1, 2, 3)]
    index = []
    for k2 in range(4):
        for k1 in range(4):
            a = jnp.where(core == 0, y - k2, y - k1) % 4
            b = jnp.where(core == 0, x - k1, x - k2) % 4
            index.append(a * 4 + b)
    index = jnp.stack(index).astype(jnp.int32)

    def gathered(cut, after):
        block = jnp.concatenate([p[:, cut] for p in line], 0)
        if after is not None:
            block = lax.optimization_barrier((block, *after))[0]
        return [block] + [crossed(block, "y", "x", k) for k in (1, 2, 3)]

    away_parts = gathered(slice(0, 256), None)
    sent = product(index, head, away_parts, False)
    back = lax.ppermute(sent, "zh", [(0, 1), (1, 0)])
    home_parts = gathered(slice(256, 512), away_parts[1:])
    kept = product(index, head, home_parts, True)

    scale = scale_of(back[256, :256].astype(jnp.float32))
    guided = kept + back[:256].astype(jnp.float32) * scale[:, None]
    peak = jnp.max(guided, axis=1)
    expo = jnp.exp(guided - peak[:, None])
    stats = jnp.stack([peak, jnp.sum(expo, axis=1), jnp.sum(expo * guided, axis=1)])
    for axis in ("zl", "x", "y"):
        stats = merged([stats] + [shifted(stats, axis, k) for k in (1, 2, 3)])
    lse = stats[0] + jnp.log(stats[1])
    entropy = lse - stats[2] / stats[1]
    logprob = guided - lse[:, None]
    deviation = -logprob - entropy[:, None]
    typical = jax.nn.sigmoid(2.0 * (limits[:, None] - jnp.abs(deviation)))
    return logprob.astype(jnp.bfloat16), typical.astype(jnp.bfloat16), entropy


def solution(mesh):
    torus = Mesh(mesh.devices.reshape(SIZES), AXES)
    vocab = ("y", "x", "zl")
    return jax.shard_map(
        local,
        mesh=torus,
        in_specs=(P("cfg", None, ("zh", *vocab)), P("zh", vocab), P("zh"), P("zh")),
        out_specs=(P(("zh", "cfg"), vocab), P(("zh", "cfg"), vocab), P(("zh", "cfg"))),
        check_vma=False,
    )
```

time: 892 us -> 133 us (0.15); the launches traced: 882 us -> 132 us
  waiting for transfers between devices: 495 us -> 53.7 us
  blocking collectives: 354 us -> 0 us
  starting transfers between devices: 0.08 us -> 43.6 us
  Pallas kernels: 0 us -> 21.9 us
  matrix products: 15.1 us -> 0 us
  between operations: 14.1 us -> 0.85 us
    all_gather x1 -> x0, waiting for transfers between devices: 377 us -> none  [local(): lax.all_gather(rows_input, 'vocab', axis=1, tiled=True)]
    psum x1 -> x0, blocking collectives: 184 us -> none  [finish(): lax.psum((jnp.sum(expo, axis=1), jnp.sum(expo * guided, axis=1)), 'vocab')]
    pmax x1 -> x0, blocking collectives: 171 us -> none  [finish(): peak = lax.pmax(local_peak, 'vocab')]
    reduce_scatter x1 -> x0, waiting for transfers between devices: 114 us -> none  [local(): lax.psum_scatter(partial_sums, 'rows', scatter_dimension=0, tiled=True)]
    ppermute x1 -> x24, waiting for transfers between devices: 4.19 us -> 53.7 us  [the longest x9 25.8 us: crossed(): return lax.ppermute(block, axes, pairs(axes, move))]
    ppermute x1 -> x24, starting transfers between devices: 0.01 us -> 43.6 us  [the longest x12 19.9 us: shifted(): lax.ppermute(block, axis, pairs((axis,), lambda at: {axis: at[axis] + k}))]
    pallas_call x0 -> x4, Pallas kernels: none -> 21.9 us  [the longest x2 18.6 us: product(): pl.pallas_call(product_kernel, out_shape=out, grid_spec=pltpu.PrefetchSca...]
    dot_general x1 -> x0, matrix products: 15.1 us -> none  [local(): jnp.dot(lax.all_gather(rows_input, 'vocab', axis=1, tiled=True), head, pr...]
  transfers between devices with their start and end apart: 3 -> 24, of which waited for: 3 -> 14; matrix products, arithmetic and copies ran while one was open for 0% -> 3% of each run, Pallas kernels for 0% -> 0%
where the time goes in v1:
time: 133 us; the launch traced here: 132 us
  waiting for transfers between devices  53.7 us (40%)
  starting transfers between devices  43.6 us (33%)
  Pallas kernels  21.9 us (16%)
  local copies, waits for them, and re-layouts  7.25 us (5%)
  other arithmetic  4.91 us (4%)
    ppermute x9, waiting for transfers between devices, crossed(): return lax.ppermute(block, axes, pairs(axes, move))  25.8 us
    ppermute x12, starting transfers between devices, shifted(): lax.ppermute(block, axis, pairs((axis,), lambda at: {axis: at[axis] + k}))  19.9 us
    pallas_call x2, Pallas kernels, product(): pl.pallas_call(product_kernel, out_shape=out, grid_spec=pltpu.PrefetchSca...  18.6 us
    ppermute x12, waiting for transfers between devices, shifted(): lax.ppermute(block, axis, pairs((axis,), lambda at: {axis: at[axis] + k}))  16.9 us
    ppermute x9, starting transfers between devices, crossed(): return lax.ppermute(block, axes, pairs(axes, move))  11.7 us
    ppermute x1, waiting for transfers between devices, local(): back = lax.ppermute(sent, 'zh', [(0, 1), (1, 0)])  11 us
    ppermute x1, starting transfers between devices, local(): away_guide = lax.ppermute(guide, 'zh', [(0, 1), (1, 0)])  7.19 us
    unnamed x14, local copies, waits for them, and re-layouts  5.28 us
  transfers between devices with their start and end apart: 24, of which 14 were waited for; matrix products, arithmetic and copies ran while one was open for 3% of the time, Pallas kernels for 0%

profile of v1, /device:TPU:2, one launch (start us, length us, event | category | flops | bytes accessed | tf_op | source)
XLA Modules:
  0.0 132.2 jit_solution(7506647761034869595)
XLA Ops:
  1.4 7.2 %collective-permute-start.1 = (f32[256]{0:T(256)S(1)}, f32[256]{0:T(256)S(1)}, u32[]{:S(2)}, u32[]{:S(2)}) collective-permute-start(f32[256]{0:T(256)S(1)} %multiply_add_fusion.6), channel_id=1, source_target_pairs={{0,1},{1,0},{2,3},{3,2},{4,5},{5,4},{6,7},{7,6},{8,9},{9,8},{10,11... | collective-permute-start | bytes 3080 | tf_op jit(solution)/shard_map/ppermute | solution.py:196
  13.0 3.3 %collective-permute-start.4 = (s16[80,512]{1,0:T(8,128)(2,1)}, s16[80,512]{1,0:T(8,128)(2,1)S(1)}, u32[]{:S(2)}, u32[]{:S(2)}) collective-permute-start(s16[80,512]{1,0:T(8,128)(2,1)} %mix.1.a_ref), channel_id=1, source_target_pairs={{0,6},{2,0},{4,2},{6,4},{1,7},{3,1},{5,3},{7,5},{8,14},{10,8},{12,... | collective-permute-start | bytes 245768 | tf_op jit(solution)/shard_map/ppermute | solution.py:32
  17.6 1.8 %collective-permute-done.4.d_ref = s16[80,512]{1,0:T(8,128)(2,1)S(1)} collective-permute-done((s16[80,512]{1,0:T(8,128)(2,1)}, s16[80,512]{1,0:T(8,128)(2,1)S(1)}, u32[]{:S(2)}, u32[]{:S(2)}) %collective-permute-start.4) | collective-permute-done | bytes 81952 | tf_op jit(solution)/shard_map/ppermute | solution.py:32
  19.4 4.5 %collective-permute-done.3.c_ref = s16[80,512]{1,0:T(8,128)(2,1)S(1)} collective-permute-done((s16[80,512]{1,0:T(8,128)(2,1)}, s16[80,512]{1,0:T(8,128)(2,1)S(1)}, u32[]{:S(2)}, u32[]{:S(2)}) %collective-permute-start.3) | collective-permute-done | bytes 81952 | tf_op jit(solution)/shard_map/ppermute | solution.py:32
  25.1 1.7 %stack.119 = s16[272,512]{1,0:T(8,128)(2,1)} custom-call(s32[4]{0:T(128)} %pad_add_fusion.2.place_ref, s16[80,512]{1,0:T(8,128)(2,1)} %mix.1.a_ref, s16[80,512]{1,0:T(8,128)(2,1)} %copy-done.3, s16[80,512]{1,0:T(8,128)(2,1)} %copy-done.2, s16[80,512]{1,0:T(8,128)(2,1)} %copy-done.1), custom_call_target="tpu_custom_call" | custom-call | tf_op jit(solution)/shard_map/stack/pallas_call | solution.py:93
  27.4 2.4 %collective-permute-start.6 = (s16[272,512]{1,0:T(8,128)(2,1)}, s16[272,512]{1,0:T(8,128)(2,1)S(1)}, u32[]{:S(2)}, u32[]{:S(2)}) collective-permute-start(s16[272,512]{1,0:T(8,128)(2,1)} %stack.119), channel_id=1, source_target_pairs={{0,16},{8,24},{16,0},{24,8},{32,48},{40,56},{48,32},{56,40},{64,80... | collective-permute-start | bytes 835592 | tf_op jit(solution)/shard_map/ppermute | solution.py:42
  30.8 1.9 %collective-permute-start.5 = (s16[272,512]{1,0:T(8,128)(2,1)}, s16[272,512]{1,0:T(8,128)(2,1)S(1)}, u32[]{:S(2)}, u32[]{:S(2)}) collective-permute-start(s16[272,512]{1,0:T(8,128)(2,1)} %stack.119), channel_id=1, source_target_pairs={{0,8},{8,16},{16,24},{24,0},{32,40},{40,48},{48,56},{56,32},{64,72... | collective-permute-start | bytes 835592 | tf_op jit(solution)/shard_map/ppermute | solution.py:42
  33.6 3.9 %collective-permute-done.6 = s16[272,512]{1,0:T(8,128)(2,1)S(1)} collective-permute-done((s16[272,512]{1,0:T(8,128)(2,1)}, s16[272,512]{1,0:T(8,128)(2,1)S(1)}, u32[]{:S(2)}, u32[]{:S(2)}) %collective-permute-start.6) | collective-permute-done | bytes 278560 | tf_op jit(solution)/shard_map/ppermute | solution.py:42
  38.7 3.1 %collective-permute-start.10 = (s16[1088,256]{1,0:T(8,128)(2,1)S(1)}, s16[1088,256]{1,0:T(8,128)(2,1)S(1)}, u32[]{:S(2)}, u32[]{:S(2)}) collective-permute-start(s16[1088,256]{1,0:T(8,128)(2,1)S(1)} %pad_add_fusion.1.refs_0_), channel_id=1, source_target_pairs={{0,96},{8,104},{16,112},{24,120},{32,0},{40,8},{48,16},{56,24},{64... | collective-permute-start | bytes 1671176 | tf_op jit(solution)/shard_map/ppermute | solution.py:42
  43.5 11.3 %collective-permute-done.10.refs_3_ = s16[1088,256]{1,0:T(8,128)(2,1)S(1)} collective-permute-done((s16[1088,256]{1,0:T(8,128)(2,1)S(1)}, s16[1088,256]{1,0:T(8,128)(2,1)S(1)}, u32[]{:S(2)}, u32[]{:S(2)}) %collective-permute-start.10) | collective-permute-done | bytes 557088 | tf_op jit(solution)/shard_map/ppermute | solution.py:42
  54.9 4.0 %collective-permute-done.8.refs_1_ = s16[1088,256]{1,0:T(8,128)(2,1)S(1)} collective-permute-done((s16[1088,256]{1,0:T(8,128)(2,1)S(1)}, s16[1088,256]{1,0:T(8,128)(2,1)S(1)}, u32[]{:S(2)}, u32[]{:S(2)}) %collective-permute-start.8) | collective-permute-done | bytes 557088 | tf_op jit(solution)/shard_map/ppermute | solution.py:42
  58.8 3.4 %copy-done = bf16[4096,1024]{1,0:T(8,128)(2,1)S(1)} copy-done((bf16[4096,1024]{1,0:T(8,128)(2,1)S(1)}, bf16[4096,1024]{1,0:T(8,128)(2,1)}, u32[]{:S(2)}) %copy-start) | copy-done | bytes 8388632
  62.2 9.4 %product.3 = s16[272,1024]{1,0:T(8,128)(2,1)S(1)} custom-call(s32[16]{0:T(128)S(1)} %stack.107.index_ref, bf16[4096,1024]{1,0:T(8,128)(2,1)S(1)} %copy-done, s16[1088,256]{1,0:T(8,128)(2,1)S(1)} %pad_add_fusion.1.refs_0_, s16[1088,256]{1,0:T(8,128)(2,1)S(1)} %collective-permute-done.8.refs_1_, s16[1088,256]{1,0:T(8,128)(2,1)S(1)} %collective-permute-done.9.refs_2_, ...), custom_call_target="tpu_custom_call" | custom-call | flops 4294967296 | bytes 10485760 | tf_op jit(solution)/shard_map/product/pallas_call | solution.py:151
  71.6 4.8 %collective-permute-start.14 = (s16[272,1024]{1,0:T(8,128)(2,1)S(1)}, s16[272,1024]{1,0:T(8,128)(2,1)S(1)}, u32[]{:S(2)}, u32[]{:S(2)}) collective-permute-start(s16[272,1024]{1,0:T(8,128)(2,1)S(1)} %product.3), channel_id=1, source_target_pairs={{0,1},{1,0},{2,3},{3,2},{4,5},{5,4},{6,7},{7,6},{8,9},{9,8},{10,11... | collective-permute-start | bytes 1671176 | tf_op jit(solution)/shard_map/ppermute | solution.py:221
  78.6 11.0 %collective-permute-done.14 = s16[272,1024]{1,0:T(8,128)(2,1)S(1)} collective-permute-done((s16[272,1024]{1,0:T(8,128)(2,1)S(1)}, s16[272,1024]{1,0:T(8,128)(2,1)S(1)}, u32[]{:S(2)}, u32[]{:S(2)}) %collective-permute-start.14) | collective-permute-done | bytes 557088 | tf_op jit(solution)/shard_map/ppermute | solution.py:221
  89.7 4.5 %collective-permute-done.11.refs_1_ = s16[1088,256]{1,0:T(8,128)(2,1)S(1)} collective-permute-done((s16[1088,256]{1,0:T(8,128)(2,1)S(1)}, s16[1088,256]{1,0:T(8,128)(2,1)S(1)}, u32[]{:S(2)}, u32[]{:S(2)}) %collective-permute-start.11) | collective-permute-done | bytes 557088 | tf_op jit(solution)/shard_map/ppermute | solution.py:42
  94.2 9.2 %product.2 = f32[256,1024]{1,0:T(8,128)S(1)} custom-call(s32[16]{0:T(128)S(1)} %stack.107.index_ref, bf16[4096,1024]{1,0:T(8,128)(2,1)S(1)} %copy-done, s16[1088,256]{1,0:T(8,128)(2,1)S(1)} %pad_add_fusion.refs_0_, s16[1088,256]{1,0:T(8,128)(2,1)S(1)} %collective-permute-done.11.refs_1_, s16[1088,256]{1,0:T(8,128)(2,1)S(1)} %collective-permute-done.12.refs_2_, ...), custom_call_target="tpu_custom_call" | custom-call | flops 4294967296 | bytes 10485760 | tf_op jit(solution)/shard_map/product/pallas_call | solution.py:151
  105.6 5.4 %collective-permute-start.16 = (f32[3,256]{1,0:T(4,128)S(1)}, f32[3,256]{1,0:T(4,128)S(1)}, u32[]{:S(2)}, u32[]{:S(2)}) collective-permute-start(f32[3,256]{1,0:T(4,128)S(1)} %pad_maximum_fusion.2), channel_id=1, source_target_pairs={{0,4},{2,6},{4,0},{6,2},{1,5},{3,7},{5,1},{7,3},{8,12},{10,14},{12... | collective-permute-start | bytes 9224 | tf_op jit(solution)/shard_map/ppermute | solution.py:32
  111.0 1.9 %collective-permute-start.15 = (f32[3,256]{1,0:T(4,128)S(1)}, f32[3,256]{1,0:T(4,128)S(1)}, u32[]{:S(2)}, u32[]{:S(2)}) collective-permute-start(f32[3,256]{1,0:T(4,128)S(1)} %pad_maximum_fusion.2), channel_id=1, source_target_pairs={{0,2},{2,4},{4,6},{6,0},{1,3},{3,5},{5,7},{7,1},{8,10},{10,12},{12... | collective-permute-start | bytes 9224 | tf_op jit(solution)/shard_map/ppermute | solution.py:32
  113.0 3.5 %collective-permute-done.15 = f32[3,256]{1,0:T(4,128)S(1)} collective-permute-done((f32[3,256]{1,0:T(4,128)S(1)}, f32[3,256]{1,0:T(4,128)S(1)}, u32[]{:S(2)}, u32[]{:S(2)}) %collective-permute-start.15) | collective-permute-done | bytes 3104 | tf_op jit(solution)/shard_map/ppermute | solution.py:32
  116.5 2.8 %collective-permute-start.20 = (f32[3,256]{1,0:T(4,128)S(1)}, f32[3,256]{1,0:T(4,128)S(1)}, u32[]{:S(2)}, u32[]{:S(2)}) collective-permute-start(f32[3,256]{1,0:T(4,128)S(1)} %pad_maximum_fusion.3), channel_id=1, source_target_pairs={{0,24},{8,0},{16,8},{24,16},{1,25},{9,1},{17,9},{25,17},{2,26},{10... | collective-permute-start | bytes 9224 | tf_op jit(solution)/shard_map/ppermute | solution.py:32
  119.5 1.9 %collective-permute-start.18 = (f32[3,256]{1,0:T(4,128)S(1)}, f32[3,256]{1,0:T(4,128)S(1)}, u32[]{:S(2)}, u32[]{:S(2)}) collective-permute-start(f32[3,256]{1,0:T(4,128)S(1)} %pad_maximum_fusion.3), channel_id=1, source_target_pairs={{0,8},{8,16},{16,24},{24,0},{1,9},{9,17},{17,25},{25,1},{2,10},{10... | collective-permute-start | bytes 9224 | tf_op jit(solution)/shard_map/ppermute | solution.py:32
  121.3 3.0 %collective-permute-done.19 = f32[3,256]{1,0:T(4,128)S(1)} collective-permute-done((f32[3,256]{1,0:T(4,128)S(1)}, f32[3,256]{1,0:T(4,128)S(1)}, u32[]{:S(2)}, u32[]{:S(2)}) %collective-permute-start.19) | collective-permute-done | bytes 3104 | tf_op jit(solution)/shard_map/ppermute | solution.py:32
  128.1 2.5 %collective-permute-done.22 = f32[3,256]{1,0:T(4,128)S(1)} collective-permute-done((f32[3,256]{1,0:T(4,128)S(1)}, f32[3,256]{1,0:T(4,128)S(1)}, u32[]{:S(2)}, u32[]{:S(2)}) %collective-permute-start.22) | collective-permute-done | bytes 3104 | tf_op jit(solution)/shard_map/ppermute | solution.py:32
  (72 shorter events, 23.1 us)
Async XLA Ops:
  1.4 8.8 %collective-permute-start.1 = (f32[256]{0:T(256)S(1)}, f32[256]{0:T(256)S(1)}, u32[]{:S(2)}, u32[]{:S(2)}) collective-permute-start(f32[256]{0:T(256)S(1)} %multiply_add_fusion.6), channel_id=1, source_target_pairs={{0,1},{1,0},{2,3},{3,2},{4,5},{5,4},{6,7},{7,6},{8,9},{9,8},{10,11... | collective-permute-start | bytes 3080 | tf_op jit(solution)/shard_map/ppermute | solution.py:196
  9.4 1.4 %collective-permute-start = (bf16[64,512]{1,0:T(8,128)(2,1)S(1)}, bf16[64,512]{1,0:T(8,128)(2,1)S(1)}, u32[]{:S(2)}, u32[]{:S(2)}) collective-permute-start(bf16[64,512]{1,0:T(8,128)(2,1)S(1)} %pad_maximum_fusion.1), channel_id=1, source_target_pairs={{0,128},{128,0},{1,129},{129,1},{2,130},{130,2},{3,131},{131,3},{4... | collective-permute-start | bytes 196616 | tf_op jit(solution)/shard_map/ppermute | solution.py:193
  13.0 6.4 %collective-permute-start.4 = (s16[80,512]{1,0:T(8,128)(2,1)}, s16[80,512]{1,0:T(8,128)(2,1)S(1)}, u32[]{:S(2)}, u32[]{:S(2)}) collective-permute-start(s16[80,512]{1,0:T(8,128)(2,1)} %mix.1.a_ref), channel_id=1, source_target_pairs={{0,6},{2,0},{4,2},{6,4},{1,7},{3,1},{5,3},{7,5},{8,14},{10,8},{12,... | collective-permute-start | bytes 245768 | tf_op jit(solution)/shard_map/ppermute | solution.py:32
  16.3 7.5 %collective-permute-start.3 = (s16[80,512]{1,0:T(8,128)(2,1)}, s16[80,512]{1,0:T(8,128)(2,1)S(1)}, u32[]{:S(2)}, u32[]{:S(2)}) collective-permute-start(s16[80,512]{1,0:T(8,128)(2,1)} %mix.1.a_ref), channel_id=1, source_target_pairs={{0,4},{2,6},{4,0},{6,2},{1,5},{3,7},{5,1},{7,3},{8,12},{10,14},{12... | collective-permute-start | bytes 245768 | tf_op jit(solution)/shard_map/ppermute | solution.py:32
  16.3 7.5 %collective-permute-start.2 = (s16[80,512]{1,0:T(8,128)(2,1)}, s16[80,512]{1,0:T(8,128)(2,1)S(1)}, u32[]{:S(2)}, u32[]{:S(2)}) collective-permute-start(s16[80,512]{1,0:T(8,128)(2,1)} %mix.1.a_ref), channel_id=1, source_target_pairs={{0,2},{2,4},{4,6},{6,0},{1,3},{3,5},{5,7},{7,1},{8,10},{10,12},{12... | collective-permute-start | bytes 245768 | tf_op jit(solution)/shard_map/ppermute | solution.py:32
  26.9 6.8 %collective-permute-start.7 = (s16[272,512]{1,0:T(8,128)(2,1)}, s16[272,512]{1,0:T(8,128)(2,1)S(1)}, u32[]{:S(2)}, u32[]{:S(2)}) collective-permute-start(s16[272,512]{1,0:T(8,128)(2,1)} %stack.119), channel_id=1, source_target_pairs={{0,24},{8,0},{16,8},{24,16},{32,56},{40,32},{48,40},{56,48},{64,88... | collective-permute-start | bytes 835592 | tf_op jit(solution)/shard_map/ppermute | solution.py:42
  27.4 10.1 %collective-permute-start.6 = (s16[272,512]{1,0:T(8,128)(2,1)}, s16[272,512]{1,0:T(8,128)(2,1)S(1)}, u32[]{:S(2)}, u32[]{:S(2)}) collective-permute-start(s16[272,512]{1,0:T(8,128)(2,1)} %stack.119), channel_id=1, source_target_pairs={{0,16},{8,24},{16,0},{24,8},{32,48},{40,56},{48,32},{56,40},{64,80... | collective-permute-start | bytes 835592 | tf_op jit(solution)/shard_map/ppermute | solution.py:42
  30.8 7.9 %collective-permute-start.5 = (s16[272,512]{1,0:T(8,128)(2,1)}, s16[272,512]{1,0:T(8,128)(2,1)S(1)}, u32[]{:S(2)}, u32[]{:S(2)}) collective-permute-start(s16[272,512]{1,0:T(8,128)(2,1)} %stack.119), channel_id=1, source_target_pairs={{0,8},{8,16},{16,24},{24,0},{32,40},{40,48},{48,56},{56,32},{64,72... | collective-permute-start | bytes 835592 | tf_op jit(solution)/shard_map/ppermute | solution.py:42
  38.7 16.1 %collective-permute-start.10 = (s16[1088,256]{1,0:T(8,128)(2,1)S(1)}, s16[1088,256]{1,0:T(8,128)(2,1)S(1)}, u32[]{:S(2)}, u32[]{:S(2)}) collective-permute-start(s16[1088,256]{1,0:T(8,128)(2,1)S(1)} %pad_add_fusion.1.refs_0_), channel_id=1, source_target_pairs={{0,96},{8,104},{16,112},{24,120},{32,0},{40,8},{48,16},{56,24},{64... | collective-permute-start | bytes 1671176 | tf_op jit(solution)/shard_map/ppermute | solution.py:42
  41.8 13.0 %collective-permute-start.9 = (s16[1088,256]{1,0:T(8,128)(2,1)S(1)}, s16[1088,256]{1,0:T(8,128)(2,1)S(1)}, u32[]{:S(2)}, u32[]{:S(2)}) collective-permute-start(s16[1088,256]{1,0:T(8,128)(2,1)S(1)} %pad_add_fusion.1.refs_0_), channel_id=1, source_target_pairs={{0,64},{8,72},{16,80},{24,88},{32,96},{40,104},{48,112},{56,120},{... | collective-permute-start | bytes 1671176 | tf_op jit(solution)/shard_map/ppermute | solution.py:42
  42.5 16.4 %collective-permute-start.8 = (s16[1088,256]{1,0:T(8,128)(2,1)S(1)}, s16[1088,256]{1,0:T(8,128)(2,1)S(1)}, u32[]{:S(2)}, u32[]{:S(2)}) collective-permute-start(s16[1088,256]{1,0:T(8,128)(2,1)S(1)} %pad_add_fusion.1.refs_0_), channel_id=1, source_target_pairs={{0,32},{8,40},{16,48},{24,56},{32,64},{40,72},{48,80},{56,88},{64,... | collective-permute-start | bytes 1671176 | tf_op jit(solution)/shard_map/ppermute | solution.py:42
  71.6 18.0 %collective-permute-start.14 = (s16[272,1024]{1,0:T(8,128)(2,1)S(1)}, s16[272,1024]{1,0:T(8,128)(2,1)S(1)}, u32[]{:S(2)}, u32[]{:S(2)}) collective-permute-start(s16[272,1024]{1,0:T(8,128)(2,1)S(1)} %product.3), channel_id=1, source_target_pairs={{0,1},{1,0},{2,3},{3,2},{4,5},{5,4},{6,7},{7,6},{8,9},{9,8},{10,11... | collective-permute-start | bytes 1671176 | tf_op jit(solution)/shard_map/ppermute | solution.py:221
  76.5 13.2 %collective-permute-start.13 = (s16[1088,256]{1,0:T(8,128)(2,1)S(1)}, s16[1088,256]{1,0:T(8,128)(2,1)S(1)}, u32[]{:S(2)}, u32[]{:S(2)}) collective-permute-start(s16[1088,256]{1,0:T(8,128)(2,1)S(1)} %pad_add_fusion.refs_0_), channel_id=1, source_target_pairs={{0,96},{8,104},{16,112},{24,120},{32,0},{40,8},{48,16},{56,24},{64... | collective-permute-start | bytes 1671176 | tf_op jit(solution)/shard_map/ppermute | solution.py:42
  77.2 12.5 %collective-permute-start.12 = (s16[1088,256]{1,0:T(8,128)(2,1)S(1)}, s16[1088,256]{1,0:T(8,128)(2,1)S(1)}, u32[]{:S(2)}, u32[]{:S(2)}) collective-permute-start(s16[1088,256]{1,0:T(8,128)(2,1)S(1)} %pad_add_fusion.refs_0_), channel_id=1, source_target_pairs={{0,64},{8,72},{16,80},{24,88},{32,96},{40,104},{48,112},{56,120},{... | collective-permute-start | bytes 1671176 | tf_op jit(solution)/shard_map/ppermute | solution.py:42
  77.8 16.4 %collective-permute-start.11 = (s16[1088,256]{1,0:T(8,128)(2,1)S(1)}, s16[1088,256]{1,0:T(8,128)(2,1)S(1)}, u32[]{:S(2)}, u32[]{:S(2)}) collective-permute-start(s16[1088,256]{1,0:T(8,128)(2,1)S(1)} %pad_add_fusion.refs_0_), channel_id=1, source_target_pairs={{0,32},{8,40},{16,48},{24,56},{32,64},{40,72},{48,80},{56,88},{64,... | collective-permute-start | bytes 1671176 | tf_op jit(solution)/shard_map/ppermute | solution.py:42
  104.1 8.9 %collective-permute-start.17 = (f32[3,256]{1,0:T(4,128)S(1)}, f32[3,256]{1,0:T(4,128)S(1)}, u32[]{:S(2)}, u32[]{:S(2)}) collective-permute-start(f32[3,256]{1,0:T(4,128)S(1)} %pad_maximum_fusion.2), channel_id=1, source_target_pairs={{0,6},{2,0},{4,2},{6,4},{1,7},{3,1},{5,3},{7,5},{8,14},{10,8},{12,... | collective-permute-start | bytes 9224 | tf_op jit(solution)/shard_map/ppermute | solution.py:32
  105.6 7.4 %collective-permute-start.16 = (f32[3,256]{1,0:T(4,128)S(1)}, f32[3,256]{1,0:T(4,128)S(1)}, u32[]{:S(2)}, u32[]{:S(2)}) collective-permute-start(f32[3,256]{1,0:T(4,128)S(1)} %pad_maximum_fusion.2), channel_id=1, source_target_pairs={{0,4},{2,6},{4,0},{6,2},{1,5},{3,7},{5,1},{7,3},{8,12},{10,14},{12... | collective-permute-start | bytes 9224 | tf_op jit(solution)/shard_map/ppermute | solution.py:32
  111.0 5.4 %collective-permute-start.15 = (f32[3,256]{1,0:T(4,128)S(1)}, f32[3,256]{1,0:T(4,128)S(1)}, u32[]{:S(2)}, u32[]{:S(2)}) collective-permute-start(f32[3,256]{1,0:T(4,128)S(1)} %pad_maximum_fusion.2), channel_id=1, source_target_pairs={{0,2},{2,4},{4,6},{6,0},{1,3},{3,5},{5,7},{7,1},{8,10},{10,12},{12... | collective-permute-start | bytes 9224 | tf_op jit(solution)/shard_map/ppermute | solution.py:32
  116.5 4.8 %collective-permute-start.20 = (f32[3,256]{1,0:T(4,128)S(1)}, f32[3,256]{1,0:T(4,128)S(1)}, u32[]{:S(2)}, u32[]{:S(2)}) collective-permute-start(f32[3,256]{1,0:T(4,128)S(1)} %pad_maximum_fusion.3), channel_id=1, source_target_pairs={{0,24},{8,0},{16,8},{24,16},{1,25},{9,1},{17,9},{25,17},{2,26},{10... | collective-permute-start | bytes 9224 | tf_op jit(solution)/shard_map/ppermute | solution.py:32
  119.3 5.1 %collective-permute-start.19 = (f32[3,256]{1,0:T(4,128)S(1)}, f32[3,256]{1,0:T(4,128)S(1)}, u32[]{:S(2)}, u32[]{:S(2)}) collective-permute-start(f32[3,256]{1,0:T(4,128)S(1)} %pad_maximum_fusion.3), channel_id=1, source_target_pairs={{0,16},{8,24},{16,0},{24,8},{1,17},{9,25},{17,1},{25,9},{2,18},{10... | collective-permute-start | bytes 9224 | tf_op jit(solution)/shard_map/ppermute | solution.py:32
  119.5 4.9 %collective-permute-start.18 = (f32[3,256]{1,0:T(4,128)S(1)}, f32[3,256]{1,0:T(4,128)S(1)}, u32[]{:S(2)}, u32[]{:S(2)}) collective-permute-start(f32[3,256]{1,0:T(4,128)S(1)} %pad_maximum_fusion.3), channel_id=1, source_target_pairs={{0,8},{8,16},{16,24},{24,0},{1,9},{9,17},{17,25},{25,1},{2,10},{10... | collective-permute-start | bytes 9224 | tf_op jit(solution)/shard_map/ppermute | solution.py:32
  124.4 3.7 %collective-permute-start.23 = (f32[3,256]{1,0:T(4,128)S(1)}, f32[3,256]{1,0:T(4,128)S(1)}, u32[]{:S(2)}, u32[]{:S(2)}) collective-permute-start(f32[3,256]{1,0:T(4,128)S(1)} %pad_maximum_fusion.4), channel_id=1, source_target_pairs={{0,96},{32,0},{64,32},{96,64},{1,97},{33,1},{65,33},{97,65},{2,98}... | collective-permute-start | bytes 9224 | tf_op jit(solution)/shard_map/ppermute | solution.py:32
  125.5 5.1 %collective-permute-start.22 = (f32[3,256]{1,0:T(4,128)S(1)}, f32[3,256]{1,0:T(4,128)S(1)}, u32[]{:S(2)}, u32[]{:S(2)}) collective-permute-start(f32[3,256]{1,0:T(4,128)S(1)} %pad_maximum_fusion.4), channel_id=1, source_target_pairs={{0,64},{32,96},{64,0},{96,32},{1,65},{33,97},{65,1},{97,33},{2,66}... | collective-permute-start | bytes 9224 | tf_op jit(solution)/shard_map/ppermute | solution.py:32
  125.9 4.9 %collective-permute-start.21 = (f32[3,256]{1,0:T(4,128)S(1)}, f32[3,256]{1,0:T(4,128)S(1)}, u32[]{:S(2)}, u32[]{:S(2)}) collective-permute-start(f32[3,256]{1,0:T(4,128)S(1)} %pad_maximum_fusion.4), channel_id=1, source_target_pairs={{0,32},{32,64},{64,96},{96,0},{1,33},{33,65},{65,97},{97,1},{2,34}... | collective-permute-start | bytes 9224 | tf_op jit(solution)/shard_map/ppermute | solution.py:32
  (7 other events, 46.9 us)

commit v2 on v1

v2 whole, which is shorter than its diff:
```python
import math

import jax
import jax.numpy as jnp
from jax import lax
from jax.experimental import pallas as pl
from jax.experimental.pallas import tpu as pltpu
from jax.sharding import Mesh, PartitionSpec as P

AXES = ("cfg", "y", "x", "zl", "zh")
SIZES = (2, 4, 4, 4, 2)
TOP = 32767.0
STEP = math.log(2.0) / 256.0


def pairs(axes, move):
    dims = [SIZES[AXES.index(a)] for a in axes]
    route = []
    for i in range(math.prod(dims)):
        rest, at = i, {}
        for a, n in reversed(list(zip(axes, dims))):
            at[a], rest = rest % n, rest // n
        to = move(dict(at))
        j = 0
        for a, n in zip(axes, dims):
            j = j * n + to[a] % n
        route.append((i, j))
    return route


def shifted(block, axis, k):
    return lax.ppermute(block, axis, pairs((axis,), lambda at: {axis: at[axis] + k}))


def crossed(block, first, second, k):
    def move(at):
        along = first if at["cfg"] == 0 else second
        at[along] += k
        return at

    axes = ("cfg", "y", "x")
    return lax.ppermute(block, axes, pairs(axes, move))


def code_of(largest):
    return jnp.ceil(jnp.log(jnp.maximum(largest, 1e-30)) * (1.0 / STEP)) + 1.0


def scale_of(code):
    return jnp.exp(code * STEP) * (1.0 / TOP)


def coded(values, scale):
    return jnp.clip(jnp.round(values / scale), -TOP, TOP).astype(jnp.int32).astype(jnp.int16)


def in_vmem(count):
    return [pl.BlockSpec(memory_space=pltpu.VMEM)] * count


def room(mib):
    return pltpu.CompilerParams(vmem_limit_bytes=mib << 20)


def load_kernel(*refs):
    count = len(refs) // 2
    loads = [pltpu.make_async_copy(refs[i], refs[count + i], refs[-1].at[i]) for i in range(count)]
    for load in loads:
        load.start()
    for load in loads:
        load.wait()


def load(*arrays):
    return pl.pallas_call(
        load_kernel,
        out_shape=[jax.ShapeDtypeStruct(a.shape, a.dtype) for a in arrays],
        in_specs=[pl.BlockSpec(memory_space=pl.ANY)] * len(arrays),
        out_specs=in_vmem(len(arrays)),
        scratch_shapes=[pltpu.SemaphoreType.DMA((len(arrays),))],
        compiler_params=room(50),
        cost_estimate=pl.CostEstimate(flops=0, bytes_accessed=16 << 20, transcendentals=0),
        name="load",
    )(*arrays)


def mix_kernel(place_ref, own_ref, other_ref, own_scale_ref, away_scale_ref, out_ref):
    core, far = place_ref[0], place_ref[1]
    first = core == 0
    for n, half in enumerate((1 - far, far)):
        cut = pl.ds(pl.multiple_of(half * 512 + core * 256, 256), 256)
        scale_ref = away_scale_ref if n == 0 else own_scale_ref
        scales = scale_ref[:, pl.ds(pl.multiple_of(core * 256, 256), 256)]
        guide = 1.0 + 0.5 * scales.astype(jnp.float32)
        own = own_ref[:, cut].astype(jnp.float32)
        other = other_ref[:, cut].astype(jnp.float32)
        cond = jnp.where(first, own, other)
        uncond = jnp.where(first, other, own)
        mixed = uncond + guide * (cond - uncond)
        code = code_of(jnp.max(jnp.abs(mixed), axis=0, keepdims=True))
        at = slice(256 * n, 256 * n + 256)
        out_ref[:64, at] = coded(mixed, scale_of(code))
        out_ref[64:, at] = jnp.broadcast_to(code, (16, 256)).astype(jnp.int32).astype(jnp.int16)


def mix(place, own, other, own_scale, away_scale):
    return pl.pallas_call(
        mix_kernel,
        out_shape=jax.ShapeDtypeStruct((80, 512), jnp.int16),
        in_specs=[pl.BlockSpec(memory_space=pltpu.SMEM)] + in_vmem(4),
        out_specs=in_vmem(1)[0],
        compiler_params=room(4),
        name="mix",
    )(place, own, other, own_scale, away_scale)


def stack_kernel(place_ref, a_ref, b_ref, c_ref, d_ref, *out_refs):
    row = lax.broadcasted_iota(jnp.int32, (16, 256), 0)
    for n, out_ref in enumerate(out_refs):
        at = slice(256 * n, 256 * n + 256)
        codes = jnp.zeros((16, 256), jnp.int32)
        for k, ref in enumerate((a_ref, b_ref, c_ref, d_ref)):
            place = place_ref[k]
            out_ref[pl.ds(pl.multiple_of(place * 64, 64), 64), :] = ref[:64, at]
            codes = jnp.where(row == place, ref[64:, at].astype(jnp.int32), codes)
        out_ref[256:] = codes.astype(jnp.int16)


def stack(place, parts):
    return pl.pallas_call(
        stack_kernel,
        out_shape=[jax.ShapeDtypeStruct((272, 256), jnp.int16)] * 2,
        in_specs=[pl.BlockSpec(memory_space=pltpu.SMEM)] + in_vmem(4),
        out_specs=in_vmem(2),
        compiler_params=room(4),
        name="stack",
    )(place, *parts)


def product_kernel(index_ref, head_ref, *refs):
    parts, out_ref, total_ref = refs[:4], refs[4], refs[5]
    count = total_ref.shape[0] // 2
    dims = (((0,), (0,)), ((), ()))
    for k, part in enumerate(parts):
        total = None
        for piece in range(4):
            base = 272 * piece
            scale = scale_of(part[base + 256 : base + 272].astype(jnp.float32))
            high, low = [], []
            for j in range(4):
                values = part[base + 64 * j : base + 64 * j + 64].astype(jnp.float32) * scale[j : j + 1]
                top = values.astype(jnp.bfloat16)
                high.append(top)
                low.append((values - top.astype(jnp.float32)).astype(jnp.bfloat16))
            both = jnp.concatenate([jnp.concatenate(high, 0), jnp.concatenate(low, 0)], 1)
            weight = head_ref[pl.ds(pl.multiple_of(index_ref[4 * k + piece] * 256, 256), 256), :]
            term = lax.dot_general(both, weight, dims, preferred_element_type=jnp.float32)
            total = term if total is None else total + term
        if k == 0:
            total_ref[...] = total
        else:
            total_ref[...] += total
    total = total_ref[:count] + total_ref[count:]
    if out_ref.dtype == jnp.float32:
        out_ref[...] = total
    else:
        code = code_of(jnp.max(jnp.abs(total), axis=1, keepdims=True))
        out_ref[:count] = coded(total, scale_of(code))
        across = jnp.transpose(jnp.broadcast_to(code, (count, 128)))[:16]
        out_ref[count:] = jnp.zeros((16, total.shape[1]), jnp.int16)
        out_ref[count:, :count] = across.astype(jnp.int32).astype(jnp.int16)


def product(index, head, parts, keep):
    tokens, width = parts[0].shape[1], head.shape[1]
    out = (
        jax.ShapeDtypeStruct((tokens, width), jnp.float32)
        if keep
        else jax.ShapeDtypeStruct((tokens + 16, width), jnp.int16)
    )
    return pl.pallas_call(
        product_kernel,
        out_shape=out,
        in_specs=[pl.BlockSpec(memory_space=pltpu.SMEM)] + in_vmem(5),
        out_specs=in_vmem(1)[0],
        scratch_shapes=[pltpu.VMEM((2 * tokens, width), jnp.float32)],
        compiler_params=room(24),
        cost_estimate=pl.CostEstimate(
            flops=4 * tokens * 4096 * width, bytes_accessed=10 << 20, transcendentals=0
        ),
        name="product",
    )(index, head, *parts)


def join_kernel(kept_ref, back_ref, guided_ref, stats_ref):
    count = kept_ref.shape[0]
    codes = back_ref[count:, :count].astype(jnp.float32)[:1]
    scale = jnp.transpose(jnp.broadcast_to(scale_of(codes), (128, count)))[:, :1]
    guided = kept_ref[...] + back_ref[:count].astype(jnp.float32) * scale
    peak = jnp.max(guided, axis=1, keepdims=True)
    expo = jnp.exp(guided - peak)
    total = jnp.sum(expo, axis=1, keepdims=True)
    moment = jnp.sum(expo * guided, axis=1, keepdims=True)
    lane = lax.broadcasted_iota(jnp.int32, (count, 128), 1)
    table = jnp.where(lane == 0, peak, jnp.where(lane == 1, total, moment))
    stats_ref[...] = jnp.transpose(table)[:8]
    guided_ref[...] = guided


def join(kept, back):
    return pl.pallas_call(
        join_kernel,
        out_shape=(
            jax.ShapeDtypeStruct(kept.shape, jnp.float32),
            jax.ShapeDtypeStruct((8, kept.shape[0]), jnp.float32),
        ),
        in_specs=in_vmem(2),
        out_specs=in_vmem(2),
        compiler_params=room(12),
        name="join",
    )(kept, back)


def merged(stats):
    peak = stats[0][:1]
    for s in stats[1:]:
        peak = jnp.maximum(peak, s[:1])
    total = moment = 0.0
    for s in stats:
        weight = jnp.exp(s[:1] - peak)
        total += s[1:2] * weight
        moment += s[2:3] * weight
    return jnp.concatenate([peak, total, moment, stats[0][3:]])


def local(hidden, head, scale_index, threshold):
    core, far = lax.axis_index("cfg"), lax.axis_index("zh")
    y, x, zl = lax.axis_index("y"), lax.axis_index("x"), lax.axis_index("zl")
    features = hidden[0].T
    other = lax.ppermute(features, "cfg", [(0, 1), (1, 0)])
    away_scale = lax.ppermute(scale_index, "zh", [(0, 1), (1, 0)])
    limits = lax.dynamic_slice_in_dim(threshold, core * 256, 256, 0).astype(jnp.float32) / 8.0

    head, own, own_scale = load(head, features, scale_index[None])
    mixed = mix(jnp.stack([core, far]), own, other, own_scale, away_scale[None])
    mixed, head = lax.optimization_barrier((mixed, head))
    near = [mixed] + [shifted(mixed, "zl", k) for k in (1, 2, 3)]
    place = jnp.stack([(zl - k) % 4 for k in range(4)])
    away_column, home_column = stack(place, near)

    index = []
    for k2 in range(4):
        for k1 in range(4):
            a = jnp.where(core == 0, y - k2, y - k1) % 4
            b = jnp.where(core == 0, x - k1, x - k2) % 4
            index.append(a * 4 + b)
    index = jnp.stack(index).astype(jnp.int32)

    def spread(block, first, second):
        return [block] + [crossed(block, first, second, k) for k in (1, 2, 3)]

    away_line = spread(away_column, "x", "y")
    away_parts = spread(jnp.concatenate(away_line, 0), "y", "x")
    home_column = lax.optimization_barrier((home_column, *away_line))[0]
    home_line = spread(home_column, "x", "y")
    sent = product(index, head, away_parts, False)
    home_block = jnp.concatenate(home_line, 0)
    home_block = lax.optimization_barrier((home_block, *away_parts))[0]
    home_parts = spread(home_block, "y", "x")
    back = lax.ppermute(sent, "zh", [(0, 1), (1, 0)])
    kept = product(index, head, home_parts, True)

    guided, stats = join(kept, back)
    for axis in ("zl", "x", "y"):
        stats = merged([stats] + [shifted(stats, axis, k) for k in (1, 2, 3)])
    lse = stats[0] + jnp.log(stats[1])
    entropy = lse - stats[2] / stats[1]
    logprob = guided - lse[:, None]
    deviation = -logprob - entropy[:, None]
    typical = jax.nn.sigmoid(2.0 * (limits[:, None] - jnp.abs(deviation)))
    return logprob.astype(jnp.bfloat16), typical.astype(jnp.bfloat16), entropy


def solution(mesh):
    torus = Mesh(mesh.devices.reshape(SIZES), AXES)
    vocab = ("y", "x", "zl")
    return jax.shard_map(
        local,
        mesh=torus,
        in_specs=(P("cfg", None, ("zh", *vocab)), P("zh", vocab), P("zh"), P("zh")),
        out_specs=(P(("zh", "cfg"), vocab), P(("zh", "cfg"), vocab), P(("zh", "cfg"))),
        check_vma=False,
    )
```

time: 133 us -> 123 us (0.925)
  waiting for transfers between devices: 53.7 us -> 48 us
  starting transfers between devices: 43.6 us -> 47.9 us
  other arithmetic: 4.91 us -> 1.68 us
  Pallas kernels: 21.9 us -> 18.9 us
  local copies, waits for them, and re-layouts: 7.25 us -> 5.11 us
    ppermute x12, starting transfers between devices: 19.9 us -> 23.9 us  [shifted(): lax.ppermute(block, axis, pairs((axis,), lambda at: {axis: at[axis] + k}))]
    ppermute x1, waiting for transfers between devices: 11 us -> 7.15 us  [local(): back = lax.ppermute(sent, 'zh', [(0, 1), (1, 0)])]
    ppermute x9 -> x12, starting transfers between devices: 11.7 us -> 15.5 us  [crossed(): return lax.ppermute(block, axes, pairs(axes, move))]
    ppermute x1, starting transfers between devices: 4.82 us -> 1.16 us  [local(): back = lax.ppermute(sent, 'zh', [(0, 1), (1, 0)])]
    pallas_call x4 -> x6, Pallas kernels: 21.9 us -> 18.9 us  [the longest x2 10.4 us: product(): pl.pallas_call(product_kernel, out_shape=out, in_specs=[pl.BlockSpec(memo...]
    ppermute x9 -> x12, waiting for transfers between devices: 25.8 us -> 23.9 us  [crossed(): return lax.ppermute(block, axes, pairs(axes, move))]
    unnamed x14 -> x13, local copies, waits for them, and re-layouts: 5.28 us -> 5.01 us
  transfers between devices with their start and end apart: 24 -> 27, of which waited for: 14 -> 16; matrix products, arithmetic and copies ran while one was open for 3% -> 0% of each run, Pallas kernels for 0% -> 14%
where the time goes in v2:
time: 123 us; the launch traced here: 122 us
  waiting for transfers between devices  48 us (39%)
  starting transfers between devices  47.9 us (39%)
  Pallas kernels  18.9 us (15%)
  local copies, waits for them, and re-layouts  5.11 us (4%)
  other arithmetic  1.68 us (1%)
    ppermute x12, waiting for transfers between devices, crossed(): return lax.ppermute(block, axes, pairs(axes, move))  23.9 us
    ppermute x12, starting transfers between devices, shifted(): lax.ppermute(block, axis, pairs((axis,), lambda at: {axis: at[axis] + k}))  23.9 us
    ppermute x12, waiting for transfers between devices, shifted(): lax.ppermute(block, axis, pairs((axis,), lambda at: {axis: at[axis] + k}))  16.9 us
    ppermute x12, starting transfers between devices, crossed(): return lax.ppermute(block, axes, pairs(axes, move))  15.5 us
    pallas_call x2, Pallas kernels, product(): pl.pallas_call(product_kernel, out_shape=out, in_specs=[pl.BlockSpec(memo...  10.4 us
    ppermute x1, starting transfers between devices, local(): away_scale = lax.ppermute(scale_index, 'zh', [(0, 1), (1, 0)])  7.28 us
    ppermute x1, waiting for transfers between devices, local(): back = lax.ppermute(sent, 'zh', [(0, 1), (1, 0)])  7.15 us
    pallas_call x1, Pallas kernels, load(): pl.pallas_call(load_kernel, out_shape=[jax.ShapeDtypeStruct(a.shape, a.dt...  6.68 us
  transfers between devices with their start and end apart: 27, of which 16 were waited for; matrix products, arithmetic and copies ran while one was open for 0% of the time, Pallas kernels for 14%

profile of v2, /device:TPU:2, one launch (start us, length us, event | category | flops | bytes accessed | tf_op | source)
XLA Modules:
  0.0 122.4 jit_solution(10698111077213904097)
XLA Ops:
  0.7 7.3 %collective-permute-start.1 = (s32[512]{0:T(512)}, s32[512]{0:T(512)S(1)}, u32[]{:S(2)}, u32[]{:S(2)}) collective-permute-start(s32[512]{0:T(512)} %param.6), channel_id=1, source_target_pairs={{0,1},{1,0},{2,3},{3,2},{4,5},{5,4},{6,7},{7,6},{8,9},{9,8},{10,11... | collective-permute-start | bytes 6152 | tf_op jit(solution)/shard_map/ppermute | solution.py:241
  9.7 6.7 %load.1 = (bf16[4096,1024]{1,0:T(8,128)(2,1)}, bf16[64,1024]{1,0:T(8,128)(2,1)S(1)}, s32[1,512]{1,0:T(1,128)S(1)}) custom-call(bf16[4096,1024]{1,0:T(8,128)(2,1)} %refs_0_.1, bf16[64,1024]{1,0:T(8,128)(2,1)S(1)} %bitcast.30, s32[1,512]{1,0:T(1,128)S(1)} %bitcast.31), custom_call_target="tpu_custom_call" | custom-call | bytes 16777216 | tf_op jit(solution)/shard_map/load/pallas_call | solution.py:75
  17.0 2.0 %collective-permute-start.4 = (s16[80,512]{1,0:T(8,128)(2,1)S(1)}, s16[80,512]{1,0:T(8,128)(2,1)S(1)}, u32[]{:S(2)}, u32[]{:S(2)}) collective-permute-start(s16[80,512]{1,0:T(8,128)(2,1)S(1)} %mix.1.a_ref), channel_id=1, source_target_pairs={{0,6},{2,0},{4,2},{6,4},{1,7},{3,1},{5,3},{7,5},{8,14},{10,8},{12,... | collective-permute-start | bytes 245768 | tf_op jit(solution)/shard_map/ppermute | solution.py:32
  21.9 5.5 %collective-permute-done.3.c_ref = s16[80,512]{1,0:T(8,128)(2,1)S(1)} collective-permute-done((s16[80,512]{1,0:T(8,128)(2,1)S(1)}, s16[80,512]{1,0:T(8,128)(2,1)S(1)}, u32[]{:S(2)}, u32[]{:S(2)}) %collective-permute-start.3) | collective-permute-done | bytes 81952 | tf_op jit(solution)/shard_map/ppermute | solution.py:32
  30.1 2.1 %collective-permute-start.6 = (s16[272,256]{1,0:T(8,128)(2,1)S(1)}, s16[272,256]{1,0:T(8,128)(2,1)S(1)}, u32[]{:S(2)}, u32[]{:S(2)}) collective-permute-start(s16[272,256]{1,0:T(8,128)(2,1)S(1)} %get-tuple-element.20), channel_id=1, source_target_pairs={{0,16},{8,24},{16,0},{24,8},{32,48},{40,56},{48,32},{56,40},{64,80... | collective-permute-start | bytes 417800 | tf_op jit(solution)/shard_map/ppermute | solution.py:42
  33.1 3.6 %collective-permute-done.6 = s16[272,256]{1,0:T(8,128)(2,1)S(1)} collective-permute-done((s16[272,256]{1,0:T(8,128)(2,1)S(1)}, s16[272,256]{1,0:T(8,128)(2,1)S(1)}, u32[]{:S(2)}, u32[]{:S(2)}) %collective-permute-start.6) | collective-permute-done | bytes 139296 | tf_op jit(solution)/shard_map/ppermute | solution.py:42
  36.8 3.1 %collective-permute-start.13 = (s16[1088,256]{1,0:T(8,128)(2,1)S(1)}, s16[1088,256]{1,0:T(8,128)(2,1)S(1)}, u32[]{:S(2)}, u32[]{:S(2)}) collective-permute-start(s16[1088,256]{1,0:T(8,128)(2,1)S(1)} %constant_dynamic-update-slice_fusion.refs_0_), channel_id=1, source_target_pairs={{0,96},{8,104},{16,112},{24,120},{32,0},{40,8},{48,16},{56,24},{64... | collective-permute-start | bytes 1671176 | tf_op jit(solution)/shard_map/ppermute | solution.py:42
  41.5 1.7 %collective-permute-start.10 = (s16[272,256]{1,0:T(8,128)(2,1)S(1)}, s16[272,256]{1,0:T(8,128)(2,1)S(1)}, u32[]{:S(2)}, u32[]{:S(2)}) collective-permute-start(s16[272,256]{1,0:T(8,128)(2,1)S(1)} %get-tuple-element.21), channel_id=1, source_target_pairs={{0,24},{8,0},{16,8},{24,16},{32,56},{40,32},{48,40},{56,48},{64,88... | collective-permute-start | bytes 417800 | tf_op jit(solution)/shard_map/ppermute | solution.py:42
  44.3 3.5 %collective-permute-done.10 = s16[272,256]{1,0:T(8,128)(2,1)S(1)} collective-permute-done((s16[272,256]{1,0:T(8,128)(2,1)S(1)}, s16[272,256]{1,0:T(8,128)(2,1)S(1)}, u32[]{:S(2)}, u32[]{:S(2)}) %collective-permute-start.10) | collective-permute-done | bytes 139296 | tf_op jit(solution)/shard_map/ppermute | solution.py:42
  49.6 2.3 %collective-permute-done.9 = s16[272,256]{1,0:T(8,128)(2,1)S(1)} collective-permute-done((s16[272,256]{1,0:T(8,128)(2,1)S(1)}, s16[272,256]{1,0:T(8,128)(2,1)S(1)}, u32[]{:S(2)}, u32[]{:S(2)}) %collective-permute-start.9) | collective-permute-done | bytes 139296 | tf_op jit(solution)/shard_map/ppermute | solution.py:42
  51.9 5.8 %collective-permute-done.8 = s16[272,256]{1,0:T(8,128)(2,1)S(1)} collective-permute-done((s16[272,256]{1,0:T(8,128)(2,1)S(1)}, s16[272,256]{1,0:T(8,128)(2,1)S(1)}, u32[]{:S(2)}, u32[]{:S(2)}) %collective-permute-start.8) | collective-permute-done | bytes 139296 | tf_op jit(solution)/shard_map/ppermute | solution.py:42
  57.8 2.1 %collective-permute-done.11.refs_1_ = s16[1088,256]{1,0:T(8,128)(2,1)S(1)} collective-permute-done((s16[1088,256]{1,0:T(8,128)(2,1)S(1)}, s16[1088,256]{1,0:T(8,128)(2,1)S(1)}, u32[]{:S(2)}, u32[]{:S(2)}) %collective-permute-start.11) | collective-permute-done | bytes 557088 | tf_op jit(solution)/shard_map/ppermute | solution.py:42
  61.9 3.4 %copy-done.2 = bf16[4096,1024]{1,0:T(8,128)(2,1)S(1)} copy-done((bf16[4096,1024]{1,0:T(8,128)(2,1)S(1)}, bf16[4096,1024]{1,0:T(8,128)(2,1)}, u32[]{:S(2)}) %copy-start.2) | copy-done | bytes 8388632
  65.3 5.3 %product.3 = s16[272,1024]{1,0:T(8,128)(2,1)S(1)} custom-call(s32[16]{0:T(128)S(1)} %stack.92.index_ref, bf16[4096,1024]{1,0:T(8,128)(2,1)S(1)} %copy-done.2, s16[1088,256]{1,0:T(8,128)(2,1)S(1)} %constant_dynamic-update-slice_fusion.refs_0_, s16[1088,256]{1,0:T(8,128)(2,1)S(1)} %collective-permute-done.11.refs_1_, ...), custom_call_target="tpu_custom_call" | custom-call | flops 4294967296 | bytes 10485760 | tf_op jit(solution)/shard_map/product/pallas_call | solution.py:181
  71.8 5.7 %collective-permute-done.14.refs_1_ = s16[1088,256]{1,0:T(8,128)(2,1)S(1)} collective-permute-done((s16[1088,256]{1,0:T(8,128)(2,1)S(1)}, s16[1088,256]{1,0:T(8,128)(2,1)S(1)}, u32[]{:S(2)}, u32[]{:S(2)}) %collective-permute-start.14) | collective-permute-done | bytes 557088 | tf_op jit(solution)/shard_map/ppermute | solution.py:42
  77.5 5.1 %product.2.kept_ref = f32[256,1024]{1,0:T(8,128)S(1)} custom-call(s32[16]{0:T(128)S(1)} %stack.92.index_ref, bf16[4096,1024]{1,0:T(8,128)(2,1)S(1)} %copy-done.2, s16[1088,256]{1,0:T(8,128)(2,1)S(1)} %pad_add_fusion.refs_0_, s16[1088,256]{1,0:T(8,128)(2,1)S(1)} %collective-permute-done.14.refs_1_, s16[1088,256]{1,0:T(8,128)(2,1)S(1)} %collective-permute-done.15.refs_2_, ...), custom_call_target="tpu_custom_call" | custom-call | flops 4294967296 | bytes 10485760 | tf_op jit(solution)/shard_map/product/pallas_call | solution.py:181
  82.6 7.2 %collective-permute-done.17.back_ref = s16[272,1024]{1,0:T(8,128)(2,1)S(1)} collective-permute-done((s16[272,1024]{1,0:T(8,128)(2,1)S(1)}, s16[272,1024]{1,0:T(8,128)(2,1)S(1)}, u32[]{:S(2)}, u32[]{:S(2)}) %collective-permute-start.17) | collective-permute-done | bytes 557088 | tf_op jit(solution)/shard_map/ppermute | solution.py:270
  90.3 4.5 %collective-permute-start.20 = (f32[8,256]{1,0:T(8,128)S(1)}, f32[8,256]{1,0:T(8,128)S(1)}, u32[]{:S(2)}, u32[]{:S(2)}) collective-permute-start(f32[8,256]{1,0:T(8,128)S(1)} %get-tuple-element.24), channel_id=1, source_target_pairs={{0,6},{2,0},{4,2},{6,4},{1,7},{3,1},{5,3},{7,5},{8,14},{10,8},{12,... | collective-permute-start | bytes 24584 | tf_op jit(solution)/shard_map/ppermute | solution.py:32
  94.8 6.9 %collective-permute-start.19 = (f32[8,256]{1,0:T(8,128)S(1)}, f32[8,256]{1,0:T(8,128)S(1)}, u32[]{:S(2)}, u32[]{:S(2)}) collective-permute-start(f32[8,256]{1,0:T(8,128)S(1)} %get-tuple-element.24), channel_id=1, source_target_pairs={{0,4},{2,6},{4,0},{6,2},{1,5},{3,7},{5,1},{7,3},{8,12},{10,14},{12... | collective-permute-start | bytes 24584 | tf_op jit(solution)/shard_map/ppermute | solution.py:32
  101.7 1.9 %collective-permute-start.18 = (f32[8,256]{1,0:T(8,128)S(1)}, f32[8,256]{1,0:T(8,128)S(1)}, u32[]{:S(2)}, u32[]{:S(2)}) collective-permute-start(f32[8,256]{1,0:T(8,128)S(1)} %get-tuple-element.24), channel_id=1, source_target_pairs={{0,2},{2,4},{4,6},{6,0},{1,3},{3,5},{5,7},{7,1},{8,10},{10,12},{12... | collective-permute-start | bytes 24584 | tf_op jit(solution)/shard_map/ppermute | solution.py:32
  103.6 3.5 %collective-permute-done.18 = f32[8,256]{1,0:T(8,128)S(1)} collective-permute-done((f32[8,256]{1,0:T(8,128)S(1)}, f32[8,256]{1,0:T(8,128)S(1)}, u32[]{:S(2)}, u32[]{:S(2)}) %collective-permute-start.18) | collective-permute-done | bytes 8224 | tf_op jit(solution)/shard_map/ppermute | solution.py:32
  107.6 2.1 %collective-permute-start.22 = (f32[8,256]{1,0:T(8,128)S(1)}, f32[8,256]{1,0:T(8,128)S(1)}, u32[]{:S(2)}, u32[]{:S(2)}) collective-permute-start(f32[8,256]{1,0:T(8,128)S(1)} %maximum_maximum_fusion), channel_id=1, source_target_pairs={{0,16},{8,24},{16,0},{24,8},{1,17},{9,25},{17,1},{25,9},{2,18},{10... | collective-permute-start | bytes 24584 | tf_op jit(solution)/shard_map/ppermute | solution.py:32
  109.6 1.8 %collective-permute-start.21 = (f32[8,256]{1,0:T(8,128)S(1)}, f32[8,256]{1,0:T(8,128)S(1)}, u32[]{:S(2)}, u32[]{:S(2)}) collective-permute-start(f32[8,256]{1,0:T(8,128)S(1)} %maximum_maximum_fusion), channel_id=1, source_target_pairs={{0,8},{8,16},{16,24},{24,0},{1,9},{9,17},{17,25},{25,1},{2,10},{10... | collective-permute-start | bytes 24584 | tf_op jit(solution)/shard_map/ppermute | solution.py:32
  117.1 2.9 %collective-permute-done.25 = f32[8,256]{1,0:T(8,128)S(1)} collective-permute-done((f32[8,256]{1,0:T(8,128)S(1)}, f32[8,256]{1,0:T(8,128)S(1)}, u32[]{:S(2)}, u32[]{:S(2)}) %collective-permute-start.25) | collective-permute-done | bytes 8224 | tf_op jit(solution)/shard_map/ppermute | solution.py:32
  (66 shorter events, 25.6 us)
Async XLA Ops:
  0.6 15.7 %collective-permute-start = (bf16[64,1024]{1,0:T(8,128)(2,1)}, bf16[64,1024]{1,0:T(8,128)(2,1)S(1)}, u32[]{:S(2)}, u32[]{:S(2)}) collective-permute-start(bf16[64,1024]{1,0:T(8,128)(2,1)} %bitcast.29), channel_id=1, source_target_pairs={{0,128},{128,0},{1,129},{129,1},{2,130},{130,2},{3,131},{131,3},{4... | collective-permute-start | bytes 393224 | tf_op jit(solution)/shard_map/ppermute | solution.py:240
  0.7 15.6 %collective-permute-start.1 = (s32[512]{0:T(512)}, s32[512]{0:T(512)S(1)}, u32[]{:S(2)}, u32[]{:S(2)}) collective-permute-start(s32[512]{0:T(512)} %param.6), channel_id=1, source_target_pairs={{0,1},{1,0},{2,3},{3,2},{4,5},{5,4},{6,7},{7,6},{8,9},{9,8},{10,11... | collective-permute-start | bytes 6152 | tf_op jit(solution)/shard_map/ppermute | solution.py:241
  17.0 4.9 %collective-permute-start.4 = (s16[80,512]{1,0:T(8,128)(2,1)S(1)}, s16[80,512]{1,0:T(8,128)(2,1)S(1)}, u32[]{:S(2)}, u32[]{:S(2)}) collective-permute-start(s16[80,512]{1,0:T(8,128)(2,1)S(1)} %mix.1.a_ref), channel_id=1, source_target_pairs={{0,6},{2,0},{4,2},{6,4},{1,7},{3,1},{5,3},{7,5},{8,14},{10,8},{12,... | collective-permute-start | bytes 245768 | tf_op jit(solution)/shard_map/ppermute | solution.py:32
  19.0 8.4 %collective-permute-start.3 = (s16[80,512]{1,0:T(8,128)(2,1)S(1)}, s16[80,512]{1,0:T(8,128)(2,1)S(1)}, u32[]{:S(2)}, u32[]{:S(2)}) collective-permute-start(s16[80,512]{1,0:T(8,128)(2,1)S(1)} %mix.1.a_ref), channel_id=1, source_target_pairs={{0,4},{2,6},{4,0},{6,2},{1,5},{3,7},{5,1},{7,3},{8,12},{10,14},{12... | collective-permute-start | bytes 245768 | tf_op jit(solution)/shard_map/ppermute | solution.py:32
  19.6 7.8 %collective-permute-start.2 = (s16[80,512]{1,0:T(8,128)(2,1)S(1)}, s16[80,512]{1,0:T(8,128)(2,1)S(1)}, u32[]{:S(2)}, u32[]{:S(2)}) collective-permute-start(s16[80,512]{1,0:T(8,128)(2,1)S(1)} %mix.1.a_ref), channel_id=1, source_target_pairs={{0,2},{2,4},{4,6},{6,0},{1,3},{3,5},{5,7},{7,1},{8,10},{10,12},{12... | collective-permute-start | bytes 245768 | tf_op jit(solution)/shard_map/ppermute | solution.py:32
  28.0 5.1 %collective-permute-start.5 = (s16[272,256]{1,0:T(8,128)(2,1)S(1)}, s16[272,256]{1,0:T(8,128)(2,1)S(1)}, u32[]{:S(2)}, u32[]{:S(2)}) collective-permute-start(s16[272,256]{1,0:T(8,128)(2,1)S(1)} %get-tuple-element.20), channel_id=1, source_target_pairs={{0,8},{8,16},{16,24},{24,0},{32,40},{40,48},{48,56},{56,32},{64,72... | collective-permute-start | bytes 417800 | tf_op jit(solution)/shard_map/ppermute | solution.py:42
  29.6 7.2 %collective-permute-start.7 = (s16[272,256]{1,0:T(8,128)(2,1)S(1)}, s16[272,256]{1,0:T(8,128)(2,1)S(1)}, u32[]{:S(2)}, u32[]{:S(2)}) collective-permute-start(s16[272,256]{1,0:T(8,128)(2,1)S(1)} %get-tuple-element.20), channel_id=1, source_target_pairs={{0,24},{8,0},{16,8},{24,16},{32,56},{40,32},{48,40},{56,48},{64,88... | collective-permute-start | bytes 417800 | tf_op jit(solution)/shard_map/ppermute | solution.py:42
  30.1 6.6 %collective-permute-start.6 = (s16[272,256]{1,0:T(8,128)(2,1)S(1)}, s16[272,256]{1,0:T(8,128)(2,1)S(1)}, u32[]{:S(2)}, u32[]{:S(2)}) collective-permute-start(s16[272,256]{1,0:T(8,128)(2,1)S(1)} %get-tuple-element.20), channel_id=1, source_target_pairs={{0,16},{8,24},{16,0},{24,8},{32,48},{40,56},{48,32},{56,40},{64,80... | collective-permute-start | bytes 417800 | tf_op jit(solution)/shard_map/ppermute | solution.py:42
  36.8 21.0 %collective-permute-start.13 = (s16[1088,256]{1,0:T(8,128)(2,1)S(1)}, s16[1088,256]{1,0:T(8,128)(2,1)S(1)}, u32[]{:S(2)}, u32[]{:S(2)}) collective-permute-start(s16[1088,256]{1,0:T(8,128)(2,1)S(1)} %constant_dynamic-update-slice_fusion.refs_0_), channel_id=1, source_target_pairs={{0,96},{8,104},{16,112},{24,120},{32,0},{40,8},{48,16},{56,24},{64... | collective-permute-start | bytes 1671176 | tf_op jit(solution)/shard_map/ppermute | solution.py:42
  39.9 17.9 %collective-permute-start.12 = (s16[1088,256]{1,0:T(8,128)(2,1)S(1)}, s16[1088,256]{1,0:T(8,128)(2,1)S(1)}, u32[]{:S(2)}, u32[]{:S(2)}) collective-permute-start(s16[1088,256]{1,0:T(8,128)(2,1)S(1)} %constant_dynamic-update-slice_fusion.refs_0_), channel_id=1, source_target_pairs={{0,64},{8,72},{16,80},{24,88},{32,96},{40,104},{48,112},{56,120},{... | collective-permute-start | bytes 1671176 | tf_op jit(solution)/shard_map/ppermute | solution.py:42
  40.5 19.4 %collective-permute-start.11 = (s16[1088,256]{1,0:T(8,128)(2,1)S(1)}, s16[1088,256]{1,0:T(8,128)(2,1)S(1)}, u32[]{:S(2)}, u32[]{:S(2)}) collective-permute-start(s16[1088,256]{1,0:T(8,128)(2,1)S(1)} %constant_dynamic-update-slice_fusion.refs_0_), channel_id=1, source_target_pairs={{0,32},{8,40},{16,48},{24,56},{32,64},{40,72},{48,80},{56,88},{64,... | collective-permute-start | bytes 1671176 | tf_op jit(solution)/shard_map/ppermute | solution.py:42
  41.5 6.4 %collective-permute-start.10 = (s16[272,256]{1,0:T(8,128)(2,1)S(1)}, s16[272,256]{1,0:T(8,128)(2,1)S(1)}, u32[]{:S(2)}, u32[]{:S(2)}) collective-permute-start(s16[272,256]{1,0:T(8,128)(2,1)S(1)} %get-tuple-element.21), channel_id=1, source_target_pairs={{0,24},{8,0},{16,8},{24,16},{32,56},{40,32},{48,40},{56,48},{64,88... | collective-permute-start | bytes 417800 | tf_op jit(solution)/shard_map/ppermute | solution.py:42
  43.1 8.8 %collective-permute-start.9 = (s16[272,256]{1,0:T(8,128)(2,1)S(1)}, s16[272,256]{1,0:T(8,128)(2,1)S(1)}, u32[]{:S(2)}, u32[]{:S(2)}) collective-permute-start(s16[272,256]{1,0:T(8,128)(2,1)S(1)} %get-tuple-element.21), channel_id=1, source_target_pairs={{0,16},{8,24},{16,0},{24,8},{32,48},{40,56},{48,32},{56,40},{64,80... | collective-permute-start | bytes 417800 | tf_op jit(solution)/shard_map/ppermute | solution.py:42
  47.9 9.9 %collective-permute-start.8 = (s16[272,256]{1,0:T(8,128)(2,1)S(1)}, s16[272,256]{1,0:T(8,128)(2,1)S(1)}, u32[]{:S(2)}, u32[]{:S(2)}) collective-permute-start(s16[272,256]{1,0:T(8,128)(2,1)S(1)} %get-tuple-element.21), channel_id=1, source_target_pairs={{0,8},{8,16},{16,24},{24,0},{32,40},{40,48},{48,56},{56,32},{64,72... | collective-permute-start | bytes 417800 | tf_op jit(solution)/shard_map/ppermute | solution.py:42
  59.9 11.9 %collective-permute-start.16 = (s16[1088,256]{1,0:T(8,128)(2,1)S(1)}, s16[1088,256]{1,0:T(8,128)(2,1)S(1)}, u32[]{:S(2)}, u32[]{:S(2)}) collective-permute-start(s16[1088,256]{1,0:T(8,128)(2,1)S(1)} %pad_add_fusion.refs_0_), channel_id=1, source_target_pairs={{0,96},{8,104},{16,112},{24,120},{32,0},{40,8},{48,16},{56,24},{64... | collective-permute-start | bytes 1671176 | tf_op jit(solution)/shard_map/ppermute | solution.py:42
  60.5 11.3 %collective-permute-start.15 = (s16[1088,256]{1,0:T(8,128)(2,1)S(1)}, s16[1088,256]{1,0:T(8,128)(2,1)S(1)}, u32[]{:S(2)}, u32[]{:S(2)}) collective-permute-start(s16[1088,256]{1,0:T(8,128)(2,1)S(1)} %pad_add_fusion.refs_0_), channel_id=1, source_target_pairs={{0,64},{8,72},{16,80},{24,88},{32,96},{40,104},{48,112},{56,120},{... | collective-permute-start | bytes 1671176 | tf_op jit(solution)/shard_map/ppermute | solution.py:42
  61.1 16.4 %collective-permute-start.14 = (s16[1088,256]{1,0:T(8,128)(2,1)S(1)}, s16[1088,256]{1,0:T(8,128)(2,1)S(1)}, u32[]{:S(2)}, u32[]{:S(2)}) collective-permute-start(s16[1088,256]{1,0:T(8,128)(2,1)S(1)} %pad_add_fusion.refs_0_), channel_id=1, source_target_pairs={{0,32},{8,40},{16,48},{24,56},{32,64},{40,72},{48,80},{56,88},{64,... | collective-permute-start | bytes 1671176 | tf_op jit(solution)/shard_map/ppermute | solution.py:42
  70.6 19.1 %collective-permute-start.17 = (s16[272,1024]{1,0:T(8,128)(2,1)S(1)}, s16[272,1024]{1,0:T(8,128)(2,1)S(1)}, u32[]{:S(2)}, u32[]{:S(2)}) collective-permute-start(s16[272,1024]{1,0:T(8,128)(2,1)S(1)} %product.3), channel_id=1, source_target_pairs={{0,1},{1,0},{2,3},{3,2},{4,5},{5,4},{6,7},{7,6},{8,9},{9,8},{10,11... | collective-permute-start | bytes 1671176 | tf_op jit(solution)/shard_map/ppermute | solution.py:270
  90.3 13.3 %collective-permute-start.20 = (f32[8,256]{1,0:T(8,128)S(1)}, f32[8,256]{1,0:T(8,128)S(1)}, u32[]{:S(2)}, u32[]{:S(2)}) collective-permute-start(f32[8,256]{1,0:T(8,128)S(1)} %get-tuple-element.24), channel_id=1, source_target_pairs={{0,6},{2,0},{4,2},{6,4},{1,7},{3,1},{5,3},{7,5},{8,14},{10,8},{12,... | collective-permute-start | bytes 24584 | tf_op jit(solution)/shard_map/ppermute | solution.py:32
  94.8 8.9 %collective-permute-start.19 = (f32[8,256]{1,0:T(8,128)S(1)}, f32[8,256]{1,0:T(8,128)S(1)}, u32[]{:S(2)}, u32[]{:S(2)}) collective-permute-start(f32[8,256]{1,0:T(8,128)S(1)} %get-tuple-element.24), channel_id=1, source_target_pairs={{0,4},{2,6},{4,0},{6,2},{1,5},{3,7},{5,1},{7,3},{8,12},{10,14},{12... | collective-permute-start | bytes 24584 | tf_op jit(solution)/shard_map/ppermute | solution.py:32
  101.7 5.4 %collective-permute-start.18 = (f32[8,256]{1,0:T(8,128)S(1)}, f32[8,256]{1,0:T(8,128)S(1)}, u32[]{:S(2)}, u32[]{:S(2)}) collective-permute-start(f32[8,256]{1,0:T(8,128)S(1)} %get-tuple-element.24), channel_id=1, source_target_pairs={{0,2},{2,4},{4,6},{6,0},{1,3},{3,5},{5,7},{7,1},{8,10},{10,12},{12... | collective-permute-start | bytes 24584 | tf_op jit(solution)/shard_map/ppermute | solution.py:32
  107.6 5.2 %collective-permute-start.22 = (f32[8,256]{1,0:T(8,128)S(1)}, f32[8,256]{1,0:T(8,128)S(1)}, u32[]{:S(2)}, u32[]{:S(2)}) collective-permute-start(f32[8,256]{1,0:T(8,128)S(1)} %maximum_maximum_fusion), channel_id=1, source_target_pairs={{0,16},{8,24},{16,0},{24,8},{1,17},{9,25},{17,1},{25,9},{2,18},{10... | collective-permute-start | bytes 24584 | tf_op jit(solution)/shard_map/ppermute | solution.py:32
  114.9 5.2 %collective-permute-start.25 = (f32[8,256]{1,0:T(8,128)S(1)}, f32[8,256]{1,0:T(8,128)S(1)}, u32[]{:S(2)}, u32[]{:S(2)}) collective-permute-start(f32[8,256]{1,0:T(8,128)S(1)} %maximum_maximum_fusion.1), channel_id=1, source_target_pairs={{0,64},{32,96},{64,0},{96,32},{1,65},{33,97},{65,1},{97,33},{2,66}... | collective-permute-start | bytes 24584 | tf_op jit(solution)/shard_map/ppermute | solution.py:32
  116.2 4.9 %collective-permute-start.24 = (f32[8,256]{1,0:T(8,128)S(1)}, f32[8,256]{1,0:T(8,128)S(1)}, u32[]{:S(2)}, u32[]{:S(2)}) collective-permute-start(f32[8,256]{1,0:T(8,128)S(1)} %maximum_maximum_fusion.1), channel_id=1, source_target_pairs={{0,32},{32,64},{64,96},{96,0},{1,33},{33,65},{65,97},{97,1},{2,34}... | collective-permute-start | bytes 24584 | tf_op jit(solution)/shard_map/ppermute | solution.py:32
  (8 other events, 63.4 us)

commit v3 on v2

--- a/solution.py
+++ b/solution.py
@@ -10,6 +10,7 @@
 AXES = ("cfg", "y", "x", "zl", "zh")
 SIZES = (2, 4, 4, 4, 2)
 TOP = 32767.0
+CHUNKS = ((0, 256), (256, 256))
 STEP = math.log(2.0) / 256.0
 
 
@@ -78,7 +79,7 @@
         in_specs=[pl.BlockSpec(memory_space=pl.ANY)] * len(arrays),
         out_specs=in_vmem(len(arrays)),
         scratch_shapes=[pltpu.SemaphoreType.DMA((len(arrays),))],
-        compiler_params=room(50),
+        compiler_params=room(44),
         cost_estimate=pl.CostEstimate(flops=0, bytes_accessed=16 << 20, transcendentals=0),
         name="load",
     )(*arrays)
@@ -114,24 +115,23 @@
     )(place, own, other, own_scale, away_scale)
 
 
-def stack_kernel(place_ref, a_ref, b_ref, c_ref, d_ref, *out_refs):
-    row = lax.broadcasted_iota(jnp.int32, (16, 256), 0)
-    for n, out_ref in enumerate(out_refs):
-        at = slice(256 * n, 256 * n + 256)
-        codes = jnp.zeros((16, 256), jnp.int32)
-        for k, ref in enumerate((a_ref, b_ref, c_ref, d_ref)):
-            place = place_ref[k]
-            out_ref[pl.ds(pl.multiple_of(place * 64, 64), 64), :] = ref[:64, at]
-            codes = jnp.where(row == place, ref[64:, at].astype(jnp.int32), codes)
-        out_ref[256:] = codes.astype(jnp.int16)
+def stack_kernel(place_ref, a_ref, b_ref, c_ref, d_ref, out_ref):
+    width = a_ref.shape[1]
+    row = lax.broadcasted_iota(jnp.int32, (16, width), 0)
+    codes = jnp.zeros((16, width), jnp.int32)
+    for k, ref in enumerate((a_ref, b_ref, c_ref, d_ref)):
+        place = place_ref[k]
+        out_ref[pl.ds(pl.multiple_of(place * 64, 64), 64), :] = ref[:64]
+        codes = jnp.where(row == place, ref[64:].astype(jnp.int32), codes)
+    out_ref[256:] = codes.astype(jnp.int16)
 
 
 def stack(place, parts):
     return pl.pallas_call(
         stack_kernel,
-        out_shape=[jax.ShapeDtypeStruct((272, 256), jnp.int16)] * 2,
+        out_shape=jax.ShapeDtypeStruct((272, parts[0].shape[1]), jnp.int16),
         in_specs=[pl.BlockSpec(memory_space=pltpu.SMEM)] + in_vmem(4),
-        out_specs=in_vmem(2),
+        out_specs=in_vmem(1)[0],
         compiler_params=room(4),
         name="stack",
     )(place, *parts)
@@ -192,45 +192,38 @@
     )(index, head, *parts)
 
 
-def join_kernel(kept_ref, back_ref, guided_ref, stats_ref):
-    count = kept_ref.shape[0]
-    codes = back_ref[count:, :count].astype(jnp.float32)[:1]
-    scale = jnp.transpose(jnp.broadcast_to(scale_of(codes), (128, count)))[:, :1]
-    guided = kept_ref[...] + back_ref[:count].astype(jnp.float32) * scale
-    peak = jnp.max(guided, axis=1, keepdims=True)
-    expo = jnp.exp(guided - peak)
-    total = jnp.sum(expo, axis=1, keepdims=True)
-    moment = jnp.sum(expo * guided, axis=1, keepdims=True)
-    lane = lax.broadcasted_iota(jnp.int32, (count, 128), 1)
-    table = jnp.where(lane == 0, peak, jnp.where(lane == 1, total, moment))
-    stats_ref[...] = jnp.transpose(table)[:8]
-    guided_ref[...] = guided
-
-
-def join(kept, back):
+def join_kernel(kept_ref, *refs):
+    backs, guided_ref, stats_ref = refs[:-2], refs[-2], refs[-1]
+    start = 0
+    for back_ref in backs:
+        count = back_ref.shape[0] - 16
+        rows = slice(start, start + count)
+        codes = back_ref[count:, :count].astype(jnp.float32)[:1]
+        scale = jnp.transpose(jnp.broadcast_to(scale_of(codes), (128, count)))[:, :1]
+        guided = kept_ref[rows] + back_ref[:count].astype(jnp.float32) * scale
+        peak = jnp.max(guided, axis=1, keepdims=True)
+        expo = jnp.exp(guided - peak)
+        total = jnp.sum(expo, axis=1, keepdims=True)
+        moment = jnp.sum(expo * guided, axis=1, keepdims=True)
+        lane = lax.broadcasted_iota(jnp.int32, (count, 128), 1)
+        table = jnp.where(lane == 0, peak + jnp.log(total), moment / total)
+        stats_ref[:, rows] = jnp.transpose(table)[:2]
+        guided_ref[rows] = guided
+        start += count
+
+
+def join(kept, backs):
     return pl.pallas_call(
         join_kernel,
         out_shape=(
             jax.ShapeDtypeStruct(kept.shape, jnp.float32),
-            jax.ShapeDtypeStruct((8, kept.shape[0]), jnp.float32),
+            jax.ShapeDtypeStruct((2, kept.shape[0]), jnp.float32),
         ),
-        in_specs=in_vmem(2),
+        in_specs=in_vmem(1 + len(backs)),
         out_specs=in_vmem(2),
         compiler_params=room(12),
         name="join",
-    )(kept, back)
-
-
-def merged(stats):
-    peak = stats[0][:1]
-    for s in stats[1:]:
-        peak = jnp.maximum(peak, s[:1])
-    total = moment = 0.0
-    for s in stats:
-        weight = jnp.exp(s[:1] - peak)
-        total += s[1:2] * weight
-        moment += s[2:3] * weight
-    return jnp.concatenate([peak, total, moment, stats[0][3:]])
+    )(kept, *backs)
 
 
 def local(hidden, head, scale_index, threshold):
@@ -246,7 +239,7 @@
     mixed, head = lax.optimization_barrier((mixed, head))
     near = [mixed] + [shifted(mixed, "zl", k) for k in (1, 2, 3)]
     place = jnp.stack([(zl - k) % 4 for k in range(4)])
-    away_column, home_column = stack(place, near)
+    column = stack(place, near)
 
     index = []
     for k2 in range(4):
@@ -259,22 +252,25 @@
     def spread(block, first, second):
         return [block] + [crossed(block, first, second, k) for k in (1, 2, 3)]
 
-    away_line = spread(away_column, "x", "y")
-    away_parts = spread(jnp.concatenate(away_line, 0), "y", "x")
-    home_column = lax.optimization_barrier((home_column, *away_line))[0]
-    home_line = spread(home_column, "x", "y")
-    sent = product(index, head, away_parts, False)
-    home_block = jnp.concatenate(home_line, 0)
-    home_block = lax.optimization_barrier((home_block, *away_parts))[0]
-    home_parts = spread(home_block, "y", "x")
-    back = lax.ppermute(sent, "zh", [(0, 1), (1, 0)])
-    kept = product(index, head, home_parts, True)
-
-    guided, stats = join(kept, back)
-    for axis in ("zl", "x", "y"):
-        stats = merged([stats] + [shifted(stats, axis, k) for k in (1, 2, 3)])
-    lse = stats[0] + jnp.log(stats[1])
-    entropy = lse - stats[2] / stats[1]
+    line = spread(column, "x", "y")
+    backs, before = [], ()
+    for start, count in CHUNKS:
+        block = jnp.concatenate([part[:, start : start + count] for part in line], 0)
+        if start == 256:
+            block = lax.optimization_barrier((block, *before))[0]
+        before = spread(block, "y", "x")
+        result = product(index, head, before, start >= 256)
+        if start < 256:
+            backs.append(lax.ppermute(result, "zh", [(0, 1), (1, 0)]))
+
+    guided, stats = join(result, backs)
+    stats = lax.all_to_all(jnp.broadcast_to(stats, (64, 2, 256)), ("y", "x", "zl"), 0, 0, tiled=True)
+    each, mean = stats[:, 0], stats[:, 1]
+    top = jnp.max(each, axis=0)
+    weight = jnp.exp(each - top)
+    total = jnp.sum(weight, axis=0)
+    lse = top + jnp.log(total)
+    entropy = lse - jnp.sum(weight * mean, axis=0) / total
     logprob = guided - lse[:, None]
     deviation = -logprob - entropy[:, None]
     typical = jax.nn.sigmoid(2.0 * (limits[:, None] - jnp.abs(deviation)))

time: 123 us -> 121 us (0.984)
  starting transfers between devices: 47.9 us -> 40.3 us
  waiting for transfers between devices: 48 us -> 52.8 us
  local copies, waits for them, and re-layouts: 5.11 us -> 9.09 us
  Pallas kernels: 18.9 us -> 15.6 us
    ppermute x12 -> x3, starting transfers between devices: 23.9 us -> 3.58 us  [shifted(): lax.ppermute(block, axis, pairs((axis,), lambda at: {axis: at[axis] + k}))]
    all_to_all x0 -> x1, starting transfers between devices: none -> 16.5 us  [local(): lax.all_to_all(jnp.broadcast_to(stats, (64, 2, 256)), ('y', 'x', 'zl'), 0...]
    ppermute x12 -> x3, waiting for transfers between devices: 16.9 us -> 6.75 us  [shifted(): lax.ppermute(block, axis, pairs((axis,), lambda at: {axis: at[axis] + k}))]
    all_to_all x0 -> x1, waiting for transfers between devices: none -> 9.39 us  [local(): lax.all_to_all(jnp.broadcast_to(stats, (64, 2, 256)), ('y', 'x', 'zl'), 0...]
    ppermute x12 -> x9, starting transfers between devices: 15.5 us -> 11.7 us  [crossed(): return lax.ppermute(block, axes, pairs(axes, move))]
    ppermute x12 -> x9, waiting for transfers between devices: 23.9 us -> 27.7 us  [crossed(): return lax.ppermute(block, axes, pairs(axes, move))]
    pallas_call x1, Pallas kernels: 6.68 us -> 3.41 us  [load(): pl.pallas_call(load_kernel, out_shape=[jax.ShapeDtypeStruct(a.shape, a.dt...]
    unnamed x13 -> x12, local copies, waits for them, and re-layouts: 5.01 us -> 8.22 us
  transfers between devices with their start and end apart: 27 -> 16, of which waited for: 16 -> 10; matrix products, arithmetic and copies ran while one was open for 0% -> 0% of each run, Pallas kernels for 14% -> 11%
where the time goes in v3:
time: 121 us; the launch traced here: 120 us
  waiting for transfers between devices  52.8 us (44%)
  starting transfers between devices  40.3 us (33%)
  Pallas kernels  15.6 us (13%)
  local copies, waits for them, and re-layouts  9.09 us (8%)
  other arithmetic  1.78 us (1%)
    ppermute x9, waiting for transfers between devices, crossed(): return lax.ppermute(block, axes, pairs(axes, move))  27.7 us
    all_to_all x1, starting transfers between devices, local(): lax.all_to_all(jnp.broadcast_to(stats, (64, 2, 256)), ('y', 'x', 'zl'), 0...  16.5 us
    ppermute x9, starting transfers between devices, crossed(): return lax.ppermute(block, axes, pairs(axes, move))  11.7 us
    pallas_call x2, Pallas kernels, product(): pl.pallas_call(product_kernel, out_shape=out, in_specs=[pl.BlockSpec(memo...  10.4 us
    all_to_all x1, waiting for transfers between devices, local(): lax.all_to_all(jnp.broadcast_to(stats, (64, 2, 256)), ('y', 'x', 'zl'), 0...  9.39 us
    ppermute x1, waiting for transfers between devices, local(): backs.append(lax.ppermute(result, 'zh', [(0, 1), (1, 0)]))  8.96 us
    unnamed x12, local copies, waits for them, and re-layouts  8.22 us
    ppermute x1, starting transfers between devices, local(): away_scale = lax.ppermute(scale_index, 'zh', [(0, 1), (1, 0)])  7.28 us
  transfers between devices with their start and end apart: 16, of which 10 were waited for; matrix products, arithmetic and copies ran while one was open for 0% of the time, Pallas kernels for 11%

profile of v3, /device:TPU:2, one launch (start us, length us, event | category | flops | bytes accessed | tf_op | source)
XLA Modules:
  0.0 120.3 jit_solution(12753756012724397517)
XLA Ops:
  0.7 7.3 %collective-permute-start.1 = (s32[512]{0:T(512)}, s32[512]{0:T(512)S(1)}, u32[]{:S(2)}, u32[]{:S(2)}) collective-permute-start(s32[512]{0:T(512)} %param.6), channel_id=1, source_target_pairs={{0,1},{1,0},{2,3},{3,2},{4,5},{5,4},{6,7},{7,6},{8,9},{9,8},{10,11... | collective-permute-start | bytes 6152 | tf_op jit(solution)/shard_map/ppermute | solution.py:234
  9.7 3.4 %load.1 = (bf16[4096,1024]{1,0:T(8,128)(2,1)S(1)}, bf16[64,1024]{1,0:T(8,128)(2,1)S(1)}, s32[1,512]{1,0:T(1,128)S(1)}) custom-call(bf16[4096,1024]{1,0:T(8,128)(2,1)} %refs_0_.1, bf16[64,1024]{1,0:T(8,128)(2,1)S(1)} %bitcast.42, s32[1,512]{1,0:T(1,128)S(1)} %bitcast.43), custom_call_target="tpu_custom_call" | custom-call | bytes 16777216 | tf_op jit(solution)/shard_map/load/pallas_call | solution.py:76
  13.1 3.2 %copy-done.2 = bf16[4096,1024]{1,0:T(8,128)(2,1)} copy-done((bf16[4096,1024]{1,0:T(8,128)(2,1)}, bf16[4096,1024]{1,0:T(8,128)(2,1)S(1)}, u32[]{:S(2)}) %copy-start.2) | copy-done | bytes 8388632
  17.0 2.0 %collective-permute-start.4 = (s16[80,512]{1,0:T(8,128)(2,1)S(1)}, s16[80,512]{1,0:T(8,128)(2,1)S(1)}, u32[]{:S(2)}, u32[]{:S(2)}) collective-permute-start(s16[80,512]{1,0:T(8,128)(2,1)S(1)} %mix.1.a_ref), channel_id=1, source_target_pairs={{0,6},{2,0},{4,2},{6,4},{1,7},{3,1},{5,3},{7,5},{8,14},{10,8},{12,... | collective-permute-start | bytes 245768 | tf_op jit(solution)/shard_map/ppermute | solution.py:33
  19.5 1.0 collective-permute-start.2
  20.6 1.2 collective-permute-done.4.d_ref
  21.8 5.5 %collective-permute-done.3.c_ref = s16[80,512]{1,0:T(8,128)(2,1)S(1)} collective-permute-done((s16[80,512]{1,0:T(8,128)(2,1)S(1)}, s16[80,512]{1,0:T(8,128)(2,1)S(1)}, u32[]{:S(2)}, u32[]{:S(2)}) %collective-permute-start.3) | collective-permute-done | bytes 81952 | tf_op jit(solution)/shard_map/ppermute | solution.py:33
  28.6 2.4 %collective-permute-start.6 = (s16[272,512]{1,0:T(8,128)(2,1)S(1)}, s16[272,512]{1,0:T(8,128)(2,1)S(1)}, u32[]{:S(2)}, u32[]{:S(2)}) collective-permute-start(s16[272,512]{1,0:T(8,128)(2,1)S(1)} %stack.101), channel_id=1, source_target_pairs={{0,16},{8,24},{16,0},{24,8},{32,48},{40,56},{48,32},{56,40},{64,80... | collective-permute-start | bytes 835592 | tf_op jit(solution)/shard_map/ppermute | solution.py:43
  31.0 1.9 %collective-permute-start.5 = (s16[272,512]{1,0:T(8,128)(2,1)S(1)}, s16[272,512]{1,0:T(8,128)(2,1)S(1)}, u32[]{:S(2)}, u32[]{:S(2)}) collective-permute-start(s16[272,512]{1,0:T(8,128)(2,1)S(1)} %stack.101), channel_id=1, source_target_pairs={{0,8},{8,16},{16,24},{24,0},{32,40},{40,48},{48,56},{56,32},{64,72... | collective-permute-start | bytes 835592 | tf_op jit(solution)/shard_map/ppermute | solution.py:43
  32.9 1.7 %collective-permute-done.7 = s16[272,512]{1,0:T(8,128)(2,1)S(1)} collective-permute-done((s16[272,512]{1,0:T(8,128)(2,1)S(1)}, s16[272,512]{1,0:T(8,128)(2,1)S(1)}, u32[]{:S(2)}, u32[]{:S(2)}) %collective-permute-start.7) | collective-permute-done | bytes 278560 | tf_op jit(solution)/shard_map/ppermute | solution.py:43
  34.6 3.9 %collective-permute-done.6 = s16[272,512]{1,0:T(8,128)(2,1)S(1)} collective-permute-done((s16[272,512]{1,0:T(8,128)(2,1)S(1)}, s16[272,512]{1,0:T(8,128)(2,1)S(1)}, u32[]{:S(2)}, u32[]{:S(2)}) %collective-permute-start.6) | collective-permute-done | bytes 278560 | tf_op jit(solution)/shard_map/ppermute | solution.py:43
  38.5 1.1 collective-permute-done.5
  39.7 3.1 %collective-permute-start.10 = (s16[1088,256]{1,0:T(8,128)(2,1)S(1)}, s16[1088,256]{1,0:T(8,128)(2,1)S(1)}, u32[]{:S(2)}, u32[]{:S(2)}) collective-permute-start(s16[1088,256]{1,0:T(8,128)(2,1)S(1)} %pad_add_fusion.1.refs_0_), channel_id=1, source_target_pairs={{0,96},{8,104},{16,112},{24,120},{32,0},{40,8},{48,16},{56,24},{64... | collective-permute-start | bytes 1671176 | tf_op jit(solution)/shard_map/ppermute | solution.py:43
  44.6 11.3 %collective-permute-done.10.refs_3_ = s16[1088,256]{1,0:T(8,128)(2,1)S(1)} collective-permute-done((s16[1088,256]{1,0:T(8,128)(2,1)S(1)}, s16[1088,256]{1,0:T(8,128)(2,1)S(1)}, u32[]{:S(2)}, u32[]{:S(2)}) %collective-permute-start.10) | collective-permute-done | bytes 557088 | tf_op jit(solution)/shard_map/ppermute | solution.py:43
  55.8 4.0 %collective-permute-done.8.refs_1_ = s16[1088,256]{1,0:T(8,128)(2,1)S(1)} collective-permute-done((s16[1088,256]{1,0:T(8,128)(2,1)S(1)}, s16[1088,256]{1,0:T(8,128)(2,1)S(1)}, u32[]{:S(2)}, u32[]{:S(2)}) %collective-permute-start.8) | collective-permute-done | bytes 557088 | tf_op jit(solution)/shard_map/ppermute | solution.py:43
  61.9 3.4 %copy-done.3 = bf16[4096,1024]{1,0:T(8,128)(2,1)S(1)} copy-done((bf16[4096,1024]{1,0:T(8,128)(2,1)S(1)}, bf16[4096,1024]{1,0:T(8,128)(2,1)}, u32[]{:S(2)}) %copy-start.3) | copy-done | bytes 8388632
  65.3 5.3 %product.3 = s16[272,1024]{1,0:T(8,128)(2,1)S(1)} custom-call(s32[16]{0:T(128)S(1)} %stack.92.index_ref, bf16[4096,1024]{1,0:T(8,128)(2,1)S(1)} %copy-done.3, s16[1088,256]{1,0:T(8,128)(2,1)S(1)} %pad_add_fusion.1.refs_0_, s16[1088,256]{1,0:T(8,128)(2,1)S(1)} %collective-permute-done.8.refs_1_, s16[1088,256]{1,0:T(8,128)(2,1)S(1)} %collective-permute-done.9.refs_2_, ...), custom_call_target="tpu_custom_call" | custom-call | flops 4294967296 | bytes 10485760 | tf_op jit(solution)/shard_map/product/pallas_call | solution.py:181
  70.6 1.2 collective-permute-start.14
  71.7 5.7 %collective-permute-done.11.refs_1_ = s16[1088,256]{1,0:T(8,128)(2,1)S(1)} collective-permute-done((s16[1088,256]{1,0:T(8,128)(2,1)S(1)}, s16[1088,256]{1,0:T(8,128)(2,1)S(1)}, u32[]{:S(2)}, u32[]{:S(2)}) %collective-permute-start.11) | collective-permute-done | bytes 557088 | tf_op jit(solution)/shard_map/ppermute | solution.py:43
  77.4 5.1 %product.2.kept_ref = f32[256,1024]{1,0:T(8,128)S(1)} custom-call(s32[16]{0:T(128)S(1)} %stack.92.index_ref, bf16[4096,1024]{1,0:T(8,128)(2,1)S(1)} %copy-done.3, s16[1088,256]{1,0:T(8,128)(2,1)S(1)} %pad_add_fusion.refs_0_, s16[1088,256]{1,0:T(8,128)(2,1)S(1)} %collective-permute-done.11.refs_1_, s16[1088,256]{1,0:T(8,128)(2,1)S(1)} %collective-permute-done.12.refs_2_, ...), custom_call_target="tpu_custom_call" | custom-call | flops 4294967296 | bytes 10485760 | tf_op jit(solution)/shard_map/product/pallas_call | solution.py:181
  82.5 9.0 %collective-permute-done.14.refs_0_ = s16[272,1024]{1,0:T(8,128)(2,1)S(1)} collective-permute-done((s16[272,1024]{1,0:T(8,128)(2,1)S(1)}, s16[272,1024]{1,0:T(8,128)(2,1)S(1)}, u32[]{:S(2)}, u32[]{:S(2)}) %collective-permute-start.14) | collective-permute-done | bytes 557088 | tf_op jit(solution)/shard_map/ppermute | solution.py:264
  92.8 16.5 %all-to-all-start = ((f32[64,2,256]{2,1,0:T(2,128)}), f32[64,2,256]{2,1,0:T(2,128)S(1)}, u32[]{:S(2)}, u32[]{:S(2)}) async-start(f32[64,2,256]{2,1,0:T(2,128)} %broadcast_in_dim.15), calls=%async_computation | async-start | bytes 262144 | tf_op jit(solution)/shard_map/all_to_all | solution.py:267
  109.4 9.4 %all-to-all-done = f32[64,2,256]{2,1,0:T(2,128)S(1)} async-done(((f32[64,2,256]{2,1,0:T(2,128)}), f32[64,2,256]{2,1,0:T(2,128)S(1)}, u32[]{:S(2)}, u32[]{:S(2)}) %all-to-all-start) | async-done | bytes 131104 | tf_op jit(solution)/shard_map/all_to_all | solution.py:267
  119.0 1.3 %divide_convert_fusion = (bf16[256,1024]{1,0:T(8,128)(2,1)}, bf16[256,1024]{1,0:T(8,128)(2,1)}) fusion(f32[256,1024]{1,0:T(8,128)S(1)} %get-tuple-element.17, f32[256]{0:T(256)S(1)} %get-tuple-element.34, f32[256]{0:T(256)S(1)} %convert_multiply_fusion, f32[256]{0:T(256)S(1)} %get-tuple-element.35), kind=kLoop, calls=%fused_computation | loop fusion | flops 2883584 | bytes 2100224 | tf_op jit(solution)/shard_map/convert_element_type | solution.py:277
  (41 shorter events, 9.7 us)
Async XLA Ops:
  0.6 15.7 %collective-permute-start = (bf16[64,1024]{1,0:T(8,128)(2,1)}, bf16[64,1024]{1,0:T(8,128)(2,1)S(1)}, u32[]{:S(2)}, u32[]{:S(2)}) collective-permute-start(bf16[64,1024]{1,0:T(8,128)(2,1)} %bitcast.41), channel_id=1, source_target_pairs={{0,128},{128,0},{1,129},{129,1},{2,130},{130,2},{3,131},{131,3},{4... | collective-permute-start | bytes 393224 | tf_op jit(solution)/shard_map/ppermute | solution.py:233
  0.7 15.6 %collective-permute-start.1 = (s32[512]{0:T(512)}, s32[512]{0:T(512)S(1)}, u32[]{:S(2)}, u32[]{:S(2)}) collective-permute-start(s32[512]{0:T(512)} %param.6), channel_id=1, source_target_pairs={{0,1},{1,0},{2,3},{3,2},{4,5},{5,4},{6,7},{7,6},{8,9},{9,8},{10,11... | collective-permute-start | bytes 6152 | tf_op jit(solution)/shard_map/ppermute | solution.py:234
  8.1 0.9 copy-start
  9.0 0.7 copy-start.1
  13.1 3.2 %copy-start.2 = (bf16[4096,1024]{1,0:T(8,128)(2,1)}, bf16[4096,1024]{1,0:T(8,128)(2,1)S(1)}, u32[]{:S(2)}) copy-start(bf16[4096,1024]{1,0:T(8,128)(2,1)S(1)} %get-tuple-element.14.head_ref) | copy-start | bytes 25165828
  17.0 4.9 %collective-permute-start.4 = (s16[80,512]{1,0:T(8,128)(2,1)S(1)}, s16[80,512]{1,0:T(8,128)(2,1)S(1)}, u32[]{:S(2)}, u32[]{:S(2)}) collective-permute-start(s16[80,512]{1,0:T(8,128)(2,1)S(1)} %mix.1.a_ref), channel_id=1, source_target_pairs={{0,6},{2,0},{4,2},{6,4},{1,7},{3,1},{5,3},{7,5},{8,14},{10,8},{12,... | collective-permute-start | bytes 245768 | tf_op jit(solution)/shard_map/ppermute | solution.py:33
  19.0 8.4 %collective-permute-start.3 = (s16[80,512]{1,0:T(8,128)(2,1)S(1)}, s16[80,512]{1,0:T(8,128)(2,1)S(1)}, u32[]{:S(2)}, u32[]{:S(2)}) collective-permute-start(s16[80,512]{1,0:T(8,128)(2,1)S(1)} %mix.1.a_ref), channel_id=1, source_target_pairs={{0,4},{2,6},{4,0},{6,2},{1,5},{3,7},{5,1},{7,3},{8,12},{10,14},{12... | collective-permute-start | bytes 245768 | tf_op jit(solution)/shard_map/ppermute | solution.py:33
  19.5 7.8 %collective-permute-start.2 = (s16[80,512]{1,0:T(8,128)(2,1)S(1)}, s16[80,512]{1,0:T(8,128)(2,1)S(1)}, u32[]{:S(2)}, u32[]{:S(2)}) collective-permute-start(s16[80,512]{1,0:T(8,128)(2,1)S(1)} %mix.1.a_ref), channel_id=1, source_target_pairs={{0,2},{2,4},{4,6},{6,0},{1,3},{3,5},{5,7},{7,1},{8,10},{10,12},{12... | collective-permute-start | bytes 245768 | tf_op jit(solution)/shard_map/ppermute | solution.py:33
  28.0 6.6 %collective-permute-start.7 = (s16[272,512]{1,0:T(8,128)(2,1)S(1)}, s16[272,512]{1,0:T(8,128)(2,1)S(1)}, u32[]{:S(2)}, u32[]{:S(2)}) collective-permute-start(s16[272,512]{1,0:T(8,128)(2,1)S(1)} %stack.101), channel_id=1, source_target_pairs={{0,24},{8,0},{16,8},{24,16},{32,56},{40,32},{48,40},{56,48},{64,88... | collective-permute-start | bytes 835592 | tf_op jit(solution)/shard_map/ppermute | solution.py:43
  28.6 9.9 %collective-permute-start.6 = (s16[272,512]{1,0:T(8,128)(2,1)S(1)}, s16[272,512]{1,0:T(8,128)(2,1)S(1)}, u32[]{:S(2)}, u32[]{:S(2)}) collective-permute-start(s16[272,512]{1,0:T(8,128)(2,1)S(1)} %stack.101), channel_id=1, source_target_pairs={{0,16},{8,24},{16,0},{24,8},{32,48},{40,56},{48,32},{56,40},{64,80... | collective-permute-start | bytes 835592 | tf_op jit(solution)/shard_map/ppermute | solution.py:43
  31.0 8.6 %collective-permute-start.5 = (s16[272,512]{1,0:T(8,128)(2,1)S(1)}, s16[272,512]{1,0:T(8,128)(2,1)S(1)}, u32[]{:S(2)}, u32[]{:S(2)}) collective-permute-start(s16[272,512]{1,0:T(8,128)(2,1)S(1)} %stack.101), channel_id=1, source_target_pairs={{0,8},{8,16},{16,24},{24,0},{32,40},{40,48},{48,56},{56,32},{64,72... | collective-permute-start | bytes 835592 | tf_op jit(solution)/shard_map/ppermute | solution.py:43
  39.7 16.1 %collective-permute-start.10 = (s16[1088,256]{1,0:T(8,128)(2,1)S(1)}, s16[1088,256]{1,0:T(8,128)(2,1)S(1)}, u32[]{:S(2)}, u32[]{:S(2)}) collective-permute-start(s16[1088,256]{1,0:T(8,128)(2,1)S(1)} %pad_add_fusion.1.refs_0_), channel_id=1, source_target_pairs={{0,96},{8,104},{16,112},{24,120},{32,0},{40,8},{48,16},{56,24},{64... | collective-permute-start | bytes 1671176 | tf_op jit(solution)/shard_map/ppermute | solution.py:43
  42.8 13.0 %collective-permute-start.9 = (s16[1088,256]{1,0:T(8,128)(2,1)S(1)}, s16[1088,256]{1,0:T(8,128)(2,1)S(1)}, u32[]{:S(2)}, u32[]{:S(2)}) collective-permute-start(s16[1088,256]{1,0:T(8,128)(2,1)S(1)} %pad_add_fusion.1.refs_0_), channel_id=1, source_target_pairs={{0,64},{8,72},{16,80},{24,88},{32,96},{40,104},{48,112},{56,120},{... | collective-permute-start | bytes 1671176 | tf_op jit(solution)/shard_map/ppermute | solution.py:43
  43.4 16.4 %collective-permute-start.8 = (s16[1088,256]{1,0:T(8,128)(2,1)S(1)}, s16[1088,256]{1,0:T(8,128)(2,1)S(1)}, u32[]{:S(2)}, u32[]{:S(2)}) collective-permute-start(s16[1088,256]{1,0:T(8,128)(2,1)S(1)} %pad_add_fusion.1.refs_0_), channel_id=1, source_target_pairs={{0,32},{8,40},{16,48},{24,56},{32,64},{40,72},{48,80},{56,88},{64,... | collective-permute-start | bytes 1671176 | tf_op jit(solution)/shard_map/ppermute | solution.py:43
  59.8 11.9 %collective-permute-start.13 = (s16[1088,256]{1,0:T(8,128)(2,1)S(1)}, s16[1088,256]{1,0:T(8,128)(2,1)S(1)}, u32[]{:S(2)}, u32[]{:S(2)}) collective-permute-start(s16[1088,256]{1,0:T(8,128)(2,1)S(1)} %pad_add_fusion.refs_0_), channel_id=1, source_target_pairs={{0,96},{8,104},{16,112},{24,120},{32,0},{40,8},{48,16},{56,24},{64... | collective-permute-start | bytes 1671176 | tf_op jit(solution)/shard_map/ppermute | solution.py:43
  60.4 11.3 %collective-permute-start.12 = (s16[1088,256]{1,0:T(8,128)(2,1)S(1)}, s16[1088,256]{1,0:T(8,128)(2,1)S(1)}, u32[]{:S(2)}, u32[]{:S(2)}) collective-permute-start(s16[1088,256]{1,0:T(8,128)(2,1)S(1)} %pad_add_fusion.refs_0_), channel_id=1, source_target_pairs={{0,64},{8,72},{16,80},{24,88},{32,96},{40,104},{48,112},{56,120},{... | collective-permute-start | bytes 1671176 | tf_op jit(solution)/shard_map/ppermute | solution.py:43
  61.1 16.4 %collective-permute-start.11 = (s16[1088,256]{1,0:T(8,128)(2,1)S(1)}, s16[1088,256]{1,0:T(8,128)(2,1)S(1)}, u32[]{:S(2)}, u32[]{:S(2)}) collective-permute-start(s16[1088,256]{1,0:T(8,128)(2,1)S(1)} %pad_add_fusion.refs_0_), channel_id=1, source_target_pairs={{0,32},{8,40},{16,48},{24,56},{32,64},{40,72},{48,80},{56,88},{64,... | collective-permute-start | bytes 1671176 | tf_op jit(solution)/shard_map/ppermute | solution.py:43
  61.9 3.4 %copy-start.3 = (bf16[4096,1024]{1,0:T(8,128)(2,1)S(1)}, bf16[4096,1024]{1,0:T(8,128)(2,1)}, u32[]{:S(2)}) copy-start(bf16[4096,1024]{1,0:T(8,128)(2,1)} %copy-done.2) | copy-start | bytes 25165828
  70.5 38.8 %copy-start.5 = (s32[512]{0:T(512)S(1)}, s32[512]{0:T(512)}, u32[]{:S(2)}) copy-start(s32[512]{0:T(512)} %param.7) | copy-start | bytes 6148
  70.6 20.9 %collective-permute-start.14 = (s16[272,1024]{1,0:T(8,128)(2,1)S(1)}, s16[272,1024]{1,0:T(8,128)(2,1)S(1)}, u32[]{:S(2)}, u32[]{:S(2)}) collective-permute-start(s16[272,1024]{1,0:T(8,128)(2,1)S(1)} %product.3), channel_id=1, source_target_pairs={{0,1},{1,0},{2,3},{3,2},{4,5},{5,4},{6,7},{7,6},{8,9},{9,8},{10,11... | collective-permute-start | bytes 1671176 | tf_op jit(solution)/shard_map/ppermute | solution.py:264
  92.8 26.0 %all-to-all-start = ((f32[64,2,256]{2,1,0:T(2,128)}), f32[64,2,256]{2,1,0:T(2,128)S(1)}, u32[]{:S(2)}, u32[]{:S(2)}) async-start(f32[64,2,256]{2,1,0:T(2,128)} %broadcast_in_dim.15), calls=%async_computation | async-start | bytes 262144 | tf_op jit(solution)/shard_map/all_to_all | solution.py:267
  119.0 1.3 %copy-start.4 = (f32[256]{0:T(256)}, f32[256]{0:T(256)S(1)}, u32[]{:S(2)}) copy-start(f32[256]{0:T(256)S(1)} %get-tuple-element.34) | copy-start | bytes 3076

commit v4 on v3

--- a/solution.py
+++ b/solution.py
@@ -1,3 +1,4 @@
+import functools
 import math
 
 import jax
@@ -10,7 +11,7 @@
 AXES = ("cfg", "y", "x", "zl", "zh")
 SIZES = (2, 4, 4, 4, 2)
 TOP = 32767.0
-CHUNKS = ((0, 256), (256, 256))
+CHUNKS = ((0, 128), (128, 128), (256, 256))
 STEP = math.log(2.0) / 256.0
 
 
@@ -63,26 +64,23 @@
     return pltpu.CompilerParams(vmem_limit_bytes=mib << 20)
 
 
-def load_kernel(*refs):
-    count = len(refs) // 2
-    loads = [pltpu.make_async_copy(refs[i], refs[count + i], refs[-1].at[i]) for i in range(count)]
-    for load in loads:
-        load.start()
-    for load in loads:
-        load.wait()
-
-
-def load(*arrays):
+def load_kernel(head_ref, out_ref, done):
+    copy = pltpu.make_async_copy(head_ref, out_ref, done)
+    copy.start()
+    copy.wait()
+
+
+def load(head):
     return pl.pallas_call(
         load_kernel,
-        out_shape=[jax.ShapeDtypeStruct(a.shape, a.dtype) for a in arrays],
-        in_specs=[pl.BlockSpec(memory_space=pl.ANY)] * len(arrays),
-        out_specs=in_vmem(len(arrays)),
-        scratch_shapes=[pltpu.SemaphoreType.DMA((len(arrays),))],
+        out_shape=jax.ShapeDtypeStruct(head.shape, head.dtype),
+        in_specs=[pl.BlockSpec(memory_space=pl.ANY)],
+        out_specs=in_vmem(1)[0],
+        scratch_shapes=[pltpu.SemaphoreType.DMA],
         compiler_params=room(44),
         cost_estimate=pl.CostEstimate(flops=0, bytes_accessed=16 << 20, transcendentals=0),
         name="load",
-    )(*arrays)
+    )(head)
 
 
 def mix_kernel(place_ref, own_ref, other_ref, own_scale_ref, away_scale_ref, out_ref):
@@ -120,7 +118,7 @@
     row = lax.broadcasted_iota(jnp.int32, (16, width), 0)
     codes = jnp.zeros((16, width), jnp.int32)
     for k, ref in enumerate((a_ref, b_ref, c_ref, d_ref)):
-        place = place_ref[k]
+        place = (place_ref[4] - k) & 3
         out_ref[pl.ds(pl.multiple_of(place * 64, 64), 64), :] = ref[:64]
         codes = jnp.where(row == place, ref[64:].astype(jnp.int32), codes)
     out_ref[256:] = codes.astype(jnp.int16)
@@ -137,8 +135,26 @@
     )(place, *parts)
 
 
-def product_kernel(index_ref, head_ref, *refs):
+def pack_kernel(start, *refs):
+    out_ref = refs[-1]
+    for k in range(4):
+        out_ref[272 * k : 272 * k + 272] = refs[k][:, start : start + out_ref.shape[1]]
+
+
+def pack(line, start, count, after):
+    return pl.pallas_call(
+        functools.partial(pack_kernel, start),
+        out_shape=jax.ShapeDtypeStruct((1088, count), jnp.int16),
+        in_specs=in_vmem(4) + [pl.BlockSpec(memory_space=pl.ANY)] * len(after),
+        out_specs=in_vmem(1)[0],
+        compiler_params=room(4),
+        name="pack",
+    )(*line, *after)
+
+
+def product_kernel(place_ref, head_ref, *refs):
     parts, out_ref, total_ref = refs[:4], refs[4], refs[5]
+    core, y, x = place_ref[0], place_ref[2], place_ref[3]
     count = total_ref.shape[0] // 2
     dims = (((0,), (0,)), ((), ()))
     for k, part in enumerate(parts):
@@ -153,7 +169,9 @@
                 high.append(top)
                 low.append((values - top.astype(jnp.float32)).astype(jnp.bfloat16))
             both = jnp.concatenate([jnp.concatenate(high, 0), jnp.concatenate(low, 0)], 1)
-            weight = head_ref[pl.ds(pl.multiple_of(index_ref[4 * k + piece] * 256, 256), 256), :]
+            row = jnp.where(core == 0, y - k, y - piece) & 3
+            column = jnp.where(core == 0, x - piece, x - k) & 3
+            weight = head_ref[pl.ds(pl.multiple_of((row * 4 + column) * 256, 256), 256), :]
             term = lax.dot_general(both, weight, dims, preferred_element_type=jnp.float32)
             total = term if total is None else total + term
         if k == 0:
@@ -171,7 +189,7 @@
         out_ref[count:, :count] = across.astype(jnp.int32).astype(jnp.int16)
 
 
-def product(index, head, parts, keep):
+def product(place, head, parts, keep):
     tokens, width = parts[0].shape[1], head.shape[1]
     out = (
         jax.ShapeDtypeStruct((tokens, width), jnp.float32)
@@ -189,7 +207,7 @@
             flops=4 * tokens * 4096 * width, bytes_accessed=10 << 20, transcendentals=0
         ),
         name="product",
-    )(index, head, *parts)
+    )(place, head, *parts)
 
 
 def join_kernel(kept_ref, *refs):
@@ -207,9 +225,15 @@
         moment = jnp.sum(expo * guided, axis=1, keepdims=True)
         lane = lax.broadcasted_iota(jnp.int32, (count, 128), 1)
         table = jnp.where(lane == 0, peak + jnp.log(total), moment / total)
-        stats_ref[:, rows] = jnp.transpose(table)[:2]
+        own = jnp.transpose(table)
+        for at in range(0, count, 128):
+            for i in range(2):
+                spot = 2 * i + (start + at) // 128
+                line = own[i : i + 1, at : at + 128]
+                stats_ref[:, spot : spot + 1] = jnp.broadcast_to(line[None], (64, 1, 128))
         guided_ref[rows] = guided
         start += count
+    stats_ref[:, 4:] = jnp.zeros((64, 4, 128), jnp.float32)
 
 
 def join(kept, backs):
@@ -217,7 +241,7 @@
         join_kernel,
         out_shape=(
             jax.ShapeDtypeStruct(kept.shape, jnp.float32),
-            jax.ShapeDtypeStruct((2, kept.shape[0]), jnp.float32),
+            jax.ShapeDtypeStruct((64, 8, 128), jnp.float32),
         ),
         in_specs=in_vmem(1 + len(backs)),
         out_specs=in_vmem(2),
@@ -229,48 +253,42 @@
 def local(hidden, head, scale_index, threshold):
     core, far = lax.axis_index("cfg"), lax.axis_index("zh")
     y, x, zl = lax.axis_index("y"), lax.axis_index("x"), lax.axis_index("zl")
+    slot = jnp.arange(8)
+    place = jnp.zeros((8,), jnp.int32)
+    for i, at in enumerate((core, far, y, x, zl)):
+        place = jnp.where(slot == i, at, place)
     features = hidden[0].T
     other = lax.ppermute(features, "cfg", [(0, 1), (1, 0)])
     away_scale = lax.ppermute(scale_index, "zh", [(0, 1), (1, 0)])
     limits = lax.dynamic_slice_in_dim(threshold, core * 256, 256, 0).astype(jnp.float32) / 8.0
 
-    head, own, own_scale = load(head, features, scale_index[None])
-    mixed = mix(jnp.stack([core, far]), own, other, own_scale, away_scale[None])
-    mixed, head = lax.optimization_barrier((mixed, head))
+    mixed = mix(place, features, other, scale_index[None], away_scale[None])
+    head = load(lax.optimization_barrier((head, mixed))[0])
     near = [mixed] + [shifted(mixed, "zl", k) for k in (1, 2, 3)]
-    place = jnp.stack([(zl - k) % 4 for k in range(4)])
     column = stack(place, near)
-
-    index = []
-    for k2 in range(4):
-        for k1 in range(4):
-            a = jnp.where(core == 0, y - k2, y - k1) % 4
-            b = jnp.where(core == 0, x - k1, x - k2) % 4
-            index.append(a * 4 + b)
-    index = jnp.stack(index).astype(jnp.int32)
 
     def spread(block, first, second):
         return [block] + [crossed(block, first, second, k) for k in (1, 2, 3)]
 
     line = spread(column, "x", "y")
-    backs, before = [], ()
+    backs, before = [], (head,)
     for start, count in CHUNKS:
-        block = jnp.concatenate([part[:, start : start + count] for part in line], 0)
-        if start == 256:
-            block = lax.optimization_barrier((block, *before))[0]
-        before = spread(block, "y", "x")
-        result = product(index, head, before, start >= 256)
+        if start == 128:
+            before = before[1:2]
+        before = spread(pack(line, start, count, before), "y", "x")
+        result = product(place, head, before, start >= 256)
         if start < 256:
             backs.append(lax.ppermute(result, "zh", [(0, 1), (1, 0)]))
 
     guided, stats = join(result, backs)
-    stats = lax.all_to_all(jnp.broadcast_to(stats, (64, 2, 256)), ("y", "x", "zl"), 0, 0, tiled=True)
-    each, mean = stats[:, 0], stats[:, 1]
+    stats = lax.all_to_all(stats, ("y", "x", "zl"), 0, 0, tiled=True)
+    each, mean = stats[:, :2], stats[:, 2:4]
     top = jnp.max(each, axis=0)
     weight = jnp.exp(each - top)
     total = jnp.sum(weight, axis=0)
     lse = top + jnp.log(total)
     entropy = lse - jnp.sum(weight * mean, axis=0) / total
+    lse, entropy = lse.reshape(256), entropy.reshape(256)
     logprob = guided - lse[:, None]
     deviation = -logprob - entropy[:, None]
     typical = jax.nn.sigmoid(2.0 * (limits[:, None] - jnp.abs(deviation)))

time: 121 us -> 115 us (0.950)
  starting transfers between devices: 40.3 us -> 49.6 us
  waiting for transfers between devices: 52.8 us -> 43.6 us
  local copies, waits for them, and re-layouts: 9.09 us -> 1.6 us
  Pallas kernels: 15.6 us -> 17.3 us
    ppermute x9 -> x12, waiting for transfers between devices: 27.7 us -> 18.4 us  [crossed(): return lax.ppermute(block, axes, pairs(axes, move))]
    unnamed x12 -> x8, local copies, waits for them, and re-layouts: 8.22 us -> 1.6 us
    ppermute x1 -> x2, starting transfers between devices: 1.16 us -> 6.1 us  [local(): backs.append(lax.ppermute(result, 'zh', [(0, 1), (1, 0)]))]
    ppermute x9 -> x12, starting transfers between devices: 11.7 us -> 16.1 us  [crossed(): return lax.ppermute(block, axes, pairs(axes, move))]
    ppermute x1 -> x2, waiting for transfers between devices: 8.96 us -> 6.86 us  [local(): backs.append(lax.ppermute(result, 'zh', [(0, 1), (1, 0)]))]
    ppermute x1, waiting for transfers between devices: 0.01 us -> 1.77 us  [local(): away_scale = lax.ppermute(scale_index, 'zh', [(0, 1), (1, 0)])]
    pallas_call x2 -> x3, Pallas kernels: 10.4 us -> 11.2 us  [product(): pl.pallas_call(product_kernel, out_shape=out, in_specs=[pl.BlockSpec(memo...]
    pallas_call x1 -> x4, Pallas kernels: 3.41 us -> 3.52 us  [the longest x1 3.39 us: load(): pl.pallas_call(load_kernel, out_shape=jax.ShapeDtypeStruct(head.shape, he...]
  transfers between devices with their start and end apart: 16 -> 20, of which waited for: 10 -> 13; matrix products, arithmetic and copies ran while one was open for 0% -> 0% of each run, Pallas kernels for 11% -> 13%
where the time goes in v4:
time: 115 us; the launch traced here: 114 us
  starting transfers between devices  49.6 us (43%)
  waiting for transfers between devices  43.6 us (38%)
  Pallas kernels  17.3 us (15%)
  local copies, waits for them, and re-layouts  1.6 us (1%)
  other arithmetic  1.54 us (1%)
    ppermute x12, waiting for transfers between devices, crossed(): return lax.ppermute(block, axes, pairs(axes, move))  18.4 us
    ppermute x12, starting transfers between devices, crossed(): return lax.ppermute(block, axes, pairs(axes, move))  16.1 us
    all_to_all x1, starting transfers between devices, local(): stats = lax.all_to_all(stats, ('y', 'x', 'zl'), 0, 0, tiled=True)  16 us
    pallas_call x3, Pallas kernels, product(): pl.pallas_call(product_kernel, out_shape=out, in_specs=[pl.BlockSpec(memo...  11.2 us
    all_to_all x1, waiting for transfers between devices, local(): stats = lax.all_to_all(stats, ('y', 'x', 'zl'), 0, 0, tiled=True)  10.3 us
    ppermute x1, starting transfers between devices, local(): away_scale = lax.ppermute(scale_index, 'zh', [(0, 1), (1, 0)])  7.28 us
    ppermute x2, waiting for transfers between devices, local(): backs.append(lax.ppermute(result, 'zh', [(0, 1), (1, 0)]))  6.86 us
    ppermute x3, waiting for transfers between devices, shifted(): lax.ppermute(block, axis, pairs((axis,), lambda at: {axis: at[axis] + k}))  6.21 us
  transfers between devices with their start and end apart: 20, of which 13 were waited for; matrix products, arithmetic and copies ran while one was open for 0% of the time, Pallas kernels for 13%

profile of v4, /device:TPU:2, one launch (start us, length us, event | category | flops | bytes accessed | tf_op | source)
XLA Modules:
  0.0 114.4 jit_solution(8311748814848479084)
XLA Ops:
  0.7 7.3 %collective-permute-start.1 = (s32[512]{0:T(512)}, s32[512]{0:T(512)S(1)}, u32[]{:S(2)}, u32[]{:S(2)}) collective-permute-start(s32[512]{0:T(512)} %param.6), channel_id=1, source_target_pairs={{0,1},{1,0},{2,3},{3,2},{4,5},{5,4},{6,7},{7,6},{8,9},{9,8},{10,11... | collective-permute-start | bytes 6152 | tf_op jit(solution)/shard_map/ppermute | solution.py:262
  8.0 1.8 %collective-permute-done.1 = s32[512]{0:T(512)S(1)} collective-permute-done((s32[512]{0:T(512)}, s32[512]{0:T(512)S(1)}, u32[]{:S(2)}, u32[]{:S(2)}) %collective-permute-start.1) | collective-permute-done | bytes 2080 | tf_op jit(solution)/shard_map/ppermute | solution.py:262
  12.0 3.4 %collective-permute-start.4 = (s16[80,512]{1,0:T(8,128)(2,1)S(1)}, s16[80,512]{1,0:T(8,128)(2,1)S(1)}, u32[]{:S(2)}, u32[]{:S(2)}) collective-permute-start(s16[80,512]{1,0:T(8,128)(2,1)S(1)} %mix.1.a_ref), channel_id=1, source_target_pairs={{0,6},{2,0},{4,2},{6,4},{1,7},{3,1},{5,3},{7,5},{8,14},{10,8},{12,... | collective-permute-start | bytes 245768 | tf_op jit(solution)/shard_map/ppermute | solution.py:34
  16.1 2.2 %collective-permute-done.4.d_ref = s16[80,512]{1,0:T(8,128)(2,1)S(1)} collective-permute-done((s16[80,512]{1,0:T(8,128)(2,1)S(1)}, s16[80,512]{1,0:T(8,128)(2,1)S(1)}, u32[]{:S(2)}, u32[]{:S(2)}) %collective-permute-start.4) | collective-permute-done | bytes 81952 | tf_op jit(solution)/shard_map/ppermute | solution.py:34
  18.3 4.0 %collective-permute-done.3.c_ref = s16[80,512]{1,0:T(8,128)(2,1)S(1)} collective-permute-done((s16[80,512]{1,0:T(8,128)(2,1)S(1)}, s16[80,512]{1,0:T(8,128)(2,1)S(1)}, u32[]{:S(2)}, u32[]{:S(2)}) %collective-permute-start.3) | collective-permute-done | bytes 81952 | tf_op jit(solution)/shard_map/ppermute | solution.py:34
  23.5 2.4 %collective-permute-start.6 = (s16[272,512]{1,0:T(8,128)(2,1)S(1)}, s16[272,512]{1,0:T(8,128)(2,1)S(1)}, u32[]{:S(2)}, u32[]{:S(2)}) collective-permute-start(s16[272,512]{1,0:T(8,128)(2,1)S(1)} %stack.1.refs_0_), channel_id=1, source_target_pairs={{0,16},{8,24},{16,0},{24,8},{32,48},{40,56},{48,32},{56,40},{64,80... | collective-permute-start | bytes 835592 | tf_op jit(solution)/shard_map/ppermute | solution.py:44
  25.9 1.8 %collective-permute-start.5 = (s16[272,512]{1,0:T(8,128)(2,1)S(1)}, s16[272,512]{1,0:T(8,128)(2,1)S(1)}, u32[]{:S(2)}, u32[]{:S(2)}) collective-permute-start(s16[272,512]{1,0:T(8,128)(2,1)S(1)} %stack.1.refs_0_), channel_id=1, source_target_pairs={{0,8},{8,16},{16,24},{24,0},{32,40},{40,48},{48,56},{56,32},{64,72... | collective-permute-start | bytes 835592 | tf_op jit(solution)/shard_map/ppermute | solution.py:44
  27.7 3.4 %load.1.refs_4_.head_ref = bf16[4096,1024]{1,0:T(8,128)(2,1)S(1)} custom-call(bf16[4096,1024]{1,0:T(8,128)(2,1)} %head_ref), custom_call_target="tpu_custom_call" | custom-call | bytes 16777216 | tf_op jit(solution)/shard_map/load/pallas_call | solution.py:74
  31.1 2.3 %collective-permute-done.6.refs_2_ = s16[272,512]{1,0:T(8,128)(2,1)S(1)} collective-permute-done((s16[272,512]{1,0:T(8,128)(2,1)S(1)}, s16[272,512]{1,0:T(8,128)(2,1)S(1)}, u32[]{:S(2)}, u32[]{:S(2)}) %collective-permute-start.6) | collective-permute-done | bytes 278560 | tf_op jit(solution)/shard_map/ppermute | solution.py:44
  34.7 1.7 %collective-permute-start.8 = (s16[1088,128]{1,0:T(8,128)(2,1)S(1)}, s16[1088,128]{1,0:T(8,128)(2,1)S(1)}, u32[]{:S(2)}, u32[]{:S(2)}) collective-permute-start(s16[1088,128]{1,0:T(8,128)(2,1)S(1)} %pack.3.refs_0_), channel_id=1, source_target_pairs={{0,32},{8,40},{16,48},{24,56},{32,64},{40,72},{48,80},{56,88},{64,... | collective-permute-start | bytes 835592 | tf_op jit(solution)/shard_map/ppermute | solution.py:44
  36.3 6.2 %collective-permute-done.8.refs_4_.refs_1_ = s16[1088,128]{1,0:T(8,128)(2,1)S(1)} collective-permute-done((s16[1088,128]{1,0:T(8,128)(2,1)S(1)}, s16[1088,128]{1,0:T(8,128)(2,1)S(1)}, u32[]{:S(2)}, u32[]{:S(2)}) %collective-permute-start.8) | collective-permute-done | bytes 278560 | tf_op jit(solution)/shard_map/ppermute | solution.py:44
  42.6 1.9 %collective-permute-start.11 = (s16[1088,128]{1,0:T(8,128)(2,1)S(1)}, s16[1088,128]{1,0:T(8,128)(2,1)S(1)}, u32[]{:S(2)}, u32[]{:S(2)}) collective-permute-start(s16[1088,128]{1,0:T(8,128)(2,1)S(1)} %pack.4.refs_4_.refs_0_), channel_id=1, source_target_pairs={{0,96},{8,104},{16,112},{24,120},{32,0},{40,8},{48,16},{56,24},{64... | collective-permute-start | bytes 835592 | tf_op jit(solution)/shard_map/ppermute | solution.py:44
  46.0 2.3 %collective-permute-start.16 = (s16[1088,128]{1,0:T(8,128)(2,1)S(1)}, s16[1088,128]{1,0:T(8,128)(2,1)S(1)}, u32[]{:S(2)}, u32[]{:S(2)}) collective-permute-start(s16[1088,128]{1,0:T(8,128)(2,1)S(1)} %pack.3.refs_0_), channel_id=1, source_target_pairs={{0,96},{8,104},{16,112},{24,120},{32,0},{40,8},{48,16},{56,24},{64... | collective-permute-start | bytes 835592 | tf_op jit(solution)/shard_map/ppermute | solution.py:44
  48.3 1.7 %collective-permute-start.15 = (s16[1088,128]{1,0:T(8,128)(2,1)S(1)}, s16[1088,128]{1,0:T(8,128)(2,1)S(1)}, u32[]{:S(2)}, u32[]{:S(2)}) collective-permute-start(s16[1088,128]{1,0:T(8,128)(2,1)S(1)} %pack.3.refs_0_), channel_id=1, source_target_pairs={{0,64},{8,72},{16,80},{24,88},{32,96},{40,104},{48,112},{56,120},{... | collective-permute-start | bytes 835592 | tf_op jit(solution)/shard_map/ppermute | solution.py:44
  50.0 1.5 %collective-permute-done.11.refs_7_.refs_3_ = s16[1088,128]{1,0:T(8,128)(2,1)S(1)} collective-permute-done((s16[1088,128]{1,0:T(8,128)(2,1)S(1)}, s16[1088,128]{1,0:T(8,128)(2,1)S(1)}, u32[]{:S(2)}, u32[]{:S(2)}) %collective-permute-start.11) | collective-permute-done | bytes 278560 | tf_op jit(solution)/shard_map/ppermute | solution.py:44
  52.6 2.9 %collective-permute-done.9.refs_5_.refs_1_ = s16[1088,128]{1,0:T(8,128)(2,1)S(1)} collective-permute-done((s16[1088,128]{1,0:T(8,128)(2,1)S(1)}, s16[1088,128]{1,0:T(8,128)(2,1)S(1)}, u32[]{:S(2)}, u32[]{:S(2)}) %collective-permute-start.9) | collective-permute-done | bytes 278560 | tf_op jit(solution)/shard_map/ppermute | solution.py:44
  58.5 3.1 %product.4 = s16[144,1024]{1,0:T(8,128)(2,1)S(1)} custom-call(s32[8]{0:T(128)S(1)} %compare_select_fusion.4.place_ref, bf16[4096,1024]{1,0:T(8,128)(2,1)S(1)} %load.1.refs_4_.head_ref, s16[1088,128]{1,0:T(8,128)(2,1)S(1)} %pack.3.refs_0_, s16[1088,128]{1,0:T(8,128)(2,1)S(1)} %collective-permute-done.8.refs_4_.refs_1_, ...), custom_call_target="tpu_custom_call" | custom-call | flops 2147483648 | bytes 10485760 | tf_op jit(solution)/shard_map/product/pallas_call | solution.py:199
  61.6 5.9 %collective-permute-start.17 = (s16[144,1024]{1,0:T(8,128)(2,1)S(1)}, s16[144,1024]{1,0:T(8,128)(2,1)S(1)}, u32[]{:S(2)}, u32[]{:S(2)}) collective-permute-start(s16[144,1024]{1,0:T(8,128)(2,1)S(1)} %product.4), channel_id=1, source_target_pairs={{0,1},{1,0},{2,3},{3,2},{4,5},{5,4},{6,7},{7,6},{8,9},{9,8},{10,11... | collective-permute-start | bytes 884744 | tf_op jit(solution)/shard_map/ppermute | solution.py:281
  67.4 3.1 %product.5 = s16[144,1024]{1,0:T(8,128)(2,1)S(1)} custom-call(s32[8]{0:T(128)S(1)} %compare_select_fusion.4.place_ref, bf16[4096,1024]{1,0:T(8,128)(2,1)S(1)} %load.1.refs_4_.head_ref, s16[1088,128]{1,0:T(8,128)(2,1)S(1)} %pack.4.refs_4_.refs_0_, s16[1088,128]{1,0:T(8,128)(2,1)S(1)} %collective-permute-done.9.refs_5_.refs_1_, ...), custom_call_target="tpu_custom_call" | custom-call | flops 2147483648 | bytes 10485760 | tf_op jit(solution)/shard_map/product/pallas_call | solution.py:199
  70.8 2.4 %collective-permute-done.12.refs_1_ = s16[1088,256]{1,0:T(8,128)(2,1)S(1)} collective-permute-done((s16[1088,256]{1,0:T(8,128)(2,1)S(1)}, s16[1088,256]{1,0:T(8,128)(2,1)S(1)}, u32[]{:S(2)}, u32[]{:S(2)}) %collective-permute-start.12) | collective-permute-done | bytes 557088 | tf_op jit(solution)/shard_map/ppermute | solution.py:44
  73.2 5.1 %product.3.kept_ref = f32[256,1024]{1,0:T(8,128)S(1)} custom-call(s32[8]{0:T(128)S(1)} %compare_select_fusion.4.place_ref, bf16[4096,1024]{1,0:T(8,128)(2,1)S(1)} %load.1.refs_4_.head_ref, s16[1088,256]{1,0:T(8,128)(2,1)S(1)} %pack.5.refs_0_, s16[1088,256]{1,0:T(8,128)(2,1)S(1)} %collective-permute-done.12.refs_1_, ...), custom_call_target="tpu_custom_call" | custom-call | flops 4294967296 | bytes 10485760 | tf_op jit(solution)/shard_map/product/pallas_call | solution.py:199
  78.3 6.9 %collective-permute-done.18.refs_1_ = s16[144,1024]{1,0:T(8,128)(2,1)S(1)} collective-permute-done((s16[144,1024]{1,0:T(8,128)(2,1)S(1)}, s16[144,1024]{1,0:T(8,128)(2,1)S(1)}, u32[]{:S(2)}, u32[]{:S(2)}) %collective-permute-start.18) | collective-permute-done | bytes 294944 | tf_op jit(solution)/shard_map/ppermute | solution.py:281
  86.5 16.0 %all-to-all-start = ((f32[64,8,128]{2,1,0:T(8,128)}), f32[64,8,128]{2,1,0:T(8,128)S(1)}, u32[]{:S(2)}, u32[]{:S(2)}) async-start(f32[64,8,128]{2,1,0:T(8,128)} %get-tuple-element.8), calls=%async_computation | async-start | bytes 524288 | tf_op jit(solution)/shard_map/all_to_all | solution.py:284
  102.6 10.3 %all-to-all-done = f32[64,8,128]{2,1,0:T(8,128)S(1)} async-done(((f32[64,8,128]{2,1,0:T(8,128)}), f32[64,8,128]{2,1,0:T(8,128)S(1)}, u32[]{:S(2)}, u32[]{:S(2)}) %all-to-all-start) | async-done | bytes 262176 | tf_op jit(solution)/shard_map/all_to_all | solution.py:284
  (40 shorter events, 14.3 us)
Async XLA Ops:
  0.6 9.2 %collective-permute-start = (bf16[64,1024]{1,0:T(8,128)(2,1)}, bf16[64,1024]{1,0:T(8,128)(2,1)S(1)}, u32[]{:S(2)}, u32[]{:S(2)}) collective-permute-start(bf16[64,1024]{1,0:T(8,128)(2,1)} %bitcast.10), channel_id=1, source_target_pairs={{0,128},{128,0},{1,129},{129,1},{2,130},{130,2},{3,131},{131,3},{4... | collective-permute-start | bytes 393224 | tf_op jit(solution)/shard_map/ppermute | solution.py:261
  0.7 9.1 %collective-permute-start.1 = (s32[512]{0:T(512)}, s32[512]{0:T(512)S(1)}, u32[]{:S(2)}, u32[]{:S(2)}) collective-permute-start(s32[512]{0:T(512)} %param.6), channel_id=1, source_target_pairs={{0,1},{1,0},{2,3},{3,2},{4,5},{5,4},{6,7},{7,6},{8,9},{9,8},{10,11... | collective-permute-start | bytes 6152 | tf_op jit(solution)/shard_map/ppermute | solution.py:262
  9.8 0.9 copy-start
  10.7 0.7 copy-start.1
  12.0 6.3 %collective-permute-start.4 = (s16[80,512]{1,0:T(8,128)(2,1)S(1)}, s16[80,512]{1,0:T(8,128)(2,1)S(1)}, u32[]{:S(2)}, u32[]{:S(2)}) collective-permute-start(s16[80,512]{1,0:T(8,128)(2,1)S(1)} %mix.1.a_ref), channel_id=1, source_target_pairs={{0,6},{2,0},{4,2},{6,4},{1,7},{3,1},{5,3},{7,5},{8,14},{10,8},{12,... | collective-permute-start | bytes 245768 | tf_op jit(solution)/shard_map/ppermute | solution.py:34
  15.4 6.9 %collective-permute-start.3 = (s16[80,512]{1,0:T(8,128)(2,1)S(1)}, s16[80,512]{1,0:T(8,128)(2,1)S(1)}, u32[]{:S(2)}, u32[]{:S(2)}) collective-permute-start(s16[80,512]{1,0:T(8,128)(2,1)S(1)} %mix.1.a_ref), channel_id=1, source_target_pairs={{0,4},{2,6},{4,0},{6,2},{1,5},{3,7},{5,1},{7,3},{8,12},{10,14},{12... | collective-permute-start | bytes 245768 | tf_op jit(solution)/shard_map/ppermute | solution.py:34
  15.4 6.9 %collective-permute-start.2 = (s16[80,512]{1,0:T(8,128)(2,1)S(1)}, s16[80,512]{1,0:T(8,128)(2,1)S(1)}, u32[]{:S(2)}, u32[]{:S(2)}) collective-permute-start(s16[80,512]{1,0:T(8,128)(2,1)S(1)} %mix.1.a_ref), channel_id=1, source_target_pairs={{0,2},{2,4},{4,6},{6,0},{1,3},{3,5},{5,7},{7,1},{8,10},{10,12},{12... | collective-permute-start | bytes 245768 | tf_op jit(solution)/shard_map/ppermute | solution.py:34
  22.9 8.2 %collective-permute-start.7 = (s16[272,512]{1,0:T(8,128)(2,1)S(1)}, s16[272,512]{1,0:T(8,128)(2,1)S(1)}, u32[]{:S(2)}, u32[]{:S(2)}) collective-permute-start(s16[272,512]{1,0:T(8,128)(2,1)S(1)} %stack.1.refs_0_), channel_id=1, source_target_pairs={{0,24},{8,0},{16,8},{24,16},{32,56},{40,32},{48,40},{56,48},{64,88... | collective-permute-start | bytes 835592 | tf_op jit(solution)/shard_map/ppermute | solution.py:44
  23.5 9.9 %collective-permute-start.6 = (s16[272,512]{1,0:T(8,128)(2,1)S(1)}, s16[272,512]{1,0:T(8,128)(2,1)S(1)}, u32[]{:S(2)}, u32[]{:S(2)}) collective-permute-start(s16[272,512]{1,0:T(8,128)(2,1)S(1)} %stack.1.refs_0_), channel_id=1, source_target_pairs={{0,16},{8,24},{16,0},{24,8},{32,48},{40,56},{48,32},{56,40},{64,80... | collective-permute-start | bytes 835592 | tf_op jit(solution)/shard_map/ppermute | solution.py:44
  25.9 8.7 %collective-permute-start.5 = (s16[272,512]{1,0:T(8,128)(2,1)S(1)}, s16[272,512]{1,0:T(8,128)(2,1)S(1)}, u32[]{:S(2)}, u32[]{:S(2)}) collective-permute-start(s16[272,512]{1,0:T(8,128)(2,1)S(1)} %stack.1.refs_0_), channel_id=1, source_target_pairs={{0,8},{8,16},{16,24},{24,0},{32,40},{40,48},{48,56},{56,32},{64,72... | collective-permute-start | bytes 835592 | tf_op jit(solution)/shard_map/ppermute | solution.py:44
  34.7 7.8 %collective-permute-start.8 = (s16[1088,128]{1,0:T(8,128)(2,1)S(1)}, s16[1088,128]{1,0:T(8,128)(2,1)S(1)}, u32[]{:S(2)}, u32[]{:S(2)}) collective-permute-start(s16[1088,128]{1,0:T(8,128)(2,1)S(1)} %pack.3.refs_0_), channel_id=1, source_target_pairs={{0,32},{8,40},{16,48},{24,56},{32,64},{40,72},{48,80},{56,88},{64,... | collective-permute-start | bytes 835592 | tf_op jit(solution)/shard_map/ppermute | solution.py:44
  42.6 9.0 %collective-permute-start.11 = (s16[1088,128]{1,0:T(8,128)(2,1)S(1)}, s16[1088,128]{1,0:T(8,128)(2,1)S(1)}, u32[]{:S(2)}, u32[]{:S(2)}) collective-permute-start(s16[1088,128]{1,0:T(8,128)(2,1)S(1)} %pack.4.refs_4_.refs_0_), channel_id=1, source_target_pairs={{0,96},{8,104},{16,112},{24,120},{32,0},{40,8},{48,16},{56,24},{64... | collective-permute-start | bytes 835592 | tf_op jit(solution)/shard_map/ppermute | solution.py:44
  44.4 8.2 %collective-permute-start.10 = (s16[1088,128]{1,0:T(8,128)(2,1)S(1)}, s16[1088,128]{1,0:T(8,128)(2,1)S(1)}, u32[]{:S(2)}, u32[]{:S(2)}) collective-permute-start(s16[1088,128]{1,0:T(8,128)(2,1)S(1)} %pack.4.refs_4_.refs_0_), channel_id=1, source_target_pairs={{0,64},{8,72},{16,80},{24,88},{32,96},{40,104},{48,112},{56,120},{... | collective-permute-start | bytes 835592 | tf_op jit(solution)/shard_map/ppermute | solution.py:44
  45.1 10.4 %collective-permute-start.9 = (s16[1088,128]{1,0:T(8,128)(2,1)S(1)}, s16[1088,128]{1,0:T(8,128)(2,1)S(1)}, u32[]{:S(2)}, u32[]{:S(2)}) collective-permute-start(s16[1088,128]{1,0:T(8,128)(2,1)S(1)} %pack.4.refs_4_.refs_0_), channel_id=1, source_target_pairs={{0,32},{8,40},{16,48},{24,56},{32,64},{40,72},{48,80},{56,88},{64,... | collective-permute-start | bytes 835592 | tf_op jit(solution)/shard_map/ppermute | solution.py:44
  46.0 11.6 %collective-permute-start.16 = (s16[1088,128]{1,0:T(8,128)(2,1)S(1)}, s16[1088,128]{1,0:T(8,128)(2,1)S(1)}, u32[]{:S(2)}, u32[]{:S(2)}) collective-permute-start(s16[1088,128]{1,0:T(8,128)(2,1)S(1)} %pack.3.refs_0_), channel_id=1, source_target_pairs={{0,96},{8,104},{16,112},{24,120},{32,0},{40,8},{48,16},{56,24},{64... | collective-permute-start | bytes 835592 | tf_op jit(solution)/shard_map/ppermute | solution.py:44
  48.3 10.2 %collective-permute-start.15 = (s16[1088,128]{1,0:T(8,128)(2,1)S(1)}, s16[1088,128]{1,0:T(8,128)(2,1)S(1)}, u32[]{:S(2)}, u32[]{:S(2)}) collective-permute-start(s16[1088,128]{1,0:T(8,128)(2,1)S(1)} %pack.3.refs_0_), channel_id=1, source_target_pairs={{0,64},{8,72},{16,80},{24,88},{32,96},{40,104},{48,112},{56,120},{... | collective-permute-start | bytes 835592 | tf_op jit(solution)/shard_map/ppermute | solution.py:44
  55.5 15.3 %collective-permute-start.14 = (s16[1088,256]{1,0:T(8,128)(2,1)S(1)}, s16[1088,256]{1,0:T(8,128)(2,1)S(1)}, u32[]{:S(2)}, u32[]{:S(2)}) collective-permute-start(s16[1088,256]{1,0:T(8,128)(2,1)S(1)} %pack.5.refs_0_), channel_id=1, source_target_pairs={{0,96},{8,104},{16,112},{24,120},{32,0},{40,8},{48,16},{56,24},{64... | collective-permute-start | bytes 1671176 | tf_op jit(solution)/shard_map/ppermute | solution.py:44
  56.2 14.6 %collective-permute-start.13 = (s16[1088,256]{1,0:T(8,128)(2,1)S(1)}, s16[1088,256]{1,0:T(8,128)(2,1)S(1)}, u32[]{:S(2)}, u32[]{:S(2)}) collective-permute-start(s16[1088,256]{1,0:T(8,128)(2,1)S(1)} %pack.5.refs_0_), channel_id=1, source_target_pairs={{0,64},{8,72},{16,80},{24,88},{32,96},{40,104},{48,112},{56,120},{... | collective-permute-start | bytes 1671176 | tf_op jit(solution)/shard_map/ppermute | solution.py:44
  56.8 16.4 %collective-permute-start.12 = (s16[1088,256]{1,0:T(8,128)(2,1)S(1)}, s16[1088,256]{1,0:T(8,128)(2,1)S(1)}, u32[]{:S(2)}, u32[]{:S(2)}) collective-permute-start(s16[1088,256]{1,0:T(8,128)(2,1)S(1)} %pack.5.refs_0_), channel_id=1, source_target_pairs={{0,32},{8,40},{16,48},{24,56},{32,64},{40,72},{48,80},{56,88},{64,... | collective-permute-start | bytes 1671176 | tf_op jit(solution)/shard_map/ppermute | solution.py:44
  61.6 16.7 %collective-permute-start.17 = (s16[144,1024]{1,0:T(8,128)(2,1)S(1)}, s16[144,1024]{1,0:T(8,128)(2,1)S(1)}, u32[]{:S(2)}, u32[]{:S(2)}) collective-permute-start(s16[144,1024]{1,0:T(8,128)(2,1)S(1)} %product.4), channel_id=1, source_target_pairs={{0,1},{1,0},{2,3},{3,2},{4,5},{5,4},{6,7},{7,6},{8,9},{9,8},{10,11... | collective-permute-start | bytes 884744 | tf_op jit(solution)/shard_map/ppermute | solution.py:281
  70.5 32.0 %copy-start.3 = (s32[512]{0:T(512)S(1)}, s32[512]{0:T(512)}, u32[]{:S(2)}) copy-start(s32[512]{0:T(512)} %param.7) | copy-start | bytes 6148
  70.5 14.6 %collective-permute-start.18 = (s16[144,1024]{1,0:T(8,128)(2,1)S(1)}, s16[144,1024]{1,0:T(8,128)(2,1)S(1)}, u32[]{:S(2)}, u32[]{:S(2)}) collective-permute-start(s16[144,1024]{1,0:T(8,128)(2,1)S(1)} %product.5), channel_id=1, source_target_pairs={{0,1},{1,0},{2,3},{3,2},{4,5},{5,4},{6,7},{7,6},{8,9},{9,8},{10,11... | collective-permute-start | bytes 884744 | tf_op jit(solution)/shard_map/ppermute | solution.py:281
  86.5 26.4 %all-to-all-start = ((f32[64,8,128]{2,1,0:T(8,128)}), f32[64,8,128]{2,1,0:T(8,128)S(1)}, u32[]{:S(2)}, u32[]{:S(2)}) async-start(f32[64,8,128]{2,1,0:T(8,128)} %get-tuple-element.8), calls=%async_computation | async-start | bytes 524288 | tf_op jit(solution)/shard_map/all_to_all | solution.py:284
  113.1 1.3 %copy-start.2 = (f32[256]{0:T(256)}, f32[256]{0:T(256)S(1)}, u32[]{:S(2)}) copy-start(f32[256]{0:T(256)S(1)} %get-tuple-element.11) | copy-start | bytes 3076

commit v5 on v4

--- a/solution.py
+++ b/solution.py
@@ -1,4 +1,3 @@
-import functools
 import math
 
 import jax
@@ -11,7 +10,6 @@
 AXES = ("cfg", "y", "x", "zl", "zh")
 SIZES = (2, 4, 4, 4, 2)
 TOP = 32767.0
-CHUNKS = ((0, 128), (128, 128), (256, 256))
 STEP = math.log(2.0) / 256.0
 
 
@@ -60,30 +58,39 @@
     return [pl.BlockSpec(memory_space=pltpu.VMEM)] * count
 
 
+def anywhere(arrays):
+    return [pl.BlockSpec(memory_space=pl.ANY)] * len(arrays)
+
+
 def room(mib):
     return pltpu.CompilerParams(vmem_limit_bytes=mib << 20)
 
 
-def load_kernel(head_ref, out_ref, done):
-    copy = pltpu.make_async_copy(head_ref, out_ref, done)
-    copy.start()
-    copy.wait()
-
-
-def load(head):
+def load_kernel(*refs):
+    count = len(refs) // 2
+    copies = [pltpu.make_async_copy(refs[i], refs[count + i], refs[-1].at[i]) for i in range(count)]
+    for copy in copies:
+        copy.start()
+    for copy in copies:
+        copy.wait()
+
+
+def load(*arrays):
     return pl.pallas_call(
         load_kernel,
-        out_shape=jax.ShapeDtypeStruct(head.shape, head.dtype),
-        in_specs=[pl.BlockSpec(memory_space=pl.ANY)],
-        out_specs=in_vmem(1)[0],
-        scratch_shapes=[pltpu.SemaphoreType.DMA],
+        out_shape=[jax.ShapeDtypeStruct(a.shape, a.dtype) for a in arrays],
+        in_specs=anywhere(arrays),
+        out_specs=in_vmem(len(arrays)),
+        scratch_shapes=[pltpu.SemaphoreType.DMA((len(arrays),))],
         compiler_params=room(44),
-        cost_estimate=pl.CostEstimate(flops=0, bytes_accessed=16 << 20, transcendentals=0),
+        cost_estimate=pl.CostEstimate(
+            flops=0, bytes_accessed=2 * sum(a.size * a.dtype.itemsize for a in arrays), transcendentals=0
+        ),
         name="load",
-    )(head)
-
-
-def mix_kernel(place_ref, own_ref, other_ref, own_scale_ref, away_scale_ref, out_ref):
+    )(*arrays)
+
+
+def mix_kernel(place_ref, own_ref, other_ref, own_scale_ref, away_scale_ref, *out_refs):
     core, far = place_ref[0], place_ref[1]
     first = core == 0
     for n, half in enumerate((1 - far, far)):
@@ -97,23 +104,38 @@
         uncond = jnp.where(first, other, own)
         mixed = uncond + guide * (cond - uncond)
         code = code_of(jnp.max(jnp.abs(mixed), axis=0, keepdims=True))
-        at = slice(256 * n, 256 * n + 256)
-        out_ref[:64, at] = coded(mixed, scale_of(code))
-        out_ref[64:, at] = jnp.broadcast_to(code, (16, 256)).astype(jnp.int32).astype(jnp.int16)
+        out_refs[n][:64] = coded(mixed, scale_of(code))
+        out_refs[n][64:] = jnp.broadcast_to(code, (16, 256)).astype(jnp.int32).astype(jnp.int16)
 
 
 def mix(place, own, other, own_scale, away_scale):
     return pl.pallas_call(
         mix_kernel,
-        out_shape=jax.ShapeDtypeStruct((80, 512), jnp.int16),
+        out_shape=[jax.ShapeDtypeStruct((80, 256), jnp.int16)] * 2,
         in_specs=[pl.BlockSpec(memory_space=pltpu.SMEM)] + in_vmem(4),
-        out_specs=in_vmem(1)[0],
+        out_specs=in_vmem(2),
         compiler_params=room(4),
         name="mix",
     )(place, own, other, own_scale, away_scale)
 
 
-def stack_kernel(place_ref, a_ref, b_ref, c_ref, d_ref, out_ref):
+def hold_kernel(block_ref, *refs):
+    refs[-1][...] = block_ref[...]
+
+
+def hold(block, after):
+    return pl.pallas_call(
+        hold_kernel,
+        out_shape=jax.ShapeDtypeStruct(block.shape, block.dtype),
+        in_specs=in_vmem(1) + anywhere(after),
+        out_specs=in_vmem(1)[0],
+        compiler_params=room(4),
+        name="hold",
+    )(block, *after)
+
+
+def stack_kernel(place_ref, a_ref, b_ref, c_ref, d_ref, *refs):
+    out_ref = refs[-1]
     width = a_ref.shape[1]
     row = lax.broadcasted_iota(jnp.int32, (16, width), 0)
     codes = jnp.zeros((16, width), jnp.int32)
@@ -124,28 +146,27 @@
     out_ref[256:] = codes.astype(jnp.int16)
 
 
-def stack(place, parts):
+def stack(place, parts, after):
     return pl.pallas_call(
         stack_kernel,
         out_shape=jax.ShapeDtypeStruct((272, parts[0].shape[1]), jnp.int16),
-        in_specs=[pl.BlockSpec(memory_space=pltpu.SMEM)] + in_vmem(4),
+        in_specs=[pl.BlockSpec(memory_space=pltpu.SMEM)] + in_vmem(4) + anywhere(after),
         out_specs=in_vmem(1)[0],
         compiler_params=room(4),
         name="stack",
-    )(place, *parts)
-
-
-def pack_kernel(start, *refs):
-    out_ref = refs[-1]
+    )(place, *parts, *after)
+
+
+def pack_kernel(*refs):
     for k in range(4):
-        out_ref[272 * k : 272 * k + 272] = refs[k][:, start : start + out_ref.shape[1]]
-
-
-def pack(line, start, count, after):
-    return pl.pallas_call(
-        functools.partial(pack_kernel, start),
-        out_shape=jax.ShapeDtypeStruct((1088, count), jnp.int16),
-        in_specs=in_vmem(4) + [pl.BlockSpec(memory_space=pl.ANY)] * len(after),
+        refs[-1][272 * k : 272 * k + 272] = refs[k][...]
+
+
+def pack(line, after):
+    return pl.pallas_call(
+        pack_kernel,
+        out_shape=jax.ShapeDtypeStruct((1088, line[0].shape[1]), jnp.int16),
+        in_specs=in_vmem(4) + anywhere(after),
         out_specs=in_vmem(1)[0],
         compiler_params=room(4),
         name="pack",
@@ -153,7 +174,7 @@
 
 
 def product_kernel(place_ref, head_ref, *refs):
-    parts, out_ref, total_ref = refs[:4], refs[4], refs[5]
+    parts, out_ref, total_ref = refs[:4], refs[-2], refs[-1]
     core, y, x = place_ref[0], place_ref[2], place_ref[3]
     count = total_ref.shape[0] // 2
     dims = (((0,), (0,)), ((), ()))
@@ -189,7 +210,7 @@
         out_ref[count:, :count] = across.astype(jnp.int32).astype(jnp.int16)
 
 
-def product(place, head, parts, keep):
+def product(place, head, parts, keep, after):
     tokens, width = parts[0].shape[1], head.shape[1]
     out = (
         jax.ShapeDtypeStruct((tokens, width), jnp.float32)
@@ -199,7 +220,7 @@
     return pl.pallas_call(
         product_kernel,
         out_shape=out,
-        in_specs=[pl.BlockSpec(memory_space=pltpu.SMEM)] + in_vmem(5),
+        in_specs=[pl.BlockSpec(memory_space=pltpu.SMEM)] + in_vmem(5) + anywhere(after),
         out_specs=in_vmem(1)[0],
         scratch_shapes=[pltpu.VMEM((2 * tokens, width), jnp.float32)],
         compiler_params=room(24),
@@ -207,47 +228,37 @@
             flops=4 * tokens * 4096 * width, bytes_accessed=10 << 20, transcendentals=0
         ),
         name="product",
-    )(place, head, *parts)
-
-
-def join_kernel(kept_ref, *refs):
-    backs, guided_ref, stats_ref = refs[:-2], refs[-2], refs[-1]
-    start = 0
-    for back_ref in backs:
-        count = back_ref.shape[0] - 16
-        rows = slice(start, start + count)
-        codes = back_ref[count:, :count].astype(jnp.float32)[:1]
-        scale = jnp.transpose(jnp.broadcast_to(scale_of(codes), (128, count)))[:, :1]
-        guided = kept_ref[rows] + back_ref[:count].astype(jnp.float32) * scale
-        peak = jnp.max(guided, axis=1, keepdims=True)
-        expo = jnp.exp(guided - peak)
-        total = jnp.sum(expo, axis=1, keepdims=True)
-        moment = jnp.sum(expo * guided, axis=1, keepdims=True)
-        lane = lax.broadcasted_iota(jnp.int32, (count, 128), 1)
-        table = jnp.where(lane == 0, peak + jnp.log(total), moment / total)
-        own = jnp.transpose(table)
-        for at in range(0, count, 128):
-            for i in range(2):
-                spot = 2 * i + (start + at) // 128
-                line = own[i : i + 1, at : at + 128]
-                stats_ref[:, spot : spot + 1] = jnp.broadcast_to(line[None], (64, 1, 128))
-        guided_ref[rows] = guided
-        start += count
-    stats_ref[:, 4:] = jnp.zeros((64, 4, 128), jnp.float32)
-
-
-def join(kept, backs):
+    )(place, head, *parts, *after)
+
+
+def join_kernel(kept_ref, back_ref, guided_ref, stats_ref):
+    codes = back_ref[256:, :256].astype(jnp.float32)[:1]
+    scale = jnp.transpose(jnp.broadcast_to(scale_of(codes), (128, 256)))[:, :1]
+    guided = kept_ref[...] + back_ref[:256].astype(jnp.float32) * scale
+    peak = jnp.max(guided, axis=1, keepdims=True)
+    expo = jnp.exp(guided - peak)
+    total = jnp.sum(expo, axis=1, keepdims=True)
+    moment = jnp.sum(expo * guided, axis=1, keepdims=True)
+    lane = lax.broadcasted_iota(jnp.int32, (256, 128), 1)
+    table = jnp.transpose(jnp.where(lane == 0, peak + jnp.log(total), moment / total))
+    rows = [table[i : i + 1, at : at + 128] for i in (0, 1) for at in (0, 128)]
+    tile = jnp.concatenate(rows + [jnp.zeros((4, 128), jnp.float32)], 0)
+    stats_ref[...] = jnp.broadcast_to(tile[None], (64, 8, 128))
+    guided_ref[...] = guided
+
+
+def join(kept, back):
     return pl.pallas_call(
         join_kernel,
         out_shape=(
             jax.ShapeDtypeStruct(kept.shape, jnp.float32),
             jax.ShapeDtypeStruct((64, 8, 128), jnp.float32),
         ),
-        in_specs=in_vmem(1 + len(backs)),
+        in_specs=in_vmem(2),
         out_specs=in_vmem(2),
         compiler_params=room(12),
         name="join",
-    )(kept, *backs)
+    )(kept, back)
 
 
 def local(hidden, head, scale_index, threshold):
@@ -262,25 +273,28 @@
     away_scale = lax.ppermute(scale_index, "zh", [(0, 1), (1, 0)])
     limits = lax.dynamic_slice_in_dim(threshold, core * 256, 256, 0).astype(jnp.float32) / 8.0
 
-    mixed = mix(place, features, other, scale_index[None], away_scale[None])
-    head = load(lax.optimization_barrier((head, mixed))[0])
-    near = [mixed] + [shifted(mixed, "zl", k) for k in (1, 2, 3)]
-    column = stack(place, near)
+    own, own_scale = load(features, scale_index[None])
+    away, home = mix(place, own, other, own_scale, away_scale[None])
+    (head,) = load(lax.optimization_barrier((head, away))[0])
+
+    def near(block):
+        return [block] + [shifted(block, "zl", k) for k in (1, 2, 3)]
 
     def spread(block, first, second):
         return [block] + [crossed(block, first, second, k) for k in (1, 2, 3)]
 
-    line = spread(column, "x", "y")
-    backs, before = [], (head,)
-    for start, count in CHUNKS:
-        if start == 128:
-            before = before[1:2]
-        before = spread(pack(line, start, count, before), "y", "x")
-        result = product(place, head, before, start >= 256)
-        if start < 256:
-            backs.append(lax.ppermute(result, "zh", [(0, 1), (1, 0)]))
-
-    guided, stats = join(result, backs)
+    away_near = near(away)
+    home_near = near(hold(home, away_near[1:]))
+    away_line = spread(stack(place, away_near, (head,)), "x", "y")
+    away_block = pack(away_line, ())
+    away_parts = spread(away_block, "y", "x")
+    home_line = spread(stack(place, home_near, (away_block,)), "x", "y")
+    sent = product(place, head, away_parts, False, ())
+    back = lax.ppermute(sent, "zh", [(0, 1), (1, 0)])
+    home_parts = spread(pack(home_line, (sent,)), "y", "x")
+    kept = product(place, head, home_parts, True, ())
+
+    guided, stats = join(kept, back)
     stats = lax.all_to_all(stats, ("y", "x", "zl"), 0, 0, tiled=True)
     each, mean = stats[:, :2], stats[:, 2:4]
     top = jnp.max(each, axis=0)

time: 115 us -> 107 us (0.930)
  waiting for transfers between devices: 43.6 us -> 31.5 us
  starting transfers between devices: 49.6 us -> 54.4 us
    ppermute x12, waiting for transfers between devices: 18.4 us -> 7.12 us  [crossed(): return lax.ppermute(block, axes, pairs(axes, move))]
    all_to_all x1, starting transfers between devices: 16 us -> 7.34 us  [local(): stats = lax.all_to_all(stats, ('y', 'x', 'zl'), 0, 0, tiled=True)]
    ppermute x12, starting transfers between devices: 16.1 us -> 21.6 us  [crossed(): return lax.ppermute(block, axes, pairs(axes, move))]
    ppermute x3 -> x6, starting transfers between devices: 4.11 us -> 8.48 us  [shifted(): lax.ppermute(block, axis, pairs((axis,), lambda at: {axis: at[axis] + k}))]
    ppermute x2 -> x1, starting transfers between devices: 6.1 us -> 9.59 us  [local(): back = lax.ppermute(sent, 'zh', [(0, 1), (1, 0)])]
    ppermute x1, waiting for transfers between devices: 1.77 us -> 0.02 us  [local(): away_scale = lax.ppermute(scale_index, 'zh', [(0, 1), (1, 0)])]
    pallas_call x3 -> x2, Pallas kernels: 11.2 us -> 10.4 us  [product(): pl.pallas_call(product_kernel, out_shape=out, in_specs=[pl.BlockSpec(memo...]
    ppermute x2 -> x1, waiting for transfers between devices: 6.86 us -> 7.63 us  [local(): back = lax.ppermute(sent, 'zh', [(0, 1), (1, 0)])]
  transfers between devices with their start and end apart: 20 -> 22, of which waited for: 13 -> 9; matrix products, arithmetic and copies ran while one was open for 0% -> 0% of each run, Pallas kernels for 13% -> 14%
where the time goes in v5:
time: 107 us
  starting transfers between devices  54.4 us (51%)
  waiting for transfers between devices  31.5 us (29%)
  Pallas kernels  17.1 us (16%)
  local copies, waits for them, and re-layouts  1.6 us (1%)
  other arithmetic  1.54 us (1%)
    ppermute x12, starting transfers between devices, crossed(): return lax.ppermute(block, axes, pairs(axes, move))  21.6 us
    pallas_call x2, Pallas kernels, product(): pl.pallas_call(product_kernel, out_shape=out, in_specs=[pl.BlockSpec(memo...  10.4 us
    all_to_all x1, waiting for transfers between devices, local(): stats = lax.all_to_all(stats, ('y', 'x', 'zl'), 0, 0, tiled=True)  10.3 us
    ppermute x1, starting transfers between devices, local(): back = lax.ppermute(sent, 'zh', [(0, 1), (1, 0)])  9.59 us
    ppermute x6, starting transfers between devices, shifted(): lax.ppermute(block, axis, pairs((axis,), lambda at: {axis: at[axis] + k}))  8.48 us
    ppermute x1, waiting for transfers between devices, local(): back = lax.ppermute(sent, 'zh', [(0, 1), (1, 0)])  7.63 us
    all_to_all x1, starting transfers between devices, local(): stats = lax.all_to_all(stats, ('y', 'x', 'zl'), 0, 0, tiled=True)  7.34 us
    ppermute x1, starting transfers between devices, local(): away_scale = lax.ppermute(scale_index, 'zh', [(0, 1), (1, 0)])  7.28 us
  transfers between devices with their start and end apart: 22, of which 9 were waited for; matrix products, arithmetic and copies ran while one was open for 0% of the time, Pallas kernels for 14%

profile of v5, /device:TPU:2, one launch (start us, length us, event | category | flops | bytes accessed | tf_op | source)
XLA Modules:
  0.0 106.8 jit_solution(4234652537475288672)
XLA Ops:
  0.7 7.3 %collective-permute-start.1 = (s32[512]{0:T(512)}, s32[512]{0:T(512)S(1)}, u32[]{:S(2)}, u32[]{:S(2)}) collective-permute-start(s32[512]{0:T(512)} %param.6), channel_id=1, source_target_pairs={{0,1},{1,0},{2,3},{3,2},{4,5},{5,4},{6,7},{7,6},{8,9},{9,8},{10,11... | collective-permute-start | bytes 6152 | tf_op jit(solution)/shard_map/ppermute | solution.py:273
  11.5 2.9 %collective-permute-start.3 = (s16[80,256]{1,0:T(8,128)(2,1)S(1)}, s16[80,256]{1,0:T(8,128)(2,1)S(1)}, u32[]{:S(2)}, u32[]{:S(2)}) collective-permute-start(s16[80,256]{1,0:T(8,128)(2,1)S(1)} %get-tuple-element.12.a_ref), channel_id=1, source_target_pairs={{0,4},{2,6},{4,0},{6,2},{1,5},{3,7},{5,1},{7,3},{8,12},{10,14},{12... | collective-permute-start | bytes 122888 | tf_op jit(solution)/shard_map/ppermute | solution.py:32
  15.4 3.4 %load.3.refs_0_.head_ref = bf16[4096,1024]{1,0:T(8,128)(2,1)S(1)} custom-call(bf16[4096,1024]{1,0:T(8,128)(2,1)} %refs_0_), custom_call_target="tpu_custom_call" | custom-call | bytes 16777216 | tf_op jit(solution)/shard_map/load/pallas_call | solution.py:79
  20.0 1.5 %collective-permute-start.8 = (s16[272,256]{1,0:T(8,128)(2,1)S(1)}, s16[272,256]{1,0:T(8,128)(2,1)S(1)}, u32[]{:S(2)}, u32[]{:S(2)}) collective-permute-start(s16[272,256]{1,0:T(8,128)(2,1)S(1)} %stack.2.refs_0_), channel_id=1, source_target_pairs={{0,8},{8,16},{16,24},{24,0},{32,40},{40,48},{48,56},{56,32},{64,72... | collective-permute-start | bytes 417800 | tf_op jit(solution)/shard_map/ppermute | solution.py:42
  21.5 3.3 %collective-permute-start.9 = (s16[272,256]{1,0:T(8,128)(2,1)S(1)}, s16[272,256]{1,0:T(8,128)(2,1)S(1)}, u32[]{:S(2)}, u32[]{:S(2)}) collective-permute-start(s16[272,256]{1,0:T(8,128)(2,1)S(1)} %stack.2.refs_0_), channel_id=1, source_target_pairs={{0,16},{8,24},{16,0},{24,8},{32,48},{40,56},{48,32},{56,40},{64,80... | collective-permute-start | bytes 417800 | tf_op jit(solution)/shard_map/ppermute | solution.py:42
  25.8 2.3 %collective-permute-done.9.refs_2_ = s16[272,256]{1,0:T(8,128)(2,1)S(1)} collective-permute-done((s16[272,256]{1,0:T(8,128)(2,1)S(1)}, s16[272,256]{1,0:T(8,128)(2,1)S(1)}, u32[]{:S(2)}, u32[]{:S(2)}) %collective-permute-start.9) | collective-permute-done | bytes 139296 | tf_op jit(solution)/shard_map/ppermute | solution.py:42
  28.1 1.7 %collective-permute-start.14 = (s16[1088,256]{1,0:T(8,128)(2,1)S(1)}, s16[1088,256]{1,0:T(8,128)(2,1)S(1)}, u32[]{:S(2)}, u32[]{:S(2)}) collective-permute-start(s16[1088,256]{1,0:T(8,128)(2,1)S(1)} %pack.2.refs_0_), channel_id=1, source_target_pairs={{0,32},{8,40},{16,48},{24,56},{32,64},{40,72},{48,80},{56,88},{64,... | collective-permute-start | bytes 1671176 | tf_op jit(solution)/shard_map/ppermute | solution.py:42
  29.8 2.9 %collective-permute-start.15 = (s16[1088,256]{1,0:T(8,128)(2,1)S(1)}, s16[1088,256]{1,0:T(8,128)(2,1)S(1)}, u32[]{:S(2)}, u32[]{:S(2)}) collective-permute-start(s16[1088,256]{1,0:T(8,128)(2,1)S(1)} %pack.2.refs_0_), channel_id=1, source_target_pairs={{0,64},{8,72},{16,80},{24,88},{32,96},{40,104},{48,112},{56,120},{... | collective-permute-start | bytes 1671176 | tf_op jit(solution)/shard_map/ppermute | solution.py:42
  32.7 1.3 %collective-permute-start.16 = (s16[1088,256]{1,0:T(8,128)(2,1)S(1)}, s16[1088,256]{1,0:T(8,128)(2,1)S(1)}, u32[]{:S(2)}, u32[]{:S(2)}) collective-permute-start(s16[1088,256]{1,0:T(8,128)(2,1)S(1)} %pack.2.refs_0_), channel_id=1, source_target_pairs={{0,96},{8,104},{16,112},{24,120},{32,0},{40,8},{48,16},{56,24},{64... | collective-permute-start | bytes 1671176 | tf_op jit(solution)/shard_map/ppermute | solution.py:42
  35.1 1.9 %collective-permute-start.6 = (s16[80,256]{1,0:T(8,128)(2,1)S(1)}, s16[80,256]{1,0:T(8,128)(2,1)S(1)}, u32[]{:S(2)}, u32[]{:S(2)}) collective-permute-start(s16[80,256]{1,0:T(8,128)(2,1)S(1)} %hold.1.a_ref), channel_id=1, source_target_pairs={{0,4},{2,6},{4,0},{6,2},{1,5},{3,7},{5,1},{7,3},{8,12},{10,14},{12... | collective-permute-start | bytes 122888 | tf_op jit(solution)/shard_map/ppermute | solution.py:32
  37.0 2.9 %collective-permute-done.5.b_ref = s16[80,256]{1,0:T(8,128)(2,1)S(1)} collective-permute-done((s16[80,256]{1,0:T(8,128)(2,1)S(1)}, s16[80,256]{1,0:T(8,128)(2,1)S(1)}, u32[]{:S(2)}, u32[]{:S(2)}) %collective-permute-start.5) | collective-permute-done | bytes 40992 | tf_op jit(solution)/shard_map/ppermute | solution.py:32
  40.7 3.2 %collective-permute-done.7.d_ref = s16[80,256]{1,0:T(8,128)(2,1)S(1)} collective-permute-done((s16[80,256]{1,0:T(8,128)(2,1)S(1)}, s16[80,256]{1,0:T(8,128)(2,1)S(1)}, u32[]{:S(2)}, u32[]{:S(2)}) %collective-permute-start.7) | collective-permute-done | bytes 40992 | tf_op jit(solution)/shard_map/ppermute | solution.py:32
  44.4 1.8 %collective-permute-start.11 = (s16[272,256]{1,0:T(8,128)(2,1)S(1)}, s16[272,256]{1,0:T(8,128)(2,1)S(1)}, u32[]{:S(2)}, u32[]{:S(2)}) collective-permute-start(s16[272,256]{1,0:T(8,128)(2,1)S(1)} %stack.3.refs_0_), channel_id=1, source_target_pairs={{0,8},{8,16},{16,24},{24,0},{32,40},{40,48},{48,56},{56,32},{64,72... | collective-permute-start | bytes 417800 | tf_op jit(solution)/shard_map/ppermute | solution.py:42
  46.2 3.6 %collective-permute-start.12 = (s16[272,256]{1,0:T(8,128)(2,1)S(1)}, s16[272,256]{1,0:T(8,128)(2,1)S(1)}, u32[]{:S(2)}, u32[]{:S(2)}) collective-permute-start(s16[272,256]{1,0:T(8,128)(2,1)S(1)} %stack.3.refs_0_), channel_id=1, source_target_pairs={{0,16},{8,24},{16,0},{24,8},{32,48},{40,56},{48,32},{56,40},{64,80... | collective-permute-start | bytes 417800 | tf_op jit(solution)/shard_map/ppermute | solution.py:42
  50.5 5.3 %product.2.refs_4_ = s16[272,1024]{1,0:T(8,128)(2,1)S(1)} custom-call(s32[8]{0:T(128)S(1)} %compare_select_fusion.4.place_ref, bf16[4096,1024]{1,0:T(8,128)(2,1)S(1)} %load.3.refs_0_.head_ref, s16[1088,256]{1,0:T(8,128)(2,1)S(1)} %pack.2.refs_0_, s16[1088,256]{1,0:T(8,128)(2,1)S(1)} %collective-permute-done.14.refs_1_, ...), custom_call_target="tpu_custom_call" | custom-call | flops 4294967296 | bytes 10485760 | tf_op jit(solution)/shard_map/product/pallas_call | solution.py:220
  56.6 1.3 %collective-permute-start.18 = (s16[1088,256]{1,0:T(8,128)(2,1)S(1)}, s16[1088,256]{1,0:T(8,128)(2,1)S(1)}, u32[]{:S(2)}, u32[]{:S(2)}) collective-permute-start(s16[1088,256]{1,0:T(8,128)(2,1)S(1)} %pack.3.refs_0_), channel_id=1, source_target_pairs={{0,64},{8,72},{16,80},{24,88},{32,96},{40,104},{48,112},{56,120},{... | collective-permute-start | bytes 1671176 | tf_op jit(solution)/shard_map/ppermute | solution.py:42
  58.0 2.1 %collective-permute-start.19 = (s16[1088,256]{1,0:T(8,128)(2,1)S(1)}, s16[1088,256]{1,0:T(8,128)(2,1)S(1)}, u32[]{:S(2)}, u32[]{:S(2)}) collective-permute-start(s16[1088,256]{1,0:T(8,128)(2,1)S(1)} %pack.3.refs_0_), channel_id=1, source_target_pairs={{0,96},{8,104},{16,112},{24,120},{32,0},{40,8},{48,16},{56,24},{64... | collective-permute-start | bytes 1671176 | tf_op jit(solution)/shard_map/ppermute | solution.py:42
  60.1 9.6 %collective-permute-start.20 = (s16[272,1024]{1,0:T(8,128)(2,1)S(1)}, s16[272,1024]{1,0:T(8,128)(2,1)S(1)}, u32[]{:S(2)}, u32[]{:S(2)}) collective-permute-start(s16[272,1024]{1,0:T(8,128)(2,1)S(1)} %product.2.refs_4_), channel_id=1, source_target_pairs={{0,1},{1,0},{2,3},{3,2},{4,5},{5,4},{6,7},{7,6},{8,9},{9,8},{10,11... | collective-permute-start | bytes 1671176 | tf_op jit(solution)/shard_map/ppermute | solution.py:293
  69.7 3.0 %collective-permute-done.17.refs_1_ = s16[1088,256]{1,0:T(8,128)(2,1)S(1)} collective-permute-done((s16[1088,256]{1,0:T(8,128)(2,1)S(1)}, s16[1088,256]{1,0:T(8,128)(2,1)S(1)}, u32[]{:S(2)}, u32[]{:S(2)}) %collective-permute-start.17) | collective-permute-done | bytes 557088 | tf_op jit(solution)/shard_map/ppermute | solution.py:42
  73.6 5.1 %product.3.kept_ref = f32[256,1024]{1,0:T(8,128)S(1)} custom-call(s32[8]{0:T(128)S(1)} %compare_select_fusion.4.place_ref, bf16[4096,1024]{1,0:T(8,128)(2,1)S(1)} %load.3.refs_0_.head_ref, s16[1088,256]{1,0:T(8,128)(2,1)S(1)} %pack.3.refs_0_, s16[1088,256]{1,0:T(8,128)(2,1)S(1)} %collective-permute-done.17.refs_1_, ...), custom_call_target="tpu_custom_call" | custom-call | flops 4294967296 | bytes 10485760 | tf_op jit(solution)/shard_map/product/pallas_call | solution.py:220
  78.7 7.6 %collective-permute-done.20.back_ref = s16[272,1024]{1,0:T(8,128)(2,1)S(1)} collective-permute-done((s16[272,1024]{1,0:T(8,128)(2,1)S(1)}, s16[272,1024]{1,0:T(8,128)(2,1)S(1)}, u32[]{:S(2)}, u32[]{:S(2)}) %collective-permute-start.20) | collective-permute-done | bytes 557088 | tf_op jit(solution)/shard_map/ppermute | solution.py:293
  86.3 1.3 %join.1 = (f32[256,1024]{1,0:T(8,128)S(1)}, f32[64,8,128]{2,1,0:T(8,128)}) custom-call(f32[256,1024]{1,0:T(8,128)S(1)} %product.3.kept_ref, s16[272,1024]{1,0:T(8,128)(2,1)S(1)} %collective-permute-done.20.back_ref), custom_call_target="tpu_custom_call" | custom-call | tf_op jit(solution)/shard_map/join/pallas_call | solution.py:251
  87.6 7.3 %all-to-all-start = ((f32[64,8,128]{2,1,0:T(8,128)}), f32[64,8,128]{2,1,0:T(8,128)S(1)}, u32[]{:S(2)}, u32[]{:S(2)}) async-start(f32[64,8,128]{2,1,0:T(8,128)} %get-tuple-element.16), calls=%async_computation | async-start | bytes 524288 | tf_op jit(solution)/shard_map/all_to_all | solution.py:298
  95.1 10.3 %all-to-all-done = f32[64,8,128]{2,1,0:T(8,128)S(1)} async-done(((f32[64,8,128]{2,1,0:T(8,128)}), f32[64,8,128]{2,1,0:T(8,128)S(1)}, u32[]{:S(2)}, u32[]{:S(2)}) %all-to-all-start) | async-done | bytes 262176 | tf_op jit(solution)/shard_map/all_to_all | solution.py:298
  (45 shorter events, 13.1 us)
Async XLA Ops:
  0.6 9.2 %collective-permute-start = (bf16[64,1024]{1,0:T(8,128)(2,1)}, bf16[64,1024]{1,0:T(8,128)(2,1)S(1)}, u32[]{:S(2)}, u32[]{:S(2)}) collective-permute-start(bf16[64,1024]{1,0:T(8,128)(2,1)} %bitcast.10), channel_id=1, source_target_pairs={{0,128},{128,0},{1,129},{129,1},{2,130},{130,2},{3,131},{131,3},{4... | collective-permute-start | bytes 393224 | tf_op jit(solution)/shard_map/ppermute | solution.py:272
  0.7 9.1 %collective-permute-start.1 = (s32[512]{0:T(512)}, s32[512]{0:T(512)S(1)}, u32[]{:S(2)}, u32[]{:S(2)}) collective-permute-start(s32[512]{0:T(512)} %param.6), channel_id=1, source_target_pairs={{0,1},{1,0},{2,3},{3,2},{4,5},{5,4},{6,7},{7,6},{8,9},{9,8},{10,11... | collective-permute-start | bytes 6152 | tf_op jit(solution)/shard_map/ppermute | solution.py:273
  10.4 8.4 %collective-permute-start.2 = (s16[80,256]{1,0:T(8,128)(2,1)S(1)}, s16[80,256]{1,0:T(8,128)(2,1)S(1)}, u32[]{:S(2)}, u32[]{:S(2)}) collective-permute-start(s16[80,256]{1,0:T(8,128)(2,1)S(1)} %get-tuple-element.12.a_ref), channel_id=1, source_target_pairs={{0,2},{2,4},{4,6},{6,0},{1,3},{3,5},{5,7},{7,1},{8,10},{10,12},{12... | collective-permute-start | bytes 122888 | tf_op jit(solution)/shard_map/ppermute | solution.py:32
  11.5 7.3 %collective-permute-start.3 = (s16[80,256]{1,0:T(8,128)(2,1)S(1)}, s16[80,256]{1,0:T(8,128)(2,1)S(1)}, u32[]{:S(2)}, u32[]{:S(2)}) collective-permute-start(s16[80,256]{1,0:T(8,128)(2,1)S(1)} %get-tuple-element.12.a_ref), channel_id=1, source_target_pairs={{0,4},{2,6},{4,0},{6,2},{1,5},{3,7},{5,1},{7,3},{8,12},{10,14},{12... | collective-permute-start | bytes 122888 | tf_op jit(solution)/shard_map/ppermute | solution.py:32
  14.4 4.4 %collective-permute-start.4 = (s16[80,256]{1,0:T(8,128)(2,1)S(1)}, s16[80,256]{1,0:T(8,128)(2,1)S(1)}, u32[]{:S(2)}, u32[]{:S(2)}) collective-permute-start(s16[80,256]{1,0:T(8,128)(2,1)S(1)} %get-tuple-element.12.a_ref), channel_id=1, source_target_pairs={{0,6},{2,0},{4,2},{6,4},{1,7},{3,1},{5,3},{7,5},{8,14},{10,8},{12,... | collective-permute-start | bytes 122888 | tf_op jit(solution)/shard_map/ppermute | solution.py:32
  19.4 5.4 %collective-permute-start.10 = (s16[272,256]{1,0:T(8,128)(2,1)S(1)}, s16[272,256]{1,0:T(8,128)(2,1)S(1)}, u32[]{:S(2)}, u32[]{:S(2)}) collective-permute-start(s16[272,256]{1,0:T(8,128)(2,1)S(1)} %stack.2.refs_0_), channel_id=1, source_target_pairs={{0,24},{8,0},{16,8},{24,16},{32,56},{40,32},{48,40},{56,48},{64,88... | collective-permute-start | bytes 417800 | tf_op jit(solution)/shard_map/ppermute | solution.py:42
  20.0 5.8 %collective-permute-start.8 = (s16[272,256]{1,0:T(8,128)(2,1)S(1)}, s16[272,256]{1,0:T(8,128)(2,1)S(1)}, u32[]{:S(2)}, u32[]{:S(2)}) collective-permute-start(s16[272,256]{1,0:T(8,128)(2,1)S(1)} %stack.2.refs_0_), channel_id=1, source_target_pairs={{0,8},{8,16},{16,24},{24,0},{32,40},{40,48},{48,56},{56,32},{64,72... | collective-permute-start | bytes 417800 | tf_op jit(solution)/shard_map/ppermute | solution.py:42
  21.5 6.6 %collective-permute-start.9 = (s16[272,256]{1,0:T(8,128)(2,1)S(1)}, s16[272,256]{1,0:T(8,128)(2,1)S(1)}, u32[]{:S(2)}, u32[]{:S(2)}) collective-permute-start(s16[272,256]{1,0:T(8,128)(2,1)S(1)} %stack.2.refs_0_), channel_id=1, source_target_pairs={{0,16},{8,24},{16,0},{24,8},{32,48},{40,56},{48,32},{56,40},{64,80... | collective-permute-start | bytes 417800 | tf_op jit(solution)/shard_map/ppermute | solution.py:42
  28.1 21.7 %collective-permute-start.14 = (s16[1088,256]{1,0:T(8,128)(2,1)S(1)}, s16[1088,256]{1,0:T(8,128)(2,1)S(1)}, u32[]{:S(2)}, u32[]{:S(2)}) collective-permute-start(s16[1088,256]{1,0:T(8,128)(2,1)S(1)} %pack.2.refs_0_), channel_id=1, source_target_pairs={{0,32},{8,40},{16,48},{24,56},{32,64},{40,72},{48,80},{56,88},{64,... | collective-permute-start | bytes 1671176 | tf_op jit(solution)/shard_map/ppermute | solution.py:42
  29.8 20.7 %collective-permute-start.15 = (s16[1088,256]{1,0:T(8,128)(2,1)S(1)}, s16[1088,256]{1,0:T(8,128)(2,1)S(1)}, u32[]{:S(2)}, u32[]{:S(2)}) collective-permute-start(s16[1088,256]{1,0:T(8,128)(2,1)S(1)} %pack.2.refs_0_), channel_id=1, source_target_pairs={{0,64},{8,72},{16,80},{24,88},{32,96},{40,104},{48,112},{56,120},{... | collective-permute-start | bytes 1671176 | tf_op jit(solution)/shard_map/ppermute | solution.py:42
  32.7 17.8 %collective-permute-start.16 = (s16[1088,256]{1,0:T(8,128)(2,1)S(1)}, s16[1088,256]{1,0:T(8,128)(2,1)S(1)}, u32[]{:S(2)}, u32[]{:S(2)}) collective-permute-start(s16[1088,256]{1,0:T(8,128)(2,1)S(1)} %pack.2.refs_0_), channel_id=1, source_target_pairs={{0,96},{8,104},{16,112},{24,120},{32,0},{40,8},{48,16},{56,24},{64... | collective-permute-start | bytes 1671176 | tf_op jit(solution)/shard_map/ppermute | solution.py:42
  34.0 5.8 %collective-permute-start.5 = (s16[80,256]{1,0:T(8,128)(2,1)S(1)}, s16[80,256]{1,0:T(8,128)(2,1)S(1)}, u32[]{:S(2)}, u32[]{:S(2)}) collective-permute-start(s16[80,256]{1,0:T(8,128)(2,1)S(1)} %hold.1.a_ref), channel_id=1, source_target_pairs={{0,2},{2,4},{4,6},{6,0},{1,3},{3,5},{5,7},{7,1},{8,10},{10,12},{12... | collective-permute-start | bytes 122888 | tf_op jit(solution)/shard_map/ppermute | solution.py:32
  35.1 5.7 %collective-permute-start.6 = (s16[80,256]{1,0:T(8,128)(2,1)S(1)}, s16[80,256]{1,0:T(8,128)(2,1)S(1)}, u32[]{:S(2)}, u32[]{:S(2)}) collective-permute-start(s16[80,256]{1,0:T(8,128)(2,1)S(1)} %hold.1.a_ref), channel_id=1, source_target_pairs={{0,4},{2,6},{4,0},{6,2},{1,5},{3,7},{5,1},{7,3},{8,12},{10,14},{12... | collective-permute-start | bytes 122888 | tf_op jit(solution)/shard_map/ppermute | solution.py:32
  39.9 4.0 %collective-permute-start.7 = (s16[80,256]{1,0:T(8,128)(2,1)S(1)}, s16[80,256]{1,0:T(8,128)(2,1)S(1)}, u32[]{:S(2)}, u32[]{:S(2)}) collective-permute-start(s16[80,256]{1,0:T(8,128)(2,1)S(1)} %hold.1.a_ref), channel_id=1, source_target_pairs={{0,6},{2,0},{4,2},{6,4},{1,7},{3,1},{5,3},{7,5},{8,14},{10,8},{12,... | collective-permute-start | bytes 122888 | tf_op jit(solution)/shard_map/ppermute | solution.py:32
  44.4 11.4 %collective-permute-start.11 = (s16[272,256]{1,0:T(8,128)(2,1)S(1)}, s16[272,256]{1,0:T(8,128)(2,1)S(1)}, u32[]{:S(2)}, u32[]{:S(2)}) collective-permute-start(s16[272,256]{1,0:T(8,128)(2,1)S(1)} %stack.3.refs_0_), channel_id=1, source_target_pairs={{0,8},{8,16},{16,24},{24,0},{32,40},{40,48},{48,56},{56,32},{64,72... | collective-permute-start | bytes 417800 | tf_op jit(solution)/shard_map/ppermute | solution.py:42
  46.2 9.6 %collective-permute-start.12 = (s16[272,256]{1,0:T(8,128)(2,1)S(1)}, s16[272,256]{1,0:T(8,128)(2,1)S(1)}, u32[]{:S(2)}, u32[]{:S(2)}) collective-permute-start(s16[272,256]{1,0:T(8,128)(2,1)S(1)} %stack.3.refs_0_), channel_id=1, source_target_pairs={{0,16},{8,24},{16,0},{24,8},{32,48},{40,56},{48,32},{56,40},{64,80... | collective-permute-start | bytes 417800 | tf_op jit(solution)/shard_map/ppermute | solution.py:42
  49.8 6.0 %collective-permute-start.13 = (s16[272,256]{1,0:T(8,128)(2,1)S(1)}, s16[272,256]{1,0:T(8,128)(2,1)S(1)}, u32[]{:S(2)}, u32[]{:S(2)}) collective-permute-start(s16[272,256]{1,0:T(8,128)(2,1)S(1)} %stack.3.refs_0_), channel_id=1, source_target_pairs={{0,24},{8,0},{16,8},{24,16},{32,56},{40,32},{48,40},{56,48},{64,88... | collective-permute-start | bytes 417800 | tf_op jit(solution)/shard_map/ppermute | solution.py:42
  55.9 39.1 %copy-start.3 = (s32[512]{0:T(512)S(1)}, s32[512]{0:T(512)}, u32[]{:S(2)}) copy-start(s32[512]{0:T(512)} %param.7) | copy-start | bytes 6148
  55.9 16.8 %collective-permute-start.17 = (s16[1088,256]{1,0:T(8,128)(2,1)S(1)}, s16[1088,256]{1,0:T(8,128)(2,1)S(1)}, u32[]{:S(2)}, u32[]{:S(2)}) collective-permute-start(s16[1088,256]{1,0:T(8,128)(2,1)S(1)} %pack.3.refs_0_), channel_id=1, source_target_pairs={{0,32},{8,40},{16,48},{24,56},{32,64},{40,72},{48,80},{56,88},{64,... | collective-permute-start | bytes 1671176 | tf_op jit(solution)/shard_map/ppermute | solution.py:42
  56.6 16.0 %collective-permute-start.18 = (s16[1088,256]{1,0:T(8,128)(2,1)S(1)}, s16[1088,256]{1,0:T(8,128)(2,1)S(1)}, u32[]{:S(2)}, u32[]{:S(2)}) collective-permute-start(s16[1088,256]{1,0:T(8,128)(2,1)S(1)} %pack.3.refs_0_), channel_id=1, source_target_pairs={{0,64},{8,72},{16,80},{24,88},{32,96},{40,104},{48,112},{56,120},{... | collective-permute-start | bytes 1671176 | tf_op jit(solution)/shard_map/ppermute | solution.py:42
  58.0 15.6 %collective-permute-start.19 = (s16[1088,256]{1,0:T(8,128)(2,1)S(1)}, s16[1088,256]{1,0:T(8,128)(2,1)S(1)}, u32[]{:S(2)}, u32[]{:S(2)}) collective-permute-start(s16[1088,256]{1,0:T(8,128)(2,1)S(1)} %pack.3.refs_0_), channel_id=1, source_target_pairs={{0,96},{8,104},{16,112},{24,120},{32,0},{40,8},{48,16},{56,24},{64... | collective-permute-start | bytes 1671176 | tf_op jit(solution)/shard_map/ppermute | solution.py:42
  60.1 26.2 %collective-permute-start.20 = (s16[272,1024]{1,0:T(8,128)(2,1)S(1)}, s16[272,1024]{1,0:T(8,128)(2,1)S(1)}, u32[]{:S(2)}, u32[]{:S(2)}) collective-permute-start(s16[272,1024]{1,0:T(8,128)(2,1)S(1)} %product.2.refs_4_), channel_id=1, source_target_pairs={{0,1},{1,0},{2,3},{3,2},{4,5},{5,4},{6,7},{7,6},{8,9},{9,8},{10,11... | collective-permute-start | bytes 1671176 | tf_op jit(solution)/shard_map/ppermute | solution.py:293
  87.6 17.8 %all-to-all-start = ((f32[64,8,128]{2,1,0:T(8,128)}), f32[64,8,128]{2,1,0:T(8,128)S(1)}, u32[]{:S(2)}, u32[]{:S(2)}) async-start(f32[64,8,128]{2,1,0:T(8,128)} %get-tuple-element.16), calls=%async_computation | async-start | bytes 524288 | tf_op jit(solution)/shard_map/all_to_all | solution.py:298
  105.6 1.3 %copy-start.2 = (f32[256]{0:T(256)}, f32[256]{0:T(256)S(1)}, u32[]{:S(2)}) copy-start(f32[256]{0:T(256)S(1)} %get-tuple-element.19) | copy-start | bytes 3076
  (2 other events, 1.6 us)

commit v6 on v5

--- a/solution.py
+++ b/solution.py
@@ -40,6 +40,12 @@
 
     axes = ("cfg", "y", "x")
     return lax.ppermute(block, axes, pairs(axes, move))
+
+
+def nearest_other(at):
+    z = at["zh"] * 4 + at["zl"]
+    z = (z + (2 if z % 4 >= 2 else 6)) % 8
+    return {"zh": z // 4, "zl": z % 4}
 
 
 def code_of(largest):
@@ -117,21 +123,6 @@
         compiler_params=room(4),
         name="mix",
     )(place, own, other, own_scale, away_scale)
-
-
-def hold_kernel(block_ref, *refs):
-    refs[-1][...] = block_ref[...]
-
-
-def hold(block, after):
-    return pl.pallas_call(
-        hold_kernel,
-        out_shape=jax.ShapeDtypeStruct(block.shape, block.dtype),
-        in_specs=in_vmem(1) + anywhere(after),
-        out_specs=in_vmem(1)[0],
-        compiler_params=room(4),
-        name="hold",
-    )(block, *after)
 
 
 def stack_kernel(place_ref, a_ref, b_ref, c_ref, d_ref, *refs):
@@ -270,7 +261,7 @@
         place = jnp.where(slot == i, at, place)
     features = hidden[0].T
     other = lax.ppermute(features, "cfg", [(0, 1), (1, 0)])
-    away_scale = lax.ppermute(scale_index, "zh", [(0, 1), (1, 0)])
+    away_scale = lax.ppermute(scale_index, ("zl", "zh"), pairs(("zl", "zh"), nearest_other))
     limits = lax.dynamic_slice_in_dim(threshold, core * 256, 256, 0).astype(jnp.float32) / 8.0
 
     own, own_scale = load(features, scale_index[None])
@@ -284,11 +275,12 @@
         return [block] + [crossed(block, first, second, k) for k in (1, 2, 3)]
 
     away_near = near(away)
-    home_near = near(hold(home, away_near[1:]))
-    away_line = spread(stack(place, away_near, (head,)), "x", "y")
-    away_block = pack(away_line, ())
-    away_parts = spread(away_block, "y", "x")
-    home_line = spread(stack(place, home_near, (away_block,)), "x", "y")
+    home_near = near(home)
+    away_column = stack(place, away_near, (head,))
+    away_line = spread(away_column, "x", "y")
+    home_column = stack(place, home_near, (away_column,))
+    home_line = spread(home_column, "x", "y")
+    away_parts = spread(pack(away_line, (home_column,)), "y", "x")
     sent = product(place, head, away_parts, False, ())
     back = lax.ppermute(sent, "zh", [(0, 1), (1, 0)])
     home_parts = spread(pack(home_line, (sent,)), "y", "x")

time: 107 us -> 108 us (level)
  waiting for transfers between devices: 31.5 us -> 43.5 us
  starting transfers between devices: 54.4 us -> 43.4 us
    ppermute x12, waiting for transfers between devices: 7.12 us -> 20.6 us  [crossed(): return lax.ppermute(block, axes, pairs(axes, move))]
    ppermute x12, starting transfers between devices: 21.6 us -> 16.8 us  [crossed(): return lax.ppermute(block, axes, pairs(axes, move))]
    ppermute x1, starting transfers between devices: 9.59 us -> 6.14 us  [local(): back = lax.ppermute(sent, 'zh', [(0, 1), (1, 0)])]
    ppermute x1, waiting for transfers between devices: 7.63 us -> 6.03 us  [local(): back = lax.ppermute(sent, 'zh', [(0, 1), (1, 0)])]
    all_to_all x1, starting transfers between devices: 7.34 us -> 6.04 us  [local(): stats = lax.all_to_all(stats, ('y', 'x', 'zl'), 0, 0, tiled=True)]
  transfers between devices with their start and end apart: 22 -> 22, of which waited for: 9 -> 9; matrix products, arithmetic and copies ran while one was open for 0% -> 0% of each run, Pallas kernels for 14% -> 13%
where the time goes in v6:
time: 108 us
  waiting for transfers between devices  43.5 us (40%)
  starting transfers between devices  43.4 us (40%)
  Pallas kernels  17.1 us (16%)
  local copies, waits for them, and re-layouts  1.6 us (1%)
  other arithmetic  1.54 us (1%)
    ppermute x12, waiting for transfers between devices, crossed(): return lax.ppermute(block, axes, pairs(axes, move))  20.6 us
    ppermute x12, starting transfers between devices, crossed(): return lax.ppermute(block, axes, pairs(axes, move))  16.8 us
    pallas_call x2, Pallas kernels, product(): pl.pallas_call(product_kernel, out_shape=out, in_specs=[pl.BlockSpec(memo...  10.4 us
    all_to_all x1, waiting for transfers between devices, local(): stats = lax.all_to_all(stats, ('y', 'x', 'zl'), 0, 0, tiled=True)  10.3 us
    ppermute x6, starting transfers between devices, shifted(): lax.ppermute(block, axis, pairs((axis,), lambda at: {axis: at[axis] + k}))  7.86 us
    ppermute x6, waiting for transfers between devices, shifted(): lax.ppermute(block, axis, pairs((axis,), lambda at: {axis: at[axis] + k}))  6.51 us
    ppermute x1, starting transfers between devices, local(): lax.ppermute(scale_index, ('zl', 'zh'), pairs(('zl', 'zh'), nearest_other))  6.39 us
    ppermute x1, starting transfers between devices, local(): back = lax.ppermute(sent, 'zh', [(0, 1), (1, 0)])  6.14 us
  transfers between devices with their start and end apart: 22, of which 9 were waited for; matrix products, arithmetic and copies ran while one was open for 0% of the time, Pallas kernels for 13%

profile of v6, /device:TPU:2, one launch (start us, length us, event | category | flops | bytes accessed | tf_op | source)
XLA Modules:
  0.0 107.8 jit_solution(3091706821980504283)
XLA Ops:
  0.7 6.4 %collective-permute-start.1 = (s32[512]{0:T(512)}, s32[512]{0:T(512)S(1)}, u32[]{:S(2)}, u32[]{:S(2)}) collective-permute-start(s32[512]{0:T(512)} %param.6), channel_id=1, source_target_pairs={{0,5},{1,4},{2,7},{3,6},{4,1},{5,0},{6,3},{7,2},{8,13},{9,12},{10,... | collective-permute-start | bytes 6152 | tf_op jit(solution)/shard_map/ppermute | solution.py:264
  10.6 2.0 %collective-permute-start.6 = (s16[80,256]{1,0:T(8,128)(2,1)S(1)}, s16[80,256]{1,0:T(8,128)(2,1)S(1)}, u32[]{:S(2)}, u32[]{:S(2)}) collective-permute-start(s16[80,256]{1,0:T(8,128)(2,1)S(1)} %get-tuple-element.12.a_ref), channel_id=1, source_target_pairs={{0,4},{2,6},{4,0},{6,2},{1,5},{3,7},{5,1},{7,3},{8,12},{10,14},{12... | collective-permute-start | bytes 122888 | tf_op jit(solution)/shard_map/ppermute | solution.py:32
  12.6 1.4 %collective-permute-start.7 = (s16[80,256]{1,0:T(8,128)(2,1)S(1)}, s16[80,256]{1,0:T(8,128)(2,1)S(1)}, u32[]{:S(2)}, u32[]{:S(2)}) collective-permute-start(s16[80,256]{1,0:T(8,128)(2,1)S(1)} %get-tuple-element.12.a_ref), channel_id=1, source_target_pairs={{0,6},{2,0},{4,2},{6,4},{1,7},{3,1},{5,3},{7,5},{8,14},{10,8},{12,... | collective-permute-start | bytes 122888 | tf_op jit(solution)/shard_map/ppermute | solution.py:32
  14.0 3.4 %load.3.refs_0_.head_ref = bf16[4096,1024]{1,0:T(8,128)(2,1)S(1)} custom-call(bf16[4096,1024]{1,0:T(8,128)(2,1)} %refs_0_), custom_call_target="tpu_custom_call" | custom-call | bytes 16777216 | tf_op jit(solution)/shard_map/load/pallas_call | solution.py:85
  18.0 1.6 %collective-permute-start.11 = (s16[272,256]{1,0:T(8,128)(2,1)S(1)}, s16[272,256]{1,0:T(8,128)(2,1)S(1)}, u32[]{:S(2)}, u32[]{:S(2)}) collective-permute-start(s16[272,256]{1,0:T(8,128)(2,1)S(1)} %stack.2.refs_0_), channel_id=1, source_target_pairs={{0,8},{8,16},{16,24},{24,0},{32,40},{40,48},{48,56},{56,32},{64,72... | collective-permute-start | bytes 417800 | tf_op jit(solution)/shard_map/ppermute | solution.py:42
  20.7 2.2 %collective-permute-start.13 = (s16[272,256]{1,0:T(8,128)(2,1)S(1)}, s16[272,256]{1,0:T(8,128)(2,1)S(1)}, u32[]{:S(2)}, u32[]{:S(2)}) collective-permute-start(s16[272,256]{1,0:T(8,128)(2,1)S(1)} %stack.2.refs_0_), channel_id=1, source_target_pairs={{0,24},{8,0},{16,8},{24,16},{32,56},{40,32},{48,40},{56,48},{64,88... | collective-permute-start | bytes 417800 | tf_op jit(solution)/shard_map/ppermute | solution.py:42
  23.5 2.3 %collective-permute-start.3 = (s16[80,256]{1,0:T(8,128)(2,1)S(1)}, s16[80,256]{1,0:T(8,128)(2,1)S(1)}, u32[]{:S(2)}, u32[]{:S(2)}) collective-permute-start(s16[80,256]{1,0:T(8,128)(2,1)S(1)} %get-tuple-element.14.a_ref), channel_id=1, source_target_pairs={{0,4},{2,6},{4,0},{6,2},{1,5},{3,7},{5,1},{7,3},{8,12},{10,14},{12... | collective-permute-start | bytes 122888 | tf_op jit(solution)/shard_map/ppermute | solution.py:32
  25.8 3.0 %collective-permute-done.2.b_ref = s16[80,256]{1,0:T(8,128)(2,1)S(1)} collective-permute-done((s16[80,256]{1,0:T(8,128)(2,1)S(1)}, s16[80,256]{1,0:T(8,128)(2,1)S(1)}, u32[]{:S(2)}, u32[]{:S(2)}) %collective-permute-start.2) | collective-permute-done | bytes 40992 | tf_op jit(solution)/shard_map/ppermute | solution.py:32
  29.4 3.3 %collective-permute-done.4.d_ref = s16[80,256]{1,0:T(8,128)(2,1)S(1)} collective-permute-done((s16[80,256]{1,0:T(8,128)(2,1)S(1)}, s16[80,256]{1,0:T(8,128)(2,1)S(1)}, u32[]{:S(2)}, u32[]{:S(2)}) %collective-permute-start.4) | collective-permute-done | bytes 40992 | tf_op jit(solution)/shard_map/ppermute | solution.py:32
  33.4 2.0 %collective-permute-start.14 = (s16[1088,256]{1,0:T(8,128)(2,1)S(1)}, s16[1088,256]{1,0:T(8,128)(2,1)S(1)}, u32[]{:S(2)}, u32[]{:S(2)}) collective-permute-start(s16[1088,256]{1,0:T(8,128)(2,1)S(1)} %pack.2.refs_0_), channel_id=1, source_target_pairs={{0,32},{8,40},{16,48},{24,56},{32,64},{40,72},{48,80},{56,88},{64,... | collective-permute-start | bytes 1671176 | tf_op jit(solution)/shard_map/ppermute | solution.py:42
  35.4 2.5 %collective-permute-start.15 = (s16[1088,256]{1,0:T(8,128)(2,1)S(1)}, s16[1088,256]{1,0:T(8,128)(2,1)S(1)}, u32[]{:S(2)}, u32[]{:S(2)}) collective-permute-start(s16[1088,256]{1,0:T(8,128)(2,1)S(1)} %pack.2.refs_0_), channel_id=1, source_target_pairs={{0,64},{8,72},{16,80},{24,88},{32,96},{40,104},{48,112},{56,120},{... | collective-permute-start | bytes 1671176 | tf_op jit(solution)/shard_map/ppermute | solution.py:42
  37.9 1.3 %collective-permute-start.16 = (s16[1088,256]{1,0:T(8,128)(2,1)S(1)}, s16[1088,256]{1,0:T(8,128)(2,1)S(1)}, u32[]{:S(2)}, u32[]{:S(2)}) collective-permute-start(s16[1088,256]{1,0:T(8,128)(2,1)S(1)} %pack.2.refs_0_), channel_id=1, source_target_pairs={{0,96},{8,104},{16,112},{24,120},{32,0},{40,8},{48,16},{56,24},{64... | collective-permute-start | bytes 1671176 | tf_op jit(solution)/shard_map/ppermute | solution.py:42
  39.3 1.4 %collective-permute-start.10 = (s16[272,256]{1,0:T(8,128)(2,1)S(1)}, s16[272,256]{1,0:T(8,128)(2,1)S(1)}, u32[]{:S(2)}, u32[]{:S(2)}) collective-permute-start(s16[272,256]{1,0:T(8,128)(2,1)S(1)} %stack.3.refs_4_.refs_0_), channel_id=1, source_target_pairs={{0,24},{8,0},{16,8},{24,16},{32,56},{40,32},{48,40},{56,48},{64,88... | collective-permute-start | bytes 417800 | tf_op jit(solution)/shard_map/ppermute | solution.py:42
  41.3 11.8 %collective-permute-done.14.refs_1_ = s16[1088,256]{1,0:T(8,128)(2,1)S(1)} collective-permute-done((s16[1088,256]{1,0:T(8,128)(2,1)S(1)}, s16[1088,256]{1,0:T(8,128)(2,1)S(1)}, u32[]{:S(2)}, u32[]{:S(2)}) %collective-permute-start.14) | collective-permute-done | bytes 557088 | tf_op jit(solution)/shard_map/ppermute | solution.py:42
  53.2 5.3 %product.2.refs_4_ = s16[272,1024]{1,0:T(8,128)(2,1)S(1)} custom-call(s32[8]{0:T(128)S(1)} %compare_select_fusion.4.place_ref, bf16[4096,1024]{1,0:T(8,128)(2,1)S(1)} %load.3.refs_0_.head_ref, s16[1088,256]{1,0:T(8,128)(2,1)S(1)} %pack.2.refs_0_, s16[1088,256]{1,0:T(8,128)(2,1)S(1)} %collective-permute-done.14.refs_1_, ...), custom_call_target="tpu_custom_call" | custom-call | flops 4294967296 | bytes 10485760 | tf_op jit(solution)/shard_map/product/pallas_call | solution.py:211
  60.0 2.1 %collective-permute-start.18 = (s16[1088,256]{1,0:T(8,128)(2,1)S(1)}, s16[1088,256]{1,0:T(8,128)(2,1)S(1)}, u32[]{:S(2)}, u32[]{:S(2)}) collective-permute-start(s16[1088,256]{1,0:T(8,128)(2,1)S(1)} %pack.3.refs_0_), channel_id=1, source_target_pairs={{0,64},{8,72},{16,80},{24,88},{32,96},{40,104},{48,112},{56,120},{... | collective-permute-start | bytes 1671176 | tf_op jit(solution)/shard_map/ppermute | solution.py:42
  62.1 1.7 %collective-permute-start.19 = (s16[1088,256]{1,0:T(8,128)(2,1)S(1)}, s16[1088,256]{1,0:T(8,128)(2,1)S(1)}, u32[]{:S(2)}, u32[]{:S(2)}) collective-permute-start(s16[1088,256]{1,0:T(8,128)(2,1)S(1)} %pack.3.refs_0_), channel_id=1, source_target_pairs={{0,96},{8,104},{16,112},{24,120},{32,0},{40,8},{48,16},{56,24},{64... | collective-permute-start | bytes 1671176 | tf_op jit(solution)/shard_map/ppermute | solution.py:42
  63.8 6.1 %collective-permute-start.20 = (s16[272,1024]{1,0:T(8,128)(2,1)S(1)}, s16[272,1024]{1,0:T(8,128)(2,1)S(1)}, u32[]{:S(2)}, u32[]{:S(2)}) collective-permute-start(s16[272,1024]{1,0:T(8,128)(2,1)S(1)} %product.2.refs_4_), channel_id=1, source_target_pairs={{0,1},{1,0},{2,3},{3,2},{4,5},{5,4},{6,7},{7,6},{8,9},{9,8},{10,11... | collective-permute-start | bytes 1671176 | tf_op jit(solution)/shard_map/ppermute | solution.py:285
  70.0 6.6 %collective-permute-done.17.refs_1_ = s16[1088,256]{1,0:T(8,128)(2,1)S(1)} collective-permute-done((s16[1088,256]{1,0:T(8,128)(2,1)S(1)}, s16[1088,256]{1,0:T(8,128)(2,1)S(1)}, u32[]{:S(2)}, u32[]{:S(2)}) %collective-permute-start.17) | collective-permute-done | bytes 557088 | tf_op jit(solution)/shard_map/ppermute | solution.py:42
  77.5 5.1 %product.3.kept_ref = f32[256,1024]{1,0:T(8,128)S(1)} custom-call(s32[8]{0:T(128)S(1)} %compare_select_fusion.4.place_ref, bf16[4096,1024]{1,0:T(8,128)(2,1)S(1)} %load.3.refs_0_.head_ref, s16[1088,256]{1,0:T(8,128)(2,1)S(1)} %pack.3.refs_0_, s16[1088,256]{1,0:T(8,128)(2,1)S(1)} %collective-permute-done.17.refs_1_, ...), custom_call_target="tpu_custom_call" | custom-call | flops 4294967296 | bytes 10485760 | tf_op jit(solution)/shard_map/product/pallas_call | solution.py:211
  82.6 6.0 %collective-permute-done.20.back_ref = s16[272,1024]{1,0:T(8,128)(2,1)S(1)} collective-permute-done((s16[272,1024]{1,0:T(8,128)(2,1)S(1)}, s16[272,1024]{1,0:T(8,128)(2,1)S(1)}, u32[]{:S(2)}, u32[]{:S(2)}) %collective-permute-start.20) | collective-permute-done | bytes 557088 | tf_op jit(solution)/shard_map/ppermute | solution.py:285
  88.6 1.3 %join.1 = (f32[256,1024]{1,0:T(8,128)S(1)}, f32[64,8,128]{2,1,0:T(8,128)}) custom-call(f32[256,1024]{1,0:T(8,128)S(1)} %product.3.kept_ref, s16[272,1024]{1,0:T(8,128)(2,1)S(1)} %collective-permute-done.20.back_ref), custom_call_target="tpu_custom_call" | custom-call | tf_op jit(solution)/shard_map/join/pallas_call | solution.py:242
  89.9 6.0 %all-to-all-start = ((f32[64,8,128]{2,1,0:T(8,128)}), f32[64,8,128]{2,1,0:T(8,128)S(1)}, u32[]{:S(2)}, u32[]{:S(2)}) async-start(f32[64,8,128]{2,1,0:T(8,128)} %get-tuple-element.16), calls=%async_computation | async-start | bytes 524288 | tf_op jit(solution)/shard_map/all_to_all | solution.py:290
  96.0 10.3 %all-to-all-done = f32[64,8,128]{2,1,0:T(8,128)S(1)} async-done(((f32[64,8,128]{2,1,0:T(8,128)}), f32[64,8,128]{2,1,0:T(8,128)S(1)}, u32[]{:S(2)}, u32[]{:S(2)}) %all-to-all-start) | async-done | bytes 262176 | tf_op jit(solution)/shard_map/all_to_all | solution.py:290
  (44 shorter events, 11.8 us)
Async XLA Ops:
  0.6 8.3 %collective-permute-start = (bf16[64,1024]{1,0:T(8,128)(2,1)}, bf16[64,1024]{1,0:T(8,128)(2,1)S(1)}, u32[]{:S(2)}, u32[]{:S(2)}) collective-permute-start(bf16[64,1024]{1,0:T(8,128)(2,1)} %bitcast.10), channel_id=1, source_target_pairs={{0,128},{128,0},{1,129},{129,1},{2,130},{130,2},{3,131},{131,3},{4... | collective-permute-start | bytes 393224 | tf_op jit(solution)/shard_map/ppermute | solution.py:263
  0.7 8.2 %collective-permute-start.1 = (s32[512]{0:T(512)}, s32[512]{0:T(512)S(1)}, u32[]{:S(2)}, u32[]{:S(2)}) collective-permute-start(s32[512]{0:T(512)} %param.6), channel_id=1, source_target_pairs={{0,5},{1,4},{2,7},{3,6},{4,1},{5,0},{6,3},{7,2},{8,13},{9,12},{10,... | collective-permute-start | bytes 6152 | tf_op jit(solution)/shard_map/ppermute | solution.py:264
  9.5 7.9 %collective-permute-start.5 = (s16[80,256]{1,0:T(8,128)(2,1)S(1)}, s16[80,256]{1,0:T(8,128)(2,1)S(1)}, u32[]{:S(2)}, u32[]{:S(2)}) collective-permute-start(s16[80,256]{1,0:T(8,128)(2,1)S(1)} %get-tuple-element.12.a_ref), channel_id=1, source_target_pairs={{0,2},{2,4},{4,6},{6,0},{1,3},{3,5},{5,7},{7,1},{8,10},{10,12},{12... | collective-permute-start | bytes 122888 | tf_op jit(solution)/shard_map/ppermute | solution.py:32
  10.6 6.8 %collective-permute-start.6 = (s16[80,256]{1,0:T(8,128)(2,1)S(1)}, s16[80,256]{1,0:T(8,128)(2,1)S(1)}, u32[]{:S(2)}, u32[]{:S(2)}) collective-permute-start(s16[80,256]{1,0:T(8,128)(2,1)S(1)} %get-tuple-element.12.a_ref), channel_id=1, source_target_pairs={{0,4},{2,6},{4,0},{6,2},{1,5},{3,7},{5,1},{7,3},{8,12},{10,14},{12... | collective-permute-start | bytes 122888 | tf_op jit(solution)/shard_map/ppermute | solution.py:32
  12.6 4.8 %collective-permute-start.7 = (s16[80,256]{1,0:T(8,128)(2,1)S(1)}, s16[80,256]{1,0:T(8,128)(2,1)S(1)}, u32[]{:S(2)}, u32[]{:S(2)}) collective-permute-start(s16[80,256]{1,0:T(8,128)(2,1)S(1)} %get-tuple-element.12.a_ref), channel_id=1, source_target_pairs={{0,6},{2,0},{4,2},{6,4},{1,7},{3,1},{5,3},{7,5},{8,14},{10,8},{12,... | collective-permute-start | bytes 122888 | tf_op jit(solution)/shard_map/ppermute | solution.py:32
  18.0 15.3 %collective-permute-start.11 = (s16[272,256]{1,0:T(8,128)(2,1)S(1)}, s16[272,256]{1,0:T(8,128)(2,1)S(1)}, u32[]{:S(2)}, u32[]{:S(2)}) collective-permute-start(s16[272,256]{1,0:T(8,128)(2,1)S(1)} %stack.2.refs_0_), channel_id=1, source_target_pairs={{0,8},{8,16},{16,24},{24,0},{32,40},{40,48},{48,56},{56,32},{64,72... | collective-permute-start | bytes 417800 | tf_op jit(solution)/shard_map/ppermute | solution.py:42
  19.6 13.7 %collective-permute-start.12 = (s16[272,256]{1,0:T(8,128)(2,1)S(1)}, s16[272,256]{1,0:T(8,128)(2,1)S(1)}, u32[]{:S(2)}, u32[]{:S(2)}) collective-permute-start(s16[272,256]{1,0:T(8,128)(2,1)S(1)} %stack.2.refs_0_), channel_id=1, source_target_pairs={{0,16},{8,24},{16,0},{24,8},{32,48},{40,56},{48,32},{56,40},{64,80... | collective-permute-start | bytes 417800 | tf_op jit(solution)/shard_map/ppermute | solution.py:42
  20.7 12.6 %collective-permute-start.13 = (s16[272,256]{1,0:T(8,128)(2,1)S(1)}, s16[272,256]{1,0:T(8,128)(2,1)S(1)}, u32[]{:S(2)}, u32[]{:S(2)}) collective-permute-start(s16[272,256]{1,0:T(8,128)(2,1)S(1)} %stack.2.refs_0_), channel_id=1, source_target_pairs={{0,24},{8,0},{16,8},{24,16},{32,56},{40,32},{48,40},{56,48},{64,88... | collective-permute-start | bytes 417800 | tf_op jit(solution)/shard_map/ppermute | solution.py:42
  22.8 5.9 %collective-permute-start.2 = (s16[80,256]{1,0:T(8,128)(2,1)S(1)}, s16[80,256]{1,0:T(8,128)(2,1)S(1)}, u32[]{:S(2)}, u32[]{:S(2)}) collective-permute-start(s16[80,256]{1,0:T(8,128)(2,1)S(1)} %get-tuple-element.14.a_ref), channel_id=1, source_target_pairs={{0,2},{2,4},{4,6},{6,0},{1,3},{3,5},{5,7},{7,1},{8,10},{10,12},{12... | collective-permute-start | bytes 122888 | tf_op jit(solution)/shard_map/ppermute | solution.py:32
  23.5 5.9 %collective-permute-start.3 = (s16[80,256]{1,0:T(8,128)(2,1)S(1)}, s16[80,256]{1,0:T(8,128)(2,1)S(1)}, u32[]{:S(2)}, u32[]{:S(2)}) collective-permute-start(s16[80,256]{1,0:T(8,128)(2,1)S(1)} %get-tuple-element.14.a_ref), channel_id=1, source_target_pairs={{0,4},{2,6},{4,0},{6,2},{1,5},{3,7},{5,1},{7,3},{8,12},{10,14},{12... | collective-permute-start | bytes 122888 | tf_op jit(solution)/shard_map/ppermute | solution.py:32
  28.7 4.0 %collective-permute-start.4 = (s16[80,256]{1,0:T(8,128)(2,1)S(1)}, s16[80,256]{1,0:T(8,128)(2,1)S(1)}, u32[]{:S(2)}, u32[]{:S(2)}) collective-permute-start(s16[80,256]{1,0:T(8,128)(2,1)S(1)} %get-tuple-element.14.a_ref), channel_id=1, source_target_pairs={{0,6},{2,0},{4,2},{6,4},{1,7},{3,1},{5,3},{7,5},{8,14},{10,8},{12,... | collective-permute-start | bytes 122888 | tf_op jit(solution)/shard_map/ppermute | solution.py:32
  33.4 19.8 %collective-permute-start.14 = (s16[1088,256]{1,0:T(8,128)(2,1)S(1)}, s16[1088,256]{1,0:T(8,128)(2,1)S(1)}, u32[]{:S(2)}, u32[]{:S(2)}) collective-permute-start(s16[1088,256]{1,0:T(8,128)(2,1)S(1)} %pack.2.refs_0_), channel_id=1, source_target_pairs={{0,32},{8,40},{16,48},{24,56},{32,64},{40,72},{48,80},{56,88},{64,... | collective-permute-start | bytes 1671176 | tf_op jit(solution)/shard_map/ppermute | solution.py:42
  35.4 17.8 %collective-permute-start.15 = (s16[1088,256]{1,0:T(8,128)(2,1)S(1)}, s16[1088,256]{1,0:T(8,128)(2,1)S(1)}, u32[]{:S(2)}, u32[]{:S(2)}) collective-permute-start(s16[1088,256]{1,0:T(8,128)(2,1)S(1)} %pack.2.refs_0_), channel_id=1, source_target_pairs={{0,64},{8,72},{16,80},{24,88},{32,96},{40,104},{48,112},{56,120},{... | collective-permute-start | bytes 1671176 | tf_op jit(solution)/shard_map/ppermute | solution.py:42
  37.9 15.2 %collective-permute-start.16 = (s16[1088,256]{1,0:T(8,128)(2,1)S(1)}, s16[1088,256]{1,0:T(8,128)(2,1)S(1)}, u32[]{:S(2)}, u32[]{:S(2)}) collective-permute-start(s16[1088,256]{1,0:T(8,128)(2,1)S(1)} %pack.2.refs_0_), channel_id=1, source_target_pairs={{0,96},{8,104},{16,112},{24,120},{32,0},{40,8},{48,16},{56,24},{64... | collective-permute-start | bytes 1671176 | tf_op jit(solution)/shard_map/ppermute | solution.py:42
  39.3 19.2 %collective-permute-start.10 = (s16[272,256]{1,0:T(8,128)(2,1)S(1)}, s16[272,256]{1,0:T(8,128)(2,1)S(1)}, u32[]{:S(2)}, u32[]{:S(2)}) collective-permute-start(s16[272,256]{1,0:T(8,128)(2,1)S(1)} %stack.3.refs_4_.refs_0_), channel_id=1, source_target_pairs={{0,24},{8,0},{16,8},{24,16},{32,56},{40,32},{48,40},{56,48},{64,88... | collective-permute-start | bytes 417800 | tf_op jit(solution)/shard_map/ppermute | solution.py:42
  40.7 17.8 %collective-permute-start.8 = (s16[272,256]{1,0:T(8,128)(2,1)S(1)}, s16[272,256]{1,0:T(8,128)(2,1)S(1)}, u32[]{:S(2)}, u32[]{:S(2)}) collective-permute-start(s16[272,256]{1,0:T(8,128)(2,1)S(1)} %stack.3.refs_4_.refs_0_), channel_id=1, source_target_pairs={{0,8},{8,16},{16,24},{24,0},{32,40},{40,48},{48,56},{56,32},{64,72... | collective-permute-start | bytes 417800 | tf_op jit(solution)/shard_map/ppermute | solution.py:42
  53.1 6.6 %collective-permute-start.9 = (s16[272,256]{1,0:T(8,128)(2,1)S(1)}, s16[272,256]{1,0:T(8,128)(2,1)S(1)}, u32[]{:S(2)}, u32[]{:S(2)}) collective-permute-start(s16[272,256]{1,0:T(8,128)(2,1)S(1)} %stack.3.refs_4_.refs_0_), channel_id=1, source_target_pairs={{0,16},{8,24},{16,0},{24,8},{32,48},{40,56},{48,32},{56,40},{64,80... | collective-permute-start | bytes 417800 | tf_op jit(solution)/shard_map/ppermute | solution.py:42
  59.8 36.2 %copy-start.3 = (s32[512]{0:T(512)S(1)}, s32[512]{0:T(512)}, u32[]{:S(2)}) copy-start(s32[512]{0:T(512)} %param.7) | copy-start | bytes 6148
  59.8 16.8 %collective-permute-start.17 = (s16[1088,256]{1,0:T(8,128)(2,1)S(1)}, s16[1088,256]{1,0:T(8,128)(2,1)S(1)}, u32[]{:S(2)}, u32[]{:S(2)}) collective-permute-start(s16[1088,256]{1,0:T(8,128)(2,1)S(1)} %pack.3.refs_0_), channel_id=1, source_target_pairs={{0,32},{8,40},{16,48},{24,56},{32,64},{40,72},{48,80},{56,88},{64,... | collective-permute-start | bytes 1671176 | tf_op jit(solution)/shard_map/ppermute | solution.py:42
  60.0 16.6 %collective-permute-start.18 = (s16[1088,256]{1,0:T(8,128)(2,1)S(1)}, s16[1088,256]{1,0:T(8,128)(2,1)S(1)}, u32[]{:S(2)}, u32[]{:S(2)}) collective-permute-start(s16[1088,256]{1,0:T(8,128)(2,1)S(1)} %pack.3.refs_0_), channel_id=1, source_target_pairs={{0,64},{8,72},{16,80},{24,88},{32,96},{40,104},{48,112},{56,120},{... | collective-permute-start | bytes 1671176 | tf_op jit(solution)/shard_map/ppermute | solution.py:42
  62.1 15.4 %collective-permute-start.19 = (s16[1088,256]{1,0:T(8,128)(2,1)S(1)}, s16[1088,256]{1,0:T(8,128)(2,1)S(1)}, u32[]{:S(2)}, u32[]{:S(2)}) collective-permute-start(s16[1088,256]{1,0:T(8,128)(2,1)S(1)} %pack.3.refs_0_), channel_id=1, source_target_pairs={{0,96},{8,104},{16,112},{24,120},{32,0},{40,8},{48,16},{56,24},{64... | collective-permute-start | bytes 1671176 | tf_op jit(solution)/shard_map/ppermute | solution.py:42
  63.8 24.7 %collective-permute-start.20 = (s16[272,1024]{1,0:T(8,128)(2,1)S(1)}, s16[272,1024]{1,0:T(8,128)(2,1)S(1)}, u32[]{:S(2)}, u32[]{:S(2)}) collective-permute-start(s16[272,1024]{1,0:T(8,128)(2,1)S(1)} %product.2.refs_4_), channel_id=1, source_target_pairs={{0,1},{1,0},{2,3},{3,2},{4,5},{5,4},{6,7},{7,6},{8,9},{9,8},{10,11... | collective-permute-start | bytes 1671176 | tf_op jit(solution)/shard_map/ppermute | solution.py:285
  89.9 16.5 %all-to-all-start = ((f32[64,8,128]{2,1,0:T(8,128)}), f32[64,8,128]{2,1,0:T(8,128)S(1)}, u32[]{:S(2)}, u32[]{:S(2)}) async-start(f32[64,8,128]{2,1,0:T(8,128)} %get-tuple-element.16), calls=%async_computation | async-start | bytes 524288 | tf_op jit(solution)/shard_map/all_to_all | solution.py:290
  106.6 1.3 %copy-start.2 = (f32[256]{0:T(256)}, f32[256]{0:T(256)S(1)}, u32[]{:S(2)}) copy-start(f32[256]{0:T(256)S(1)} %get-tuple-element.19) | copy-start | bytes 3076
  (2 other events, 1.6 us)

commit v7 on v6

--- a/solution.py
+++ b/solution.py
@@ -280,10 +280,10 @@
     away_line = spread(away_column, "x", "y")
     home_column = stack(place, home_near, (away_column,))
     home_line = spread(home_column, "x", "y")
-    away_parts = spread(pack(away_line, (home_column,)), "y", "x")
+    away_parts = spread(pack(away_line, (home_near[1],home_near[2])), "y", "x")
     sent = product(place, head, away_parts, False, ())
     back = lax.ppermute(sent, "zh", [(0, 1), (1, 0)])
-    home_parts = spread(pack(home_line, (sent,)), "y", "x")
+    home_parts = spread(pack(home_line, (away_parts[1], away_parts[3])), "y", "x")
     kept = product(place, head, home_parts, True, ())
 
     guided, stats = join(kept, back)

time: 108 us -> 112 us (1.037)
  starting transfers between devices: 43.4 us -> 46 us
  waiting for transfers between devices: 43.5 us -> 44.8 us
    ppermute x1, waiting for transfers between devices: 6.03 us -> 11.8 us  [local(): back = lax.ppermute(sent, 'zh', [(0, 1), (1, 0)])]
    ppermute x12, waiting for transfers between devices: 20.6 us -> 15.8 us  [crossed(): return lax.ppermute(block, axes, pairs(axes, move))]
    all_to_all x1, starting transfers between devices: 6.04 us -> 8.56 us  [local(): stats = lax.all_to_all(stats, ('y', 'x', 'zl'), 0, 0, tiled=True)]
    ppermute x1, starting transfers between devices: 6.14 us -> 3.82 us  [local(): back = lax.ppermute(sent, 'zh', [(0, 1), (1, 0)])]
    ppermute x6, starting transfers between devices: 7.86 us -> 10.1 us  [shifted(): lax.ppermute(block, axis, pairs((axis,), lambda at: {axis: at[axis] + k}))]
    all_to_all x1, waiting for transfers between devices: 10.3 us -> 12 us  [local(): stats = lax.all_to_all(stats, ('y', 'x', 'zl'), 0, 0, tiled=True)]
    ppermute x6, waiting for transfers between devices: 6.51 us -> 5.19 us  [shifted(): lax.ppermute(block, axis, pairs((axis,), lambda at: {axis: at[axis] + k}))]
where the time goes in v7:
time: 112 us
  starting transfers between devices  46 us (41%)
  waiting for transfers between devices  44.8 us (40%)
  Pallas kernels  17.1 us (15%)
  local copies, waits for them, and re-layouts  1.6 us (1%)
  other arithmetic  1.54 us (1%)
    ppermute x12, starting transfers between devices, crossed(): return lax.ppermute(block, axes, pairs(axes, move))  17 us
    ppermute x12, waiting for transfers between devices, crossed(): return lax.ppermute(block, axes, pairs(axes, move))  15.8 us
    all_to_all x1, waiting for transfers between devices, local(): stats = lax.all_to_all(stats, ('y', 'x', 'zl'), 0, 0, tiled=True)  12 us
    ppermute x1, waiting for transfers between devices, local(): back = lax.ppermute(sent, 'zh', [(0, 1), (1, 0)])  11.8 us
    pallas_call x2, Pallas kernels, product(): pl.pallas_call(product_kernel, out_shape=out, in_specs=[pl.BlockSpec(memo...  10.4 us
    ppermute x6, starting transfers between devices, shifted(): lax.ppermute(block, axis, pairs((axis,), lambda at: {axis: at[axis] + k}))  10.1 us
    all_to_all x1, starting transfers between devices, local(): stats = lax.all_to_all(stats, ('y', 'x', 'zl'), 0, 0, tiled=True)  8.56 us
    ppermute x1, starting transfers between devices, local(): lax.ppermute(scale_index, ('zl', 'zh'), pairs(('zl', 'zh'), nearest_other))  6.39 us
  transfers between devices with their start and end apart: 22, of which 9 were waited for; matrix products, arithmetic and copies ran while one was open for 0% of the time, Pallas kernels for 13%

profile of v7, /device:TPU:2, one launch (start us, length us, event | category | flops | bytes accessed | tf_op | source)
XLA Modules:
  0.0 111.8 jit_solution(1691557462727564792)
XLA Ops:
  0.7 6.4 %collective-permute-start.1 = (s32[512]{0:T(512)}, s32[512]{0:T(512)S(1)}, u32[]{:S(2)}, u32[]{:S(2)}) collective-permute-start(s32[512]{0:T(512)} %param.6), channel_id=1, source_target_pairs={{0,5},{1,4},{2,7},{3,6},{4,1},{5,0},{6,3},{7,2},{8,13},{9,12},{10,... | collective-permute-start | bytes 6152 | tf_op jit(solution)/shard_map/ppermute | solution.py:264
  10.6 2.0 %collective-permute-start.6 = (s16[80,256]{1,0:T(8,128)(2,1)S(1)}, s16[80,256]{1,0:T(8,128)(2,1)S(1)}, u32[]{:S(2)}, u32[]{:S(2)}) collective-permute-start(s16[80,256]{1,0:T(8,128)(2,1)S(1)} %get-tuple-element.12.a_ref), channel_id=1, source_target_pairs={{0,4},{2,6},{4,0},{6,2},{1,5},{3,7},{5,1},{7,3},{8,12},{10,14},{12... | collective-permute-start | bytes 122888 | tf_op jit(solution)/shard_map/ppermute | solution.py:32
  12.6 1.4 %collective-permute-start.7 = (s16[80,256]{1,0:T(8,128)(2,1)S(1)}, s16[80,256]{1,0:T(8,128)(2,1)S(1)}, u32[]{:S(2)}, u32[]{:S(2)}) collective-permute-start(s16[80,256]{1,0:T(8,128)(2,1)S(1)} %get-tuple-element.12.a_ref), channel_id=1, source_target_pairs={{0,6},{2,0},{4,2},{6,4},{1,7},{3,1},{5,3},{7,5},{8,14},{10,8},{12,... | collective-permute-start | bytes 122888 | tf_op jit(solution)/shard_map/ppermute | solution.py:32
  14.0 3.4 %load.3.refs_0_.head_ref = bf16[4096,1024]{1,0:T(8,128)(2,1)S(1)} custom-call(bf16[4096,1024]{1,0:T(8,128)(2,1)} %refs_0_), custom_call_target="tpu_custom_call" | custom-call | bytes 16777216 | tf_op jit(solution)/shard_map/load/pallas_call | solution.py:85
  18.0 1.6 %collective-permute-start.11 = (s16[272,256]{1,0:T(8,128)(2,1)S(1)}, s16[272,256]{1,0:T(8,128)(2,1)S(1)}, u32[]{:S(2)}, u32[]{:S(2)}) collective-permute-start(s16[272,256]{1,0:T(8,128)(2,1)S(1)} %stack.2.refs_0_), channel_id=1, source_target_pairs={{0,8},{8,16},{16,24},{24,0},{32,40},{40,48},{48,56},{56,32},{64,72... | collective-permute-start | bytes 417800 | tf_op jit(solution)/shard_map/ppermute | solution.py:42
  20.7 2.2 %collective-permute-start.13 = (s16[272,256]{1,0:T(8,128)(2,1)S(1)}, s16[272,256]{1,0:T(8,128)(2,1)S(1)}, u32[]{:S(2)}, u32[]{:S(2)}) collective-permute-start(s16[272,256]{1,0:T(8,128)(2,1)S(1)} %stack.2.refs_0_), channel_id=1, source_target_pairs={{0,24},{8,0},{16,8},{24,16},{32,56},{40,32},{48,40},{56,48},{64,88... | collective-permute-start | bytes 417800 | tf_op jit(solution)/shard_map/ppermute | solution.py:42
  23.5 2.3 %collective-permute-start.3 = (s16[80,256]{1,0:T(8,128)(2,1)S(1)}, s16[80,256]{1,0:T(8,128)(2,1)S(1)}, u32[]{:S(2)}, u32[]{:S(2)}) collective-permute-start(s16[80,256]{1,0:T(8,128)(2,1)S(1)} %get-tuple-element.14.a_ref), channel_id=1, source_target_pairs={{0,4},{2,6},{4,0},{6,2},{1,5},{3,7},{5,1},{7,3},{8,12},{10,14},{12... | collective-permute-start | bytes 122888 | tf_op jit(solution)/shard_map/ppermute | solution.py:32
  25.8 3.0 %collective-permute-done.2.b_ref.refs_4_ = s16[80,256]{1,0:T(8,128)(2,1)S(1)} collective-permute-done((s16[80,256]{1,0:T(8,128)(2,1)S(1)}, s16[80,256]{1,0:T(8,128)(2,1)S(1)}, u32[]{:S(2)}, u32[]{:S(2)}) %collective-permute-start.2) | collective-permute-done | bytes 40992 | tf_op jit(solution)/shard_map/ppermute | solution.py:32
  29.3 1.7 %collective-permute-start.14 = (s16[1088,256]{1,0:T(8,128)(2,1)S(1)}, s16[1088,256]{1,0:T(8,128)(2,1)S(1)}, u32[]{:S(2)}, u32[]{:S(2)}) collective-permute-start(s16[1088,256]{1,0:T(8,128)(2,1)S(1)} %pack.2.refs_0_), channel_id=1, source_target_pairs={{0,32},{8,40},{16,48},{24,56},{32,64},{40,72},{48,80},{56,88},{64,... | collective-permute-start | bytes 1671176 | tf_op jit(solution)/shard_map/ppermute | solution.py:42
  31.0 1.7 %collective-permute-start.15 = (s16[1088,256]{1,0:T(8,128)(2,1)S(1)}, s16[1088,256]{1,0:T(8,128)(2,1)S(1)}, u32[]{:S(2)}, u32[]{:S(2)}) collective-permute-start(s16[1088,256]{1,0:T(8,128)(2,1)S(1)} %pack.2.refs_0_), channel_id=1, source_target_pairs={{0,96},{8,104},{16,112},{24,120},{32,0},{40,8},{48,16},{56,24},{64... | collective-permute-start | bytes 1671176 | tf_op jit(solution)/shard_map/ppermute | solution.py:42
  32.6 2.0 %collective-permute-start.19 = (s16[1088,256]{1,0:T(8,128)(2,1)S(1)}, s16[1088,256]{1,0:T(8,128)(2,1)S(1)}, u32[]{:S(2)}, u32[]{:S(2)}) collective-permute-start(s16[1088,256]{1,0:T(8,128)(2,1)S(1)} %pack.2.refs_0_), channel_id=1, source_target_pairs={{0,64},{8,72},{16,80},{24,88},{32,96},{40,104},{48,112},{56,120},{... | collective-permute-start | bytes 1671176 | tf_op jit(solution)/shard_map/ppermute | solution.py:42
  34.6 2.7 %collective-permute-start.4 = (s16[80,256]{1,0:T(8,128)(2,1)S(1)}, s16[80,256]{1,0:T(8,128)(2,1)S(1)}, u32[]{:S(2)}, u32[]{:S(2)}) collective-permute-start(s16[80,256]{1,0:T(8,128)(2,1)S(1)} %get-tuple-element.14.a_ref), channel_id=1, source_target_pairs={{0,6},{2,0},{4,2},{6,4},{1,7},{3,1},{5,3},{7,5},{8,14},{10,8},{12,... | collective-permute-start | bytes 122888 | tf_op jit(solution)/shard_map/ppermute | solution.py:32
  37.3 1.7 %collective-permute-done.4.d_ref = s16[80,256]{1,0:T(8,128)(2,1)S(1)} collective-permute-done((s16[80,256]{1,0:T(8,128)(2,1)S(1)}, s16[80,256]{1,0:T(8,128)(2,1)S(1)}, u32[]{:S(2)}, u32[]{:S(2)}) %collective-permute-start.4) | collective-permute-done | bytes 40992 | tf_op jit(solution)/shard_map/ppermute | solution.py:32
  39.6 1.5 %collective-permute-start.10 = (s16[272,256]{1,0:T(8,128)(2,1)S(1)}, s16[272,256]{1,0:T(8,128)(2,1)S(1)}, u32[]{:S(2)}, u32[]{:S(2)}) collective-permute-start(s16[272,256]{1,0:T(8,128)(2,1)S(1)} %stack.3.refs_0_), channel_id=1, source_target_pairs={{0,24},{8,0},{16,8},{24,16},{32,56},{40,32},{48,40},{56,48},{64,88... | collective-permute-start | bytes 417800 | tf_op jit(solution)/shard_map/ppermute | solution.py:42
  41.7 5.3 %collective-permute-done.10.refs_3_ = s16[272,256]{1,0:T(8,128)(2,1)S(1)} collective-permute-done((s16[272,256]{1,0:T(8,128)(2,1)S(1)}, s16[272,256]{1,0:T(8,128)(2,1)S(1)}, u32[]{:S(2)}, u32[]{:S(2)}) %collective-permute-start.10) | collective-permute-done | bytes 139296 | tf_op jit(solution)/shard_map/ppermute | solution.py:42
  48.2 5.3 %collective-permute-done.9.refs_2_ = s16[272,256]{1,0:T(8,128)(2,1)S(1)} collective-permute-done((s16[272,256]{1,0:T(8,128)(2,1)S(1)}, s16[272,256]{1,0:T(8,128)(2,1)S(1)}, u32[]{:S(2)}, u32[]{:S(2)}) %collective-permute-start.9) | collective-permute-done | bytes 139296 | tf_op jit(solution)/shard_map/ppermute | solution.py:42
  54.7 2.4 %collective-permute-start.18 = (s16[1088,256]{1,0:T(8,128)(2,1)S(1)}, s16[1088,256]{1,0:T(8,128)(2,1)S(1)}, u32[]{:S(2)}, u32[]{:S(2)}) collective-permute-start(s16[1088,256]{1,0:T(8,128)(2,1)S(1)} %pack.3.refs_0_), channel_id=1, source_target_pairs={{0,96},{8,104},{16,112},{24,120},{32,0},{40,8},{48,16},{56,24},{64... | collective-permute-start | bytes 1671176 | tf_op jit(solution)/shard_map/ppermute | solution.py:42
  57.1 5.3 %product.3 = s16[272,1024]{1,0:T(8,128)(2,1)S(1)} custom-call(s32[8]{0:T(128)S(1)} %compare_select_fusion.4.place_ref, bf16[4096,1024]{1,0:T(8,128)(2,1)S(1)} %load.3.refs_0_.head_ref, s16[1088,256]{1,0:T(8,128)(2,1)S(1)} %pack.2.refs_0_, s16[1088,256]{1,0:T(8,128)(2,1)S(1)} %collective-permute-done.14.refs_4_.refs_1_, ...), custom_call_target="tpu_custom_call" | custom-call | flops 4294967296 | bytes 10485760 | tf_op jit(solution)/shard_map/product/pallas_call | solution.py:211
  62.4 3.8 %collective-permute-start.20 = (s16[272,1024]{1,0:T(8,128)(2,1)S(1)}, s16[272,1024]{1,0:T(8,128)(2,1)S(1)}, u32[]{:S(2)}, u32[]{:S(2)}) collective-permute-start(s16[272,1024]{1,0:T(8,128)(2,1)S(1)} %product.3), channel_id=1, source_target_pairs={{0,1},{1,0},{2,3},{3,2},{4,5},{5,4},{6,7},{7,6},{8,9},{9,8},{10,11... | collective-permute-start | bytes 1671176 | tf_op jit(solution)/shard_map/ppermute | solution.py:285
  66.2 4.3 %collective-permute-done.16.refs_1_ = s16[1088,256]{1,0:T(8,128)(2,1)S(1)} collective-permute-done((s16[1088,256]{1,0:T(8,128)(2,1)S(1)}, s16[1088,256]{1,0:T(8,128)(2,1)S(1)}, u32[]{:S(2)}, u32[]{:S(2)}) %collective-permute-start.16) | collective-permute-done | bytes 557088 | tf_op jit(solution)/shard_map/ppermute | solution.py:42
  71.4 5.1 %product.2.kept_ref = f32[256,1024]{1,0:T(8,128)S(1)} custom-call(s32[8]{0:T(128)S(1)} %compare_select_fusion.4.place_ref, bf16[4096,1024]{1,0:T(8,128)(2,1)S(1)} %load.3.refs_0_.head_ref, s16[1088,256]{1,0:T(8,128)(2,1)S(1)} %pack.3.refs_0_, s16[1088,256]{1,0:T(8,128)(2,1)S(1)} %collective-permute-done.16.refs_1_, ...), custom_call_target="tpu_custom_call" | custom-call | flops 4294967296 | bytes 10485760 | tf_op jit(solution)/shard_map/product/pallas_call | solution.py:211
  76.5 11.8 %collective-permute-done.20.back_ref = s16[272,1024]{1,0:T(8,128)(2,1)S(1)} collective-permute-done((s16[272,1024]{1,0:T(8,128)(2,1)S(1)}, s16[272,1024]{1,0:T(8,128)(2,1)S(1)}, u32[]{:S(2)}, u32[]{:S(2)}) %collective-permute-start.20) | collective-permute-done | bytes 557088 | tf_op jit(solution)/shard_map/ppermute | solution.py:285
  89.6 8.6 %all-to-all-start = ((f32[64,8,128]{2,1,0:T(8,128)}), f32[64,8,128]{2,1,0:T(8,128)S(1)}, u32[]{:S(2)}, u32[]{:S(2)}) async-start(f32[64,8,128]{2,1,0:T(8,128)} %get-tuple-element.16), calls=%async_computation | async-start | bytes 524288 | tf_op jit(solution)/shard_map/all_to_all | solution.py:290
  98.3 12.0 %all-to-all-done = f32[64,8,128]{2,1,0:T(8,128)S(1)} async-done(((f32[64,8,128]{2,1,0:T(8,128)}), f32[64,8,128]{2,1,0:T(8,128)S(1)}, u32[]{:S(2)}, u32[]{:S(2)}) %all-to-all-start) | async-done | bytes 262176 | tf_op jit(solution)/shard_map/all_to_all | solution.py:290
  (44 shorter events, 13.8 us)
Async XLA Ops:
  0.6 8.3 %collective-permute-start = (bf16[64,1024]{1,0:T(8,128)(2,1)}, bf16[64,1024]{1,0:T(8,128)(2,1)S(1)}, u32[]{:S(2)}, u32[]{:S(2)}) collective-permute-start(bf16[64,1024]{1,0:T(8,128)(2,1)} %bitcast.10), channel_id=1, source_target_pairs={{0,128},{128,0},{1,129},{129,1},{2,130},{130,2},{3,131},{131,3},{4... | collective-permute-start | bytes 393224 | tf_op jit(solution)/shard_map/ppermute | solution.py:263
  0.7 8.2 %collective-permute-start.1 = (s32[512]{0:T(512)}, s32[512]{0:T(512)S(1)}, u32[]{:S(2)}, u32[]{:S(2)}) collective-permute-start(s32[512]{0:T(512)} %param.6), channel_id=1, source_target_pairs={{0,5},{1,4},{2,7},{3,6},{4,1},{5,0},{6,3},{7,2},{8,13},{9,12},{10,... | collective-permute-start | bytes 6152 | tf_op jit(solution)/shard_map/ppermute | solution.py:264
  9.5 7.9 %collective-permute-start.5 = (s16[80,256]{1,0:T(8,128)(2,1)S(1)}, s16[80,256]{1,0:T(8,128)(2,1)S(1)}, u32[]{:S(2)}, u32[]{:S(2)}) collective-permute-start(s16[80,256]{1,0:T(8,128)(2,1)S(1)} %get-tuple-element.12.a_ref), channel_id=1, source_target_pairs={{0,2},{2,4},{4,6},{6,0},{1,3},{3,5},{5,7},{7,1},{8,10},{10,12},{12... | collective-permute-start | bytes 122888 | tf_op jit(solution)/shard_map/ppermute | solution.py:32
  10.6 6.8 %collective-permute-start.6 = (s16[80,256]{1,0:T(8,128)(2,1)S(1)}, s16[80,256]{1,0:T(8,128)(2,1)S(1)}, u32[]{:S(2)}, u32[]{:S(2)}) collective-permute-start(s16[80,256]{1,0:T(8,128)(2,1)S(1)} %get-tuple-element.12.a_ref), channel_id=1, source_target_pairs={{0,4},{2,6},{4,0},{6,2},{1,5},{3,7},{5,1},{7,3},{8,12},{10,14},{12... | collective-permute-start | bytes 122888 | tf_op jit(solution)/shard_map/ppermute | solution.py:32
  12.6 4.8 %collective-permute-start.7 = (s16[80,256]{1,0:T(8,128)(2,1)S(1)}, s16[80,256]{1,0:T(8,128)(2,1)S(1)}, u32[]{:S(2)}, u32[]{:S(2)}) collective-permute-start(s16[80,256]{1,0:T(8,128)(2,1)S(1)} %get-tuple-element.12.a_ref), channel_id=1, source_target_pairs={{0,6},{2,0},{4,2},{6,4},{1,7},{3,1},{5,3},{7,5},{8,14},{10,8},{12,... | collective-permute-start | bytes 122888 | tf_op jit(solution)/shard_map/ppermute | solution.py:32
  18.0 11.3 %collective-permute-start.11 = (s16[272,256]{1,0:T(8,128)(2,1)S(1)}, s16[272,256]{1,0:T(8,128)(2,1)S(1)}, u32[]{:S(2)}, u32[]{:S(2)}) collective-permute-start(s16[272,256]{1,0:T(8,128)(2,1)S(1)} %stack.2.refs_0_), channel_id=1, source_target_pairs={{0,8},{8,16},{16,24},{24,0},{32,40},{40,48},{48,56},{56,32},{64,72... | collective-permute-start | bytes 417800 | tf_op jit(solution)/shard_map/ppermute | solution.py:42
  19.6 9.7 %collective-permute-start.12 = (s16[272,256]{1,0:T(8,128)(2,1)S(1)}, s16[272,256]{1,0:T(8,128)(2,1)S(1)}, u32[]{:S(2)}, u32[]{:S(2)}) collective-permute-start(s16[272,256]{1,0:T(8,128)(2,1)S(1)} %stack.2.refs_0_), channel_id=1, source_target_pairs={{0,16},{8,24},{16,0},{24,8},{32,48},{40,56},{48,32},{56,40},{64,80... | collective-permute-start | bytes 417800 | tf_op jit(solution)/shard_map/ppermute | solution.py:42
  20.7 8.6 %collective-permute-start.13 = (s16[272,256]{1,0:T(8,128)(2,1)S(1)}, s16[272,256]{1,0:T(8,128)(2,1)S(1)}, u32[]{:S(2)}, u32[]{:S(2)}) collective-permute-start(s16[272,256]{1,0:T(8,128)(2,1)S(1)} %stack.2.refs_0_), channel_id=1, source_target_pairs={{0,24},{8,0},{16,8},{24,16},{32,56},{40,32},{48,40},{56,48},{64,88... | collective-permute-start | bytes 417800 | tf_op jit(solution)/shard_map/ppermute | solution.py:42
  22.8 5.9 %collective-permute-start.2 = (s16[80,256]{1,0:T(8,128)(2,1)S(1)}, s16[80,256]{1,0:T(8,128)(2,1)S(1)}, u32[]{:S(2)}, u32[]{:S(2)}) collective-permute-start(s16[80,256]{1,0:T(8,128)(2,1)S(1)} %get-tuple-element.14.a_ref), channel_id=1, source_target_pairs={{0,2},{2,4},{4,6},{6,0},{1,3},{3,5},{5,7},{7,1},{8,10},{10,12},{12... | collective-permute-start | bytes 122888 | tf_op jit(solution)/shard_map/ppermute | solution.py:32
  23.5 5.8 %collective-permute-start.3 = (s16[80,256]{1,0:T(8,128)(2,1)S(1)}, s16[80,256]{1,0:T(8,128)(2,1)S(1)}, u32[]{:S(2)}, u32[]{:S(2)}) collective-permute-start(s16[80,256]{1,0:T(8,128)(2,1)S(1)} %get-tuple-element.14.a_ref), channel_id=1, source_target_pairs={{0,4},{2,6},{4,0},{6,2},{1,5},{3,7},{5,1},{7,3},{8,12},{10,14},{12... | collective-permute-start | bytes 122888 | tf_op jit(solution)/shard_map/ppermute | solution.py:32
  29.3 24.2 %collective-permute-start.14 = (s16[1088,256]{1,0:T(8,128)(2,1)S(1)}, s16[1088,256]{1,0:T(8,128)(2,1)S(1)}, u32[]{:S(2)}, u32[]{:S(2)}) collective-permute-start(s16[1088,256]{1,0:T(8,128)(2,1)S(1)} %pack.2.refs_0_), channel_id=1, source_target_pairs={{0,32},{8,40},{16,48},{24,56},{32,64},{40,72},{48,80},{56,88},{64,... | collective-permute-start | bytes 1671176 | tf_op jit(solution)/shard_map/ppermute | solution.py:42
  31.0 22.5 %collective-permute-start.15 = (s16[1088,256]{1,0:T(8,128)(2,1)S(1)}, s16[1088,256]{1,0:T(8,128)(2,1)S(1)}, u32[]{:S(2)}, u32[]{:S(2)}) collective-permute-start(s16[1088,256]{1,0:T(8,128)(2,1)S(1)} %pack.2.refs_0_), channel_id=1, source_target_pairs={{0,96},{8,104},{16,112},{24,120},{32,0},{40,8},{48,16},{56,24},{64... | collective-permute-start | bytes 1671176 | tf_op jit(solution)/shard_map/ppermute | solution.py:42
  32.6 24.4 %collective-permute-start.19 = (s16[1088,256]{1,0:T(8,128)(2,1)S(1)}, s16[1088,256]{1,0:T(8,128)(2,1)S(1)}, u32[]{:S(2)}, u32[]{:S(2)}) collective-permute-start(s16[1088,256]{1,0:T(8,128)(2,1)S(1)} %pack.2.refs_0_), channel_id=1, source_target_pairs={{0,64},{8,72},{16,80},{24,88},{32,96},{40,104},{48,112},{56,120},{... | collective-permute-start | bytes 1671176 | tf_op jit(solution)/shard_map/ppermute | solution.py:42
  34.6 4.4 %collective-permute-start.4 = (s16[80,256]{1,0:T(8,128)(2,1)S(1)}, s16[80,256]{1,0:T(8,128)(2,1)S(1)}, u32[]{:S(2)}, u32[]{:S(2)}) collective-permute-start(s16[80,256]{1,0:T(8,128)(2,1)S(1)} %get-tuple-element.14.a_ref), channel_id=1, source_target_pairs={{0,6},{2,0},{4,2},{6,4},{1,7},{3,1},{5,3},{7,5},{8,14},{10,8},{12,... | collective-permute-start | bytes 122888 | tf_op jit(solution)/shard_map/ppermute | solution.py:32
  39.6 7.4 %collective-permute-start.10 = (s16[272,256]{1,0:T(8,128)(2,1)S(1)}, s16[272,256]{1,0:T(8,128)(2,1)S(1)}, u32[]{:S(2)}, u32[]{:S(2)}) collective-permute-start(s16[272,256]{1,0:T(8,128)(2,1)S(1)} %stack.3.refs_0_), channel_id=1, source_target_pairs={{0,24},{8,0},{16,8},{24,16},{32,56},{40,32},{48,40},{56,48},{64,88... | collective-permute-start | bytes 417800 | tf_op jit(solution)/shard_map/ppermute | solution.py:42
  41.1 7.1 %collective-permute-start.8 = (s16[272,256]{1,0:T(8,128)(2,1)S(1)}, s16[272,256]{1,0:T(8,128)(2,1)S(1)}, u32[]{:S(2)}, u32[]{:S(2)}) collective-permute-start(s16[272,256]{1,0:T(8,128)(2,1)S(1)} %stack.3.refs_0_), channel_id=1, source_target_pairs={{0,8},{8,16},{16,24},{24,0},{32,40},{40,48},{48,56},{56,32},{64,72... | collective-permute-start | bytes 417800 | tf_op jit(solution)/shard_map/ppermute | solution.py:42
  46.9 6.6 %collective-permute-start.9 = (s16[272,256]{1,0:T(8,128)(2,1)S(1)}, s16[272,256]{1,0:T(8,128)(2,1)S(1)}, u32[]{:S(2)}, u32[]{:S(2)}) collective-permute-start(s16[272,256]{1,0:T(8,128)(2,1)S(1)} %stack.3.refs_0_), channel_id=1, source_target_pairs={{0,16},{8,24},{16,0},{24,8},{32,48},{40,56},{48,32},{56,40},{64,80... | collective-permute-start | bytes 417800 | tf_op jit(solution)/shard_map/ppermute | solution.py:42
  53.6 17.0 %collective-permute-start.16 = (s16[1088,256]{1,0:T(8,128)(2,1)S(1)}, s16[1088,256]{1,0:T(8,128)(2,1)S(1)}, u32[]{:S(2)}, u32[]{:S(2)}) collective-permute-start(s16[1088,256]{1,0:T(8,128)(2,1)S(1)} %pack.3.refs_0_), channel_id=1, source_target_pairs={{0,32},{8,40},{16,48},{24,56},{32,64},{40,72},{48,80},{56,88},{64,... | collective-permute-start | bytes 1671176 | tf_op jit(solution)/shard_map/ppermute | solution.py:42
  53.8 16.7 %collective-permute-start.17 = (s16[1088,256]{1,0:T(8,128)(2,1)S(1)}, s16[1088,256]{1,0:T(8,128)(2,1)S(1)}, u32[]{:S(2)}, u32[]{:S(2)}) collective-permute-start(s16[1088,256]{1,0:T(8,128)(2,1)S(1)} %pack.3.refs_0_), channel_id=1, source_target_pairs={{0,64},{8,72},{16,80},{24,88},{32,96},{40,104},{48,112},{56,120},{... | collective-permute-start | bytes 1671176 | tf_op jit(solution)/shard_map/ppermute | solution.py:42
  54.7 16.8 %collective-permute-start.18 = (s16[1088,256]{1,0:T(8,128)(2,1)S(1)}, s16[1088,256]{1,0:T(8,128)(2,1)S(1)}, u32[]{:S(2)}, u32[]{:S(2)}) collective-permute-start(s16[1088,256]{1,0:T(8,128)(2,1)S(1)} %pack.3.refs_0_), channel_id=1, source_target_pairs={{0,96},{8,104},{16,112},{24,120},{32,0},{40,8},{48,16},{56,24},{64... | collective-permute-start | bytes 1671176 | tf_op jit(solution)/shard_map/ppermute | solution.py:42
  62.4 35.8 %copy-start.3 = (s32[512]{0:T(512)S(1)}, s32[512]{0:T(512)}, u32[]{:S(2)}) copy-start(s32[512]{0:T(512)} %param.7) | copy-start | bytes 6148
  62.4 25.9 %collective-permute-start.20 = (s16[272,1024]{1,0:T(8,128)(2,1)S(1)}, s16[272,1024]{1,0:T(8,128)(2,1)S(1)}, u32[]{:S(2)}, u32[]{:S(2)}) collective-permute-start(s16[272,1024]{1,0:T(8,128)(2,1)S(1)} %product.3), channel_id=1, source_target_pairs={{0,1},{1,0},{2,3},{3,2},{4,5},{5,4},{6,7},{7,6},{8,9},{9,8},{10,11... | collective-permute-start | bytes 1671176 | tf_op jit(solution)/shard_map/ppermute | solution.py:285
  89.6 20.6 %all-to-all-start = ((f32[64,8,128]{2,1,0:T(8,128)}), f32[64,8,128]{2,1,0:T(8,128)S(1)}, u32[]{:S(2)}, u32[]{:S(2)}) async-start(f32[64,8,128]{2,1,0:T(8,128)} %get-tuple-element.16), calls=%async_computation | async-start | bytes 524288 | tf_op jit(solution)/shard_map/all_to_all | solution.py:290
  110.5 1.3 %copy-start.2 = (f32[256]{0:T(256)}, f32[256]{0:T(256)S(1)}, u32[]{:S(2)}) copy-start(f32[256]{0:T(256)S(1)} %get-tuple-element.19) | copy-start | bytes 3076
  (2 other events, 1.6 us)

commit v8 on v5

--- a/solution.py
+++ b/solution.py
@@ -40,6 +40,12 @@
 
     axes = ("cfg", "y", "x")
     return lax.ppermute(block, axes, pairs(axes, move))
+
+
+def nearest_other(at):
+    z = at["zh"] * 4 + at["zl"]
+    z = (z + (2 if z % 4 >= 2 else 6)) % 8
+    return {"zh": z // 4, "zl": z % 4}
 
 
 def code_of(largest):
@@ -142,7 +148,7 @@
     for k, ref in enumerate((a_ref, b_ref, c_ref, d_ref)):
         place = (place_ref[4] - k) & 3
         out_ref[pl.ds(pl.multiple_of(place * 64, 64), 64), :] = ref[:64]
-        codes = jnp.where(row == place, ref[64:].astype(jnp.int32), codes)
+        codes = jnp.where(row & 3 == place, ref[64:].astype(jnp.int32), codes)
     out_ref[256:] = codes.astype(jnp.int16)
 
 
@@ -158,14 +164,19 @@
 
 
 def pack_kernel(*refs):
+    out_ref = refs[-1]
+    row = lax.broadcasted_iota(jnp.int32, (16, out_ref.shape[1]), 0)
+    codes = jnp.zeros(row.shape, jnp.int32)
     for k in range(4):
-        refs[-1][272 * k : 272 * k + 272] = refs[k][...]
+        out_ref[256 * k : 256 * k + 256] = refs[k][:256]
+        codes = jnp.where(row >> 2 == k, refs[k][256:].astype(jnp.int32), codes)
+    out_ref[1024:] = codes.astype(jnp.int16)
 
 
 def pack(line, after):
     return pl.pallas_call(
         pack_kernel,
-        out_shape=jax.ShapeDtypeStruct((1088, line[0].shape[1]), jnp.int16),
+        out_shape=jax.ShapeDtypeStruct((1040, line[0].shape[1]), jnp.int16),
         in_specs=in_vmem(4) + anywhere(after),
         out_specs=in_vmem(1)[0],
         compiler_params=room(4),
@@ -180,12 +191,12 @@
     dims = (((0,), (0,)), ((), ()))
     for k, part in enumerate(parts):
         total = None
+        scale = scale_of(part[1024:].astype(jnp.float32))
         for piece in range(4):
-            base = 272 * piece
-            scale = scale_of(part[base + 256 : base + 272].astype(jnp.float32))
             high, low = [], []
             for j in range(4):
-                values = part[base + 64 * j : base + 64 * j + 64].astype(jnp.float32) * scale[j : j + 1]
+                at = 4 * piece + j
+                values = part[64 * at : 64 * at + 64].astype(jnp.float32) * scale[at : at + 1]
                 top = values.astype(jnp.bfloat16)
                 high.append(top)
                 low.append((values - top.astype(jnp.float32)).astype(jnp.bfloat16))
@@ -225,7 +236,7 @@
         scratch_shapes=[pltpu.VMEM((2 * tokens, width), jnp.float32)],
         compiler_params=room(24),
         cost_estimate=pl.CostEstimate(
-            flops=4 * tokens * 4096 * width, bytes_accessed=10 << 20, transcendentals=0
+            flops=0 if keep else 4 * tokens * 4096 * width, bytes_accessed=0, transcendentals=0
         ),
         name="product",
     )(place, head, *parts, *after)
@@ -270,7 +281,7 @@
         place = jnp.where(slot == i, at, place)
     features = hidden[0].T
     other = lax.ppermute(features, "cfg", [(0, 1), (1, 0)])
-    away_scale = lax.ppermute(scale_index, "zh", [(0, 1), (1, 0)])
+    away_scale = lax.ppermute(scale_index, ("zl", "zh"), pairs(("zl", "zh"), nearest_other))
     limits = lax.dynamic_slice_in_dim(threshold, core * 256, 256, 0).astype(jnp.float32) / 8.0
 
     own, own_scale = load(features, scale_index[None])

time: 107 us -> 105 us (0.981)
  starting transfers between devices: 54.4 us -> 49.6 us
  waiting for transfers between devices: 31.5 us -> 33.9 us
    ppermute x12, waiting for transfers between devices: 7.12 us -> 16.9 us  [crossed(): return lax.ppermute(block, axes, pairs(axes, move))]
    ppermute x1, waiting for transfers between devices: 7.63 us -> 0.01 us  [local(): back = lax.ppermute(sent, 'zh', [(0, 1), (1, 0)])]
    ppermute x1, starting transfers between devices: 9.59 us -> 5.12 us  [local(): back = lax.ppermute(sent, 'zh', [(0, 1), (1, 0)])]
    all_to_all x1, starting transfers between devices: 7.34 us -> 9.36 us  [local(): stats = lax.all_to_all(stats, ('y', 'x', 'zl'), 0, 0, tiled=True)]
  transfers between devices with their start and end apart: 22 -> 22, of which waited for: 9 -> 7; matrix products, arithmetic and copies ran while one was open for 0% -> 0% of each run, Pallas kernels for 14% -> 14%
where the time goes in v8:
time: 105 us; the launch traced here: 104 us
  starting transfers between devices  49.6 us (47%)
  waiting for transfers between devices  33.9 us (32%)
  Pallas kernels  17.1 us (16%)
  local copies, waits for them, and re-layouts  1.6 us (2%)
  other arithmetic  1.54 us (1%)
    ppermute x12, starting transfers between devices, crossed(): return lax.ppermute(block, axes, pairs(axes, move))  20.8 us
    ppermute x12, waiting for transfers between devices, crossed(): return lax.ppermute(block, axes, pairs(axes, move))  16.9 us
    pallas_call x2, Pallas kernels, product(): pl.pallas_call(product_kernel, out_shape=out, in_specs=[pl.BlockSpec(memo...  10.4 us
    all_to_all x1, waiting for transfers between devices, local(): stats = lax.all_to_all(stats, ('y', 'x', 'zl'), 0, 0, tiled=True)  10.3 us
    all_to_all x1, starting transfers between devices, local(): stats = lax.all_to_all(stats, ('y', 'x', 'zl'), 0, 0, tiled=True)  9.36 us
    ppermute x6, starting transfers between devices, shifted(): lax.ppermute(block, axis, pairs((axis,), lambda at: {axis: at[axis] + k}))  7.82 us
    ppermute x6, waiting for transfers between devices, shifted(): lax.ppermute(block, axis, pairs((axis,), lambda at: {axis: at[axis] + k}))  6.67 us
    ppermute x1, starting transfers between devices, local(): lax.ppermute(scale_index, ('zl', 'zh'), pairs(('zl', 'zh'), nearest_other))  6.39 us
  transfers between devices with their start and end apart: 22, of which 7 were waited for; matrix products, arithmetic and copies ran while one was open for 0% of the time, Pallas kernels for 14%

profile of v8, /device:TPU:2, one launch (start us, length us, event | category | flops | bytes accessed | tf_op | source)
XLA Modules:
  0.0 104.5 jit_solution(16677688376610625971)
XLA Ops:
  0.7 6.4 %collective-permute-start.1 = (s32[512]{0:T(512)}, s32[512]{0:T(512)S(1)}, u32[]{:S(2)}, u32[]{:S(2)}) collective-permute-start(s32[512]{0:T(512)} %param.6), channel_id=1, source_target_pairs={{0,5},{1,4},{2,7},{3,6},{4,1},{5,0},{6,3},{7,2},{8,13},{9,12},{10,... | collective-permute-start | bytes 6152 | tf_op jit(solution)/shard_map/ppermute | solution.py:284
  10.6 2.0 %collective-permute-start.3 = (s16[80,256]{1,0:T(8,128)(2,1)S(1)}, s16[80,256]{1,0:T(8,128)(2,1)S(1)}, u32[]{:S(2)}, u32[]{:S(2)}) collective-permute-start(s16[80,256]{1,0:T(8,128)(2,1)S(1)} %get-tuple-element.12.a_ref), channel_id=1, source_target_pairs={{0,4},{2,6},{4,0},{6,2},{1,5},{3,7},{5,1},{7,3},{8,12},{10,14},{12... | collective-permute-start | bytes 122888 | tf_op jit(solution)/shard_map/ppermute | solution.py:32
  12.6 1.4 %collective-permute-start.4 = (s16[80,256]{1,0:T(8,128)(2,1)S(1)}, s16[80,256]{1,0:T(8,128)(2,1)S(1)}, u32[]{:S(2)}, u32[]{:S(2)}) collective-permute-start(s16[80,256]{1,0:T(8,128)(2,1)S(1)} %get-tuple-element.12.a_ref), channel_id=1, source_target_pairs={{0,6},{2,0},{4,2},{6,4},{1,7},{3,1},{5,3},{7,5},{8,14},{10,8},{12,... | collective-permute-start | bytes 122888 | tf_op jit(solution)/shard_map/ppermute | solution.py:32
  14.0 3.4 %load.3.refs_0_.head_ref = bf16[4096,1024]{1,0:T(8,128)(2,1)S(1)} custom-call(bf16[4096,1024]{1,0:T(8,128)(2,1)} %refs_0_), custom_call_target="tpu_custom_call" | custom-call | bytes 16777216 | tf_op jit(solution)/shard_map/load/pallas_call | solution.py:85
  18.6 1.5 %collective-permute-start.8 = (s16[272,256]{1,0:T(8,128)(2,1)S(1)}, s16[272,256]{1,0:T(8,128)(2,1)S(1)}, u32[]{:S(2)}, u32[]{:S(2)}) collective-permute-start(s16[272,256]{1,0:T(8,128)(2,1)S(1)} %stack.2.refs_0_), channel_id=1, source_target_pairs={{0,8},{8,16},{16,24},{24,0},{32,40},{40,48},{48,56},{56,32},{64,72... | collective-permute-start | bytes 417800 | tf_op jit(solution)/shard_map/ppermute | solution.py:42
  20.1 3.3 %collective-permute-start.9 = (s16[272,256]{1,0:T(8,128)(2,1)S(1)}, s16[272,256]{1,0:T(8,128)(2,1)S(1)}, u32[]{:S(2)}, u32[]{:S(2)}) collective-permute-start(s16[272,256]{1,0:T(8,128)(2,1)S(1)} %stack.2.refs_0_), channel_id=1, source_target_pairs={{0,16},{8,24},{16,0},{24,8},{32,48},{40,56},{48,32},{56,40},{64,80... | collective-permute-start | bytes 417800 | tf_op jit(solution)/shard_map/ppermute | solution.py:42
  24.4 2.3 %collective-permute-done.9.refs_2_ = s16[272,256]{1,0:T(8,128)(2,1)S(1)} collective-permute-done((s16[272,256]{1,0:T(8,128)(2,1)S(1)}, s16[272,256]{1,0:T(8,128)(2,1)S(1)}, u32[]{:S(2)}, u32[]{:S(2)}) %collective-permute-start.9) | collective-permute-done | bytes 139296 | tf_op jit(solution)/shard_map/ppermute | solution.py:42
  26.7 1.7 %collective-permute-start.14 = (s16[1040,256]{1,0:T(8,128)(2,1)S(1)}, s16[1040,256]{1,0:T(8,128)(2,1)S(1)}, u32[]{:S(2)}, u32[]{:S(2)}) collective-permute-start(s16[1040,256]{1,0:T(8,128)(2,1)S(1)} %pack.2.refs_0_), channel_id=1, source_target_pairs={{0,32},{8,40},{16,48},{24,56},{32,64},{40,72},{48,80},{56,88},{64,... | collective-permute-start | bytes 1597448 | tf_op jit(solution)/shard_map/ppermute | solution.py:42
  28.3 2.9 %collective-permute-start.15 = (s16[1040,256]{1,0:T(8,128)(2,1)S(1)}, s16[1040,256]{1,0:T(8,128)(2,1)S(1)}, u32[]{:S(2)}, u32[]{:S(2)}) collective-permute-start(s16[1040,256]{1,0:T(8,128)(2,1)S(1)} %pack.2.refs_0_), channel_id=1, source_target_pairs={{0,64},{8,72},{16,80},{24,88},{32,96},{40,104},{48,112},{56,120},{... | collective-permute-start | bytes 1597448 | tf_op jit(solution)/shard_map/ppermute | solution.py:42
  31.2 1.3 %collective-permute-start.16 = (s16[1040,256]{1,0:T(8,128)(2,1)S(1)}, s16[1040,256]{1,0:T(8,128)(2,1)S(1)}, u32[]{:S(2)}, u32[]{:S(2)}) collective-permute-start(s16[1040,256]{1,0:T(8,128)(2,1)S(1)} %pack.2.refs_0_), channel_id=1, source_target_pairs={{0,96},{8,104},{16,112},{24,120},{32,0},{40,8},{48,16},{56,24},{64... | collective-permute-start | bytes 1597448 | tf_op jit(solution)/shard_map/ppermute | solution.py:42
  33.3 2.3 %collective-permute-start.6 = (s16[80,256]{1,0:T(8,128)(2,1)S(1)}, s16[80,256]{1,0:T(8,128)(2,1)S(1)}, u32[]{:S(2)}, u32[]{:S(2)}) collective-permute-start(s16[80,256]{1,0:T(8,128)(2,1)S(1)} %hold.1.a_ref), channel_id=1, source_target_pairs={{0,4},{2,6},{4,0},{6,2},{1,5},{3,7},{5,1},{7,3},{8,12},{10,14},{12... | collective-permute-start | bytes 122888 | tf_op jit(solution)/shard_map/ppermute | solution.py:32
  35.5 3.1 %collective-permute-done.5.b_ref = s16[80,256]{1,0:T(8,128)(2,1)S(1)} collective-permute-done((s16[80,256]{1,0:T(8,128)(2,1)S(1)}, s16[80,256]{1,0:T(8,128)(2,1)S(1)}, u32[]{:S(2)}, u32[]{:S(2)}) %collective-permute-start.5) | collective-permute-done | bytes 40992 | tf_op jit(solution)/shard_map/ppermute | solution.py:32
  39.1 3.6 %collective-permute-done.7.d_ref = s16[80,256]{1,0:T(8,128)(2,1)S(1)} collective-permute-done((s16[80,256]{1,0:T(8,128)(2,1)S(1)}, s16[80,256]{1,0:T(8,128)(2,1)S(1)}, u32[]{:S(2)}, u32[]{:S(2)}) %collective-permute-start.7) | collective-permute-done | bytes 40992 | tf_op jit(solution)/shard_map/ppermute | solution.py:32
  43.2 1.4 %collective-permute-start.11 = (s16[272,256]{1,0:T(8,128)(2,1)S(1)}, s16[272,256]{1,0:T(8,128)(2,1)S(1)}, u32[]{:S(2)}, u32[]{:S(2)}) collective-permute-start(s16[272,256]{1,0:T(8,128)(2,1)S(1)} %stack.3.refs_0_), channel_id=1, source_target_pairs={{0,8},{8,16},{16,24},{24,0},{32,40},{40,48},{48,56},{56,32},{64,72... | collective-permute-start | bytes 417800 | tf_op jit(solution)/shard_map/ppermute | solution.py:42
  44.6 3.4 %collective-permute-start.12 = (s16[272,256]{1,0:T(8,128)(2,1)S(1)}, s16[272,256]{1,0:T(8,128)(2,1)S(1)}, u32[]{:S(2)}, u32[]{:S(2)}) collective-permute-start(s16[272,256]{1,0:T(8,128)(2,1)S(1)} %stack.3.refs_0_), channel_id=1, source_target_pairs={{0,16},{8,24},{16,0},{24,8},{32,48},{40,56},{48,32},{56,40},{64,80... | collective-permute-start | bytes 417800 | tf_op jit(solution)/shard_map/ppermute | solution.py:42
  49.1 5.3 %product.2.refs_4_ = s16[272,1024]{1,0:T(8,128)(2,1)S(1)} custom-call(s32[8]{0:T(128)S(1)} %compare_select_fusion.4.place_ref, bf16[4096,1024]{1,0:T(8,128)(2,1)S(1)} %load.3.refs_0_.head_ref, s16[1040,256]{1,0:T(8,128)(2,1)S(1)} %pack.2.refs_0_, s16[1040,256]{1,0:T(8,128)(2,1)S(1)} %collective-permute-done.14.refs_1_, ...), custom_call_target="tpu_custom_call" | custom-call | flops 4294967296 | tf_op jit(solution)/shard_map/product/pallas_call | solution.py:231
  54.4 5.1 %collective-permute-start.20 = (s16[272,1024]{1,0:T(8,128)(2,1)S(1)}, s16[272,1024]{1,0:T(8,128)(2,1)S(1)}, u32[]{:S(2)}, u32[]{:S(2)}) collective-permute-start(s16[272,1024]{1,0:T(8,128)(2,1)S(1)} %product.2.refs_4_), channel_id=1, source_target_pairs={{0,1},{1,0},{2,3},{3,2},{4,5},{5,4},{6,7},{7,6},{8,9},{9,8},{10,11... | collective-permute-start | bytes 1671176 | tf_op jit(solution)/shard_map/ppermute | solution.py:304
  61.2 2.0 %collective-permute-start.19 = (s16[1040,256]{1,0:T(8,128)(2,1)S(1)}, s16[1040,256]{1,0:T(8,128)(2,1)S(1)}, u32[]{:S(2)}, u32[]{:S(2)}) collective-permute-start(s16[1040,256]{1,0:T(8,128)(2,1)S(1)} %pack.3.refs_0_), channel_id=1, source_target_pairs={{0,96},{8,104},{16,112},{24,120},{32,0},{40,8},{48,16},{56,24},{64... | collective-permute-start | bytes 1597448 | tf_op jit(solution)/shard_map/ppermute | solution.py:42
  63.1 12.7 %collective-permute-done.17.refs_1_ = s16[1040,256]{1,0:T(8,128)(2,1)S(1)} collective-permute-done((s16[1040,256]{1,0:T(8,128)(2,1)S(1)}, s16[1040,256]{1,0:T(8,128)(2,1)S(1)}, u32[]{:S(2)}, u32[]{:S(2)}) %collective-permute-start.17) | collective-permute-done | bytes 532512 | tf_op jit(solution)/shard_map/ppermute | solution.py:42
  76.8 5.1 %product.3.kept_ref = f32[256,1024]{1,0:T(8,128)S(1)} custom-call(s32[8]{0:T(128)S(1)} %compare_select_fusion.4.place_ref, bf16[4096,1024]{1,0:T(8,128)(2,1)S(1)} %load.3.refs_0_.head_ref, s16[1040,256]{1,0:T(8,128)(2,1)S(1)} %pack.3.refs_0_, s16[1040,256]{1,0:T(8,128)(2,1)S(1)} %collective-permute-done.17.refs_1_, ...), custom_call_target="tpu_custom_call" | custom-call | tf_op jit(solution)/shard_map/product/pallas_call | solution.py:231
  81.9 1.3 %join.1 = (f32[256,1024]{1,0:T(8,128)S(1)}, f32[64,8,128]{2,1,0:T(8,128)}) custom-call(f32[256,1024]{1,0:T(8,128)S(1)} %product.3.kept_ref, s16[272,1024]{1,0:T(8,128)(2,1)S(1)} %collective-permute-done.20.back_ref), custom_call_target="tpu_custom_call" | custom-call | tf_op jit(solution)/shard_map/join/pallas_call | solution.py:262
  83.2 9.4 %all-to-all-start = ((f32[64,8,128]{2,1,0:T(8,128)}), f32[64,8,128]{2,1,0:T(8,128)S(1)}, u32[]{:S(2)}, u32[]{:S(2)}) async-start(f32[64,8,128]{2,1,0:T(8,128)} %get-tuple-element.16), calls=%async_computation | async-start | bytes 524288 | tf_op jit(solution)/shard_map/all_to_all | solution.py:309
  92.7 10.3 %all-to-all-done = f32[64,8,128]{2,1,0:T(8,128)S(1)} async-done(((f32[64,8,128]{2,1,0:T(8,128)}), f32[64,8,128]{2,1,0:T(8,128)S(1)}, u32[]{:S(2)}, u32[]{:S(2)}) %all-to-all-start) | async-done | bytes 262176 | tf_op jit(solution)/shard_map/all_to_all | solution.py:309
  103.2 1.3 %divide_convert_fusion = (bf16[256,1024]{1,0:T(8,128)(2,1)}, bf16[256,1024]{1,0:T(8,128)(2,1)}) fusion(f32[256,1024]{1,0:T(8,128)S(1)} %get-tuple-element.15, f32[256]{0:T(256)S(1)} %get-tuple-element.19, f32[256]{0:T(256)S(1)} %convert_multiply_fusion, f32[256]{0:T(256)S(1)} %get-tuple-element.20), kind=kLoop, calls=%fused_computation | loop fusion | flops 2883584 | bytes 2100224 | tf_op jit(solution)/shard_map/convert_element_type | solution.py:320
  (45 shorter events, 11.3 us)
Async XLA Ops:
  0.6 8.3 %collective-permute-start = (bf16[64,1024]{1,0:T(8,128)(2,1)}, bf16[64,1024]{1,0:T(8,128)(2,1)S(1)}, u32[]{:S(2)}, u32[]{:S(2)}) collective-permute-start(bf16[64,1024]{1,0:T(8,128)(2,1)} %bitcast.10), channel_id=1, source_target_pairs={{0,128},{128,0},{1,129},{129,1},{2,130},{130,2},{3,131},{131,3},{4... | collective-permute-start | bytes 393224 | tf_op jit(solution)/shard_map/ppermute | solution.py:283
  0.7 8.2 %collective-permute-start.1 = (s32[512]{0:T(512)}, s32[512]{0:T(512)S(1)}, u32[]{:S(2)}, u32[]{:S(2)}) collective-permute-start(s32[512]{0:T(512)} %param.6), channel_id=1, source_target_pairs={{0,5},{1,4},{2,7},{3,6},{4,1},{5,0},{6,3},{7,2},{8,13},{9,12},{10,... | collective-permute-start | bytes 6152 | tf_op jit(solution)/shard_map/ppermute | solution.py:284
  9.5 7.9 %collective-permute-start.2 = (s16[80,256]{1,0:T(8,128)(2,1)S(1)}, s16[80,256]{1,0:T(8,128)(2,1)S(1)}, u32[]{:S(2)}, u32[]{:S(2)}) collective-permute-start(s16[80,256]{1,0:T(8,128)(2,1)S(1)} %get-tuple-element.12.a_ref), channel_id=1, source_target_pairs={{0,2},{2,4},{4,6},{6,0},{1,3},{3,5},{5,7},{7,1},{8,10},{10,12},{12... | collective-permute-start | bytes 122888 | tf_op jit(solution)/shard_map/ppermute | solution.py:32
  10.6 6.8 %collective-permute-start.3 = (s16[80,256]{1,0:T(8,128)(2,1)S(1)}, s16[80,256]{1,0:T(8,128)(2,1)S(1)}, u32[]{:S(2)}, u32[]{:S(2)}) collective-permute-start(s16[80,256]{1,0:T(8,128)(2,1)S(1)} %get-tuple-element.12.a_ref), channel_id=1, source_target_pairs={{0,4},{2,6},{4,0},{6,2},{1,5},{3,7},{5,1},{7,3},{8,12},{10,14},{12... | collective-permute-start | bytes 122888 | tf_op jit(solution)/shard_map/ppermute | solution.py:32
  12.6 4.8 %collective-permute-start.4 = (s16[80,256]{1,0:T(8,128)(2,1)S(1)}, s16[80,256]{1,0:T(8,128)(2,1)S(1)}, u32[]{:S(2)}, u32[]{:S(2)}) collective-permute-start(s16[80,256]{1,0:T(8,128)(2,1)S(1)} %get-tuple-element.12.a_ref), channel_id=1, source_target_pairs={{0,6},{2,0},{4,2},{6,4},{1,7},{3,1},{5,3},{7,5},{8,14},{10,8},{12,... | collective-permute-start | bytes 122888 | tf_op jit(solution)/shard_map/ppermute | solution.py:32
  18.0 5.4 %collective-permute-start.10 = (s16[272,256]{1,0:T(8,128)(2,1)S(1)}, s16[272,256]{1,0:T(8,128)(2,1)S(1)}, u32[]{:S(2)}, u32[]{:S(2)}) collective-permute-start(s16[272,256]{1,0:T(8,128)(2,1)S(1)} %stack.2.refs_0_), channel_id=1, source_target_pairs={{0,24},{8,0},{16,8},{24,16},{32,56},{40,32},{48,40},{56,48},{64,88... | collective-permute-start | bytes 417800 | tf_op jit(solution)/shard_map/ppermute | solution.py:42
  18.6 5.8 %collective-permute-start.8 = (s16[272,256]{1,0:T(8,128)(2,1)S(1)}, s16[272,256]{1,0:T(8,128)(2,1)S(1)}, u32[]{:S(2)}, u32[]{:S(2)}) collective-permute-start(s16[272,256]{1,0:T(8,128)(2,1)S(1)} %stack.2.refs_0_), channel_id=1, source_target_pairs={{0,8},{8,16},{16,24},{24,0},{32,40},{40,48},{48,56},{56,32},{64,72... | collective-permute-start | bytes 417800 | tf_op jit(solution)/shard_map/ppermute | solution.py:42
  20.1 6.6 %collective-permute-start.9 = (s16[272,256]{1,0:T(8,128)(2,1)S(1)}, s16[272,256]{1,0:T(8,128)(2,1)S(1)}, u32[]{:S(2)}, u32[]{:S(2)}) collective-permute-start(s16[272,256]{1,0:T(8,128)(2,1)S(1)} %stack.2.refs_0_), channel_id=1, source_target_pairs={{0,16},{8,24},{16,0},{24,8},{32,48},{40,56},{48,32},{56,40},{64,80... | collective-permute-start | bytes 417800 | tf_op jit(solution)/shard_map/ppermute | solution.py:42
  26.7 21.3 %collective-permute-start.14 = (s16[1040,256]{1,0:T(8,128)(2,1)S(1)}, s16[1040,256]{1,0:T(8,128)(2,1)S(1)}, u32[]{:S(2)}, u32[]{:S(2)}) collective-permute-start(s16[1040,256]{1,0:T(8,128)(2,1)S(1)} %pack.2.refs_0_), channel_id=1, source_target_pairs={{0,32},{8,40},{16,48},{24,56},{32,64},{40,72},{48,80},{56,88},{64,... | collective-permute-start | bytes 1597448 | tf_op jit(solution)/shard_map/ppermute | solution.py:42
  28.3 20.8 %collective-permute-start.15 = (s16[1040,256]{1,0:T(8,128)(2,1)S(1)}, s16[1040,256]{1,0:T(8,128)(2,1)S(1)}, u32[]{:S(2)}, u32[]{:S(2)}) collective-permute-start(s16[1040,256]{1,0:T(8,128)(2,1)S(1)} %pack.2.refs_0_), channel_id=1, source_target_pairs={{0,64},{8,72},{16,80},{24,88},{32,96},{40,104},{48,112},{56,120},{... | collective-permute-start | bytes 1597448 | tf_op jit(solution)/shard_map/ppermute | solution.py:42
  31.2 17.9 %collective-permute-start.16 = (s16[1040,256]{1,0:T(8,128)(2,1)S(1)}, s16[1040,256]{1,0:T(8,128)(2,1)S(1)}, u32[]{:S(2)}, u32[]{:S(2)}) collective-permute-start(s16[1040,256]{1,0:T(8,128)(2,1)S(1)} %pack.2.refs_0_), channel_id=1, source_target_pairs={{0,96},{8,104},{16,112},{24,120},{32,0},{40,8},{48,16},{56,24},{64... | collective-permute-start | bytes 1597448 | tf_op jit(solution)/shard_map/ppermute | solution.py:42
  32.6 6.0 %collective-permute-start.5 = (s16[80,256]{1,0:T(8,128)(2,1)S(1)}, s16[80,256]{1,0:T(8,128)(2,1)S(1)}, u32[]{:S(2)}, u32[]{:S(2)}) collective-permute-start(s16[80,256]{1,0:T(8,128)(2,1)S(1)} %hold.1.a_ref), channel_id=1, source_target_pairs={{0,2},{2,4},{4,6},{6,0},{1,3},{3,5},{5,7},{7,1},{8,10},{10,12},{12... | collective-permute-start | bytes 122888 | tf_op jit(solution)/shard_map/ppermute | solution.py:32
  33.3 5.8 %collective-permute-start.6 = (s16[80,256]{1,0:T(8,128)(2,1)S(1)}, s16[80,256]{1,0:T(8,128)(2,1)S(1)}, u32[]{:S(2)}, u32[]{:S(2)}) collective-permute-start(s16[80,256]{1,0:T(8,128)(2,1)S(1)} %hold.1.a_ref), channel_id=1, source_target_pairs={{0,4},{2,6},{4,0},{6,2},{1,5},{3,7},{5,1},{7,3},{8,12},{10,14},{12... | collective-permute-start | bytes 122888 | tf_op jit(solution)/shard_map/ppermute | solution.py:32
  38.6 4.0 %collective-permute-start.7 = (s16[80,256]{1,0:T(8,128)(2,1)S(1)}, s16[80,256]{1,0:T(8,128)(2,1)S(1)}, u32[]{:S(2)}, u32[]{:S(2)}) collective-permute-start(s16[80,256]{1,0:T(8,128)(2,1)S(1)} %hold.1.a_ref), channel_id=1, source_target_pairs={{0,6},{2,0},{4,2},{6,4},{1,7},{3,1},{5,3},{7,5},{8,14},{10,8},{12,... | collective-permute-start | bytes 122888 | tf_op jit(solution)/shard_map/ppermute | solution.py:32
  43.2 16.4 %collective-permute-start.11 = (s16[272,256]{1,0:T(8,128)(2,1)S(1)}, s16[272,256]{1,0:T(8,128)(2,1)S(1)}, u32[]{:S(2)}, u32[]{:S(2)}) collective-permute-start(s16[272,256]{1,0:T(8,128)(2,1)S(1)} %stack.3.refs_0_), channel_id=1, source_target_pairs={{0,8},{8,16},{16,24},{24,0},{32,40},{40,48},{48,56},{56,32},{64,72... | collective-permute-start | bytes 417800 | tf_op jit(solution)/shard_map/ppermute | solution.py:42
  44.6 14.9 %collective-permute-start.12 = (s16[272,256]{1,0:T(8,128)(2,1)S(1)}, s16[272,256]{1,0:T(8,128)(2,1)S(1)}, u32[]{:S(2)}, u32[]{:S(2)}) collective-permute-start(s16[272,256]{1,0:T(8,128)(2,1)S(1)} %stack.3.refs_0_), channel_id=1, source_target_pairs={{0,16},{8,24},{16,0},{24,8},{32,48},{40,56},{48,32},{56,40},{64,80... | collective-permute-start | bytes 417800 | tf_op jit(solution)/shard_map/ppermute | solution.py:42
  48.0 11.5 %collective-permute-start.13 = (s16[272,256]{1,0:T(8,128)(2,1)S(1)}, s16[272,256]{1,0:T(8,128)(2,1)S(1)}, u32[]{:S(2)}, u32[]{:S(2)}) collective-permute-start(s16[272,256]{1,0:T(8,128)(2,1)S(1)} %stack.3.refs_0_), channel_id=1, source_target_pairs={{0,24},{8,0},{16,8},{24,16},{32,56},{40,32},{48,40},{56,48},{64,88... | collective-permute-start | bytes 417800 | tf_op jit(solution)/shard_map/ppermute | solution.py:42
  54.4 38.2 %copy-start.3 = (s32[512]{0:T(512)S(1)}, s32[512]{0:T(512)}, u32[]{:S(2)}) copy-start(s32[512]{0:T(512)} %param.7) | copy-start | bytes 6148
  54.4 27.5 %collective-permute-start.20 = (s16[272,1024]{1,0:T(8,128)(2,1)S(1)}, s16[272,1024]{1,0:T(8,128)(2,1)S(1)}, u32[]{:S(2)}, u32[]{:S(2)}) collective-permute-start(s16[272,1024]{1,0:T(8,128)(2,1)S(1)} %product.2.refs_4_), channel_id=1, source_target_pairs={{0,1},{1,0},{2,3},{3,2},{4,5},{5,4},{6,7},{7,6},{8,9},{9,8},{10,11... | collective-permute-start | bytes 1671176 | tf_op jit(solution)/shard_map/ppermute | solution.py:304
  59.6 16.3 %collective-permute-start.17 = (s16[1040,256]{1,0:T(8,128)(2,1)S(1)}, s16[1040,256]{1,0:T(8,128)(2,1)S(1)}, u32[]{:S(2)}, u32[]{:S(2)}) collective-permute-start(s16[1040,256]{1,0:T(8,128)(2,1)S(1)} %pack.3.refs_0_), channel_id=1, source_target_pairs={{0,32},{8,40},{16,48},{24,56},{32,64},{40,72},{48,80},{56,88},{64,... | collective-permute-start | bytes 1597448 | tf_op jit(solution)/shard_map/ppermute | solution.py:42
  60.4 15.5 %collective-permute-start.18 = (s16[1040,256]{1,0:T(8,128)(2,1)S(1)}, s16[1040,256]{1,0:T(8,128)(2,1)S(1)}, u32[]{:S(2)}, u32[]{:S(2)}) collective-permute-start(s16[1040,256]{1,0:T(8,128)(2,1)S(1)} %pack.3.refs_0_), channel_id=1, source_target_pairs={{0,64},{8,72},{16,80},{24,88},{32,96},{40,104},{48,112},{56,120},{... | collective-permute-start | bytes 1597448 | tf_op jit(solution)/shard_map/ppermute | solution.py:42
  61.2 15.6 %collective-permute-start.19 = (s16[1040,256]{1,0:T(8,128)(2,1)S(1)}, s16[1040,256]{1,0:T(8,128)(2,1)S(1)}, u32[]{:S(2)}, u32[]{:S(2)}) collective-permute-start(s16[1040,256]{1,0:T(8,128)(2,1)S(1)} %pack.3.refs_0_), channel_id=1, source_target_pairs={{0,96},{8,104},{16,112},{24,120},{32,0},{40,8},{48,16},{56,24},{64... | collective-permute-start | bytes 1597448 | tf_op jit(solution)/shard_map/ppermute | solution.py:42
  83.2 19.8 %all-to-all-start = ((f32[64,8,128]{2,1,0:T(8,128)}), f32[64,8,128]{2,1,0:T(8,128)S(1)}, u32[]{:S(2)}, u32[]{:S(2)}) async-start(f32[64,8,128]{2,1,0:T(8,128)} %get-tuple-element.16), calls=%async_computation | async-start | bytes 524288 | tf_op jit(solution)/shard_map/all_to_all | solution.py:309
  103.2 1.3 %copy-start.2 = (f32[256]{0:T(256)}, f32[256]{0:T(256)S(1)}, u32[]{:S(2)}) copy-start(f32[256]{0:T(256)S(1)} %get-tuple-element.19) | copy-start | bytes 3076
  (2 other events, 1.6 us)

commit v9 on v8

--- a/solution.py
+++ b/solution.py
@@ -1,3 +1,4 @@
+import functools
 import math
 
 import jax
@@ -184,12 +185,12 @@
     )(*line, *after)
 
 
-def product_kernel(place_ref, head_ref, *refs):
-    parts, out_ref, total_ref = refs[:4], refs[-2], refs[-1]
+def product_kernel(offsets, adds, place_ref, head_ref, *refs):
+    parts, out_ref, total_ref = refs[: len(offsets)], refs[-2], refs[-1]
     core, y, x = place_ref[0], place_ref[2], place_ref[3]
     count = total_ref.shape[0] // 2
     dims = (((0,), (0,)), ((), ()))
-    for k, part in enumerate(parts):
+    for i, (k, part) in enumerate(zip(offsets, parts)):
         total = None
         scale = scale_of(part[1024:].astype(jnp.float32))
         for piece in range(4):
@@ -206,11 +207,13 @@
             weight = head_ref[pl.ds(pl.multiple_of((row * 4 + column) * 256, 256), 256), :]
             term = lax.dot_general(both, weight, dims, preferred_element_type=jnp.float32)
             total = term if total is None else total + term
-        if k == 0:
+        if i == 0:
             total_ref[...] = total
         else:
             total_ref[...] += total
     total = total_ref[:count] + total_ref[count:]
+    if adds:
+        total += refs[len(offsets)][...]
     if out_ref.dtype == jnp.float32:
         out_ref[...] = total
     else:
@@ -221,25 +224,26 @@
         out_ref[count:, :count] = across.astype(jnp.int32).astype(jnp.int16)
 
 
-def product(place, head, parts, keep, after):
-    tokens, width = parts[0].shape[1], head.shape[1]
+def product(place, head, parts, offsets, before=(), send=False, cost=0):
+    chosen = [parts[k] for k in offsets]
+    tokens, width = chosen[0].shape[1], head.shape[1]
     out = (
-        jax.ShapeDtypeStruct((tokens, width), jnp.float32)
-        if keep
-        else jax.ShapeDtypeStruct((tokens + 16, width), jnp.int16)
+        jax.ShapeDtypeStruct((tokens + 16, width), jnp.int16)
+        if send
+        else jax.ShapeDtypeStruct((tokens, width), jnp.float32)
     )
     return pl.pallas_call(
-        product_kernel,
+        functools.partial(product_kernel, offsets, len(before) > 0),
         out_shape=out,
-        in_specs=[pl.BlockSpec(memory_space=pltpu.SMEM)] + in_vmem(5) + anywhere(after),
+        in_specs=[pl.BlockSpec(memory_space=pltpu.SMEM)] + in_vmem(1 + len(chosen) + len(before)),
         out_specs=in_vmem(1)[0],
         scratch_shapes=[pltpu.VMEM((2 * tokens, width), jnp.float32)],
         compiler_params=room(24),
         cost_estimate=pl.CostEstimate(
-            flops=0 if keep else 4 * tokens * 4096 * width, bytes_accessed=0, transcendentals=0
+            flops=cost * len(offsets) * tokens * 4096 * width, bytes_accessed=0, transcendentals=0
         ),
         name="product",
-    )(place, head, *parts, *after)
+    )(place, head, *chosen, *before)
 
 
 def join_kernel(kept_ref, back_ref, guided_ref, stats_ref):
@@ -300,10 +304,14 @@
     away_block = pack(away_line, ())
     away_parts = spread(away_block, "y", "x")
     home_line = spread(stack(place, home_near, (away_block,)), "x", "y")
-    sent = product(place, head, away_parts, False, ())
+    away_sum = product(place, head, away_parts, (0,), cost=1)
+    away_sum = product(place, head, away_parts, (1,), (away_sum,), cost=1)
+    sent = product(place, head, away_parts, (2, 3), (away_sum,), True, cost=1)
     back = lax.ppermute(sent, "zh", [(0, 1), (1, 0)])
     home_parts = spread(pack(home_line, (sent,)), "y", "x")
-    kept = product(place, head, home_parts, True, ())
+    kept = product(place, head, home_parts, (0, 1))
+    kept = product(place, head, home_parts, (2,), (kept,))
+    kept = product(place, head, home_parts, (3,), (kept,))
 
     guided, stats = join(kept, back)
     stats = lax.all_to_all(stats, ("y", "x", "zl"), 0, 0, tiled=True)

time: 105 us -> 105 us (level)
  Pallas kernels: 17.1 us -> 20.1 us
  starting transfers between devices: 49.6 us -> 47.5 us
    pallas_call x2 -> x6, Pallas kernels: 10.4 us -> 13.4 us  [product(): pl.pallas_call(functools.partial(product_kernel, offsets, len(before) > 0...]
    all_to_all x1, starting transfers between devices: 9.36 us -> 7.05 us  [local(): stats = lax.all_to_all(stats, ('y', 'x', 'zl'), 0, 0, tiled=True)]
  transfers between devices with their start and end apart: 22 -> 22, of which waited for: 7 -> 6; matrix products, arithmetic and copies ran while one was open for 0% -> 0% of each run, Pallas kernels for 14% -> 17%
where the time goes in v9:
time: 105 us
  starting transfers between devices  47.5 us (45%)
  waiting for transfers between devices  33 us (31%)
  Pallas kernels  20.1 us (19%)
  local copies, waits for them, and re-layouts  1.6 us (2%)
  other arithmetic  1.54 us (1%)
    ppermute x12, starting transfers between devices, crossed(): return lax.ppermute(block, axes, pairs(axes, move))  21 us
    ppermute x12, waiting for transfers between devices, crossed(): return lax.ppermute(block, axes, pairs(axes, move))  16 us
    pallas_call x6, Pallas kernels, product(): pl.pallas_call(functools.partial(product_kernel, offsets, len(before) > 0...  13.4 us
    all_to_all x1, waiting for transfers between devices, local(): stats = lax.all_to_all(stats, ('y', 'x', 'zl'), 0, 0, tiled=True)  10.3 us
    ppermute x6, starting transfers between devices, shifted(): lax.ppermute(block, axis, pairs((axis,), lambda at: {axis: at[axis] + k}))  7.82 us
    all_to_all x1, starting transfers between devices, local(): stats = lax.all_to_all(stats, ('y', 'x', 'zl'), 0, 0, tiled=True)  7.05 us
    ppermute x6, waiting for transfers between devices, shifted(): lax.ppermute(block, axis, pairs((axis,), lambda at: {axis: at[axis] + k}))  6.67 us
    ppermute x1, starting transfers between devices, local(): lax.ppermute(scale_index, ('zl', 'zh'), pairs(('zl', 'zh'), nearest_other))  6.39 us
  transfers between devices with their start and end apart: 22, of which 6 were waited for; matrix products, arithmetic and copies ran while one was open for 0% of the time, Pallas kernels for 17%

profile of v9, /device:TPU:2, one launch (start us, length us, event | category | flops | bytes accessed | tf_op | source)
XLA Modules:
  0.0 104.6 jit_solution(15183856764870869670)
XLA Ops:
  0.7 6.4 %collective-permute-start.1 = (s32[512]{0:T(512)}, s32[512]{0:T(512)S(1)}, u32[]{:S(2)}, u32[]{:S(2)}) collective-permute-start(s32[512]{0:T(512)} %param.6), channel_id=1, source_target_pairs={{0,5},{1,4},{2,7},{3,6},{4,1},{5,0},{6,3},{7,2},{8,13},{9,12},{10,... | collective-permute-start | bytes 6152 | tf_op jit(solution)/shard_map/ppermute | solution.py:288
  10.6 2.0 %collective-permute-start.3 = (s16[80,256]{1,0:T(8,128)(2,1)S(1)}, s16[80,256]{1,0:T(8,128)(2,1)S(1)}, u32[]{:S(2)}, u32[]{:S(2)}) collective-permute-start(s16[80,256]{1,0:T(8,128)(2,1)S(1)} %get-tuple-element.12.a_ref), channel_id=1, source_target_pairs={{0,4},{2,6},{4,0},{6,2},{1,5},{3,7},{5,1},{7,3},{8,12},{10,14},{12... | collective-permute-start | bytes 122888 | tf_op jit(solution)/shard_map/ppermute | solution.py:33
  14.0 3.4 %load.3.refs_0_.head_ref = bf16[4096,1024]{1,0:T(8,128)(2,1)S(1)} custom-call(bf16[4096,1024]{1,0:T(8,128)(2,1)} %refs_0_), custom_call_target="tpu_custom_call" | custom-call | bytes 16777216 | tf_op jit(solution)/shard_map/load/pallas_call | solution.py:86
  18.6 1.5 %collective-permute-start.8 = (s16[272,256]{1,0:T(8,128)(2,1)S(1)}, s16[272,256]{1,0:T(8,128)(2,1)S(1)}, u32[]{:S(2)}, u32[]{:S(2)}) collective-permute-start(s16[272,256]{1,0:T(8,128)(2,1)S(1)} %stack.2.refs_0_), channel_id=1, source_target_pairs={{0,8},{8,16},{16,24},{24,0},{32,40},{40,48},{48,56},{56,32},{64,72... | collective-permute-start | bytes 417800 | tf_op jit(solution)/shard_map/ppermute | solution.py:43
  20.1 3.3 %collective-permute-start.9 = (s16[272,256]{1,0:T(8,128)(2,1)S(1)}, s16[272,256]{1,0:T(8,128)(2,1)S(1)}, u32[]{:S(2)}, u32[]{:S(2)}) collective-permute-start(s16[272,256]{1,0:T(8,128)(2,1)S(1)} %stack.2.refs_0_), channel_id=1, source_target_pairs={{0,16},{8,24},{16,0},{24,8},{32,48},{40,56},{48,32},{56,40},{64,80... | collective-permute-start | bytes 417800 | tf_op jit(solution)/shard_map/ppermute | solution.py:43
  24.4 2.3 %collective-permute-done.9.refs_2_ = s16[272,256]{1,0:T(8,128)(2,1)S(1)} collective-permute-done((s16[272,256]{1,0:T(8,128)(2,1)S(1)}, s16[272,256]{1,0:T(8,128)(2,1)S(1)}, u32[]{:S(2)}, u32[]{:S(2)}) %collective-permute-start.9) | collective-permute-done | bytes 139296 | tf_op jit(solution)/shard_map/ppermute | solution.py:43
  26.7 1.7 %collective-permute-start.16 = (s16[1040,256]{1,0:T(8,128)(2,1)S(1)}, s16[1040,256]{1,0:T(8,128)(2,1)S(1)}, u32[]{:S(2)}, u32[]{:S(2)}) collective-permute-start(s16[1040,256]{1,0:T(8,128)(2,1)S(1)} %pack.2.refs_0_), channel_id=1, source_target_pairs={{0,32},{8,40},{16,48},{24,56},{32,64},{40,72},{48,80},{56,88},{64,... | collective-permute-start | bytes 1597448 | tf_op jit(solution)/shard_map/ppermute | solution.py:43
  28.3 2.9 %collective-permute-start.14 = (s16[1040,256]{1,0:T(8,128)(2,1)S(1)}, s16[1040,256]{1,0:T(8,128)(2,1)S(1)}, u32[]{:S(2)}, u32[]{:S(2)}) collective-permute-start(s16[1040,256]{1,0:T(8,128)(2,1)S(1)} %pack.2.refs_0_), channel_id=1, source_target_pairs={{0,64},{8,72},{16,80},{24,88},{32,96},{40,104},{48,112},{56,120},{... | collective-permute-start | bytes 1597448 | tf_op jit(solution)/shard_map/ppermute | solution.py:43
  33.3 2.3 %collective-permute-start.6 = (s16[80,256]{1,0:T(8,128)(2,1)S(1)}, s16[80,256]{1,0:T(8,128)(2,1)S(1)}, u32[]{:S(2)}, u32[]{:S(2)}) collective-permute-start(s16[80,256]{1,0:T(8,128)(2,1)S(1)} %hold.1.a_ref), channel_id=1, source_target_pairs={{0,4},{2,6},{4,0},{6,2},{1,5},{3,7},{5,1},{7,3},{8,12},{10,14},{12... | collective-permute-start | bytes 122888 | tf_op jit(solution)/shard_map/ppermute | solution.py:33
  35.5 3.1 %collective-permute-done.5.b_ref = s16[80,256]{1,0:T(8,128)(2,1)S(1)} collective-permute-done((s16[80,256]{1,0:T(8,128)(2,1)S(1)}, s16[80,256]{1,0:T(8,128)(2,1)S(1)}, u32[]{:S(2)}, u32[]{:S(2)}) %collective-permute-start.5) | collective-permute-done | bytes 40992 | tf_op jit(solution)/shard_map/ppermute | solution.py:33
  39.1 3.6 %collective-permute-done.7.d_ref = s16[80,256]{1,0:T(8,128)(2,1)S(1)} collective-permute-done((s16[80,256]{1,0:T(8,128)(2,1)S(1)}, s16[80,256]{1,0:T(8,128)(2,1)S(1)}, u32[]{:S(2)}, u32[]{:S(2)}) %collective-permute-start.7) | collective-permute-done | bytes 40992 | tf_op jit(solution)/shard_map/ppermute | solution.py:33
  43.2 1.4 %collective-permute-start.11 = (s16[272,256]{1,0:T(8,128)(2,1)S(1)}, s16[272,256]{1,0:T(8,128)(2,1)S(1)}, u32[]{:S(2)}, u32[]{:S(2)}) collective-permute-start(s16[272,256]{1,0:T(8,128)(2,1)S(1)} %stack.3.refs_0_), channel_id=1, source_target_pairs={{0,8},{8,16},{16,24},{24,0},{32,40},{40,48},{48,56},{56,32},{64,72... | collective-permute-start | bytes 417800 | tf_op jit(solution)/shard_map/ppermute | solution.py:43
  44.6 3.4 %collective-permute-start.12 = (s16[272,256]{1,0:T(8,128)(2,1)S(1)}, s16[272,256]{1,0:T(8,128)(2,1)S(1)}, u32[]{:S(2)}, u32[]{:S(2)}) collective-permute-start(s16[272,256]{1,0:T(8,128)(2,1)S(1)} %stack.3.refs_0_), channel_id=1, source_target_pairs={{0,16},{8,24},{16,0},{24,8},{32,48},{40,56},{48,32},{56,40},{64,80... | collective-permute-start | bytes 417800 | tf_op jit(solution)/shard_map/ppermute | solution.py:43
  48.0 1.8 %product.6.refs_1_ = f32[256,1024]{1,0:T(8,128)S(1)} custom-call(s32[8]{0:T(128)S(1)} %compare_select_fusion.4.place_ref, bf16[4096,1024]{1,0:T(8,128)(2,1)S(1)} %load.3.refs_0_.head_ref, s16[1040,256]{1,0:T(8,128)(2,1)S(1)} %pack.2.refs_0_), custom_call_target="tpu_custom_call" | custom-call | flops 1073741824 | tf_op jit(solution)/shard_map/product/pallas_call | solution.py:235
  51.2 1.8 %product.7.refs_2_ = f32[256,1024]{1,0:T(8,128)S(1)} custom-call(s32[8]{0:T(128)S(1)} %compare_select_fusion.4.place_ref, bf16[4096,1024]{1,0:T(8,128)(2,1)S(1)} %load.3.refs_0_.head_ref, s16[1040,256]{1,0:T(8,128)(2,1)S(1)} %collective-permute-done.16.refs_0_, f32[256,1024]{1,0:T(8,128)S(1)} %product.6.refs_1_), custom_call_target="tpu_custom_call" | custom-call | flops 1073741824 | tf_op jit(solution)/shard_map/product/pallas_call | solution.py:235
  53.1 3.1 %product.8.refs_4_ = s16[272,1024]{1,0:T(8,128)(2,1)S(1)} custom-call(s32[8]{0:T(128)S(1)} %compare_select_fusion.4.place_ref, bf16[4096,1024]{1,0:T(8,128)(2,1)S(1)} %load.3.refs_0_.head_ref, s16[1040,256]{1,0:T(8,128)(2,1)S(1)} %collective-permute-done.14.refs_0_, s16[1040,256]{1,0:T(8,128)(2,1)S(1)} %collective-permute-done.15.refs_1_, ...), custom_call_target="tpu_custom_call" | custom-call | flops 2147483648 | tf_op jit(solution)/shard_map/product/pallas_call | solution.py:235
  56.2 5.1 %collective-permute-start.20 = (s16[272,1024]{1,0:T(8,128)(2,1)S(1)}, s16[272,1024]{1,0:T(8,128)(2,1)S(1)}, u32[]{:S(2)}, u32[]{:S(2)}) collective-permute-start(s16[272,1024]{1,0:T(8,128)(2,1)S(1)} %product.8.refs_4_), channel_id=1, source_target_pairs={{0,1},{1,0},{2,3},{3,2},{4,5},{5,4},{6,7},{7,6},{8,9},{9,8},{10,11... | collective-permute-start | bytes 1671176 | tf_op jit(solution)/shard_map/ppermute | solution.py:310
  62.9 2.0 %collective-permute-start.17 = (s16[1040,256]{1,0:T(8,128)(2,1)S(1)}, s16[1040,256]{1,0:T(8,128)(2,1)S(1)}, u32[]{:S(2)}, u32[]{:S(2)}) collective-permute-start(s16[1040,256]{1,0:T(8,128)(2,1)S(1)} %pack.3.refs_0_), channel_id=1, source_target_pairs={{0,96},{8,104},{16,112},{24,120},{32,0},{40,8},{48,16},{56,24},{64... | collective-permute-start | bytes 1597448 | tf_op jit(solution)/shard_map/ppermute | solution.py:43
  64.9 12.7 %collective-permute-done.19.refs_1_ = s16[1040,256]{1,0:T(8,128)(2,1)S(1)} collective-permute-done((s16[1040,256]{1,0:T(8,128)(2,1)S(1)}, s16[1040,256]{1,0:T(8,128)(2,1)S(1)}, u32[]{:S(2)}, u32[]{:S(2)}) %collective-permute-start.19) | collective-permute-done | bytes 532512 | tf_op jit(solution)/shard_map/ppermute | solution.py:43
  77.7 2.9 %product.9.refs_1_ = f32[256,1024]{1,0:T(8,128)S(1)} custom-call(s32[8]{0:T(128)S(1)} %compare_select_fusion.4.place_ref, bf16[4096,1024]{1,0:T(8,128)(2,1)S(1)} %load.3.refs_0_.head_ref, s16[1040,256]{1,0:T(8,128)(2,1)S(1)} %pack.3.refs_0_, s16[1040,256]{1,0:T(8,128)(2,1)S(1)} %collective-permute-done.19.refs_1_), custom_call_target="tpu_custom_call" | custom-call | tf_op jit(solution)/shard_map/product/pallas_call | solution.py:235
  80.6 1.8 %product.10.refs_1_ = f32[256,1024]{1,0:T(8,128)S(1)} custom-call(s32[8]{0:T(128)S(1)} %compare_select_fusion.4.place_ref, bf16[4096,1024]{1,0:T(8,128)(2,1)S(1)} %load.3.refs_0_.head_ref, s16[1040,256]{1,0:T(8,128)(2,1)S(1)} %collective-permute-done.18.refs_0_, f32[256,1024]{1,0:T(8,128)S(1)} %product.9.refs_1_), custom_call_target="tpu_custom_call" | custom-call | tf_op jit(solution)/shard_map/product/pallas_call | solution.py:235
  82.4 1.8 %product.11.kept_ref = f32[256,1024]{1,0:T(8,128)S(1)} custom-call(s32[8]{0:T(128)S(1)} %compare_select_fusion.4.place_ref, bf16[4096,1024]{1,0:T(8,128)(2,1)S(1)} %load.3.refs_0_.head_ref, s16[1040,256]{1,0:T(8,128)(2,1)S(1)} %collective-permute-done.17.refs_0_, f32[256,1024]{1,0:T(8,128)S(1)} %product.10.refs_1_), custom_call_target="tpu_custom_call" | custom-call | tf_op jit(solution)/shard_map/product/pallas_call | solution.py:235
  85.6 7.0 %all-to-all-start = ((f32[64,8,128]{2,1,0:T(8,128)}), f32[64,8,128]{2,1,0:T(8,128)S(1)}, u32[]{:S(2)}, u32[]{:S(2)}) async-start(f32[64,8,128]{2,1,0:T(8,128)} %get-tuple-element.16), calls=%async_computation | async-start | bytes 524288 | tf_op jit(solution)/shard_map/all_to_all | solution.py:317
  92.8 10.3 %all-to-all-done = f32[64,8,128]{2,1,0:T(8,128)S(1)} async-done(((f32[64,8,128]{2,1,0:T(8,128)}), f32[64,8,128]{2,1,0:T(8,128)S(1)}, u32[]{:S(2)}, u32[]{:S(2)}) %all-to-all-start) | async-done | bytes 262176 | tf_op jit(solution)/shard_map/all_to_all | solution.py:317
  (49 shorter events, 16.0 us)
Async XLA Ops:
  0.6 8.3 %collective-permute-start = (bf16[64,1024]{1,0:T(8,128)(2,1)}, bf16[64,1024]{1,0:T(8,128)(2,1)S(1)}, u32[]{:S(2)}, u32[]{:S(2)}) collective-permute-start(bf16[64,1024]{1,0:T(8,128)(2,1)} %bitcast.10), channel_id=1, source_target_pairs={{0,128},{128,0},{1,129},{129,1},{2,130},{130,2},{3,131},{131,3},{4... | collective-permute-start | bytes 393224 | tf_op jit(solution)/shard_map/ppermute | solution.py:287
  0.7 8.2 %collective-permute-start.1 = (s32[512]{0:T(512)}, s32[512]{0:T(512)S(1)}, u32[]{:S(2)}, u32[]{:S(2)}) collective-permute-start(s32[512]{0:T(512)} %param.6), channel_id=1, source_target_pairs={{0,5},{1,4},{2,7},{3,6},{4,1},{5,0},{6,3},{7,2},{8,13},{9,12},{10,... | collective-permute-start | bytes 6152 | tf_op jit(solution)/shard_map/ppermute | solution.py:288
  9.5 7.9 %collective-permute-start.2 = (s16[80,256]{1,0:T(8,128)(2,1)S(1)}, s16[80,256]{1,0:T(8,128)(2,1)S(1)}, u32[]{:S(2)}, u32[]{:S(2)}) collective-permute-start(s16[80,256]{1,0:T(8,128)(2,1)S(1)} %get-tuple-element.12.a_ref), channel_id=1, source_target_pairs={{0,2},{2,4},{4,6},{6,0},{1,3},{3,5},{5,7},{7,1},{8,10},{10,12},{12... | collective-permute-start | bytes 122888 | tf_op jit(solution)/shard_map/ppermute | solution.py:33
  10.6 6.8 %collective-permute-start.3 = (s16[80,256]{1,0:T(8,128)(2,1)S(1)}, s16[80,256]{1,0:T(8,128)(2,1)S(1)}, u32[]{:S(2)}, u32[]{:S(2)}) collective-permute-start(s16[80,256]{1,0:T(8,128)(2,1)S(1)} %get-tuple-element.12.a_ref), channel_id=1, source_target_pairs={{0,4},{2,6},{4,0},{6,2},{1,5},{3,7},{5,1},{7,3},{8,12},{10,14},{12... | collective-permute-start | bytes 122888 | tf_op jit(solution)/shard_map/ppermute | solution.py:33
  12.6 4.8 %collective-permute-start.4 = (s16[80,256]{1,0:T(8,128)(2,1)S(1)}, s16[80,256]{1,0:T(8,128)(2,1)S(1)}, u32[]{:S(2)}, u32[]{:S(2)}) collective-permute-start(s16[80,256]{1,0:T(8,128)(2,1)S(1)} %get-tuple-element.12.a_ref), channel_id=1, source_target_pairs={{0,6},{2,0},{4,2},{6,4},{1,7},{3,1},{5,3},{7,5},{8,14},{10,8},{12,... | collective-permute-start | bytes 122888 | tf_op jit(solution)/shard_map/ppermute | solution.py:33
  18.0 5.4 %collective-permute-start.10 = (s16[272,256]{1,0:T(8,128)(2,1)S(1)}, s16[272,256]{1,0:T(8,128)(2,1)S(1)}, u32[]{:S(2)}, u32[]{:S(2)}) collective-permute-start(s16[272,256]{1,0:T(8,128)(2,1)S(1)} %stack.2.refs_0_), channel_id=1, source_target_pairs={{0,24},{8,0},{16,8},{24,16},{32,56},{40,32},{48,40},{56,48},{64,88... | collective-permute-start | bytes 417800 | tf_op jit(solution)/shard_map/ppermute | solution.py:43
  18.6 5.8 %collective-permute-start.8 = (s16[272,256]{1,0:T(8,128)(2,1)S(1)}, s16[272,256]{1,0:T(8,128)(2,1)S(1)}, u32[]{:S(2)}, u32[]{:S(2)}) collective-permute-start(s16[272,256]{1,0:T(8,128)(2,1)S(1)} %stack.2.refs_0_), channel_id=1, source_target_pairs={{0,8},{8,16},{16,24},{24,0},{32,40},{40,48},{48,56},{56,32},{64,72... | collective-permute-start | bytes 417800 | tf_op jit(solution)/shard_map/ppermute | solution.py:43
  20.1 6.6 %collective-permute-start.9 = (s16[272,256]{1,0:T(8,128)(2,1)S(1)}, s16[272,256]{1,0:T(8,128)(2,1)S(1)}, u32[]{:S(2)}, u32[]{:S(2)}) collective-permute-start(s16[272,256]{1,0:T(8,128)(2,1)S(1)} %stack.2.refs_0_), channel_id=1, source_target_pairs={{0,16},{8,24},{16,0},{24,8},{32,48},{40,56},{48,32},{56,40},{64,80... | collective-permute-start | bytes 417800 | tf_op jit(solution)/shard_map/ppermute | solution.py:43
  26.7 23.2 %collective-permute-start.16 = (s16[1040,256]{1,0:T(8,128)(2,1)S(1)}, s16[1040,256]{1,0:T(8,128)(2,1)S(1)}, u32[]{:S(2)}, u32[]{:S(2)}) collective-permute-start(s16[1040,256]{1,0:T(8,128)(2,1)S(1)} %pack.2.refs_0_), channel_id=1, source_target_pairs={{0,32},{8,40},{16,48},{24,56},{32,64},{40,72},{48,80},{56,88},{64,... | collective-permute-start | bytes 1597448 | tf_op jit(solution)/shard_map/ppermute | solution.py:43
  28.3 24.7 %collective-permute-start.14 = (s16[1040,256]{1,0:T(8,128)(2,1)S(1)}, s16[1040,256]{1,0:T(8,128)(2,1)S(1)}, u32[]{:S(2)}, u32[]{:S(2)}) collective-permute-start(s16[1040,256]{1,0:T(8,128)(2,1)S(1)} %pack.2.refs_0_), channel_id=1, source_target_pairs={{0,64},{8,72},{16,80},{24,88},{32,96},{40,104},{48,112},{56,120},{... | collective-permute-start | bytes 1597448 | tf_op jit(solution)/shard_map/ppermute | solution.py:43
  31.2 21.8 %collective-permute-start.15 = (s16[1040,256]{1,0:T(8,128)(2,1)S(1)}, s16[1040,256]{1,0:T(8,128)(2,1)S(1)}, u32[]{:S(2)}, u32[]{:S(2)}) collective-permute-start(s16[1040,256]{1,0:T(8,128)(2,1)S(1)} %pack.2.refs_0_), channel_id=1, source_target_pairs={{0,96},{8,104},{16,112},{24,120},{32,0},{40,8},{48,16},{56,24},{64... | collective-permute-start | bytes 1597448 | tf_op jit(solution)/shard_map/ppermute | solution.py:43
  32.6 6.0 %collective-permute-start.5 = (s16[80,256]{1,0:T(8,128)(2,1)S(1)}, s16[80,256]{1,0:T(8,128)(2,1)S(1)}, u32[]{:S(2)}, u32[]{:S(2)}) collective-permute-start(s16[80,256]{1,0:T(8,128)(2,1)S(1)} %hold.1.a_ref), channel_id=1, source_target_pairs={{0,2},{2,4},{4,6},{6,0},{1,3},{3,5},{5,7},{7,1},{8,10},{10,12},{12... | collective-permute-start | bytes 122888 | tf_op jit(solution)/shard_map/ppermute | solution.py:33
  33.3 5.8 %collective-permute-start.6 = (s16[80,256]{1,0:T(8,128)(2,1)S(1)}, s16[80,256]{1,0:T(8,128)(2,1)S(1)}, u32[]{:S(2)}, u32[]{:S(2)}) collective-permute-start(s16[80,256]{1,0:T(8,128)(2,1)S(1)} %hold.1.a_ref), channel_id=1, source_target_pairs={{0,4},{2,6},{4,0},{6,2},{1,5},{3,7},{5,1},{7,3},{8,12},{10,14},{12... | collective-permute-start | bytes 122888 | tf_op jit(solution)/shard_map/ppermute | solution.py:33
  38.6 4.0 %collective-permute-start.7 = (s16[80,256]{1,0:T(8,128)(2,1)S(1)}, s16[80,256]{1,0:T(8,128)(2,1)S(1)}, u32[]{:S(2)}, u32[]{:S(2)}) collective-permute-start(s16[80,256]{1,0:T(8,128)(2,1)S(1)} %hold.1.a_ref), channel_id=1, source_target_pairs={{0,6},{2,0},{4,2},{6,4},{1,7},{3,1},{5,3},{7,5},{8,14},{10,8},{12,... | collective-permute-start | bytes 122888 | tf_op jit(solution)/shard_map/ppermute | solution.py:33
  43.2 18.1 %collective-permute-start.11 = (s16[272,256]{1,0:T(8,128)(2,1)S(1)}, s16[272,256]{1,0:T(8,128)(2,1)S(1)}, u32[]{:S(2)}, u32[]{:S(2)}) collective-permute-start(s16[272,256]{1,0:T(8,128)(2,1)S(1)} %stack.3.refs_0_), channel_id=1, source_target_pairs={{0,8},{8,16},{16,24},{24,0},{32,40},{40,48},{48,56},{56,32},{64,72... | collective-permute-start | bytes 417800 | tf_op jit(solution)/shard_map/ppermute | solution.py:43
  44.6 16.7 %collective-permute-start.12 = (s16[272,256]{1,0:T(8,128)(2,1)S(1)}, s16[272,256]{1,0:T(8,128)(2,1)S(1)}, u32[]{:S(2)}, u32[]{:S(2)}) collective-permute-start(s16[272,256]{1,0:T(8,128)(2,1)S(1)} %stack.3.refs_0_), channel_id=1, source_target_pairs={{0,16},{8,24},{16,0},{24,8},{32,48},{40,56},{48,32},{56,40},{64,80... | collective-permute-start | bytes 417800 | tf_op jit(solution)/shard_map/ppermute | solution.py:43
  49.9 11.5 %collective-permute-start.13 = (s16[272,256]{1,0:T(8,128)(2,1)S(1)}, s16[272,256]{1,0:T(8,128)(2,1)S(1)}, u32[]{:S(2)}, u32[]{:S(2)}) collective-permute-start(s16[272,256]{1,0:T(8,128)(2,1)S(1)} %stack.3.refs_0_), channel_id=1, source_target_pairs={{0,24},{8,0},{16,8},{24,16},{32,56},{40,32},{48,40},{56,48},{64,88... | collective-permute-start | bytes 417800 | tf_op jit(solution)/shard_map/ppermute | solution.py:43
  56.2 28.1 %collective-permute-start.20 = (s16[272,1024]{1,0:T(8,128)(2,1)S(1)}, s16[272,1024]{1,0:T(8,128)(2,1)S(1)}, u32[]{:S(2)}, u32[]{:S(2)}) collective-permute-start(s16[272,1024]{1,0:T(8,128)(2,1)S(1)} %product.8.refs_4_), channel_id=1, source_target_pairs={{0,1},{1,0},{2,3},{3,2},{4,5},{5,4},{6,7},{7,6},{8,9},{9,8},{10,11... | collective-permute-start | bytes 1671176 | tf_op jit(solution)/shard_map/ppermute | solution.py:310
  61.4 16.3 %collective-permute-start.19 = (s16[1040,256]{1,0:T(8,128)(2,1)S(1)}, s16[1040,256]{1,0:T(8,128)(2,1)S(1)}, u32[]{:S(2)}, u32[]{:S(2)}) collective-permute-start(s16[1040,256]{1,0:T(8,128)(2,1)S(1)} %pack.3.refs_0_), channel_id=1, source_target_pairs={{0,32},{8,40},{16,48},{24,56},{32,64},{40,72},{48,80},{56,88},{64,... | collective-permute-start | bytes 1597448 | tf_op jit(solution)/shard_map/ppermute | solution.py:43
  62.2 18.4 %collective-permute-start.18 = (s16[1040,256]{1,0:T(8,128)(2,1)S(1)}, s16[1040,256]{1,0:T(8,128)(2,1)S(1)}, u32[]{:S(2)}, u32[]{:S(2)}) collective-permute-start(s16[1040,256]{1,0:T(8,128)(2,1)S(1)} %pack.3.refs_0_), channel_id=1, source_target_pairs={{0,64},{8,72},{16,80},{24,88},{32,96},{40,104},{48,112},{56,120},{... | collective-permute-start | bytes 1597448 | tf_op jit(solution)/shard_map/ppermute | solution.py:43
  62.9 19.5 %collective-permute-start.17 = (s16[1040,256]{1,0:T(8,128)(2,1)S(1)}, s16[1040,256]{1,0:T(8,128)(2,1)S(1)}, u32[]{:S(2)}, u32[]{:S(2)}) collective-permute-start(s16[1040,256]{1,0:T(8,128)(2,1)S(1)} %pack.3.refs_0_), channel_id=1, source_target_pairs={{0,96},{8,104},{16,112},{24,120},{32,0},{40,8},{48,16},{56,24},{64... | collective-permute-start | bytes 1597448 | tf_op jit(solution)/shard_map/ppermute | solution.py:43
  82.4 10.3 %copy-start.3 = (s32[512]{0:T(512)S(1)}, s32[512]{0:T(512)}, u32[]{:S(2)}) copy-start(s32[512]{0:T(512)} %param.7) | copy-start | bytes 6148
  85.6 17.5 %all-to-all-start = ((f32[64,8,128]{2,1,0:T(8,128)}), f32[64,8,128]{2,1,0:T(8,128)S(1)}, u32[]{:S(2)}, u32[]{:S(2)}) async-start(f32[64,8,128]{2,1,0:T(8,128)} %get-tuple-element.16), calls=%async_computation | async-start | bytes 524288 | tf_op jit(solution)/shard_map/all_to_all | solution.py:317
  103.3 1.3 %copy-start.2 = (f32[256]{0:T(256)}, f32[256]{0:T(256)S(1)}, u32[]{:S(2)}) copy-start(f32[256]{0:T(256)S(1)} %get-tuple-element.19) | copy-start | bytes 3076
  (2 other events, 1.6 us)

commit v10 on v9

--- a/solution.py
+++ b/solution.py
@@ -257,8 +257,7 @@
     lane = lax.broadcasted_iota(jnp.int32, (256, 128), 1)
     table = jnp.transpose(jnp.where(lane == 0, peak + jnp.log(total), moment / total))
     rows = [table[i : i + 1, at : at + 128] for i in (0, 1) for at in (0, 128)]
-    tile = jnp.concatenate(rows + [jnp.zeros((4, 128), jnp.float32)], 0)
-    stats_ref[...] = jnp.broadcast_to(tile[None], (64, 8, 128))
+    stats_ref[...] = jnp.broadcast_to(jnp.concatenate(rows, 0)[None], (64, 4, 128))
     guided_ref[...] = guided
 
 
@@ -267,7 +266,7 @@
         join_kernel,
         out_shape=(
             jax.ShapeDtypeStruct(kept.shape, jnp.float32),
-            jax.ShapeDtypeStruct((64, 8, 128), jnp.float32),
+            jax.ShapeDtypeStruct((64, 4, 128), jnp.float32),
         ),
         in_specs=in_vmem(2),
         out_specs=in_vmem(2),
@@ -299,19 +298,17 @@
         return [block] + [crossed(block, first, second, k) for k in (1, 2, 3)]
 
     away_near = near(away)
-    home_near = near(hold(home, away_near[1:]))
-    away_line = spread(stack(place, away_near, (head,)), "x", "y")
-    away_block = pack(away_line, ())
+    away_line = spread(stack(place, away_near, ()), "x", "y")
+    away_block = pack(away_line, (head,))
     away_parts = spread(away_block, "y", "x")
+    away_sum = product(place, head, away_parts, (0,), cost=1)
+    home_near = near(hold(home, (*away_near[1:], away_sum)))
     home_line = spread(stack(place, home_near, (away_block,)), "x", "y")
-    away_sum = product(place, head, away_parts, (0,), cost=1)
-    away_sum = product(place, head, away_parts, (1,), (away_sum,), cost=1)
-    sent = product(place, head, away_parts, (2, 3), (away_sum,), True, cost=1)
+    sent = product(place, head, away_parts, (1, 2, 3), (away_sum,), True, cost=1)
     back = lax.ppermute(sent, "zh", [(0, 1), (1, 0)])
     home_parts = spread(pack(home_line, (sent,)), "y", "x")
-    kept = product(place, head, home_parts, (0, 1))
-    kept = product(place, head, home_parts, (2,), (kept,))
-    kept = product(place, head, home_parts, (3,), (kept,))
+    kept = product(place, head, home_parts, (0,))
+    kept = product(place, head, home_parts, (1, 2, 3), (kept,))
 
     guided, stats = join(kept, back)
     stats = lax.all_to_all(stats, ("y", "x", "zl"), 0, 0, tiled=True)

time: 105 us -> 102 us (0.971)
  waiting for transfers between devices: 33 us -> 30.8 us
  Pallas kernels: 20.1 us -> 18.5 us
    ppermute x12, waiting for transfers between devices: 16 us -> 12.8 us  [crossed(): return lax.ppermute(block, axes, pairs(axes, move))]
    all_to_all x1, starting transfers between devices: 7.05 us -> 9.43 us  [local(): stats = lax.all_to_all(stats, ('y', 'x', 'zl'), 0, 0, tiled=True)]
    ppermute x12, starting transfers between devices: 21 us -> 19 us  [crossed(): return lax.ppermute(block, axes, pairs(axes, move))]
    ppermute x6, waiting for transfers between devices: 6.67 us -> 8.57 us  [shifted(): lax.ppermute(block, axis, pairs((axis,), lambda at: {axis: at[axis] + k}))]
    pallas_call x6 -> x4, Pallas kernels: 13.4 us -> 11.9 us  [product(): pl.pallas_call(functools.partial(product_kernel, offsets, len(before) > 0...]
  transfers between devices with their start and end apart: 22 -> 22, of which waited for: 6 -> 9; matrix products, arithmetic and copies ran while one was open for 0% -> 0% of each run, Pallas kernels for 17% -> 16%
where the time goes in v10:
time: 102 us
  starting transfers between devices  48.5 us (48%)
  waiting for transfers between devices  30.8 us (30%)
  Pallas kernels  18.5 us (18%)
  local copies, waits for them, and re-layouts  1.6 us (2%)
  other arithmetic  1.54 us (2%)
    ppermute x12, starting transfers between devices, crossed(): return lax.ppermute(block, axes, pairs(axes, move))  19 us
    ppermute x12, waiting for transfers between devices, crossed(): return lax.ppermute(block, axes, pairs(axes, move))  12.8 us
    pallas_call x4, Pallas kernels, product(): pl.pallas_call(functools.partial(product_kernel, offsets, len(before) > 0...  11.9 us
    all_to_all x1, starting transfers between devices, local(): stats = lax.all_to_all(stats, ('y', 'x', 'zl'), 0, 0, tiled=True)  9.43 us
    all_to_all x1, waiting for transfers between devices, local(): stats = lax.all_to_all(stats, ('y', 'x', 'zl'), 0, 0, tiled=True)  9.39 us
    ppermute x6, waiting for transfers between devices, shifted(): lax.ppermute(block, axis, pairs((axis,), lambda at: {axis: at[axis] + k}))  8.57 us
    ppermute x6, starting transfers between devices, shifted(): lax.ppermute(block, axis, pairs((axis,), lambda at: {axis: at[axis] + k}))  8.4 us
    ppermute x1, starting transfers between devices, local(): lax.ppermute(scale_index, ('zl', 'zh'), pairs(('zl', 'zh'), nearest_other))  6.39 us
  transfers between devices with their start and end apart: 22, of which 9 were waited for; matrix products, arithmetic and copies ran while one was open for 0% of the time, Pallas kernels for 16%

profile of v10, /device:TPU:2, one launch (start us, length us, event | category | flops | bytes accessed | tf_op | source)
XLA Modules:
  0.0 101.7 jit_solution(3132879345646258968)
XLA Ops:
  0.7 6.4 %collective-permute-start.1 = (s32[512]{0:T(512)}, s32[512]{0:T(512)S(1)}, u32[]{:S(2)}, u32[]{:S(2)}) collective-permute-start(s32[512]{0:T(512)} %param.6), channel_id=1, source_target_pairs={{0,5},{1,4},{2,7},{3,6},{4,1},{5,0},{6,3},{7,2},{8,13},{9,12},{10,... | collective-permute-start | bytes 6152 | tf_op jit(solution)/shard_map/ppermute | solution.py:287
  10.6 2.0 %collective-permute-start.3 = (s16[80,256]{1,0:T(8,128)(2,1)S(1)}, s16[80,256]{1,0:T(8,128)(2,1)S(1)}, u32[]{:S(2)}, u32[]{:S(2)}) collective-permute-start(s16[80,256]{1,0:T(8,128)(2,1)S(1)} %get-tuple-element.12.a_ref), channel_id=1, source_target_pairs={{0,4},{2,6},{4,0},{6,2},{1,5},{3,7},{5,1},{7,3},{8,12},{10,14},{12... | collective-permute-start | bytes 122888 | tf_op jit(solution)/shard_map/ppermute | solution.py:33
  12.6 1.4 %collective-permute-start.4 = (s16[80,256]{1,0:T(8,128)(2,1)S(1)}, s16[80,256]{1,0:T(8,128)(2,1)S(1)}, u32[]{:S(2)}, u32[]{:S(2)}) collective-permute-start(s16[80,256]{1,0:T(8,128)(2,1)S(1)} %get-tuple-element.12.a_ref), channel_id=1, source_target_pairs={{0,6},{2,0},{4,2},{6,4},{1,7},{3,1},{5,3},{7,5},{8,14},{10,8},{12,... | collective-permute-start | bytes 122888 | tf_op jit(solution)/shard_map/ppermute | solution.py:33
  14.0 1.9 %collective-permute-done.2.b_ref.refs_0_ = s16[80,256]{1,0:T(8,128)(2,1)S(1)} collective-permute-done((s16[80,256]{1,0:T(8,128)(2,1)S(1)}, s16[80,256]{1,0:T(8,128)(2,1)S(1)}, u32[]{:S(2)}, u32[]{:S(2)}) %collective-permute-start.2) | collective-permute-done | bytes 40992 | tf_op jit(solution)/shard_map/ppermute | solution.py:33
  17.4 1.6 %collective-permute-start.5 = (s16[272,256]{1,0:T(8,128)(2,1)S(1)}, s16[272,256]{1,0:T(8,128)(2,1)S(1)}, u32[]{:S(2)}, u32[]{:S(2)}) collective-permute-start(s16[272,256]{1,0:T(8,128)(2,1)S(1)} %stack.2.refs_0_), channel_id=1, source_target_pairs={{0,8},{8,16},{16,24},{24,0},{32,40},{40,48},{48,56},{56,32},{64,72... | collective-permute-start | bytes 417800 | tf_op jit(solution)/shard_map/ppermute | solution.py:43
  20.1 2.2 %collective-permute-start.7 = (s16[272,256]{1,0:T(8,128)(2,1)S(1)}, s16[272,256]{1,0:T(8,128)(2,1)S(1)}, u32[]{:S(2)}, u32[]{:S(2)}) collective-permute-start(s16[272,256]{1,0:T(8,128)(2,1)S(1)} %stack.2.refs_0_), channel_id=1, source_target_pairs={{0,24},{8,0},{16,8},{24,16},{32,56},{40,32},{48,40},{56,48},{64,88... | collective-permute-start | bytes 417800 | tf_op jit(solution)/shard_map/ppermute | solution.py:43
  22.3 3.4 %load.3.refs_4_.head_ref = bf16[4096,1024]{1,0:T(8,128)(2,1)S(1)} custom-call(bf16[4096,1024]{1,0:T(8,128)(2,1)} %refs_0_), custom_call_target="tpu_custom_call" | custom-call | bytes 16777216 | tf_op jit(solution)/shard_map/load/pallas_call | solution.py:86
  26.7 1.7 %collective-permute-start.14 = (s16[1040,256]{1,0:T(8,128)(2,1)S(1)}, s16[1040,256]{1,0:T(8,128)(2,1)S(1)}, u32[]{:S(2)}, u32[]{:S(2)}) collective-permute-start(s16[1040,256]{1,0:T(8,128)(2,1)S(1)} %pack.2.refs_0_), channel_id=1, source_target_pairs={{0,32},{8,40},{16,48},{24,56},{32,64},{40,72},{48,80},{56,88},{64,... | collective-permute-start | bytes 1597448 | tf_op jit(solution)/shard_map/ppermute | solution.py:43
  28.4 2.9 %collective-permute-start.15 = (s16[1040,256]{1,0:T(8,128)(2,1)S(1)}, s16[1040,256]{1,0:T(8,128)(2,1)S(1)}, u32[]{:S(2)}, u32[]{:S(2)}) collective-permute-start(s16[1040,256]{1,0:T(8,128)(2,1)S(1)} %pack.2.refs_0_), channel_id=1, source_target_pairs={{0,64},{8,72},{16,80},{24,88},{32,96},{40,104},{48,112},{56,120},{... | collective-permute-start | bytes 1597448 | tf_op jit(solution)/shard_map/ppermute | solution.py:43
  31.3 1.3 %collective-permute-start.16 = (s16[1040,256]{1,0:T(8,128)(2,1)S(1)}, s16[1040,256]{1,0:T(8,128)(2,1)S(1)}, u32[]{:S(2)}, u32[]{:S(2)}) collective-permute-start(s16[1040,256]{1,0:T(8,128)(2,1)S(1)} %pack.2.refs_0_), channel_id=1, source_target_pairs={{0,96},{8,104},{16,112},{24,120},{32,0},{40,8},{48,16},{56,24},{64... | collective-permute-start | bytes 1597448 | tf_op jit(solution)/shard_map/ppermute | solution.py:43
  32.6 1.8 %product.4.refs_3_ = f32[256,1024]{1,0:T(8,128)S(1)} custom-call(s32[8]{0:T(128)S(1)} %compare_select_fusion.4.place_ref, bf16[4096,1024]{1,0:T(8,128)(2,1)S(1)} %load.3.refs_4_.head_ref, s16[1040,256]{1,0:T(8,128)(2,1)S(1)} %pack.2.refs_0_), custom_call_target="tpu_custom_call" | custom-call | flops 1073741824 | tf_op jit(solution)/shard_map/product/pallas_call | solution.py:235
  34.5 3.0 %collective-permute-start.10 = (s16[80,256]{1,0:T(8,128)(2,1)S(1)}, s16[80,256]{1,0:T(8,128)(2,1)S(1)}, u32[]{:S(2)}, u32[]{:S(2)}) collective-permute-start(s16[80,256]{1,0:T(8,128)(2,1)S(1)} %hold.1.a_ref), channel_id=1, source_target_pairs={{0,6},{2,0},{4,2},{6,4},{1,7},{3,1},{5,3},{7,5},{8,14},{10,8},{12,... | collective-permute-start | bytes 122888 | tf_op jit(solution)/shard_map/ppermute | solution.py:33
  37.4 1.7 %collective-permute-done.10.d_ref = s16[80,256]{1,0:T(8,128)(2,1)S(1)} collective-permute-done((s16[80,256]{1,0:T(8,128)(2,1)S(1)}, s16[80,256]{1,0:T(8,128)(2,1)S(1)}, u32[]{:S(2)}, u32[]{:S(2)}) %collective-permute-start.10) | collective-permute-done | bytes 40992 | tf_op jit(solution)/shard_map/ppermute | solution.py:33
  40.1 3.1 %collective-permute-done.8.b_ref = s16[80,256]{1,0:T(8,128)(2,1)S(1)} collective-permute-done((s16[80,256]{1,0:T(8,128)(2,1)S(1)}, s16[80,256]{1,0:T(8,128)(2,1)S(1)}, u32[]{:S(2)}, u32[]{:S(2)}) %collective-permute-start.8) | collective-permute-done | bytes 40992 | tf_op jit(solution)/shard_map/ppermute | solution.py:33
  45.7 1.7 %collective-permute-start.12 = (s16[272,256]{1,0:T(8,128)(2,1)S(1)}, s16[272,256]{1,0:T(8,128)(2,1)S(1)}, u32[]{:S(2)}, u32[]{:S(2)}) collective-permute-start(s16[272,256]{1,0:T(8,128)(2,1)S(1)} %stack.3.refs_0_), channel_id=1, source_target_pairs={{0,16},{8,24},{16,0},{24,8},{32,48},{40,56},{48,32},{56,40},{64,80... | collective-permute-start | bytes 417800 | tf_op jit(solution)/shard_map/ppermute | solution.py:43
  47.4 2.0 %collective-permute-start.13 = (s16[272,256]{1,0:T(8,128)(2,1)S(1)}, s16[272,256]{1,0:T(8,128)(2,1)S(1)}, u32[]{:S(2)}, u32[]{:S(2)}) collective-permute-start(s16[272,256]{1,0:T(8,128)(2,1)S(1)} %stack.3.refs_0_), channel_id=1, source_target_pairs={{0,24},{8,0},{16,8},{24,16},{32,56},{40,32},{48,40},{56,48},{64,88... | collective-permute-start | bytes 417800 | tf_op jit(solution)/shard_map/ppermute | solution.py:43
  49.4 4.2 %product.5.refs_4_ = s16[272,1024]{1,0:T(8,128)(2,1)S(1)} custom-call(s32[8]{0:T(128)S(1)} %compare_select_fusion.4.place_ref, bf16[4096,1024]{1,0:T(8,128)(2,1)S(1)} %load.3.refs_4_.head_ref, s16[1040,256]{1,0:T(8,128)(2,1)S(1)} %collective-permute-done.14.refs_0_, s16[1040,256]{1,0:T(8,128)(2,1)S(1)} %collective-permute-done.15.refs_1_, ...), custom_call_target="tpu_custom_call" | custom-call | flops 3221225472 | tf_op jit(solution)/shard_map/product/pallas_call | solution.py:235
  53.7 5.1 %collective-permute-start.20 = (s16[272,1024]{1,0:T(8,128)(2,1)S(1)}, s16[272,1024]{1,0:T(8,128)(2,1)S(1)}, u32[]{:S(2)}, u32[]{:S(2)}) collective-permute-start(s16[272,1024]{1,0:T(8,128)(2,1)S(1)} %product.5.refs_4_), channel_id=1, source_target_pairs={{0,1},{1,0},{2,3},{3,2},{4,5},{5,4},{6,7},{7,6},{8,9},{9,8},{10,11... | collective-permute-start | bytes 1671176 | tf_op jit(solution)/shard_map/ppermute | solution.py:308
  60.4 2.0 %collective-permute-start.19 = (s16[1040,256]{1,0:T(8,128)(2,1)S(1)}, s16[1040,256]{1,0:T(8,128)(2,1)S(1)}, u32[]{:S(2)}, u32[]{:S(2)}) collective-permute-start(s16[1040,256]{1,0:T(8,128)(2,1)S(1)} %pack.3.refs_0_), channel_id=1, source_target_pairs={{0,96},{8,104},{16,112},{24,120},{32,0},{40,8},{48,16},{56,24},{64... | collective-permute-start | bytes 1597448 | tf_op jit(solution)/shard_map/ppermute | solution.py:43
  62.4 1.8 %product.6.refs_3_ = f32[256,1024]{1,0:T(8,128)S(1)} custom-call(s32[8]{0:T(128)S(1)} %compare_select_fusion.4.place_ref, bf16[4096,1024]{1,0:T(8,128)(2,1)S(1)} %load.3.refs_4_.head_ref, s16[1040,256]{1,0:T(8,128)(2,1)S(1)} %pack.3.refs_0_), custom_call_target="tpu_custom_call" | custom-call | tf_op jit(solution)/shard_map/product/pallas_call | solution.py:235
  64.2 10.9 %collective-permute-done.17.refs_0_ = s16[1040,256]{1,0:T(8,128)(2,1)S(1)} collective-permute-done((s16[1040,256]{1,0:T(8,128)(2,1)S(1)}, s16[1040,256]{1,0:T(8,128)(2,1)S(1)}, u32[]{:S(2)}, u32[]{:S(2)}) %collective-permute-start.17) | collective-permute-done | bytes 532512 | tf_op jit(solution)/shard_map/ppermute | solution.py:43
  76.0 4.0 %product.7.kept_ref = f32[256,1024]{1,0:T(8,128)S(1)} custom-call(s32[8]{0:T(128)S(1)} %compare_select_fusion.4.place_ref, bf16[4096,1024]{1,0:T(8,128)(2,1)S(1)} %load.3.refs_4_.head_ref, s16[1040,256]{1,0:T(8,128)(2,1)S(1)} %collective-permute-done.17.refs_0_, s16[1040,256]{1,0:T(8,128)(2,1)S(1)} %collective-permute-done.18.refs_1_, ...), custom_call_target="tpu_custom_call" | custom-call | tf_op jit(solution)/shard_map/product/pallas_call | solution.py:235
  81.3 9.4 %all-to-all-start = ((f32[64,4,128]{2,1,0:T(4,128)}), f32[64,4,128]{2,1,0:T(4,128)S(1)}, u32[]{:S(2)}, u32[]{:S(2)}) async-start(f32[64,4,128]{2,1,0:T(4,128)} %get-tuple-element.16), calls=%async_computation | async-start | bytes 262144 | tf_op jit(solution)/shard_map/all_to_all | solution.py:314
  90.9 9.4 %all-to-all-done = f32[64,4,128]{2,1,0:T(4,128)S(1)} async-done(((f32[64,4,128]{2,1,0:T(4,128)}), f32[64,4,128]{2,1,0:T(4,128)S(1)}, u32[]{:S(2)}, u32[]{:S(2)}) %all-to-all-start) | async-done | bytes 131104 | tf_op jit(solution)/shard_map/all_to_all | solution.py:314
  (47 shorter events, 16.0 us)
Async XLA Ops:
  0.6 8.3 %collective-permute-start = (bf16[64,1024]{1,0:T(8,128)(2,1)}, bf16[64,1024]{1,0:T(8,128)(2,1)S(1)}, u32[]{:S(2)}, u32[]{:S(2)}) collective-permute-start(bf16[64,1024]{1,0:T(8,128)(2,1)} %bitcast.10), channel_id=1, source_target_pairs={{0,128},{128,0},{1,129},{129,1},{2,130},{130,2},{3,131},{131,3},{4... | collective-permute-start | bytes 393224 | tf_op jit(solution)/shard_map/ppermute | solution.py:286
  0.7 8.2 %collective-permute-start.1 = (s32[512]{0:T(512)}, s32[512]{0:T(512)S(1)}, u32[]{:S(2)}, u32[]{:S(2)}) collective-permute-start(s32[512]{0:T(512)} %param.6), channel_id=1, source_target_pairs={{0,5},{1,4},{2,7},{3,6},{4,1},{5,0},{6,3},{7,2},{8,13},{9,12},{10,... | collective-permute-start | bytes 6152 | tf_op jit(solution)/shard_map/ppermute | solution.py:287
  9.5 6.3 %collective-permute-start.2 = (s16[80,256]{1,0:T(8,128)(2,1)S(1)}, s16[80,256]{1,0:T(8,128)(2,1)S(1)}, u32[]{:S(2)}, u32[]{:S(2)}) collective-permute-start(s16[80,256]{1,0:T(8,128)(2,1)S(1)} %get-tuple-element.12.a_ref), channel_id=1, source_target_pairs={{0,2},{2,4},{4,6},{6,0},{1,3},{3,5},{5,7},{7,1},{8,10},{10,12},{12... | collective-permute-start | bytes 122888 | tf_op jit(solution)/shard_map/ppermute | solution.py:33
  10.6 6.3 %collective-permute-start.3 = (s16[80,256]{1,0:T(8,128)(2,1)S(1)}, s16[80,256]{1,0:T(8,128)(2,1)S(1)}, u32[]{:S(2)}, u32[]{:S(2)}) collective-permute-start(s16[80,256]{1,0:T(8,128)(2,1)S(1)} %get-tuple-element.12.a_ref), channel_id=1, source_target_pairs={{0,4},{2,6},{4,0},{6,2},{1,5},{3,7},{5,1},{7,3},{8,12},{10,14},{12... | collective-permute-start | bytes 122888 | tf_op jit(solution)/shard_map/ppermute | solution.py:33
  12.6 4.3 %collective-permute-start.4 = (s16[80,256]{1,0:T(8,128)(2,1)S(1)}, s16[80,256]{1,0:T(8,128)(2,1)S(1)}, u32[]{:S(2)}, u32[]{:S(2)}) collective-permute-start(s16[80,256]{1,0:T(8,128)(2,1)S(1)} %get-tuple-element.12.a_ref), channel_id=1, source_target_pairs={{0,6},{2,0},{4,2},{6,4},{1,7},{3,1},{5,3},{7,5},{8,14},{10,8},{12,... | collective-permute-start | bytes 122888 | tf_op jit(solution)/shard_map/ppermute | solution.py:33
  17.4 8.2 %collective-permute-start.5 = (s16[272,256]{1,0:T(8,128)(2,1)S(1)}, s16[272,256]{1,0:T(8,128)(2,1)S(1)}, u32[]{:S(2)}, u32[]{:S(2)}) collective-permute-start(s16[272,256]{1,0:T(8,128)(2,1)S(1)} %stack.2.refs_0_), channel_id=1, source_target_pairs={{0,8},{8,16},{16,24},{24,0},{32,40},{40,48},{48,56},{56,32},{64,72... | collective-permute-start | bytes 417800 | tf_op jit(solution)/shard_map/ppermute | solution.py:43
  19.0 6.7 %collective-permute-start.6 = (s16[272,256]{1,0:T(8,128)(2,1)S(1)}, s16[272,256]{1,0:T(8,128)(2,1)S(1)}, u32[]{:S(2)}, u32[]{:S(2)}) collective-permute-start(s16[272,256]{1,0:T(8,128)(2,1)S(1)} %stack.2.refs_0_), channel_id=1, source_target_pairs={{0,16},{8,24},{16,0},{24,8},{32,48},{40,56},{48,32},{56,40},{64,80... | collective-permute-start | bytes 417800 | tf_op jit(solution)/shard_map/ppermute | solution.py:43
  20.1 6.5 %collective-permute-start.7 = (s16[272,256]{1,0:T(8,128)(2,1)S(1)}, s16[272,256]{1,0:T(8,128)(2,1)S(1)}, u32[]{:S(2)}, u32[]{:S(2)}) collective-permute-start(s16[272,256]{1,0:T(8,128)(2,1)S(1)} %stack.2.refs_0_), channel_id=1, source_target_pairs={{0,24},{8,0},{16,8},{24,16},{32,56},{40,32},{48,40},{56,48},{64,88... | collective-permute-start | bytes 417800 | tf_op jit(solution)/shard_map/ppermute | solution.py:43
  26.7 20.7 %collective-permute-start.14 = (s16[1040,256]{1,0:T(8,128)(2,1)S(1)}, s16[1040,256]{1,0:T(8,128)(2,1)S(1)}, u32[]{:S(2)}, u32[]{:S(2)}) collective-permute-start(s16[1040,256]{1,0:T(8,128)(2,1)S(1)} %pack.2.refs_0_), channel_id=1, source_target_pairs={{0,32},{8,40},{16,48},{24,56},{32,64},{40,72},{48,80},{56,88},{64,... | collective-permute-start | bytes 1597448 | tf_op jit(solution)/shard_map/ppermute | solution.py:43
  28.4 21.1 %collective-permute-start.15 = (s16[1040,256]{1,0:T(8,128)(2,1)S(1)}, s16[1040,256]{1,0:T(8,128)(2,1)S(1)}, u32[]{:S(2)}, u32[]{:S(2)}) collective-permute-start(s16[1040,256]{1,0:T(8,128)(2,1)S(1)} %pack.2.refs_0_), channel_id=1, source_target_pairs={{0,64},{8,72},{16,80},{24,88},{32,96},{40,104},{48,112},{56,120},{... | collective-permute-start | bytes 1597448 | tf_op jit(solution)/shard_map/ppermute | solution.py:43
  31.3 18.2 %collective-permute-start.16 = (s16[1040,256]{1,0:T(8,128)(2,1)S(1)}, s16[1040,256]{1,0:T(8,128)(2,1)S(1)}, u32[]{:S(2)}, u32[]{:S(2)}) collective-permute-start(s16[1040,256]{1,0:T(8,128)(2,1)S(1)} %pack.2.refs_0_), channel_id=1, source_target_pairs={{0,96},{8,104},{16,112},{24,120},{32,0},{40,8},{48,16},{56,24},{64... | collective-permute-start | bytes 1597448 | tf_op jit(solution)/shard_map/ppermute | solution.py:43
  34.5 4.7 %collective-permute-start.10 = (s16[80,256]{1,0:T(8,128)(2,1)S(1)}, s16[80,256]{1,0:T(8,128)(2,1)S(1)}, u32[]{:S(2)}, u32[]{:S(2)}) collective-permute-start(s16[80,256]{1,0:T(8,128)(2,1)S(1)} %hold.1.a_ref), channel_id=1, source_target_pairs={{0,6},{2,0},{4,2},{6,4},{1,7},{3,1},{5,3},{7,5},{8,14},{10,8},{12,... | collective-permute-start | bytes 122888 | tf_op jit(solution)/shard_map/ppermute | solution.py:33
  37.4 5.8 %collective-permute-start.8 = (s16[80,256]{1,0:T(8,128)(2,1)S(1)}, s16[80,256]{1,0:T(8,128)(2,1)S(1)}, u32[]{:S(2)}, u32[]{:S(2)}) collective-permute-start(s16[80,256]{1,0:T(8,128)(2,1)S(1)} %hold.1.a_ref), channel_id=1, source_target_pairs={{0,2},{2,4},{4,6},{6,0},{1,3},{3,5},{5,7},{7,1},{8,10},{10,12},{12... | collective-permute-start | bytes 122888 | tf_op jit(solution)/shard_map/ppermute | solution.py:33
  39.2 4.9 %collective-permute-start.9 = (s16[80,256]{1,0:T(8,128)(2,1)S(1)}, s16[80,256]{1,0:T(8,128)(2,1)S(1)}, u32[]{:S(2)}, u32[]{:S(2)}) collective-permute-start(s16[80,256]{1,0:T(8,128)(2,1)S(1)} %hold.1.a_ref), channel_id=1, source_target_pairs={{0,4},{2,6},{4,0},{6,2},{1,5},{3,7},{5,1},{7,3},{8,12},{10,14},{12... | collective-permute-start | bytes 122888 | tf_op jit(solution)/shard_map/ppermute | solution.py:33
  44.7 14.2 %collective-permute-start.11 = (s16[272,256]{1,0:T(8,128)(2,1)S(1)}, s16[272,256]{1,0:T(8,128)(2,1)S(1)}, u32[]{:S(2)}, u32[]{:S(2)}) collective-permute-start(s16[272,256]{1,0:T(8,128)(2,1)S(1)} %stack.3.refs_0_), channel_id=1, source_target_pairs={{0,8},{8,16},{16,24},{24,0},{32,40},{40,48},{48,56},{56,32},{64,72... | collective-permute-start | bytes 417800 | tf_op jit(solution)/shard_map/ppermute | solution.py:43
  45.7 13.1 %collective-permute-start.12 = (s16[272,256]{1,0:T(8,128)(2,1)S(1)}, s16[272,256]{1,0:T(8,128)(2,1)S(1)}, u32[]{:S(2)}, u32[]{:S(2)}) collective-permute-start(s16[272,256]{1,0:T(8,128)(2,1)S(1)} %stack.3.refs_0_), channel_id=1, source_target_pairs={{0,16},{8,24},{16,0},{24,8},{32,48},{40,56},{48,32},{56,40},{64,80... | collective-permute-start | bytes 417800 | tf_op jit(solution)/shard_map/ppermute | solution.py:43
  47.4 11.4 %collective-permute-start.13 = (s16[272,256]{1,0:T(8,128)(2,1)S(1)}, s16[272,256]{1,0:T(8,128)(2,1)S(1)}, u32[]{:S(2)}, u32[]{:S(2)}) collective-permute-start(s16[272,256]{1,0:T(8,128)(2,1)S(1)} %stack.3.refs_0_), channel_id=1, source_target_pairs={{0,24},{8,0},{16,8},{24,16},{32,56},{40,32},{48,40},{56,48},{64,88... | collective-permute-start | bytes 417800 | tf_op jit(solution)/shard_map/ppermute | solution.py:43
  53.7 26.4 %collective-permute-start.20 = (s16[272,1024]{1,0:T(8,128)(2,1)S(1)}, s16[272,1024]{1,0:T(8,128)(2,1)S(1)}, u32[]{:S(2)}, u32[]{:S(2)}) collective-permute-start(s16[272,1024]{1,0:T(8,128)(2,1)S(1)} %product.5.refs_4_), channel_id=1, source_target_pairs={{0,1},{1,0},{2,3},{3,2},{4,5},{5,4},{6,7},{7,6},{8,9},{9,8},{10,11... | collective-permute-start | bytes 1671176 | tf_op jit(solution)/shard_map/ppermute | solution.py:308
  58.9 16.3 %collective-permute-start.17 = (s16[1040,256]{1,0:T(8,128)(2,1)S(1)}, s16[1040,256]{1,0:T(8,128)(2,1)S(1)}, u32[]{:S(2)}, u32[]{:S(2)}) collective-permute-start(s16[1040,256]{1,0:T(8,128)(2,1)S(1)} %pack.3.refs_0_), channel_id=1, source_target_pairs={{0,32},{8,40},{16,48},{24,56},{32,64},{40,72},{48,80},{56,88},{64,... | collective-permute-start | bytes 1597448 | tf_op jit(solution)/shard_map/ppermute | solution.py:43
  59.6 15.5 %collective-permute-start.18 = (s16[1040,256]{1,0:T(8,128)(2,1)S(1)}, s16[1040,256]{1,0:T(8,128)(2,1)S(1)}, u32[]{:S(2)}, u32[]{:S(2)}) collective-permute-start(s16[1040,256]{1,0:T(8,128)(2,1)S(1)} %pack.3.refs_0_), channel_id=1, source_target_pairs={{0,64},{8,72},{16,80},{24,88},{32,96},{40,104},{48,112},{56,120},{... | collective-permute-start | bytes 1597448 | tf_op jit(solution)/shard_map/ppermute | solution.py:43
  60.4 15.6 %collective-permute-start.19 = (s16[1040,256]{1,0:T(8,128)(2,1)S(1)}, s16[1040,256]{1,0:T(8,128)(2,1)S(1)}, u32[]{:S(2)}, u32[]{:S(2)}) collective-permute-start(s16[1040,256]{1,0:T(8,128)(2,1)S(1)} %pack.3.refs_0_), channel_id=1, source_target_pairs={{0,96},{8,104},{16,112},{24,120},{32,0},{40,8},{48,16},{56,24},{64... | collective-permute-start | bytes 1597448 | tf_op jit(solution)/shard_map/ppermute | solution.py:43
  64.2 26.6 %copy-start.3 = (s32[512]{0:T(512)S(1)}, s32[512]{0:T(512)}, u32[]{:S(2)}) copy-start(s32[512]{0:T(512)} %param.7) | copy-start | bytes 6148
  81.3 18.9 %all-to-all-start = ((f32[64,4,128]{2,1,0:T(4,128)}), f32[64,4,128]{2,1,0:T(4,128)S(1)}, u32[]{:S(2)}, u32[]{:S(2)}) async-start(f32[64,4,128]{2,1,0:T(4,128)} %get-tuple-element.16), calls=%async_computation | async-start | bytes 262144 | tf_op jit(solution)/shard_map/all_to_all | solution.py:314
  100.5 1.3 %copy-start.2 = (f32[256]{0:T(256)}, f32[256]{0:T(256)S(1)}, u32[]{:S(2)}) copy-start(f32[256]{0:T(256)S(1)} %get-tuple-element.19) | copy-start | bytes 3076
  (2 other events, 1.6 us)

commit v11 on v10

--- a/solution.py
+++ b/solution.py
@@ -218,17 +218,20 @@
         out_ref[...] = total
     else:
         code = code_of(jnp.max(jnp.abs(total), axis=1, keepdims=True))
-        out_ref[:count] = coded(total, scale_of(code))
+        values = coded(total, scale_of(code))
+        half = out_ref.shape[1]
+        out_ref[:count] = values[:, :half]
+        out_ref[count : 2 * count] = values[:, half:]
         across = jnp.transpose(jnp.broadcast_to(code, (count, 128)))[:16]
-        out_ref[count:] = jnp.zeros((16, total.shape[1]), jnp.int16)
-        out_ref[count:, :count] = across.astype(jnp.int32).astype(jnp.int16)
+        out_ref[2 * count :] = jnp.zeros((16, half), jnp.int16)
+        out_ref[2 * count :, :count] = across.astype(jnp.int32).astype(jnp.int16)
 
 
 def product(place, head, parts, offsets, before=(), send=False, cost=0):
     chosen = [parts[k] for k in offsets]
     tokens, width = chosen[0].shape[1], head.shape[1]
     out = (
-        jax.ShapeDtypeStruct((tokens + 16, width), jnp.int16)
+        jax.ShapeDtypeStruct((2 * tokens + 16, width // 2), jnp.int16)
         if send
         else jax.ShapeDtypeStruct((tokens, width), jnp.float32)
     )
@@ -247,9 +250,10 @@
 
 
 def join_kernel(kept_ref, back_ref, guided_ref, stats_ref):
-    codes = back_ref[256:, :256].astype(jnp.float32)[:1]
+    codes = back_ref[512:, :256].astype(jnp.float32)[:1]
     scale = jnp.transpose(jnp.broadcast_to(scale_of(codes), (128, 256)))[:, :1]
-    guided = kept_ref[...] + back_ref[:256].astype(jnp.float32) * scale
+    values = jnp.concatenate([back_ref[:256], back_ref[256:512]], 1)
+    guided = kept_ref[...] + values.astype(jnp.float32) * scale
     peak = jnp.max(guided, axis=1, keepdims=True)
     expo = jnp.exp(guided - peak)
     total = jnp.sum(expo, axis=1, keepdims=True)
@@ -302,13 +306,15 @@
     away_block = pack(away_line, (head,))
     away_parts = spread(away_block, "y", "x")
     away_sum = product(place, head, away_parts, (0,), cost=1)
-    home_near = near(hold(home, (*away_near[1:], away_sum)))
-    home_line = spread(stack(place, home_near, (away_block,)), "x", "y")
-    sent = product(place, head, away_parts, (1, 2, 3), (away_sum,), True, cost=1)
+    home_near = near(hold(home, away_near[1:]))
+    home_line = spread(stack(place, home_near, (away_block, away_sum)), "x", "y")
+    away_sum = product(place, head, away_parts, (1, 2), (away_sum,), cost=1)
+    sent = product(place, head, away_parts, (3,), (away_sum,), True, cost=1)
     back = lax.ppermute(sent, "zh", [(0, 1), (1, 0)])
     home_parts = spread(pack(home_line, (sent,)), "y", "x")
     kept = product(place, head, home_parts, (0,))
-    kept = product(place, head, home_parts, (1, 2, 3), (kept,))
+    kept = product(place, head, home_parts, (1, 2), (kept,))
+    kept = product(place, head, home_parts, (3,), (kept,))
 
     guided, stats = join(kept, back)
     stats = lax.all_to_all(stats, ("y", "x", "zl"), 0, 0, tiled=True)

time: 102 us -> 101 us (level)
  waiting for transfers between devices: 30.8 us -> 26.9 us
  Pallas kernels: 18.5 us -> 20 us
    ppermute x6, waiting for transfers between devices: 8.57 us -> 6.38 us  [shifted(): lax.ppermute(block, axis, pairs((axis,), lambda at: {axis: at[axis] + k}))]
    ppermute x12, waiting for transfers between devices: 12.8 us -> 11.1 us  [crossed(): return lax.ppermute(block, axes, pairs(axes, move))]
    all_to_all x1, starting transfers between devices: 9.43 us -> 7.81 us  [local(): stats = lax.all_to_all(stats, ('y', 'x', 'zl'), 0, 0, tiled=True)]
    pallas_call x4 -> x6, Pallas kernels: 11.9 us -> 13.4 us  [product(): pl.pallas_call(functools.partial(product_kernel, offsets, len(before) > 0...]
    ppermute x12, starting transfers between devices: 19 us -> 20.5 us  [crossed(): return lax.ppermute(block, axes, pairs(axes, move))]
  transfers between devices with their start and end apart: 22 -> 22, of which waited for: 9 -> 6; matrix products, arithmetic and copies ran while one was open for 0% -> 0% of each run, Pallas kernels for 16% -> 18%
where the time goes in v11:
time: 101 us; the launch traced here: 100 us
  starting transfers between devices  49 us (49%)
  waiting for transfers between devices  26.9 us (27%)
  Pallas kernels  20 us (20%)
  local copies, waits for them, and re-layouts  1.6 us (2%)
  other arithmetic  1.54 us (2%)
    ppermute x12, starting transfers between devices, crossed(): return lax.ppermute(block, axes, pairs(axes, move))  20.5 us
    pallas_call x6, Pallas kernels, product(): pl.pallas_call(functools.partial(product_kernel, offsets, len(before) > 0...  13.4 us
    ppermute x12, waiting for transfers between devices, crossed(): return lax.ppermute(block, axes, pairs(axes, move))  11.1 us
    all_to_all x1, waiting for transfers between devices, local(): stats = lax.all_to_all(stats, ('y', 'x', 'zl'), 0, 0, tiled=True)  9.39 us
    ppermute x6, starting transfers between devices, shifted(): lax.ppermute(block, axis, pairs((axis,), lambda at: {axis: at[axis] + k}))  8.98 us
    all_to_all x1, starting transfers between devices, local(): stats = lax.all_to_all(stats, ('y', 'x', 'zl'), 0, 0, tiled=True)  7.81 us
    ppermute x1, starting transfers between devices, local(): lax.ppermute(scale_index, ('zl', 'zh'), pairs(('zl', 'zh'), nearest_other))  6.39 us
    ppermute x6, waiting for transfers between devices, shifted(): lax.ppermute(block, axis, pairs((axis,), lambda at: {axis: at[axis] + k}))  6.38 us
  transfers between devices with their start and end apart: 22, of which 6 were waited for; matrix products, arithmetic and copies ran while one was open for 0% of the time, Pallas kernels for 18%

profile of v11, /device:TPU:2, one launch (start us, length us, event | category | flops | bytes accessed | tf_op | source)
XLA Modules:
  0.0 100.0 jit_solution(2576787192855828835)
XLA Ops:
  0.7 6.4 %collective-permute-start.1 = (s32[512]{0:T(512)}, s32[512]{0:T(512)S(1)}, u32[]{:S(2)}, u32[]{:S(2)}) collective-permute-start(s32[512]{0:T(512)} %param.6), channel_id=1, source_target_pairs={{0,5},{1,4},{2,7},{3,6},{4,1},{5,0},{6,3},{7,2},{8,13},{9,12},{10,... | collective-permute-start | bytes 6152 | tf_op jit(solution)/shard_map/ppermute | solution.py:291
  10.6 2.0 %collective-permute-start.3 = (s16[80,256]{1,0:T(8,128)(2,1)S(1)}, s16[80,256]{1,0:T(8,128)(2,1)S(1)}, u32[]{:S(2)}, u32[]{:S(2)}) collective-permute-start(s16[80,256]{1,0:T(8,128)(2,1)S(1)} %get-tuple-element.12.a_ref), channel_id=1, source_target_pairs={{0,4},{2,6},{4,0},{6,2},{1,5},{3,7},{5,1},{7,3},{8,12},{10,14},{12... | collective-permute-start | bytes 122888 | tf_op jit(solution)/shard_map/ppermute | solution.py:33
  12.6 1.4 %collective-permute-start.4 = (s16[80,256]{1,0:T(8,128)(2,1)S(1)}, s16[80,256]{1,0:T(8,128)(2,1)S(1)}, u32[]{:S(2)}, u32[]{:S(2)}) collective-permute-start(s16[80,256]{1,0:T(8,128)(2,1)S(1)} %get-tuple-element.12.a_ref), channel_id=1, source_target_pairs={{0,6},{2,0},{4,2},{6,4},{1,7},{3,1},{5,3},{7,5},{8,14},{10,8},{12,... | collective-permute-start | bytes 122888 | tf_op jit(solution)/shard_map/ppermute | solution.py:33
  14.0 1.9 %collective-permute-done.2.refs_0_.b_ref = s16[80,256]{1,0:T(8,128)(2,1)S(1)} collective-permute-done((s16[80,256]{1,0:T(8,128)(2,1)S(1)}, s16[80,256]{1,0:T(8,128)(2,1)S(1)}, u32[]{:S(2)}, u32[]{:S(2)}) %collective-permute-start.2) | collective-permute-done | bytes 40992 | tf_op jit(solution)/shard_map/ppermute | solution.py:33
  18.1 1.5 %collective-permute-start.8 = (s16[272,256]{1,0:T(8,128)(2,1)S(1)}, s16[272,256]{1,0:T(8,128)(2,1)S(1)}, u32[]{:S(2)}, u32[]{:S(2)}) collective-permute-start(s16[272,256]{1,0:T(8,128)(2,1)S(1)} %stack.2.refs_0_), channel_id=1, source_target_pairs={{0,8},{8,16},{16,24},{24,0},{32,40},{40,48},{48,56},{56,32},{64,72... | collective-permute-start | bytes 417800 | tf_op jit(solution)/shard_map/ppermute | solution.py:43
  19.5 3.3 %collective-permute-start.9 = (s16[272,256]{1,0:T(8,128)(2,1)S(1)}, s16[272,256]{1,0:T(8,128)(2,1)S(1)}, u32[]{:S(2)}, u32[]{:S(2)}) collective-permute-start(s16[272,256]{1,0:T(8,128)(2,1)S(1)} %stack.2.refs_0_), channel_id=1, source_target_pairs={{0,16},{8,24},{16,0},{24,8},{32,48},{40,56},{48,32},{56,40},{64,80... | collective-permute-start | bytes 417800 | tf_op jit(solution)/shard_map/ppermute | solution.py:43
  22.9 3.4 %load.3.refs_4_.head_ref = bf16[4096,1024]{1,0:T(8,128)(2,1)S(1)} custom-call(bf16[4096,1024]{1,0:T(8,128)(2,1)} %refs_0_), custom_call_target="tpu_custom_call" | custom-call | bytes 16777216 | tf_op jit(solution)/shard_map/load/pallas_call | solution.py:86
  26.4 1.7 %collective-permute-start.15 = (s16[1040,256]{1,0:T(8,128)(2,1)S(1)}, s16[1040,256]{1,0:T(8,128)(2,1)S(1)}, u32[]{:S(2)}, u32[]{:S(2)}) collective-permute-start(s16[1040,256]{1,0:T(8,128)(2,1)S(1)} %pack.2.refs_0_), channel_id=1, source_target_pairs={{0,32},{8,40},{16,48},{24,56},{32,64},{40,72},{48,80},{56,88},{64,... | collective-permute-start | bytes 1597448 | tf_op jit(solution)/shard_map/ppermute | solution.py:43
  28.0 2.9 %collective-permute-start.16 = (s16[1040,256]{1,0:T(8,128)(2,1)S(1)}, s16[1040,256]{1,0:T(8,128)(2,1)S(1)}, u32[]{:S(2)}, u32[]{:S(2)}) collective-permute-start(s16[1040,256]{1,0:T(8,128)(2,1)S(1)} %pack.2.refs_0_), channel_id=1, source_target_pairs={{0,64},{8,72},{16,80},{24,88},{32,96},{40,104},{48,112},{56,120},{... | collective-permute-start | bytes 1597448 | tf_op jit(solution)/shard_map/ppermute | solution.py:43
  33.5 2.3 %collective-permute-start.6 = (s16[80,256]{1,0:T(8,128)(2,1)S(1)}, s16[80,256]{1,0:T(8,128)(2,1)S(1)}, u32[]{:S(2)}, u32[]{:S(2)}) collective-permute-start(s16[80,256]{1,0:T(8,128)(2,1)S(1)} %hold.1.a_ref), channel_id=1, source_target_pairs={{0,4},{2,6},{4,0},{6,2},{1,5},{3,7},{5,1},{7,3},{8,12},{10,14},{12... | collective-permute-start | bytes 122888 | tf_op jit(solution)/shard_map/ppermute | solution.py:33
  35.7 2.4 %collective-permute-done.5.b_ref = s16[80,256]{1,0:T(8,128)(2,1)S(1)} collective-permute-done((s16[80,256]{1,0:T(8,128)(2,1)S(1)}, s16[80,256]{1,0:T(8,128)(2,1)S(1)}, u32[]{:S(2)}, u32[]{:S(2)}) %collective-permute-start.5) | collective-permute-done | bytes 40992 | tf_op jit(solution)/shard_map/ppermute | solution.py:33
  39.2 1.8 %product.6.refs_1_.refs_2_ = f32[256,1024]{1,0:T(8,128)S(1)} custom-call(s32[8]{0:T(128)S(1)} %compare_select_fusion.4.place_ref, bf16[4096,1024]{1,0:T(8,128)(2,1)S(1)} %load.3.refs_4_.head_ref, s16[1040,256]{1,0:T(8,128)(2,1)S(1)} %pack.2.refs_0_), custom_call_target="tpu_custom_call" | custom-call | flops 1073741824 | tf_op jit(solution)/shard_map/product/pallas_call | solution.py:238
  44.0 3.4 %collective-permute-start.12 = (s16[272,256]{1,0:T(8,128)(2,1)S(1)}, s16[272,256]{1,0:T(8,128)(2,1)S(1)}, u32[]{:S(2)}, u32[]{:S(2)}) collective-permute-start(s16[272,256]{1,0:T(8,128)(2,1)S(1)} %stack.3.refs_0_), channel_id=1, source_target_pairs={{0,16},{8,24},{16,0},{24,8},{32,48},{40,56},{48,32},{56,40},{64,80... | collective-permute-start | bytes 417800 | tf_op jit(solution)/shard_map/ppermute | solution.py:43
  48.5 2.9 %product.7.refs_1_ = f32[256,1024]{1,0:T(8,128)S(1)} custom-call(s32[8]{0:T(128)S(1)} %compare_select_fusion.4.place_ref, bf16[4096,1024]{1,0:T(8,128)(2,1)S(1)} %load.3.refs_4_.head_ref, s16[1040,256]{1,0:T(8,128)(2,1)S(1)} %collective-permute-done.15.refs_0_, s16[1040,256]{1,0:T(8,128)(2,1)S(1)} %collective-permute-done.16.refs_1_, ...), custom_call_target="tpu_custom_call" | custom-call | flops 2147483648 | tf_op jit(solution)/shard_map/product/pallas_call | solution.py:238
  51.4 2.1 %product.8.refs_4_ = s16[528,512]{1,0:T(8,128)(2,1)S(1)} custom-call(s32[8]{0:T(128)S(1)} %compare_select_fusion.4.place_ref, bf16[4096,1024]{1,0:T(8,128)(2,1)S(1)} %load.3.refs_4_.head_ref, s16[1040,256]{1,0:T(8,128)(2,1)S(1)} %collective-permute-done.14.refs_0_, f32[256,1024]{1,0:T(8,128)S(1)} %product.7.refs_1_), custom_call_target="tpu_custom_call" | custom-call | flops 1073741824 | tf_op jit(solution)/shard_map/product/pallas_call | solution.py:238
  53.5 5.3 %collective-permute-start.20 = (s16[528,512]{1,0:T(8,128)(2,1)S(1)}, s16[528,512]{1,0:T(8,128)(2,1)S(1)}, u32[]{:S(2)}, u32[]{:S(2)}) collective-permute-start(s16[528,512]{1,0:T(8,128)(2,1)S(1)} %product.8.refs_4_), channel_id=1, source_target_pairs={{0,1},{1,0},{2,3},{3,2},{4,5},{5,4},{6,7},{7,6},{8,9},{9,8},{10,11... | collective-permute-start | bytes 1622024 | tf_op jit(solution)/shard_map/ppermute | solution.py:313
  59.0 1.4 %collective-permute-start.19 = (s16[1040,256]{1,0:T(8,128)(2,1)S(1)}, s16[1040,256]{1,0:T(8,128)(2,1)S(1)}, u32[]{:S(2)}, u32[]{:S(2)}) collective-permute-start(s16[1040,256]{1,0:T(8,128)(2,1)S(1)} %pack.3.refs_0_), channel_id=1, source_target_pairs={{0,64},{8,72},{16,80},{24,88},{32,96},{40,104},{48,112},{56,120},{... | collective-permute-start | bytes 1597448 | tf_op jit(solution)/shard_map/ppermute | solution.py:43
  60.4 1.8 %collective-permute-start.17 = (s16[1040,256]{1,0:T(8,128)(2,1)S(1)}, s16[1040,256]{1,0:T(8,128)(2,1)S(1)}, u32[]{:S(2)}, u32[]{:S(2)}) collective-permute-start(s16[1040,256]{1,0:T(8,128)(2,1)S(1)} %pack.3.refs_0_), channel_id=1, source_target_pairs={{0,96},{8,104},{16,112},{24,120},{32,0},{40,8},{48,16},{56,24},{64... | collective-permute-start | bytes 1597448 | tf_op jit(solution)/shard_map/ppermute | solution.py:43
  62.2 1.8 %product.9.refs_2_ = f32[256,1024]{1,0:T(8,128)S(1)} custom-call(s32[8]{0:T(128)S(1)} %compare_select_fusion.4.place_ref, bf16[4096,1024]{1,0:T(8,128)(2,1)S(1)} %load.3.refs_4_.head_ref, s16[1040,256]{1,0:T(8,128)(2,1)S(1)} %pack.3.refs_0_), custom_call_target="tpu_custom_call" | custom-call | tf_op jit(solution)/shard_map/product/pallas_call | solution.py:238
  64.0 11.1 %collective-permute-done.18.refs_0_ = s16[1040,256]{1,0:T(8,128)(2,1)S(1)} collective-permute-done((s16[1040,256]{1,0:T(8,128)(2,1)S(1)}, s16[1040,256]{1,0:T(8,128)(2,1)S(1)}, u32[]{:S(2)}, u32[]{:S(2)}) %collective-permute-start.18) | collective-permute-done | bytes 532512 | tf_op jit(solution)/shard_map/ppermute | solution.py:43
  75.1 2.9 %product.10.refs_1_ = f32[256,1024]{1,0:T(8,128)S(1)} custom-call(s32[8]{0:T(128)S(1)} %compare_select_fusion.4.place_ref, bf16[4096,1024]{1,0:T(8,128)(2,1)S(1)} %load.3.refs_4_.head_ref, s16[1040,256]{1,0:T(8,128)(2,1)S(1)} %collective-permute-done.18.refs_0_, s16[1040,256]{1,0:T(8,128)(2,1)S(1)} %collective-permute-done.19.refs_1_, ...), custom_call_target="tpu_custom_call" | custom-call | tf_op jit(solution)/shard_map/product/pallas_call | solution.py:238
  78.1 1.8 %product.11.kept_ref = f32[256,1024]{1,0:T(8,128)S(1)} custom-call(s32[8]{0:T(128)S(1)} %compare_select_fusion.4.place_ref, bf16[4096,1024]{1,0:T(8,128)(2,1)S(1)} %load.3.refs_4_.head_ref, s16[1040,256]{1,0:T(8,128)(2,1)S(1)} %collective-permute-done.17.refs_0_, f32[256,1024]{1,0:T(8,128)S(1)} %product.10.refs_1_), custom_call_target="tpu_custom_call" | custom-call | tf_op jit(solution)/shard_map/product/pallas_call | solution.py:238
  81.2 7.8 %all-to-all-start = ((f32[64,4,128]{2,1,0:T(4,128)}), f32[64,4,128]{2,1,0:T(4,128)S(1)}, u32[]{:S(2)}, u32[]{:S(2)}) async-start(f32[64,4,128]{2,1,0:T(4,128)} %get-tuple-element.16), calls=%async_computation | async-start | bytes 262144 | tf_op jit(solution)/shard_map/all_to_all | solution.py:320
  89.1 9.4 %all-to-all-done = f32[64,4,128]{2,1,0:T(4,128)S(1)} async-done(((f32[64,4,128]{2,1,0:T(4,128)}), f32[64,4,128]{2,1,0:T(4,128)S(1)}, u32[]{:S(2)}, u32[]{:S(2)}) %all-to-all-start) | async-done | bytes 131104 | tf_op jit(solution)/shard_map/all_to_all | solution.py:320
  (49 shorter events, 16.6 us)
Async XLA Ops:
  0.6 8.3 %collective-permute-start = (bf16[64,1024]{1,0:T(8,128)(2,1)}, bf16[64,1024]{1,0:T(8,128)(2,1)S(1)}, u32[]{:S(2)}, u32[]{:S(2)}) collective-permute-start(bf16[64,1024]{1,0:T(8,128)(2,1)} %bitcast.10), channel_id=1, source_target_pairs={{0,128},{128,0},{1,129},{129,1},{2,130},{130,2},{3,131},{131,3},{4... | collective-permute-start | bytes 393224 | tf_op jit(solution)/shard_map/ppermute | solution.py:290
  0.7 8.2 %collective-permute-start.1 = (s32[512]{0:T(512)}, s32[512]{0:T(512)S(1)}, u32[]{:S(2)}, u32[]{:S(2)}) collective-permute-start(s32[512]{0:T(512)} %param.6), channel_id=1, source_target_pairs={{0,5},{1,4},{2,7},{3,6},{4,1},{5,0},{6,3},{7,2},{8,13},{9,12},{10,... | collective-permute-start | bytes 6152 | tf_op jit(solution)/shard_map/ppermute | solution.py:291
  9.5 6.3 %collective-permute-start.2 = (s16[80,256]{1,0:T(8,128)(2,1)S(1)}, s16[80,256]{1,0:T(8,128)(2,1)S(1)}, u32[]{:S(2)}, u32[]{:S(2)}) collective-permute-start(s16[80,256]{1,0:T(8,128)(2,1)S(1)} %get-tuple-element.12.a_ref), channel_id=1, source_target_pairs={{0,2},{2,4},{4,6},{6,0},{1,3},{3,5},{5,7},{7,1},{8,10},{10,12},{12... | collective-permute-start | bytes 122888 | tf_op jit(solution)/shard_map/ppermute | solution.py:33
  10.6 6.3 %collective-permute-start.3 = (s16[80,256]{1,0:T(8,128)(2,1)S(1)}, s16[80,256]{1,0:T(8,128)(2,1)S(1)}, u32[]{:S(2)}, u32[]{:S(2)}) collective-permute-start(s16[80,256]{1,0:T(8,128)(2,1)S(1)} %get-tuple-element.12.a_ref), channel_id=1, source_target_pairs={{0,4},{2,6},{4,0},{6,2},{1,5},{3,7},{5,1},{7,3},{8,12},{10,14},{12... | collective-permute-start | bytes 122888 | tf_op jit(solution)/shard_map/ppermute | solution.py:33
  12.6 4.3 %collective-permute-start.4 = (s16[80,256]{1,0:T(8,128)(2,1)S(1)}, s16[80,256]{1,0:T(8,128)(2,1)S(1)}, u32[]{:S(2)}, u32[]{:S(2)}) collective-permute-start(s16[80,256]{1,0:T(8,128)(2,1)S(1)} %get-tuple-element.12.a_ref), channel_id=1, source_target_pairs={{0,6},{2,0},{4,2},{6,4},{1,7},{3,1},{5,3},{7,5},{8,14},{10,8},{12,... | collective-permute-start | bytes 122888 | tf_op jit(solution)/shard_map/ppermute | solution.py:33
  17.4 8.8 %collective-permute-start.10 = (s16[272,256]{1,0:T(8,128)(2,1)S(1)}, s16[272,256]{1,0:T(8,128)(2,1)S(1)}, u32[]{:S(2)}, u32[]{:S(2)}) collective-permute-start(s16[272,256]{1,0:T(8,128)(2,1)S(1)} %stack.2.refs_0_), channel_id=1, source_target_pairs={{0,24},{8,0},{16,8},{24,16},{32,56},{40,32},{48,40},{56,48},{64,88... | collective-permute-start | bytes 417800 | tf_op jit(solution)/shard_map/ppermute | solution.py:43
  18.1 8.2 %collective-permute-start.8 = (s16[272,256]{1,0:T(8,128)(2,1)S(1)}, s16[272,256]{1,0:T(8,128)(2,1)S(1)}, u32[]{:S(2)}, u32[]{:S(2)}) collective-permute-start(s16[272,256]{1,0:T(8,128)(2,1)S(1)} %stack.2.refs_0_), channel_id=1, source_target_pairs={{0,8},{8,16},{16,24},{24,0},{32,40},{40,48},{48,56},{56,32},{64,72... | collective-permute-start | bytes 417800 | tf_op jit(solution)/shard_map/ppermute | solution.py:43
  19.5 6.8 %collective-permute-start.9 = (s16[272,256]{1,0:T(8,128)(2,1)S(1)}, s16[272,256]{1,0:T(8,128)(2,1)S(1)}, u32[]{:S(2)}, u32[]{:S(2)}) collective-permute-start(s16[272,256]{1,0:T(8,128)(2,1)S(1)} %stack.2.refs_0_), channel_id=1, source_target_pairs={{0,16},{8,24},{16,0},{24,8},{32,48},{40,56},{48,32},{56,40},{64,80... | collective-permute-start | bytes 417800 | tf_op jit(solution)/shard_map/ppermute | solution.py:43
  26.4 21.0 %collective-permute-start.15 = (s16[1040,256]{1,0:T(8,128)(2,1)S(1)}, s16[1040,256]{1,0:T(8,128)(2,1)S(1)}, u32[]{:S(2)}, u32[]{:S(2)}) collective-permute-start(s16[1040,256]{1,0:T(8,128)(2,1)S(1)} %pack.2.refs_0_), channel_id=1, source_target_pairs={{0,32},{8,40},{16,48},{24,56},{32,64},{40,72},{48,80},{56,88},{64,... | collective-permute-start | bytes 1597448 | tf_op jit(solution)/shard_map/ppermute | solution.py:43
  28.0 20.5 %collective-permute-start.16 = (s16[1040,256]{1,0:T(8,128)(2,1)S(1)}, s16[1040,256]{1,0:T(8,128)(2,1)S(1)}, u32[]{:S(2)}, u32[]{:S(2)}) collective-permute-start(s16[1040,256]{1,0:T(8,128)(2,1)S(1)} %pack.2.refs_0_), channel_id=1, source_target_pairs={{0,64},{8,72},{16,80},{24,88},{32,96},{40,104},{48,112},{56,120},{... | collective-permute-start | bytes 1597448 | tf_op jit(solution)/shard_map/ppermute | solution.py:43
  30.9 20.5 %collective-permute-start.14 = (s16[1040,256]{1,0:T(8,128)(2,1)S(1)}, s16[1040,256]{1,0:T(8,128)(2,1)S(1)}, u32[]{:S(2)}, u32[]{:S(2)}) collective-permute-start(s16[1040,256]{1,0:T(8,128)(2,1)S(1)} %pack.2.refs_0_), channel_id=1, source_target_pairs={{0,96},{8,104},{16,112},{24,120},{32,0},{40,8},{48,16},{56,24},{64... | collective-permute-start | bytes 1597448 | tf_op jit(solution)/shard_map/ppermute | solution.py:43
  32.3 5.8 %collective-permute-start.5 = (s16[80,256]{1,0:T(8,128)(2,1)S(1)}, s16[80,256]{1,0:T(8,128)(2,1)S(1)}, u32[]{:S(2)}, u32[]{:S(2)}) collective-permute-start(s16[80,256]{1,0:T(8,128)(2,1)S(1)} %hold.1.a_ref), channel_id=1, source_target_pairs={{0,2},{2,4},{4,6},{6,0},{1,3},{3,5},{5,7},{7,1},{8,10},{10,12},{12... | collective-permute-start | bytes 122888 | tf_op jit(solution)/shard_map/ppermute | solution.py:33
  33.5 7.6 %collective-permute-start.6 = (s16[80,256]{1,0:T(8,128)(2,1)S(1)}, s16[80,256]{1,0:T(8,128)(2,1)S(1)}, u32[]{:S(2)}, u32[]{:S(2)}) collective-permute-start(s16[80,256]{1,0:T(8,128)(2,1)S(1)} %hold.1.a_ref), channel_id=1, source_target_pairs={{0,4},{2,6},{4,0},{6,2},{1,5},{3,7},{5,1},{7,3},{8,12},{10,14},{12... | collective-permute-start | bytes 122888 | tf_op jit(solution)/shard_map/ppermute | solution.py:33
  38.1 4.0 %collective-permute-start.7 = (s16[80,256]{1,0:T(8,128)(2,1)S(1)}, s16[80,256]{1,0:T(8,128)(2,1)S(1)}, u32[]{:S(2)}, u32[]{:S(2)}) collective-permute-start(s16[80,256]{1,0:T(8,128)(2,1)S(1)} %hold.1.a_ref), channel_id=1, source_target_pairs={{0,6},{2,0},{4,2},{6,4},{1,7},{3,1},{5,3},{7,5},{8,14},{10,8},{12,... | collective-permute-start | bytes 122888 | tf_op jit(solution)/shard_map/ppermute | solution.py:33
  42.7 16.1 %collective-permute-start.11 = (s16[272,256]{1,0:T(8,128)(2,1)S(1)}, s16[272,256]{1,0:T(8,128)(2,1)S(1)}, u32[]{:S(2)}, u32[]{:S(2)}) collective-permute-start(s16[272,256]{1,0:T(8,128)(2,1)S(1)} %stack.3.refs_0_), channel_id=1, source_target_pairs={{0,8},{8,16},{16,24},{24,0},{32,40},{40,48},{48,56},{56,32},{64,72... | collective-permute-start | bytes 417800 | tf_op jit(solution)/shard_map/ppermute | solution.py:43
  44.0 14.8 %collective-permute-start.12 = (s16[272,256]{1,0:T(8,128)(2,1)S(1)}, s16[272,256]{1,0:T(8,128)(2,1)S(1)}, u32[]{:S(2)}, u32[]{:S(2)}) collective-permute-start(s16[272,256]{1,0:T(8,128)(2,1)S(1)} %stack.3.refs_0_), channel_id=1, source_target_pairs={{0,16},{8,24},{16,0},{24,8},{32,48},{40,56},{48,32},{56,40},{64,80... | collective-permute-start | bytes 417800 | tf_op jit(solution)/shard_map/ppermute | solution.py:43
  47.4 11.4 %collective-permute-start.13 = (s16[272,256]{1,0:T(8,128)(2,1)S(1)}, s16[272,256]{1,0:T(8,128)(2,1)S(1)}, u32[]{:S(2)}, u32[]{:S(2)}) collective-permute-start(s16[272,256]{1,0:T(8,128)(2,1)S(1)} %stack.3.refs_0_), channel_id=1, source_target_pairs={{0,24},{8,0},{16,8},{24,16},{32,56},{40,32},{48,40},{56,48},{64,88... | collective-permute-start | bytes 417800 | tf_op jit(solution)/shard_map/ppermute | solution.py:43
  53.5 26.4 %collective-permute-start.20 = (s16[528,512]{1,0:T(8,128)(2,1)S(1)}, s16[528,512]{1,0:T(8,128)(2,1)S(1)}, u32[]{:S(2)}, u32[]{:S(2)}) collective-permute-start(s16[528,512]{1,0:T(8,128)(2,1)S(1)} %product.8.refs_4_), channel_id=1, source_target_pairs={{0,1},{1,0},{2,3},{3,2},{4,5},{5,4},{6,7},{7,6},{8,9},{9,8},{10,11... | collective-permute-start | bytes 1622024 | tf_op jit(solution)/shard_map/ppermute | solution.py:313
  58.9 16.3 %collective-permute-start.18 = (s16[1040,256]{1,0:T(8,128)(2,1)S(1)}, s16[1040,256]{1,0:T(8,128)(2,1)S(1)}, u32[]{:S(2)}, u32[]{:S(2)}) collective-permute-start(s16[1040,256]{1,0:T(8,128)(2,1)S(1)} %pack.3.refs_0_), channel_id=1, source_target_pairs={{0,32},{8,40},{16,48},{24,56},{32,64},{40,72},{48,80},{56,88},{64,... | collective-permute-start | bytes 1597448 | tf_op jit(solution)/shard_map/ppermute | solution.py:43
  59.0 16.1 %collective-permute-start.19 = (s16[1040,256]{1,0:T(8,128)(2,1)S(1)}, s16[1040,256]{1,0:T(8,128)(2,1)S(1)}, u32[]{:S(2)}, u32[]{:S(2)}) collective-permute-start(s16[1040,256]{1,0:T(8,128)(2,1)S(1)} %pack.3.refs_0_), channel_id=1, source_target_pairs={{0,64},{8,72},{16,80},{24,88},{32,96},{40,104},{48,112},{56,120},{... | collective-permute-start | bytes 1597448 | tf_op jit(solution)/shard_map/ppermute | solution.py:43
  60.4 17.7 %collective-permute-start.17 = (s16[1040,256]{1,0:T(8,128)(2,1)S(1)}, s16[1040,256]{1,0:T(8,128)(2,1)S(1)}, u32[]{:S(2)}, u32[]{:S(2)}) collective-permute-start(s16[1040,256]{1,0:T(8,128)(2,1)S(1)} %pack.3.refs_0_), channel_id=1, source_target_pairs={{0,96},{8,104},{16,112},{24,120},{32,0},{40,8},{48,16},{56,24},{64... | collective-permute-start | bytes 1597448 | tf_op jit(solution)/shard_map/ppermute | solution.py:43
  78.1 11.0 %copy-start.3 = (s32[512]{0:T(512)S(1)}, s32[512]{0:T(512)}, u32[]{:S(2)}) copy-start(s32[512]{0:T(512)} %param.7) | copy-start | bytes 6148
  81.2 17.3 %all-to-all-start = ((f32[64,4,128]{2,1,0:T(4,128)}), f32[64,4,128]{2,1,0:T(4,128)S(1)}, u32[]{:S(2)}, u32[]{:S(2)}) async-start(f32[64,4,128]{2,1,0:T(4,128)} %get-tuple-element.16), calls=%async_computation | async-start | bytes 262144 | tf_op jit(solution)/shard_map/all_to_all | solution.py:320
  98.7 1.3 %copy-start.2 = (f32[256]{0:T(256)}, f32[256]{0:T(256)S(1)}, u32[]{:S(2)}) copy-start(f32[256]{0:T(256)S(1)} %get-tuple-element.19) | copy-start | bytes 3076
  (2 other events, 1.6 us)

commit v12 on v11

--- a/solution.py
+++ b/solution.py
@@ -302,11 +302,11 @@
         return [block] + [crossed(block, first, second, k) for k in (1, 2, 3)]
 
     away_near = near(away)
-    away_line = spread(stack(place, away_near, ()), "x", "y")
-    away_block = pack(away_line, (head,))
+    home_near = near(hold(home, away_near[1:]))
+    away_line = spread(stack(place, away_near, (head,)), "x", "y")
+    away_block = pack(away_line, (home_near[1],))
     away_parts = spread(away_block, "y", "x")
     away_sum = product(place, head, away_parts, (0,), cost=1)
-    home_near = near(hold(home, away_near[1:]))
     home_line = spread(stack(place, home_near, (away_block, away_sum)), "x", "y")
     away_sum = product(place, head, away_parts, (1, 2), (away_sum,), cost=1)
     sent = product(place, head, away_parts, (3,), (away_sum,), True, cost=1)

time: 101 us -> 100 us (0.990)
  starting transfers between devices: 49 us -> 43.4 us
  waiting for transfers between devices: 26.9 us -> 31.8 us
    ppermute x12, waiting for transfers between devices: 11.1 us -> 15.4 us  [crossed(): return lax.ppermute(block, axes, pairs(axes, move))]
    ppermute x6, starting transfers between devices: 8.98 us -> 6.34 us  [shifted(): lax.ppermute(block, axis, pairs((axis,), lambda at: {axis: at[axis] + k}))]
    all_to_all x1, starting transfers between devices: 7.81 us -> 5.96 us  [local(): stats = lax.all_to_all(stats, ('y', 'x', 'zl'), 0, 0, tiled=True)]
  transfers between devices with their start and end apart: 22 -> 22, of which waited for: 6 -> 5; matrix products, arithmetic and copies ran while one was open for 0% -> 0% of each run, Pallas kernels for 18% -> 18%
where the time goes in v12:
time: 100 us; the launch traced here: 99.2 us
  starting transfers between devices  43.4 us (43%)
  waiting for transfers between devices  31.8 us (32%)
  Pallas kernels  20 us (20%)
  local copies, waits for them, and re-layouts  1.6 us (2%)
  other arithmetic  1.54 us (2%)
    ppermute x12, starting transfers between devices, crossed(): return lax.ppermute(block, axes, pairs(axes, move))  19.5 us
    ppermute x12, waiting for transfers between devices, crossed(): return lax.ppermute(block, axes, pairs(axes, move))  15.4 us
    pallas_call x6, Pallas kernels, product(): pl.pallas_call(functools.partial(product_kernel, offsets, len(before) > 0...  13.4 us
    all_to_all x1, waiting for transfers between devices, local(): stats = lax.all_to_all(stats, ('y', 'x', 'zl'), 0, 0, tiled=True)  9.39 us
    ppermute x6, waiting for transfers between devices, shifted(): lax.ppermute(block, axis, pairs((axis,), lambda at: {axis: at[axis] + k}))  7 us
    ppermute x1, starting transfers between devices, local(): lax.ppermute(scale_index, ('zl', 'zh'), pairs(('zl', 'zh'), nearest_other))  6.39 us
    ppermute x6, starting transfers between devices, shifted(): lax.ppermute(block, axis, pairs((axis,), lambda at: {axis: at[axis] + k}))  6.34 us
    all_to_all x1, starting transfers between devices, local(): stats = lax.all_to_all(stats, ('y', 'x', 'zl'), 0, 0, tiled=True)  5.96 us
  transfers between devices with their start and end apart: 22, of which 5 were waited for; matrix products, arithmetic and copies ran while one was open for 0% of the time, Pallas kernels for 18%

profile of v12, /device:TPU:2, one launch (start us, length us, event | category | flops | bytes accessed | tf_op | source)
XLA Modules:
  0.0 99.2 jit_solution(9192882594125355284)
XLA Ops:
  0.7 6.4 %collective-permute-start.1 = (s32[512]{0:T(512)}, s32[512]{0:T(512)S(1)}, u32[]{:S(2)}, u32[]{:S(2)}) collective-permute-start(s32[512]{0:T(512)} %param.6), channel_id=1, source_target_pairs={{0,5},{1,4},{2,7},{3,6},{4,1},{5,0},{6,3},{7,2},{8,13},{9,12},{10,... | collective-permute-start | bytes 6152 | tf_op jit(solution)/shard_map/ppermute | solution.py:291
  10.6 2.0 %collective-permute-start.3 = (s16[80,256]{1,0:T(8,128)(2,1)S(1)}, s16[80,256]{1,0:T(8,128)(2,1)S(1)}, u32[]{:S(2)}, u32[]{:S(2)}) collective-permute-start(s16[80,256]{1,0:T(8,128)(2,1)S(1)} %get-tuple-element.12.a_ref), channel_id=1, source_target_pairs={{0,4},{2,6},{4,0},{6,2},{1,5},{3,7},{5,1},{7,3},{8,12},{10,14},{12... | collective-permute-start | bytes 122888 | tf_op jit(solution)/shard_map/ppermute | solution.py:33
  12.6 1.4 %collective-permute-start.4 = (s16[80,256]{1,0:T(8,128)(2,1)S(1)}, s16[80,256]{1,0:T(8,128)(2,1)S(1)}, u32[]{:S(2)}, u32[]{:S(2)}) collective-permute-start(s16[80,256]{1,0:T(8,128)(2,1)S(1)} %get-tuple-element.12.a_ref), channel_id=1, source_target_pairs={{0,6},{2,0},{4,2},{6,4},{1,7},{3,1},{5,3},{7,5},{8,14},{10,8},{12,... | collective-permute-start | bytes 122888 | tf_op jit(solution)/shard_map/ppermute | solution.py:33
  14.0 3.4 %load.3.refs_0_.head_ref = bf16[4096,1024]{1,0:T(8,128)(2,1)S(1)} custom-call(bf16[4096,1024]{1,0:T(8,128)(2,1)} %refs_0_), custom_call_target="tpu_custom_call" | custom-call | bytes 16777216 | tf_op jit(solution)/shard_map/load/pallas_call | solution.py:86
  18.6 1.5 %collective-permute-start.8 = (s16[272,256]{1,0:T(8,128)(2,1)S(1)}, s16[272,256]{1,0:T(8,128)(2,1)S(1)}, u32[]{:S(2)}, u32[]{:S(2)}) collective-permute-start(s16[272,256]{1,0:T(8,128)(2,1)S(1)} %stack.2.refs_0_), channel_id=1, source_target_pairs={{0,8},{8,16},{16,24},{24,0},{32,40},{40,48},{48,56},{56,32},{64,72... | collective-permute-start | bytes 417800 | tf_op jit(solution)/shard_map/ppermute | solution.py:43
  20.1 3.3 %collective-permute-start.9 = (s16[272,256]{1,0:T(8,128)(2,1)S(1)}, s16[272,256]{1,0:T(8,128)(2,1)S(1)}, u32[]{:S(2)}, u32[]{:S(2)}) collective-permute-start(s16[272,256]{1,0:T(8,128)(2,1)S(1)} %stack.2.refs_0_), channel_id=1, source_target_pairs={{0,16},{8,24},{16,0},{24,8},{32,48},{40,56},{48,32},{56,40},{64,80... | collective-permute-start | bytes 417800 | tf_op jit(solution)/shard_map/ppermute | solution.py:43
  24.1 5.1 %collective-permute-done.5.refs_4_.b_ref = s16[80,256]{1,0:T(8,128)(2,1)S(1)} collective-permute-done((s16[80,256]{1,0:T(8,128)(2,1)S(1)}, s16[80,256]{1,0:T(8,128)(2,1)S(1)}, u32[]{:S(2)}, u32[]{:S(2)}) %collective-permute-start.5) | collective-permute-done | bytes 40992 | tf_op jit(solution)/shard_map/ppermute | solution.py:33
  29.3 1.7 %collective-permute-start.15 = (s16[1040,256]{1,0:T(8,128)(2,1)S(1)}, s16[1040,256]{1,0:T(8,128)(2,1)S(1)}, u32[]{:S(2)}, u32[]{:S(2)}) collective-permute-start(s16[1040,256]{1,0:T(8,128)(2,1)S(1)} %pack.2.refs_0_), channel_id=1, source_target_pairs={{0,32},{8,40},{16,48},{24,56},{32,64},{40,72},{48,80},{56,88},{64,... | collective-permute-start | bytes 1597448 | tf_op jit(solution)/shard_map/ppermute | solution.py:43
  30.9 2.9 %collective-permute-start.16 = (s16[1040,256]{1,0:T(8,128)(2,1)S(1)}, s16[1040,256]{1,0:T(8,128)(2,1)S(1)}, u32[]{:S(2)}, u32[]{:S(2)}) collective-permute-start(s16[1040,256]{1,0:T(8,128)(2,1)S(1)} %pack.2.refs_0_), channel_id=1, source_target_pairs={{0,64},{8,72},{16,80},{24,88},{32,96},{40,104},{48,112},{56,120},{... | collective-permute-start | bytes 1597448 | tf_op jit(solution)/shard_map/ppermute | solution.py:43
  33.8 1.3 %collective-permute-start.14 = (s16[1040,256]{1,0:T(8,128)(2,1)S(1)}, s16[1040,256]{1,0:T(8,128)(2,1)S(1)}, u32[]{:S(2)}, u32[]{:S(2)}) collective-permute-start(s16[1040,256]{1,0:T(8,128)(2,1)S(1)} %pack.2.refs_0_), channel_id=1, source_target_pairs={{0,96},{8,104},{16,112},{24,120},{32,0},{40,8},{48,16},{56,24},{64... | collective-permute-start | bytes 1597448 | tf_op jit(solution)/shard_map/ppermute | solution.py:43
  36.4 1.8 %product.6.refs_1_.refs_2_ = f32[256,1024]{1,0:T(8,128)S(1)} custom-call(s32[8]{0:T(128)S(1)} %compare_select_fusion.4.place_ref, bf16[4096,1024]{1,0:T(8,128)(2,1)S(1)} %load.3.refs_0_.head_ref, s16[1040,256]{1,0:T(8,128)(2,1)S(1)} %pack.2.refs_0_), custom_call_target="tpu_custom_call" | custom-call | flops 1073741824 | tf_op jit(solution)/shard_map/product/pallas_call | solution.py:238
  38.2 1.9 %collective-permute-done.6.c_ref = s16[80,256]{1,0:T(8,128)(2,1)S(1)} collective-permute-done((s16[80,256]{1,0:T(8,128)(2,1)S(1)}, s16[80,256]{1,0:T(8,128)(2,1)S(1)}, u32[]{:S(2)}, u32[]{:S(2)}) %collective-permute-start.6) | collective-permute-done | bytes 40992 | tf_op jit(solution)/shard_map/ppermute | solution.py:33
  40.8 3.1 %collective-permute-start.12 = (s16[272,256]{1,0:T(8,128)(2,1)S(1)}, s16[272,256]{1,0:T(8,128)(2,1)S(1)}, u32[]{:S(2)}, u32[]{:S(2)}) collective-permute-start(s16[272,256]{1,0:T(8,128)(2,1)S(1)} %stack.3.refs_0_), channel_id=1, source_target_pairs={{0,16},{8,24},{16,0},{24,8},{32,48},{40,56},{48,32},{56,40},{64,80... | collective-permute-start | bytes 417800 | tf_op jit(solution)/shard_map/ppermute | solution.py:43
  44.9 4.9 %collective-permute-done.16.refs_1_ = s16[1040,256]{1,0:T(8,128)(2,1)S(1)} collective-permute-done((s16[1040,256]{1,0:T(8,128)(2,1)S(1)}, s16[1040,256]{1,0:T(8,128)(2,1)S(1)}, u32[]{:S(2)}, u32[]{:S(2)}) %collective-permute-start.16) | collective-permute-done | bytes 532512 | tf_op jit(solution)/shard_map/ppermute | solution.py:43
  49.8 2.9 %product.7.refs_1_ = f32[256,1024]{1,0:T(8,128)S(1)} custom-call(s32[8]{0:T(128)S(1)} %compare_select_fusion.4.place_ref, bf16[4096,1024]{1,0:T(8,128)(2,1)S(1)} %load.3.refs_0_.head_ref, s16[1040,256]{1,0:T(8,128)(2,1)S(1)} %collective-permute-done.15.refs_0_, s16[1040,256]{1,0:T(8,128)(2,1)S(1)} %collective-permute-done.16.refs_1_, ...), custom_call_target="tpu_custom_call" | custom-call | flops 2147483648 | tf_op jit(solution)/shard_map/product/pallas_call | solution.py:238
  52.7 2.1 %product.8.refs_4_ = s16[528,512]{1,0:T(8,128)(2,1)S(1)} custom-call(s32[8]{0:T(128)S(1)} %compare_select_fusion.4.place_ref, bf16[4096,1024]{1,0:T(8,128)(2,1)S(1)} %load.3.refs_0_.head_ref, s16[1040,256]{1,0:T(8,128)(2,1)S(1)} %collective-permute-done.14.refs_0_, f32[256,1024]{1,0:T(8,128)S(1)} %product.7.refs_1_), custom_call_target="tpu_custom_call" | custom-call | flops 1073741824 | tf_op jit(solution)/shard_map/product/pallas_call | solution.py:238
  54.8 5.1 %collective-permute-start.20 = (s16[528,512]{1,0:T(8,128)(2,1)S(1)}, s16[528,512]{1,0:T(8,128)(2,1)S(1)}, u32[]{:S(2)}, u32[]{:S(2)}) collective-permute-start(s16[528,512]{1,0:T(8,128)(2,1)S(1)} %product.8.refs_4_), channel_id=1, source_target_pairs={{0,1},{1,0},{2,3},{3,2},{4,5},{5,4},{6,7},{7,6},{8,9},{9,8},{10,11... | collective-permute-start | bytes 1622024 | tf_op jit(solution)/shard_map/ppermute | solution.py:313
  61.4 2.5 %collective-permute-start.17 = (s16[1040,256]{1,0:T(8,128)(2,1)S(1)}, s16[1040,256]{1,0:T(8,128)(2,1)S(1)}, u32[]{:S(2)}, u32[]{:S(2)}) collective-permute-start(s16[1040,256]{1,0:T(8,128)(2,1)S(1)} %pack.3.refs_0_), channel_id=1, source_target_pairs={{0,96},{8,104},{16,112},{24,120},{32,0},{40,8},{48,16},{56,24},{64... | collective-permute-start | bytes 1597448 | tf_op jit(solution)/shard_map/ppermute | solution.py:43
  63.9 1.8 %product.9.refs_2_ = f32[256,1024]{1,0:T(8,128)S(1)} custom-call(s32[8]{0:T(128)S(1)} %compare_select_fusion.4.place_ref, bf16[4096,1024]{1,0:T(8,128)(2,1)S(1)} %load.3.refs_0_.head_ref, s16[1040,256]{1,0:T(8,128)(2,1)S(1)} %pack.3.refs_0_), custom_call_target="tpu_custom_call" | custom-call | tf_op jit(solution)/shard_map/product/pallas_call | solution.py:238
  65.7 10.5 %collective-permute-done.18.refs_0_ = s16[1040,256]{1,0:T(8,128)(2,1)S(1)} collective-permute-done((s16[1040,256]{1,0:T(8,128)(2,1)S(1)}, s16[1040,256]{1,0:T(8,128)(2,1)S(1)}, u32[]{:S(2)}, u32[]{:S(2)}) %collective-permute-start.18) | collective-permute-done | bytes 532512 | tf_op jit(solution)/shard_map/ppermute | solution.py:43
  76.2 2.9 %product.10.refs_1_ = f32[256,1024]{1,0:T(8,128)S(1)} custom-call(s32[8]{0:T(128)S(1)} %compare_select_fusion.4.place_ref, bf16[4096,1024]{1,0:T(8,128)(2,1)S(1)} %load.3.refs_0_.head_ref, s16[1040,256]{1,0:T(8,128)(2,1)S(1)} %collective-permute-done.18.refs_0_, s16[1040,256]{1,0:T(8,128)(2,1)S(1)} %collective-permute-done.19.refs_1_, ...), custom_call_target="tpu_custom_call" | custom-call | tf_op jit(solution)/shard_map/product/pallas_call | solution.py:238
  79.2 1.8 %product.11.kept_ref = f32[256,1024]{1,0:T(8,128)S(1)} custom-call(s32[8]{0:T(128)S(1)} %compare_select_fusion.4.place_ref, bf16[4096,1024]{1,0:T(8,128)(2,1)S(1)} %load.3.refs_0_.head_ref, s16[1040,256]{1,0:T(8,128)(2,1)S(1)} %collective-permute-done.17.refs_0_, f32[256,1024]{1,0:T(8,128)S(1)} %product.10.refs_1_), custom_call_target="tpu_custom_call" | custom-call | tf_op jit(solution)/shard_map/product/pallas_call | solution.py:238
  82.3 6.0 %all-to-all-start = ((f32[64,4,128]{2,1,0:T(4,128)}), f32[64,4,128]{2,1,0:T(4,128)S(1)}, u32[]{:S(2)}, u32[]{:S(2)}) async-start(f32[64,4,128]{2,1,0:T(4,128)} %get-tuple-element.16), calls=%async_computation | async-start | bytes 262144 | tf_op jit(solution)/shard_map/all_to_all | solution.py:320
  88.4 9.4 %all-to-all-done = f32[64,4,128]{2,1,0:T(4,128)S(1)} async-done(((f32[64,4,128]{2,1,0:T(4,128)}), f32[64,4,128]{2,1,0:T(4,128)S(1)}, u32[]{:S(2)}, u32[]{:S(2)}) %all-to-all-start) | async-done | bytes 131104 | tf_op jit(solution)/shard_map/all_to_all | solution.py:320
  (49 shorter events, 12.7 us)
Async XLA Ops:
  0.6 8.3 %collective-permute-start = (bf16[64,1024]{1,0:T(8,128)(2,1)}, bf16[64,1024]{1,0:T(8,128)(2,1)S(1)}, u32[]{:S(2)}, u32[]{:S(2)}) collective-permute-start(bf16[64,1024]{1,0:T(8,128)(2,1)} %bitcast.10), channel_id=1, source_target_pairs={{0,128},{128,0},{1,129},{129,1},{2,130},{130,2},{3,131},{131,3},{4... | collective-permute-start | bytes 393224 | tf_op jit(solution)/shard_map/ppermute | solution.py:290
  0.7 8.2 %collective-permute-start.1 = (s32[512]{0:T(512)}, s32[512]{0:T(512)S(1)}, u32[]{:S(2)}, u32[]{:S(2)}) collective-permute-start(s32[512]{0:T(512)} %param.6), channel_id=1, source_target_pairs={{0,5},{1,4},{2,7},{3,6},{4,1},{5,0},{6,3},{7,2},{8,13},{9,12},{10,... | collective-permute-start | bytes 6152 | tf_op jit(solution)/shard_map/ppermute | solution.py:291
  9.5 7.9 %collective-permute-start.2 = (s16[80,256]{1,0:T(8,128)(2,1)S(1)}, s16[80,256]{1,0:T(8,128)(2,1)S(1)}, u32[]{:S(2)}, u32[]{:S(2)}) collective-permute-start(s16[80,256]{1,0:T(8,128)(2,1)S(1)} %get-tuple-element.12.a_ref), channel_id=1, source_target_pairs={{0,2},{2,4},{4,6},{6,0},{1,3},{3,5},{5,7},{7,1},{8,10},{10,12},{12... | collective-permute-start | bytes 122888 | tf_op jit(solution)/shard_map/ppermute | solution.py:33
  10.6 6.8 %collective-permute-start.3 = (s16[80,256]{1,0:T(8,128)(2,1)S(1)}, s16[80,256]{1,0:T(8,128)(2,1)S(1)}, u32[]{:S(2)}, u32[]{:S(2)}) collective-permute-start(s16[80,256]{1,0:T(8,128)(2,1)S(1)} %get-tuple-element.12.a_ref), channel_id=1, source_target_pairs={{0,4},{2,6},{4,0},{6,2},{1,5},{3,7},{5,1},{7,3},{8,12},{10,14},{12... | collective-permute-start | bytes 122888 | tf_op jit(solution)/shard_map/ppermute | solution.py:33
  12.6 4.8 %collective-permute-start.4 = (s16[80,256]{1,0:T(8,128)(2,1)S(1)}, s16[80,256]{1,0:T(8,128)(2,1)S(1)}, u32[]{:S(2)}, u32[]{:S(2)}) collective-permute-start(s16[80,256]{1,0:T(8,128)(2,1)S(1)} %get-tuple-element.12.a_ref), channel_id=1, source_target_pairs={{0,6},{2,0},{4,2},{6,4},{1,7},{3,1},{5,3},{7,5},{8,14},{10,8},{12,... | collective-permute-start | bytes 122888 | tf_op jit(solution)/shard_map/ppermute | solution.py:33
  18.0 11.2 %collective-permute-start.10 = (s16[272,256]{1,0:T(8,128)(2,1)S(1)}, s16[272,256]{1,0:T(8,128)(2,1)S(1)}, u32[]{:S(2)}, u32[]{:S(2)}) collective-permute-start(s16[272,256]{1,0:T(8,128)(2,1)S(1)} %stack.2.refs_0_), channel_id=1, source_target_pairs={{0,24},{8,0},{16,8},{24,16},{32,56},{40,32},{48,40},{56,48},{64,88... | collective-permute-start | bytes 417800 | tf_op jit(solution)/shard_map/ppermute | solution.py:43
  18.6 10.6 %collective-permute-start.8 = (s16[272,256]{1,0:T(8,128)(2,1)S(1)}, s16[272,256]{1,0:T(8,128)(2,1)S(1)}, u32[]{:S(2)}, u32[]{:S(2)}) collective-permute-start(s16[272,256]{1,0:T(8,128)(2,1)S(1)} %stack.2.refs_0_), channel_id=1, source_target_pairs={{0,8},{8,16},{16,24},{24,0},{32,40},{40,48},{48,56},{56,32},{64,72... | collective-permute-start | bytes 417800 | tf_op jit(solution)/shard_map/ppermute | solution.py:43
  20.1 9.1 %collective-permute-start.9 = (s16[272,256]{1,0:T(8,128)(2,1)S(1)}, s16[272,256]{1,0:T(8,128)(2,1)S(1)}, u32[]{:S(2)}, u32[]{:S(2)}) collective-permute-start(s16[272,256]{1,0:T(8,128)(2,1)S(1)} %stack.2.refs_0_), channel_id=1, source_target_pairs={{0,16},{8,24},{16,0},{24,8},{32,48},{40,56},{48,32},{56,40},{64,80... | collective-permute-start | bytes 417800 | tf_op jit(solution)/shard_map/ppermute | solution.py:43
  23.4 5.8 %collective-permute-start.5 = (s16[80,256]{1,0:T(8,128)(2,1)S(1)}, s16[80,256]{1,0:T(8,128)(2,1)S(1)}, u32[]{:S(2)}, u32[]{:S(2)}) collective-permute-start(s16[80,256]{1,0:T(8,128)(2,1)S(1)} %hold.1.a_ref), channel_id=1, source_target_pairs={{0,2},{2,4},{4,6},{6,0},{1,3},{3,5},{5,7},{7,1},{8,10},{10,12},{12... | collective-permute-start | bytes 122888 | tf_op jit(solution)/shard_map/ppermute | solution.py:33
  29.3 14.6 %collective-permute-start.15 = (s16[1040,256]{1,0:T(8,128)(2,1)S(1)}, s16[1040,256]{1,0:T(8,128)(2,1)S(1)}, u32[]{:S(2)}, u32[]{:S(2)}) collective-permute-start(s16[1040,256]{1,0:T(8,128)(2,1)S(1)} %pack.2.refs_0_), channel_id=1, source_target_pairs={{0,32},{8,40},{16,48},{24,56},{32,64},{40,72},{48,80},{56,88},{64,... | collective-permute-start | bytes 1597448 | tf_op jit(solution)/shard_map/ppermute | solution.py:43
  30.9 18.8 %collective-permute-start.16 = (s16[1040,256]{1,0:T(8,128)(2,1)S(1)}, s16[1040,256]{1,0:T(8,128)(2,1)S(1)}, u32[]{:S(2)}, u32[]{:S(2)}) collective-permute-start(s16[1040,256]{1,0:T(8,128)(2,1)S(1)} %pack.2.refs_0_), channel_id=1, source_target_pairs={{0,64},{8,72},{16,80},{24,88},{32,96},{40,104},{48,112},{56,120},{... | collective-permute-start | bytes 1597448 | tf_op jit(solution)/shard_map/ppermute | solution.py:43
  33.8 18.9 %collective-permute-start.14 = (s16[1040,256]{1,0:T(8,128)(2,1)S(1)}, s16[1040,256]{1,0:T(8,128)(2,1)S(1)}, u32[]{:S(2)}, u32[]{:S(2)}) collective-permute-start(s16[1040,256]{1,0:T(8,128)(2,1)S(1)} %pack.2.refs_0_), channel_id=1, source_target_pairs={{0,96},{8,104},{16,112},{24,120},{32,0},{40,8},{48,16},{56,24},{64... | collective-permute-start | bytes 1597448 | tf_op jit(solution)/shard_map/ppermute | solution.py:43
  35.2 4.9 %collective-permute-start.6 = (s16[80,256]{1,0:T(8,128)(2,1)S(1)}, s16[80,256]{1,0:T(8,128)(2,1)S(1)}, u32[]{:S(2)}, u32[]{:S(2)}) collective-permute-start(s16[80,256]{1,0:T(8,128)(2,1)S(1)} %hold.1.a_ref), channel_id=1, source_target_pairs={{0,4},{2,6},{4,0},{6,2},{1,5},{3,7},{5,1},{7,3},{8,12},{10,14},{12... | collective-permute-start | bytes 122888 | tf_op jit(solution)/shard_map/ppermute | solution.py:33
  35.2 4.9 %collective-permute-start.7 = (s16[80,256]{1,0:T(8,128)(2,1)S(1)}, s16[80,256]{1,0:T(8,128)(2,1)S(1)}, u32[]{:S(2)}, u32[]{:S(2)}) collective-permute-start(s16[80,256]{1,0:T(8,128)(2,1)S(1)} %hold.1.a_ref), channel_id=1, source_target_pairs={{0,6},{2,0},{4,2},{6,4},{1,7},{3,1},{5,3},{7,5},{8,14},{10,8},{12,... | collective-permute-start | bytes 122888 | tf_op jit(solution)/shard_map/ppermute | solution.py:33
  40.7 19.2 %collective-permute-start.11 = (s16[272,256]{1,0:T(8,128)(2,1)S(1)}, s16[272,256]{1,0:T(8,128)(2,1)S(1)}, u32[]{:S(2)}, u32[]{:S(2)}) collective-permute-start(s16[272,256]{1,0:T(8,128)(2,1)S(1)} %stack.3.refs_0_), channel_id=1, source_target_pairs={{0,8},{8,16},{16,24},{24,0},{32,40},{40,48},{48,56},{56,32},{64,72... | collective-permute-start | bytes 417800 | tf_op jit(solution)/shard_map/ppermute | solution.py:43
  40.8 19.1 %collective-permute-start.12 = (s16[272,256]{1,0:T(8,128)(2,1)S(1)}, s16[272,256]{1,0:T(8,128)(2,1)S(1)}, u32[]{:S(2)}, u32[]{:S(2)}) collective-permute-start(s16[272,256]{1,0:T(8,128)(2,1)S(1)} %stack.3.refs_0_), channel_id=1, source_target_pairs={{0,16},{8,24},{16,0},{24,8},{32,48},{40,56},{48,32},{56,40},{64,80... | collective-permute-start | bytes 417800 | tf_op jit(solution)/shard_map/ppermute | solution.py:43
  43.9 16.0 %collective-permute-start.13 = (s16[272,256]{1,0:T(8,128)(2,1)S(1)}, s16[272,256]{1,0:T(8,128)(2,1)S(1)}, u32[]{:S(2)}, u32[]{:S(2)}) collective-permute-start(s16[272,256]{1,0:T(8,128)(2,1)S(1)} %stack.3.refs_0_), channel_id=1, source_target_pairs={{0,24},{8,0},{16,8},{24,16},{32,56},{40,32},{48,40},{56,48},{64,88... | collective-permute-start | bytes 417800 | tf_op jit(solution)/shard_map/ppermute | solution.py:43
  54.8 26.2 %collective-permute-start.20 = (s16[528,512]{1,0:T(8,128)(2,1)S(1)}, s16[528,512]{1,0:T(8,128)(2,1)S(1)}, u32[]{:S(2)}, u32[]{:S(2)}) collective-permute-start(s16[528,512]{1,0:T(8,128)(2,1)S(1)} %product.8.refs_4_), channel_id=1, source_target_pairs={{0,1},{1,0},{2,3},{3,2},{4,5},{5,4},{6,7},{7,6},{8,9},{9,8},{10,11... | collective-permute-start | bytes 1622024 | tf_op jit(solution)/shard_map/ppermute | solution.py:313
  60.0 16.3 %collective-permute-start.18 = (s16[1040,256]{1,0:T(8,128)(2,1)S(1)}, s16[1040,256]{1,0:T(8,128)(2,1)S(1)}, u32[]{:S(2)}, u32[]{:S(2)}) collective-permute-start(s16[1040,256]{1,0:T(8,128)(2,1)S(1)} %pack.3.refs_0_), channel_id=1, source_target_pairs={{0,32},{8,40},{16,48},{24,56},{32,64},{40,72},{48,80},{56,88},{64,... | collective-permute-start | bytes 1597448 | tf_op jit(solution)/shard_map/ppermute | solution.py:43
  60.0 16.2 %collective-permute-start.19 = (s16[1040,256]{1,0:T(8,128)(2,1)S(1)}, s16[1040,256]{1,0:T(8,128)(2,1)S(1)}, u32[]{:S(2)}, u32[]{:S(2)}) collective-permute-start(s16[1040,256]{1,0:T(8,128)(2,1)S(1)} %pack.3.refs_0_), channel_id=1, source_target_pairs={{0,64},{8,72},{16,80},{24,88},{32,96},{40,104},{48,112},{56,120},{... | collective-permute-start | bytes 1597448 | tf_op jit(solution)/shard_map/ppermute | solution.py:43
  61.4 17.8 %collective-permute-start.17 = (s16[1040,256]{1,0:T(8,128)(2,1)S(1)}, s16[1040,256]{1,0:T(8,128)(2,1)S(1)}, u32[]{:S(2)}, u32[]{:S(2)}) collective-permute-start(s16[1040,256]{1,0:T(8,128)(2,1)S(1)} %pack.3.refs_0_), channel_id=1, source_target_pairs={{0,96},{8,104},{16,112},{24,120},{32,0},{40,8},{48,16},{56,24},{64... | collective-permute-start | bytes 1597448 | tf_op jit(solution)/shard_map/ppermute | solution.py:43
  79.1 9.1 %copy-start.3 = (s32[512]{0:T(512)S(1)}, s32[512]{0:T(512)}, u32[]{:S(2)}) copy-start(s32[512]{0:T(512)} %param.7) | copy-start | bytes 6148
  82.3 15.5 %all-to-all-start = ((f32[64,4,128]{2,1,0:T(4,128)}), f32[64,4,128]{2,1,0:T(4,128)S(1)}, u32[]{:S(2)}, u32[]{:S(2)}) async-start(f32[64,4,128]{2,1,0:T(4,128)} %get-tuple-element.16), calls=%async_computation | async-start | bytes 262144 | tf_op jit(solution)/shard_map/all_to_all | solution.py:320
  97.9 1.3 %copy-start.2 = (f32[256]{0:T(256)}, f32[256]{0:T(256)S(1)}, u32[]{:S(2)}) copy-start(f32[256]{0:T(256)S(1)} %get-tuple-element.19) | copy-start | bytes 3076
  (2 other events, 1.6 us)

commit v13 on v12

--- a/solution.py
+++ b/solution.py
@@ -186,12 +186,12 @@
 
 
 def product_kernel(offsets, adds, place_ref, head_ref, *refs):
-    parts, out_ref, total_ref = refs[: len(offsets)], refs[-2], refs[-1]
+    parts, out_ref = refs[: len(offsets)], refs[-1]
     core, y, x = place_ref[0], place_ref[2], place_ref[3]
-    count = total_ref.shape[0] // 2
+    count = parts[0].shape[1]
     dims = (((0,), (0,)), ((), ()))
-    for i, (k, part) in enumerate(zip(offsets, parts)):
-        total = None
+    total = refs[len(offsets)][...] if adds else None
+    for k, part in zip(offsets, parts):
         scale = scale_of(part[1024:].astype(jnp.float32))
         for piece in range(4):
             high, low = [], []
@@ -201,19 +201,14 @@
                 top = values.astype(jnp.bfloat16)
                 high.append(top)
                 low.append((values - top.astype(jnp.float32)).astype(jnp.bfloat16))
-            both = jnp.concatenate([jnp.concatenate(high, 0), jnp.concatenate(low, 0)], 1)
             row = jnp.where(core == 0, y - k, y - piece) & 3
             column = jnp.where(core == 0, x - piece, x - k) & 3
             weight = head_ref[pl.ds(pl.multiple_of((row * 4 + column) * 256, 256), 256), :]
-            term = lax.dot_general(both, weight, dims, preferred_element_type=jnp.float32)
-            total = term if total is None else total + term
-        if i == 0:
-            total_ref[...] = total
-        else:
-            total_ref[...] += total
-    total = total_ref[:count] + total_ref[count:]
-    if adds:
-        total += refs[len(offsets)][...]
+            for side in (high, low):
+                term = lax.dot_general(
+                    jnp.concatenate(side, 0), weight, dims, preferred_element_type=jnp.float32
+                )
+                total = term if total is None else total + term
     if out_ref.dtype == jnp.float32:
         out_ref[...] = total
     else:
@@ -240,7 +235,6 @@
         out_shape=out,
         in_specs=[pl.BlockSpec(memory_space=pltpu.SMEM)] + in_vmem(1 + len(chosen) + len(before)),
         out_specs=in_vmem(1)[0],
-        scratch_shapes=[pltpu.VMEM((2 * tokens, width), jnp.float32)],
         compiler_params=room(24),
         cost_estimate=pl.CostEstimate(
             flops=cost * len(offsets) * tokens * 4096 * width, bytes_accessed=0, transcendentals=0

time: 100 us -> 100 us (level)
  no operation moved by 1% of the time
where the time goes in v13:
time: 100 us; the launch traced here: 99.2 us
  starting transfers between devices  43.4 us (43%)
  waiting for transfers between devices  31.8 us (32%)
  Pallas kernels  20 us (20%)
  local copies, waits for them, and re-layouts  1.6 us (2%)
  other arithmetic  1.54 us (2%)
    ppermute x12, starting transfers between devices, crossed(): return lax.ppermute(block, axes, pairs(axes, move))  19.5 us
    ppermute x12, waiting for transfers between devices, crossed(): return lax.ppermute(block, axes, pairs(axes, move))  15.4 us
    pallas_call x6, Pallas kernels, product(): pl.pallas_call(functools.partial(product_kernel, offsets, len(before) > 0...  13.4 us
    all_to_all x1, waiting for transfers between devices, local(): stats = lax.all_to_all(stats, ('y', 'x', 'zl'), 0, 0, tiled=True)  9.39 us
    ppermute x6, waiting for transfers between devices, shifted(): lax.ppermute(block, axis, pairs((axis,), lambda at: {axis: at[axis] + k}))  6.99 us
    ppermute x1, starting transfers between devices, local(): lax.ppermute(scale_index, ('zl', 'zh'), pairs(('zl', 'zh'), nearest_other))  6.39 us
    ppermute x6, starting transfers between devices, shifted(): lax.ppermute(block, axis, pairs((axis,), lambda at: {axis: at[axis] + k}))  6.34 us
    all_to_all x1, starting transfers between devices, local(): stats = lax.all_to_all(stats, ('y', 'x', 'zl'), 0, 0, tiled=True)  5.95 us
  transfers between devices with their start and end apart: 22, of which 5 were waited for; matrix products, arithmetic and copies ran while one was open for 0% of the time, Pallas kernels for 18%

profile of v13, /device:TPU:2, one launch (start us, length us, event | category | flops | bytes accessed | tf_op | source)
XLA Modules:
  0.0 99.2 jit_solution(5333895167372438215)
XLA Ops:
  0.7 6.4 %collective-permute-start.1 = (s32[512]{0:T(512)}, s32[512]{0:T(512)S(1)}, u32[]{:S(2)}, u32[]{:S(2)}) collective-permute-start(s32[512]{0:T(512)} %param.6), channel_id=1, source_target_pairs={{0,5},{1,4},{2,7},{3,6},{4,1},{5,0},{6,3},{7,2},{8,13},{9,12},{10,... | collective-permute-start | bytes 6152 | tf_op jit(solution)/shard_map/ppermute | solution.py:285
  10.6 2.0 %collective-permute-start.3 = (s16[80,256]{1,0:T(8,128)(2,1)S(1)}, s16[80,256]{1,0:T(8,128)(2,1)S(1)}, u32[]{:S(2)}, u32[]{:S(2)}) collective-permute-start(s16[80,256]{1,0:T(8,128)(2,1)S(1)} %get-tuple-element.12.a_ref), channel_id=1, source_target_pairs={{0,4},{2,6},{4,0},{6,2},{1,5},{3,7},{5,1},{7,3},{8,12},{10,14},{12... | collective-permute-start | bytes 122888 | tf_op jit(solution)/shard_map/ppermute | solution.py:33
  12.6 1.4 %collective-permute-start.4 = (s16[80,256]{1,0:T(8,128)(2,1)S(1)}, s16[80,256]{1,0:T(8,128)(2,1)S(1)}, u32[]{:S(2)}, u32[]{:S(2)}) collective-permute-start(s16[80,256]{1,0:T(8,128)(2,1)S(1)} %get-tuple-element.12.a_ref), channel_id=1, source_target_pairs={{0,6},{2,0},{4,2},{6,4},{1,7},{3,1},{5,3},{7,5},{8,14},{10,8},{12,... | collective-permute-start | bytes 122888 | tf_op jit(solution)/shard_map/ppermute | solution.py:33
  14.0 3.4 %load.3.refs_0_.head_ref = bf16[4096,1024]{1,0:T(8,128)(2,1)S(1)} custom-call(bf16[4096,1024]{1,0:T(8,128)(2,1)} %refs_0_), custom_call_target="tpu_custom_call" | custom-call | bytes 16777216 | tf_op jit(solution)/shard_map/load/pallas_call | solution.py:86
  18.6 1.5 %collective-permute-start.8 = (s16[272,256]{1,0:T(8,128)(2,1)S(1)}, s16[272,256]{1,0:T(8,128)(2,1)S(1)}, u32[]{:S(2)}, u32[]{:S(2)}) collective-permute-start(s16[272,256]{1,0:T(8,128)(2,1)S(1)} %stack.2.refs_0_), channel_id=1, source_target_pairs={{0,8},{8,16},{16,24},{24,0},{32,40},{40,48},{48,56},{56,32},{64,72... | collective-permute-start | bytes 417800 | tf_op jit(solution)/shard_map/ppermute | solution.py:43
  20.1 3.3 %collective-permute-start.9 = (s16[272,256]{1,0:T(8,128)(2,1)S(1)}, s16[272,256]{1,0:T(8,128)(2,1)S(1)}, u32[]{:S(2)}, u32[]{:S(2)}) collective-permute-start(s16[272,256]{1,0:T(8,128)(2,1)S(1)} %stack.2.refs_0_), channel_id=1, source_target_pairs={{0,16},{8,24},{16,0},{24,8},{32,48},{40,56},{48,32},{56,40},{64,80... | collective-permute-start | bytes 417800 | tf_op jit(solution)/shard_map/ppermute | solution.py:43
  24.1 5.1 %collective-permute-done.5.refs_4_.b_ref = s16[80,256]{1,0:T(8,128)(2,1)S(1)} collective-permute-done((s16[80,256]{1,0:T(8,128)(2,1)S(1)}, s16[80,256]{1,0:T(8,128)(2,1)S(1)}, u32[]{:S(2)}, u32[]{:S(2)}) %collective-permute-start.5) | collective-permute-done | bytes 40992 | tf_op jit(solution)/shard_map/ppermute | solution.py:33
  29.3 1.7 %collective-permute-start.15 = (s16[1040,256]{1,0:T(8,128)(2,1)S(1)}, s16[1040,256]{1,0:T(8,128)(2,1)S(1)}, u32[]{:S(2)}, u32[]{:S(2)}) collective-permute-start(s16[1040,256]{1,0:T(8,128)(2,1)S(1)} %pack.2.refs_0_), channel_id=1, source_target_pairs={{0,32},{8,40},{16,48},{24,56},{32,64},{40,72},{48,80},{56,88},{64,... | collective-permute-start | bytes 1597448 | tf_op jit(solution)/shard_map/ppermute | solution.py:43
  30.9 2.9 %collective-permute-start.16 = (s16[1040,256]{1,0:T(8,128)(2,1)S(1)}, s16[1040,256]{1,0:T(8,128)(2,1)S(1)}, u32[]{:S(2)}, u32[]{:S(2)}) collective-permute-start(s16[1040,256]{1,0:T(8,128)(2,1)S(1)} %pack.2.refs_0_), channel_id=1, source_target_pairs={{0,64},{8,72},{16,80},{24,88},{32,96},{40,104},{48,112},{56,120},{... | collective-permute-start | bytes 1597448 | tf_op jit(solution)/shard_map/ppermute | solution.py:43
  33.8 1.3 %collective-permute-start.14 = (s16[1040,256]{1,0:T(8,128)(2,1)S(1)}, s16[1040,256]{1,0:T(8,128)(2,1)S(1)}, u32[]{:S(2)}, u32[]{:S(2)}) collective-permute-start(s16[1040,256]{1,0:T(8,128)(2,1)S(1)} %pack.2.refs_0_), channel_id=1, source_target_pairs={{0,96},{8,104},{16,112},{24,120},{32,0},{40,8},{48,16},{56,24},{64... | collective-permute-start | bytes 1597448 | tf_op jit(solution)/shard_map/ppermute | solution.py:43
  36.4 1.8 %product.6.refs_1_.refs_2_ = f32[256,1024]{1,0:T(8,128)S(1)} custom-call(s32[8]{0:T(128)S(1)} %compare_select_fusion.4.place_ref, bf16[4096,1024]{1,0:T(8,128)(2,1)S(1)} %load.3.refs_0_.head_ref, s16[1040,256]{1,0:T(8,128)(2,1)S(1)} %pack.2.refs_0_), custom_call_target="tpu_custom_call" | custom-call | flops 1073741824 | tf_op jit(solution)/shard_map/product/pallas_call | solution.py:233
  38.3 1.8 %collective-permute-done.6.c_ref = s16[80,256]{1,0:T(8,128)(2,1)S(1)} collective-permute-done((s16[80,256]{1,0:T(8,128)(2,1)S(1)}, s16[80,256]{1,0:T(8,128)(2,1)S(1)}, u32[]{:S(2)}, u32[]{:S(2)}) %collective-permute-start.6) | collective-permute-done | bytes 40992 | tf_op jit(solution)/shard_map/ppermute | solution.py:33
  40.8 3.1 %collective-permute-start.12 = (s16[272,256]{1,0:T(8,128)(2,1)S(1)}, s16[272,256]{1,0:T(8,128)(2,1)S(1)}, u32[]{:S(2)}, u32[]{:S(2)}) collective-permute-start(s16[272,256]{1,0:T(8,128)(2,1)S(1)} %stack.3.refs_0_), channel_id=1, source_target_pairs={{0,16},{8,24},{16,0},{24,8},{32,48},{40,56},{48,32},{56,40},{64,80... | collective-permute-start | bytes 417800 | tf_op jit(solution)/shard_map/ppermute | solution.py:43
  44.9 4.9 %collective-permute-done.16.refs_1_ = s16[1040,256]{1,0:T(8,128)(2,1)S(1)} collective-permute-done((s16[1040,256]{1,0:T(8,128)(2,1)S(1)}, s16[1040,256]{1,0:T(8,128)(2,1)S(1)}, u32[]{:S(2)}, u32[]{:S(2)}) %collective-permute-start.16) | collective-permute-done | bytes 532512 | tf_op jit(solution)/shard_map/ppermute | solution.py:43
  49.8 2.9 %product.7.refs_1_ = f32[256,1024]{1,0:T(8,128)S(1)} custom-call(s32[8]{0:T(128)S(1)} %compare_select_fusion.4.place_ref, bf16[4096,1024]{1,0:T(8,128)(2,1)S(1)} %load.3.refs_0_.head_ref, s16[1040,256]{1,0:T(8,128)(2,1)S(1)} %collective-permute-done.15.refs_0_, s16[1040,256]{1,0:T(8,128)(2,1)S(1)} %collective-permute-done.16.refs_1_, ...), custom_call_target="tpu_custom_call" | custom-call | flops 2147483648 | tf_op jit(solution)/shard_map/product/pallas_call | solution.py:233
  52.7 2.0 %product.8.refs_4_ = s16[528,512]{1,0:T(8,128)(2,1)S(1)} custom-call(s32[8]{0:T(128)S(1)} %compare_select_fusion.4.place_ref, bf16[4096,1024]{1,0:T(8,128)(2,1)S(1)} %load.3.refs_0_.head_ref, s16[1040,256]{1,0:T(8,128)(2,1)S(1)} %collective-permute-done.14.refs_0_, f32[256,1024]{1,0:T(8,128)S(1)} %product.7.refs_1_), custom_call_target="tpu_custom_call" | custom-call | flops 1073741824 | tf_op jit(solution)/shard_map/product/pallas_call | solution.py:233
  54.8 5.1 %collective-permute-start.20 = (s16[528,512]{1,0:T(8,128)(2,1)S(1)}, s16[528,512]{1,0:T(8,128)(2,1)S(1)}, u32[]{:S(2)}, u32[]{:S(2)}) collective-permute-start(s16[528,512]{1,0:T(8,128)(2,1)S(1)} %product.8.refs_4_), channel_id=1, source_target_pairs={{0,1},{1,0},{2,3},{3,2},{4,5},{5,4},{6,7},{7,6},{8,9},{9,8},{10,11... | collective-permute-start | bytes 1622024 | tf_op jit(solution)/shard_map/ppermute | solution.py:307
  61.4 2.5 %collective-permute-start.17 = (s16[1040,256]{1,0:T(8,128)(2,1)S(1)}, s16[1040,256]{1,0:T(8,128)(2,1)S(1)}, u32[]{:S(2)}, u32[]{:S(2)}) collective-permute-start(s16[1040,256]{1,0:T(8,128)(2,1)S(1)} %pack.3.refs_0_), channel_id=1, source_target_pairs={{0,96},{8,104},{16,112},{24,120},{32,0},{40,8},{48,16},{56,24},{64... | collective-permute-start | bytes 1597448 | tf_op jit(solution)/shard_map/ppermute | solution.py:43
  63.9 1.8 %product.9.refs_2_ = f32[256,1024]{1,0:T(8,128)S(1)} custom-call(s32[8]{0:T(128)S(1)} %compare_select_fusion.4.place_ref, bf16[4096,1024]{1,0:T(8,128)(2,1)S(1)} %load.3.refs_0_.head_ref, s16[1040,256]{1,0:T(8,128)(2,1)S(1)} %pack.3.refs_0_), custom_call_target="tpu_custom_call" | custom-call | tf_op jit(solution)/shard_map/product/pallas_call | solution.py:233
  65.7 10.5 %collective-permute-done.18.refs_0_ = s16[1040,256]{1,0:T(8,128)(2,1)S(1)} collective-permute-done((s16[1040,256]{1,0:T(8,128)(2,1)S(1)}, s16[1040,256]{1,0:T(8,128)(2,1)S(1)}, u32[]{:S(2)}, u32[]{:S(2)}) %collective-permute-start.18) | collective-permute-done | bytes 532512 | tf_op jit(solution)/shard_map/ppermute | solution.py:43
  76.2 2.9 %product.10.refs_1_ = f32[256,1024]{1,0:T(8,128)S(1)} custom-call(s32[8]{0:T(128)S(1)} %compare_select_fusion.4.place_ref, bf16[4096,1024]{1,0:T(8,128)(2,1)S(1)} %load.3.refs_0_.head_ref, s16[1040,256]{1,0:T(8,128)(2,1)S(1)} %collective-permute-done.18.refs_0_, s16[1040,256]{1,0:T(8,128)(2,1)S(1)} %collective-permute-done.19.refs_1_, ...), custom_call_target="tpu_custom_call" | custom-call | tf_op jit(solution)/shard_map/product/pallas_call | solution.py:233
  79.2 1.8 %product.11.kept_ref = f32[256,1024]{1,0:T(8,128)S(1)} custom-call(s32[8]{0:T(128)S(1)} %compare_select_fusion.4.place_ref, bf16[4096,1024]{1,0:T(8,128)(2,1)S(1)} %load.3.refs_0_.head_ref, s16[1040,256]{1,0:T(8,128)(2,1)S(1)} %collective-permute-done.17.refs_0_, f32[256,1024]{1,0:T(8,128)S(1)} %product.10.refs_1_), custom_call_target="tpu_custom_call" | custom-call | tf_op jit(solution)/shard_map/product/pallas_call | solution.py:233
  82.3 6.0 %all-to-all-start = ((f32[64,4,128]{2,1,0:T(4,128)}), f32[64,4,128]{2,1,0:T(4,128)S(1)}, u32[]{:S(2)}, u32[]{:S(2)}) async-start(f32[64,4,128]{2,1,0:T(4,128)} %get-tuple-element.16), calls=%async_computation | async-start | bytes 262144 | tf_op jit(solution)/shard_map/all_to_all | solution.py:314
  88.4 9.4 %all-to-all-done = f32[64,4,128]{2,1,0:T(4,128)S(1)} async-done(((f32[64,4,128]{2,1,0:T(4,128)}), f32[64,4,128]{2,1,0:T(4,128)S(1)}, u32[]{:S(2)}, u32[]{:S(2)}) %all-to-all-start) | async-done | bytes 131104 | tf_op jit(solution)/shard_map/all_to_all | solution.py:314
  (49 shorter events, 12.7 us)
Async XLA Ops:
  0.6 8.3 %collective-permute-start = (bf16[64,1024]{1,0:T(8,128)(2,1)}, bf16[64,1024]{1,0:T(8,128)(2,1)S(1)}, u32[]{:S(2)}, u32[]{:S(2)}) collective-permute-start(bf16[64,1024]{1,0:T(8,128)(2,1)} %bitcast.10), channel_id=1, source_target_pairs={{0,128},{128,0},{1,129},{129,1},{2,130},{130,2},{3,131},{131,3},{4... | collective-permute-start | bytes 393224 | tf_op jit(solution)/shard_map/ppermute | solution.py:284
  0.7 8.2 %collective-permute-start.1 = (s32[512]{0:T(512)}, s32[512]{0:T(512)S(1)}, u32[]{:S(2)}, u32[]{:S(2)}) collective-permute-start(s32[512]{0:T(512)} %param.6), channel_id=1, source_target_pairs={{0,5},{1,4},{2,7},{3,6},{4,1},{5,0},{6,3},{7,2},{8,13},{9,12},{10,... | collective-permute-start | bytes 6152 | tf_op jit(solution)/shard_map/ppermute | solution.py:285
  9.5 7.9 %collective-permute-start.2 = (s16[80,256]{1,0:T(8,128)(2,1)S(1)}, s16[80,256]{1,0:T(8,128)(2,1)S(1)}, u32[]{:S(2)}, u32[]{:S(2)}) collective-permute-start(s16[80,256]{1,0:T(8,128)(2,1)S(1)} %get-tuple-element.12.a_ref), channel_id=1, source_target_pairs={{0,2},{2,4},{4,6},{6,0},{1,3},{3,5},{5,7},{7,1},{8,10},{10,12},{12... | collective-permute-start | bytes 122888 | tf_op jit(solution)/shard_map/ppermute | solution.py:33
  10.6 6.8 %collective-permute-start.3 = (s16[80,256]{1,0:T(8,128)(2,1)S(1)}, s16[80,256]{1,0:T(8,128)(2,1)S(1)}, u32[]{:S(2)}, u32[]{:S(2)}) collective-permute-start(s16[80,256]{1,0:T(8,128)(2,1)S(1)} %get-tuple-element.12.a_ref), channel_id=1, source_target_pairs={{0,4},{2,6},{4,0},{6,2},{1,5},{3,7},{5,1},{7,3},{8,12},{10,14},{12... | collective-permute-start | bytes 122888 | tf_op jit(solution)/shard_map/ppermute | solution.py:33
  12.6 4.8 %collective-permute-start.4 = (s16[80,256]{1,0:T(8,128)(2,1)S(1)}, s16[80,256]{1,0:T(8,128)(2,1)S(1)}, u32[]{:S(2)}, u32[]{:S(2)}) collective-permute-start(s16[80,256]{1,0:T(8,128)(2,1)S(1)} %get-tuple-element.12.a_ref), channel_id=1, source_target_pairs={{0,6},{2,0},{4,2},{6,4},{1,7},{3,1},{5,3},{7,5},{8,14},{10,8},{12,... | collective-permute-start | bytes 122888 | tf_op jit(solution)/shard_map/ppermute | solution.py:33
  18.0 11.2 %collective-permute-start.10 = (s16[272,256]{1,0:T(8,128)(2,1)S(1)}, s16[272,256]{1,0:T(8,128)(2,1)S(1)}, u32[]{:S(2)}, u32[]{:S(2)}) collective-permute-start(s16[272,256]{1,0:T(8,128)(2,1)S(1)} %stack.2.refs_0_), channel_id=1, source_target_pairs={{0,24},{8,0},{16,8},{24,16},{32,56},{40,32},{48,40},{56,48},{64,88... | collective-permute-start | bytes 417800 | tf_op jit(solution)/shard_map/ppermute | solution.py:43
  18.6 10.6 %collective-permute-start.8 = (s16[272,256]{1,0:T(8,128)(2,1)S(1)}, s16[272,256]{1,0:T(8,128)(2,1)S(1)}, u32[]{:S(2)}, u32[]{:S(2)}) collective-permute-start(s16[272,256]{1,0:T(8,128)(2,1)S(1)} %stack.2.refs_0_), channel_id=1, source_target_pairs={{0,8},{8,16},{16,24},{24,0},{32,40},{40,48},{48,56},{56,32},{64,72... | collective-permute-start | bytes 417800 | tf_op jit(solution)/shard_map/ppermute | solution.py:43
  20.1 9.1 %collective-permute-start.9 = (s16[272,256]{1,0:T(8,128)(2,1)S(1)}, s16[272,256]{1,0:T(8,128)(2,1)S(1)}, u32[]{:S(2)}, u32[]{:S(2)}) collective-permute-start(s16[272,256]{1,0:T(8,128)(2,1)S(1)} %stack.2.refs_0_), channel_id=1, source_target_pairs={{0,16},{8,24},{16,0},{24,8},{32,48},{40,56},{48,32},{56,40},{64,80... | collective-permute-start | bytes 417800 | tf_op jit(solution)/shard_map/ppermute | solution.py:43
  23.4 5.8 %collective-permute-start.5 = (s16[80,256]{1,0:T(8,128)(2,1)S(1)}, s16[80,256]{1,0:T(8,128)(2,1)S(1)}, u32[]{:S(2)}, u32[]{:S(2)}) collective-permute-start(s16[80,256]{1,0:T(8,128)(2,1)S(1)} %hold.1.a_ref), channel_id=1, source_target_pairs={{0,2},{2,4},{4,6},{6,0},{1,3},{3,5},{5,7},{7,1},{8,10},{10,12},{12... | collective-permute-start | bytes 122888 | tf_op jit(solution)/shard_map/ppermute | solution.py:33
  29.3 14.6 %collective-permute-start.15 = (s16[1040,256]{1,0:T(8,128)(2,1)S(1)}, s16[1040,256]{1,0:T(8,128)(2,1)S(1)}, u32[]{:S(2)}, u32[]{:S(2)}) collective-permute-start(s16[1040,256]{1,0:T(8,128)(2,1)S(1)} %pack.2.refs_0_), channel_id=1, source_target_pairs={{0,32},{8,40},{16,48},{24,56},{32,64},{40,72},{48,80},{56,88},{64,... | collective-permute-start | bytes 1597448 | tf_op jit(solution)/shard_map/ppermute | solution.py:43
  30.9 18.8 %collective-permute-start.16 = (s16[1040,256]{1,0:T(8,128)(2,1)S(1)}, s16[1040,256]{1,0:T(8,128)(2,1)S(1)}, u32[]{:S(2)}, u32[]{:S(2)}) collective-permute-start(s16[1040,256]{1,0:T(8,128)(2,1)S(1)} %pack.2.refs_0_), channel_id=1, source_target_pairs={{0,64},{8,72},{16,80},{24,88},{32,96},{40,104},{48,112},{56,120},{... | collective-permute-start | bytes 1597448 | tf_op jit(solution)/shard_map/ppermute | solution.py:43
  33.8 18.9 %collective-permute-start.14 = (s16[1040,256]{1,0:T(8,128)(2,1)S(1)}, s16[1040,256]{1,0:T(8,128)(2,1)S(1)}, u32[]{:S(2)}, u32[]{:S(2)}) collective-permute-start(s16[1040,256]{1,0:T(8,128)(2,1)S(1)} %pack.2.refs_0_), channel_id=1, source_target_pairs={{0,96},{8,104},{16,112},{24,120},{32,0},{40,8},{48,16},{56,24},{64... | collective-permute-start | bytes 1597448 | tf_op jit(solution)/shard_map/ppermute | solution.py:43
  35.2 4.9 %collective-permute-start.6 = (s16[80,256]{1,0:T(8,128)(2,1)S(1)}, s16[80,256]{1,0:T(8,128)(2,1)S(1)}, u32[]{:S(2)}, u32[]{:S(2)}) collective-permute-start(s16[80,256]{1,0:T(8,128)(2,1)S(1)} %hold.1.a_ref), channel_id=1, source_target_pairs={{0,4},{2,6},{4,0},{6,2},{1,5},{3,7},{5,1},{7,3},{8,12},{10,14},{12... | collective-permute-start | bytes 122888 | tf_op jit(solution)/shard_map/ppermute | solution.py:33
  35.2 4.9 %collective-permute-start.7 = (s16[80,256]{1,0:T(8,128)(2,1)S(1)}, s16[80,256]{1,0:T(8,128)(2,1)S(1)}, u32[]{:S(2)}, u32[]{:S(2)}) collective-permute-start(s16[80,256]{1,0:T(8,128)(2,1)S(1)} %hold.1.a_ref), channel_id=1, source_target_pairs={{0,6},{2,0},{4,2},{6,4},{1,7},{3,1},{5,3},{7,5},{8,14},{10,8},{12,... | collective-permute-start | bytes 122888 | tf_op jit(solution)/shard_map/ppermute | solution.py:33
  40.7 19.2 %collective-permute-start.11 = (s16[272,256]{1,0:T(8,128)(2,1)S(1)}, s16[272,256]{1,0:T(8,128)(2,1)S(1)}, u32[]{:S(2)}, u32[]{:S(2)}) collective-permute-start(s16[272,256]{1,0:T(8,128)(2,1)S(1)} %stack.3.refs_0_), channel_id=1, source_target_pairs={{0,8},{8,16},{16,24},{24,0},{32,40},{40,48},{48,56},{56,32},{64,72... | collective-permute-start | bytes 417800 | tf_op jit(solution)/shard_map/ppermute | solution.py:43
  40.8 19.1 %collective-permute-start.12 = (s16[272,256]{1,0:T(8,128)(2,1)S(1)}, s16[272,256]{1,0:T(8,128)(2,1)S(1)}, u32[]{:S(2)}, u32[]{:S(2)}) collective-permute-start(s16[272,256]{1,0:T(8,128)(2,1)S(1)} %stack.3.refs_0_), channel_id=1, source_target_pairs={{0,16},{8,24},{16,0},{24,8},{32,48},{40,56},{48,32},{56,40},{64,80... | collective-permute-start | bytes 417800 | tf_op jit(solution)/shard_map/ppermute | solution.py:43
  43.9 16.0 %collective-permute-start.13 = (s16[272,256]{1,0:T(8,128)(2,1)S(1)}, s16[272,256]{1,0:T(8,128)(2,1)S(1)}, u32[]{:S(2)}, u32[]{:S(2)}) collective-permute-start(s16[272,256]{1,0:T(8,128)(2,1)S(1)} %stack.3.refs_0_), channel_id=1, source_target_pairs={{0,24},{8,0},{16,8},{24,16},{32,56},{40,32},{48,40},{56,48},{64,88... | collective-permute-start | bytes 417800 | tf_op jit(solution)/shard_map/ppermute | solution.py:43
  54.8 26.3 %collective-permute-start.20 = (s16[528,512]{1,0:T(8,128)(2,1)S(1)}, s16[528,512]{1,0:T(8,128)(2,1)S(1)}, u32[]{:S(2)}, u32[]{:S(2)}) collective-permute-start(s16[528,512]{1,0:T(8,128)(2,1)S(1)} %product.8.refs_4_), channel_id=1, source_target_pairs={{0,1},{1,0},{2,3},{3,2},{4,5},{5,4},{6,7},{7,6},{8,9},{9,8},{10,11... | collective-permute-start | bytes 1622024 | tf_op jit(solution)/shard_map/ppermute | solution.py:307
  59.9 16.3 %collective-permute-start.18 = (s16[1040,256]{1,0:T(8,128)(2,1)S(1)}, s16[1040,256]{1,0:T(8,128)(2,1)S(1)}, u32[]{:S(2)}, u32[]{:S(2)}) collective-permute-start(s16[1040,256]{1,0:T(8,128)(2,1)S(1)} %pack.3.refs_0_), channel_id=1, source_target_pairs={{0,32},{8,40},{16,48},{24,56},{32,64},{40,72},{48,80},{56,88},{64,... | collective-permute-start | bytes 1597448 | tf_op jit(solution)/shard_map/ppermute | solution.py:43
  60.0 16.2 %collective-permute-start.19 = (s16[1040,256]{1,0:T(8,128)(2,1)S(1)}, s16[1040,256]{1,0:T(8,128)(2,1)S(1)}, u32[]{:S(2)}, u32[]{:S(2)}) collective-permute-start(s16[1040,256]{1,0:T(8,128)(2,1)S(1)} %pack.3.refs_0_), channel_id=1, source_target_pairs={{0,64},{8,72},{16,80},{24,88},{32,96},{40,104},{48,112},{56,120},{... | collective-permute-start | bytes 1597448 | tf_op jit(solution)/shard_map/ppermute | solution.py:43
  61.4 17.8 %collective-permute-start.17 = (s16[1040,256]{1,0:T(8,128)(2,1)S(1)}, s16[1040,256]{1,0:T(8,128)(2,1)S(1)}, u32[]{:S(2)}, u32[]{:S(2)}) collective-permute-start(s16[1040,256]{1,0:T(8,128)(2,1)S(1)} %pack.3.refs_0_), channel_id=1, source_target_pairs={{0,96},{8,104},{16,112},{24,120},{32,0},{40,8},{48,16},{56,24},{64... | collective-permute-start | bytes 1597448 | tf_op jit(solution)/shard_map/ppermute | solution.py:43
  79.1 9.1 %copy-start.3 = (s32[512]{0:T(512)S(1)}, s32[512]{0:T(512)}, u32[]{:S(2)}) copy-start(s32[512]{0:T(512)} %param.7) | copy-start | bytes 6148
  82.3 15.4 %all-to-all-start = ((f32[64,4,128]{2,1,0:T(4,128)}), f32[64,4,128]{2,1,0:T(4,128)S(1)}, u32[]{:S(2)}, u32[]{:S(2)}) async-start(f32[64,4,128]{2,1,0:T(4,128)} %get-tuple-element.16), calls=%async_computation | async-start | bytes 262144 | tf_op jit(solution)/shard_map/all_to_all | solution.py:314
  97.9 1.3 %copy-start.2 = (f32[256]{0:T(256)}, f32[256]{0:T(256)S(1)}, u32[]{:S(2)}) copy-start(f32[256]{0:T(256)S(1)} %get-tuple-element.19) | copy-start | bytes 3076
  (2 other events, 1.6 us)

commit v14 on v13

--- a/solution.py
+++ b/solution.py
@@ -75,7 +75,15 @@
 
 def load_kernel(*refs):
     count = len(refs) // 2
-    copies = [pltpu.make_async_copy(refs[i], refs[count + i], refs[-1].at[i]) for i in range(count)]
+    copies = []
+    for i in range(count):
+        rows = refs[i].shape[0]
+        cuts = 4 if rows >= 4096 else 1
+        for j in range(cuts):
+            part = pl.ds(j * (rows // cuts), rows // cuts)
+            copies.append(
+                pltpu.make_async_copy(refs[i].at[part], refs[count + i].at[part], refs[-1].at[4 * i + j])
+            )
     for copy in copies:
         copy.start()
     for copy in copies:
@@ -88,7 +96,7 @@
         out_shape=[jax.ShapeDtypeStruct(a.shape, a.dtype) for a in arrays],
         in_specs=anywhere(arrays),
         out_specs=in_vmem(len(arrays)),
-        scratch_shapes=[pltpu.SemaphoreType.DMA((len(arrays),))],
+        scratch_shapes=[pltpu.SemaphoreType.DMA((4 * len(arrays),))],
         compiler_params=room(44),
         cost_estimate=pl.CostEstimate(
             flops=0, bytes_accessed=2 * sum(a.size * a.dtype.itemsize for a in arrays), transcendentals=0

time: 100 us -> 100 us (level)
  no operation moved by 1% of the time
where the time goes in v14:
time: 100 us; the launch traced here: 99.2 us
  starting transfers between devices  43.2 us (43%)
  waiting for transfers between devices  31.8 us (32%)
  Pallas kernels  20.2 us (20%)
  local copies, waits for them, and re-layouts  1.6 us (2%)
  other arithmetic  1.54 us (2%)
    ppermute x12, starting transfers between devices, crossed(): return lax.ppermute(block, axes, pairs(axes, move))  19.6 us
    ppermute x12, waiting for transfers between devices, crossed(): return lax.ppermute(block, axes, pairs(axes, move))  15.3 us
    pallas_call x6, Pallas kernels, product(): pl.pallas_call(functools.partial(product_kernel, offsets, len(before) > 0...  13.4 us
    all_to_all x1, waiting for transfers between devices, local(): stats = lax.all_to_all(stats, ('y', 'x', 'zl'), 0, 0, tiled=True)  9.39 us
    ppermute x6, waiting for transfers between devices, shifted(): lax.ppermute(block, axis, pairs((axis,), lambda at: {axis: at[axis] + k}))  7.09 us
    ppermute x1, starting transfers between devices, local(): lax.ppermute(scale_index, ('zl', 'zh'), pairs(('zl', 'zh'), nearest_other))  6.39 us
    ppermute x6, starting transfers between devices, shifted(): lax.ppermute(block, axis, pairs((axis,), lambda at: {axis: at[axis] + k}))  6.24 us
    all_to_all x1, starting transfers between devices, local(): stats = lax.all_to_all(stats, ('y', 'x', 'zl'), 0, 0, tiled=True)  5.84 us
  transfers between devices with their start and end apart: 22, of which 5 were waited for; matrix products, arithmetic and copies ran while one was open for 0% of the time, Pallas kernels for 18%

profile of v14, /device:TPU:2, one launch (start us, length us, event | category | flops | bytes accessed | tf_op | source)
XLA Modules:
  0.0 99.2 jit_solution(17219111504826814111)
XLA Ops:
  0.7 6.4 %collective-permute-start.1 = (s32[512]{0:T(512)}, s32[512]{0:T(512)S(1)}, u32[]{:S(2)}, u32[]{:S(2)}) collective-permute-start(s32[512]{0:T(512)} %param.6), channel_id=1, source_target_pairs={{0,5},{1,4},{2,7},{3,6},{4,1},{5,0},{6,3},{7,2},{8,13},{9,12},{10,... | collective-permute-start | bytes 6152 | tf_op jit(solution)/shard_map/ppermute | solution.py:293
  10.7 1.9 %collective-permute-start.3 = (s16[80,256]{1,0:T(8,128)(2,1)S(1)}, s16[80,256]{1,0:T(8,128)(2,1)S(1)}, u32[]{:S(2)}, u32[]{:S(2)}) collective-permute-start(s16[80,256]{1,0:T(8,128)(2,1)S(1)} %get-tuple-element.12.a_ref), channel_id=1, source_target_pairs={{0,4},{2,6},{4,0},{6,2},{1,5},{3,7},{5,1},{7,3},{8,12},{10,14},{12... | collective-permute-start | bytes 122888 | tf_op jit(solution)/shard_map/ppermute | solution.py:33
  12.6 1.4 %collective-permute-start.4 = (s16[80,256]{1,0:T(8,128)(2,1)S(1)}, s16[80,256]{1,0:T(8,128)(2,1)S(1)}, u32[]{:S(2)}, u32[]{:S(2)}) collective-permute-start(s16[80,256]{1,0:T(8,128)(2,1)S(1)} %get-tuple-element.12.a_ref), channel_id=1, source_target_pairs={{0,6},{2,0},{4,2},{6,4},{1,7},{3,1},{5,3},{7,5},{8,14},{10,8},{12,... | collective-permute-start | bytes 122888 | tf_op jit(solution)/shard_map/ppermute | solution.py:33
  14.0 3.5 %load.3.refs_0_.head_ref = bf16[4096,1024]{1,0:T(8,128)(2,1)S(1)} custom-call(bf16[4096,1024]{1,0:T(8,128)(2,1)} %refs_0_), custom_call_target="tpu_custom_call" | custom-call | bytes 16777216 | tf_op jit(solution)/shard_map/load/pallas_call | solution.py:94
  18.8 1.5 %collective-permute-start.8 = (s16[272,256]{1,0:T(8,128)(2,1)S(1)}, s16[272,256]{1,0:T(8,128)(2,1)S(1)}, u32[]{:S(2)}, u32[]{:S(2)}) collective-permute-start(s16[272,256]{1,0:T(8,128)(2,1)S(1)} %stack.2.refs_0_), channel_id=1, source_target_pairs={{0,8},{8,16},{16,24},{24,0},{32,40},{40,48},{48,56},{56,32},{64,72... | collective-permute-start | bytes 417800 | tf_op jit(solution)/shard_map/ppermute | solution.py:43
  20.2 3.3 %collective-permute-start.9 = (s16[272,256]{1,0:T(8,128)(2,1)S(1)}, s16[272,256]{1,0:T(8,128)(2,1)S(1)}, u32[]{:S(2)}, u32[]{:S(2)}) collective-permute-start(s16[272,256]{1,0:T(8,128)(2,1)S(1)} %stack.2.refs_0_), channel_id=1, source_target_pairs={{0,16},{8,24},{16,0},{24,8},{32,48},{40,56},{48,32},{56,40},{64,80... | collective-permute-start | bytes 417800 | tf_op jit(solution)/shard_map/ppermute | solution.py:43
  24.2 5.2 %collective-permute-done.5.refs_4_.b_ref = s16[80,256]{1,0:T(8,128)(2,1)S(1)} collective-permute-done((s16[80,256]{1,0:T(8,128)(2,1)S(1)}, s16[80,256]{1,0:T(8,128)(2,1)S(1)}, u32[]{:S(2)}, u32[]{:S(2)}) %collective-permute-start.5) | collective-permute-done | bytes 40992 | tf_op jit(solution)/shard_map/ppermute | solution.py:33
  29.5 1.7 %collective-permute-start.15 = (s16[1040,256]{1,0:T(8,128)(2,1)S(1)}, s16[1040,256]{1,0:T(8,128)(2,1)S(1)}, u32[]{:S(2)}, u32[]{:S(2)}) collective-permute-start(s16[1040,256]{1,0:T(8,128)(2,1)S(1)} %pack.2.refs_0_), channel_id=1, source_target_pairs={{0,32},{8,40},{16,48},{24,56},{32,64},{40,72},{48,80},{56,88},{64,... | collective-permute-start | bytes 1597448 | tf_op jit(solution)/shard_map/ppermute | solution.py:43
  31.1 2.9 %collective-permute-start.16 = (s16[1040,256]{1,0:T(8,128)(2,1)S(1)}, s16[1040,256]{1,0:T(8,128)(2,1)S(1)}, u32[]{:S(2)}, u32[]{:S(2)}) collective-permute-start(s16[1040,256]{1,0:T(8,128)(2,1)S(1)} %pack.2.refs_0_), channel_id=1, source_target_pairs={{0,64},{8,72},{16,80},{24,88},{32,96},{40,104},{48,112},{56,120},{... | collective-permute-start | bytes 1597448 | tf_op jit(solution)/shard_map/ppermute | solution.py:43
  34.0 1.3 %collective-permute-start.14 = (s16[1040,256]{1,0:T(8,128)(2,1)S(1)}, s16[1040,256]{1,0:T(8,128)(2,1)S(1)}, u32[]{:S(2)}, u32[]{:S(2)}) collective-permute-start(s16[1040,256]{1,0:T(8,128)(2,1)S(1)} %pack.2.refs_0_), channel_id=1, source_target_pairs={{0,96},{8,104},{16,112},{24,120},{32,0},{40,8},{48,16},{56,24},{64... | collective-permute-start | bytes 1597448 | tf_op jit(solution)/shard_map/ppermute | solution.py:43
  36.5 1.8 %product.6.refs_1_.refs_2_ = f32[256,1024]{1,0:T(8,128)S(1)} custom-call(s32[8]{0:T(128)S(1)} %compare_select_fusion.4.place_ref, bf16[4096,1024]{1,0:T(8,128)(2,1)S(1)} %load.3.refs_0_.head_ref, s16[1040,256]{1,0:T(8,128)(2,1)S(1)} %pack.2.refs_0_), custom_call_target="tpu_custom_call" | custom-call | flops 1073741824 | tf_op jit(solution)/shard_map/product/pallas_call | solution.py:241
  38.4 1.9 %collective-permute-done.6.c_ref = s16[80,256]{1,0:T(8,128)(2,1)S(1)} collective-permute-done((s16[80,256]{1,0:T(8,128)(2,1)S(1)}, s16[80,256]{1,0:T(8,128)(2,1)S(1)}, u32[]{:S(2)}, u32[]{:S(2)}) %collective-permute-start.6) | collective-permute-done | bytes 40992 | tf_op jit(solution)/shard_map/ppermute | solution.py:33
  40.9 3.1 %collective-permute-start.12 = (s16[272,256]{1,0:T(8,128)(2,1)S(1)}, s16[272,256]{1,0:T(8,128)(2,1)S(1)}, u32[]{:S(2)}, u32[]{:S(2)}) collective-permute-start(s16[272,256]{1,0:T(8,128)(2,1)S(1)} %stack.3.refs_0_), channel_id=1, source_target_pairs={{0,16},{8,24},{16,0},{24,8},{32,48},{40,56},{48,32},{56,40},{64,80... | collective-permute-start | bytes 417800 | tf_op jit(solution)/shard_map/ppermute | solution.py:43
  45.1 4.8 %collective-permute-done.16.refs_1_ = s16[1040,256]{1,0:T(8,128)(2,1)S(1)} collective-permute-done((s16[1040,256]{1,0:T(8,128)(2,1)S(1)}, s16[1040,256]{1,0:T(8,128)(2,1)S(1)}, u32[]{:S(2)}, u32[]{:S(2)}) %collective-permute-start.16) | collective-permute-done | bytes 532512 | tf_op jit(solution)/shard_map/ppermute | solution.py:43
  49.9 2.9 %product.7.refs_1_ = f32[256,1024]{1,0:T(8,128)S(1)} custom-call(s32[8]{0:T(128)S(1)} %compare_select_fusion.4.place_ref, bf16[4096,1024]{1,0:T(8,128)(2,1)S(1)} %load.3.refs_0_.head_ref, s16[1040,256]{1,0:T(8,128)(2,1)S(1)} %collective-permute-done.15.refs_0_, s16[1040,256]{1,0:T(8,128)(2,1)S(1)} %collective-permute-done.16.refs_1_, ...), custom_call_target="tpu_custom_call" | custom-call | flops 2147483648 | tf_op jit(solution)/shard_map/product/pallas_call | solution.py:241
  52.9 2.0 %product.8.refs_4_ = s16[528,512]{1,0:T(8,128)(2,1)S(1)} custom-call(s32[8]{0:T(128)S(1)} %compare_select_fusion.4.place_ref, bf16[4096,1024]{1,0:T(8,128)(2,1)S(1)} %load.3.refs_0_.head_ref, s16[1040,256]{1,0:T(8,128)(2,1)S(1)} %collective-permute-done.14.refs_0_, f32[256,1024]{1,0:T(8,128)S(1)} %product.7.refs_1_), custom_call_target="tpu_custom_call" | custom-call | flops 1073741824 | tf_op jit(solution)/shard_map/product/pallas_call | solution.py:241
  54.9 5.1 %collective-permute-start.20 = (s16[528,512]{1,0:T(8,128)(2,1)S(1)}, s16[528,512]{1,0:T(8,128)(2,1)S(1)}, u32[]{:S(2)}, u32[]{:S(2)}) collective-permute-start(s16[528,512]{1,0:T(8,128)(2,1)S(1)} %product.8.refs_4_), channel_id=1, source_target_pairs={{0,1},{1,0},{2,3},{3,2},{4,5},{5,4},{6,7},{7,6},{8,9},{9,8},{10,11... | collective-permute-start | bytes 1622024 | tf_op jit(solution)/shard_map/ppermute | solution.py:315
  61.5 2.5 %collective-permute-start.17 = (s16[1040,256]{1,0:T(8,128)(2,1)S(1)}, s16[1040,256]{1,0:T(8,128)(2,1)S(1)}, u32[]{:S(2)}, u32[]{:S(2)}) collective-permute-start(s16[1040,256]{1,0:T(8,128)(2,1)S(1)} %pack.3.refs_0_), channel_id=1, source_target_pairs={{0,96},{8,104},{16,112},{24,120},{32,0},{40,8},{48,16},{56,24},{64... | collective-permute-start | bytes 1597448 | tf_op jit(solution)/shard_map/ppermute | solution.py:43
  64.0 1.8 %product.9.refs_2_ = f32[256,1024]{1,0:T(8,128)S(1)} custom-call(s32[8]{0:T(128)S(1)} %compare_select_fusion.4.place_ref, bf16[4096,1024]{1,0:T(8,128)(2,1)S(1)} %load.3.refs_0_.head_ref, s16[1040,256]{1,0:T(8,128)(2,1)S(1)} %pack.3.refs_0_), custom_call_target="tpu_custom_call" | custom-call | tf_op jit(solution)/shard_map/product/pallas_call | solution.py:241
  65.8 10.5 %collective-permute-done.18.refs_0_ = s16[1040,256]{1,0:T(8,128)(2,1)S(1)} collective-permute-done((s16[1040,256]{1,0:T(8,128)(2,1)S(1)}, s16[1040,256]{1,0:T(8,128)(2,1)S(1)}, u32[]{:S(2)}, u32[]{:S(2)}) %collective-permute-start.18) | collective-permute-done | bytes 532512 | tf_op jit(solution)/shard_map/ppermute | solution.py:43
  76.3 2.9 %product.10.refs_1_ = f32[256,1024]{1,0:T(8,128)S(1)} custom-call(s32[8]{0:T(128)S(1)} %compare_select_fusion.4.place_ref, bf16[4096,1024]{1,0:T(8,128)(2,1)S(1)} %load.3.refs_0_.head_ref, s16[1040,256]{1,0:T(8,128)(2,1)S(1)} %collective-permute-done.18.refs_0_, s16[1040,256]{1,0:T(8,128)(2,1)S(1)} %collective-permute-done.19.refs_1_, ...), custom_call_target="tpu_custom_call" | custom-call | tf_op jit(solution)/shard_map/product/pallas_call | solution.py:241
  79.3 1.8 %product.11.kept_ref = f32[256,1024]{1,0:T(8,128)S(1)} custom-call(s32[8]{0:T(128)S(1)} %compare_select_fusion.4.place_ref, bf16[4096,1024]{1,0:T(8,128)(2,1)S(1)} %load.3.refs_0_.head_ref, s16[1040,256]{1,0:T(8,128)(2,1)S(1)} %collective-permute-done.17.refs_0_, f32[256,1024]{1,0:T(8,128)S(1)} %product.10.refs_1_), custom_call_target="tpu_custom_call" | custom-call | tf_op jit(solution)/shard_map/product/pallas_call | solution.py:241
  82.4 5.8 %all-to-all-start = ((f32[64,4,128]{2,1,0:T(4,128)}), f32[64,4,128]{2,1,0:T(4,128)S(1)}, u32[]{:S(2)}, u32[]{:S(2)}) async-start(f32[64,4,128]{2,1,0:T(4,128)} %get-tuple-element.16), calls=%async_computation | async-start | bytes 262144 | tf_op jit(solution)/shard_map/all_to_all | solution.py:322
  88.4 9.4 %all-to-all-done = f32[64,4,128]{2,1,0:T(4,128)S(1)} async-done(((f32[64,4,128]{2,1,0:T(4,128)}), f32[64,4,128]{2,1,0:T(4,128)S(1)}, u32[]{:S(2)}, u32[]{:S(2)}) %all-to-all-start) | async-done | bytes 131104 | tf_op jit(solution)/shard_map/all_to_all | solution.py:322
  (49 shorter events, 12.7 us)
Async XLA Ops:
  0.6 8.3 %collective-permute-start = (bf16[64,1024]{1,0:T(8,128)(2,1)}, bf16[64,1024]{1,0:T(8,128)(2,1)S(1)}, u32[]{:S(2)}, u32[]{:S(2)}) collective-permute-start(bf16[64,1024]{1,0:T(8,128)(2,1)} %bitcast.10), channel_id=1, source_target_pairs={{0,128},{128,0},{1,129},{129,1},{2,130},{130,2},{3,131},{131,3},{4... | collective-permute-start | bytes 393224 | tf_op jit(solution)/shard_map/ppermute | solution.py:292
  0.7 8.2 %collective-permute-start.1 = (s32[512]{0:T(512)}, s32[512]{0:T(512)S(1)}, u32[]{:S(2)}, u32[]{:S(2)}) collective-permute-start(s32[512]{0:T(512)} %param.6), channel_id=1, source_target_pairs={{0,5},{1,4},{2,7},{3,6},{4,1},{5,0},{6,3},{7,2},{8,13},{9,12},{10,... | collective-permute-start | bytes 6152 | tf_op jit(solution)/shard_map/ppermute | solution.py:293
  9.6 8.0 %collective-permute-start.2 = (s16[80,256]{1,0:T(8,128)(2,1)S(1)}, s16[80,256]{1,0:T(8,128)(2,1)S(1)}, u32[]{:S(2)}, u32[]{:S(2)}) collective-permute-start(s16[80,256]{1,0:T(8,128)(2,1)S(1)} %get-tuple-element.12.a_ref), channel_id=1, source_target_pairs={{0,2},{2,4},{4,6},{6,0},{1,3},{3,5},{5,7},{7,1},{8,10},{10,12},{12... | collective-permute-start | bytes 122888 | tf_op jit(solution)/shard_map/ppermute | solution.py:33
  10.7 6.9 %collective-permute-start.3 = (s16[80,256]{1,0:T(8,128)(2,1)S(1)}, s16[80,256]{1,0:T(8,128)(2,1)S(1)}, u32[]{:S(2)}, u32[]{:S(2)}) collective-permute-start(s16[80,256]{1,0:T(8,128)(2,1)S(1)} %get-tuple-element.12.a_ref), channel_id=1, source_target_pairs={{0,4},{2,6},{4,0},{6,2},{1,5},{3,7},{5,1},{7,3},{8,12},{10,14},{12... | collective-permute-start | bytes 122888 | tf_op jit(solution)/shard_map/ppermute | solution.py:33
  12.6 4.9 %collective-permute-start.4 = (s16[80,256]{1,0:T(8,128)(2,1)S(1)}, s16[80,256]{1,0:T(8,128)(2,1)S(1)}, u32[]{:S(2)}, u32[]{:S(2)}) collective-permute-start(s16[80,256]{1,0:T(8,128)(2,1)S(1)} %get-tuple-element.12.a_ref), channel_id=1, source_target_pairs={{0,6},{2,0},{4,2},{6,4},{1,7},{3,1},{5,3},{7,5},{8,14},{10,8},{12,... | collective-permute-start | bytes 122888 | tf_op jit(solution)/shard_map/ppermute | solution.py:33
  18.1 11.2 %collective-permute-start.10 = (s16[272,256]{1,0:T(8,128)(2,1)S(1)}, s16[272,256]{1,0:T(8,128)(2,1)S(1)}, u32[]{:S(2)}, u32[]{:S(2)}) collective-permute-start(s16[272,256]{1,0:T(8,128)(2,1)S(1)} %stack.2.refs_0_), channel_id=1, source_target_pairs={{0,24},{8,0},{16,8},{24,16},{32,56},{40,32},{48,40},{56,48},{64,88... | collective-permute-start | bytes 417800 | tf_op jit(solution)/shard_map/ppermute | solution.py:43
  18.8 10.6 %collective-permute-start.8 = (s16[272,256]{1,0:T(8,128)(2,1)S(1)}, s16[272,256]{1,0:T(8,128)(2,1)S(1)}, u32[]{:S(2)}, u32[]{:S(2)}) collective-permute-start(s16[272,256]{1,0:T(8,128)(2,1)S(1)} %stack.2.refs_0_), channel_id=1, source_target_pairs={{0,8},{8,16},{16,24},{24,0},{32,40},{40,48},{48,56},{56,32},{64,72... | collective-permute-start | bytes 417800 | tf_op jit(solution)/shard_map/ppermute | solution.py:43
  20.2 9.1 %collective-permute-start.9 = (s16[272,256]{1,0:T(8,128)(2,1)S(1)}, s16[272,256]{1,0:T(8,128)(2,1)S(1)}, u32[]{:S(2)}, u32[]{:S(2)}) collective-permute-start(s16[272,256]{1,0:T(8,128)(2,1)S(1)} %stack.2.refs_0_), channel_id=1, source_target_pairs={{0,16},{8,24},{16,0},{24,8},{32,48},{40,56},{48,32},{56,40},{64,80... | collective-permute-start | bytes 417800 | tf_op jit(solution)/shard_map/ppermute | solution.py:43
  23.6 5.8 %collective-permute-start.5 = (s16[80,256]{1,0:T(8,128)(2,1)S(1)}, s16[80,256]{1,0:T(8,128)(2,1)S(1)}, u32[]{:S(2)}, u32[]{:S(2)}) collective-permute-start(s16[80,256]{1,0:T(8,128)(2,1)S(1)} %hold.1.a_ref), channel_id=1, source_target_pairs={{0,2},{2,4},{4,6},{6,0},{1,3},{3,5},{5,7},{7,1},{8,10},{10,12},{12... | collective-permute-start | bytes 122888 | tf_op jit(solution)/shard_map/ppermute | solution.py:33
  29.5 14.6 %collective-permute-start.15 = (s16[1040,256]{1,0:T(8,128)(2,1)S(1)}, s16[1040,256]{1,0:T(8,128)(2,1)S(1)}, u32[]{:S(2)}, u32[]{:S(2)}) collective-permute-start(s16[1040,256]{1,0:T(8,128)(2,1)S(1)} %pack.2.refs_0_), channel_id=1, source_target_pairs={{0,32},{8,40},{16,48},{24,56},{32,64},{40,72},{48,80},{56,88},{64,... | collective-permute-start | bytes 1597448 | tf_op jit(solution)/shard_map/ppermute | solution.py:43
  31.1 18.8 %collective-permute-start.16 = (s16[1040,256]{1,0:T(8,128)(2,1)S(1)}, s16[1040,256]{1,0:T(8,128)(2,1)S(1)}, u32[]{:S(2)}, u32[]{:S(2)}) collective-permute-start(s16[1040,256]{1,0:T(8,128)(2,1)S(1)} %pack.2.refs_0_), channel_id=1, source_target_pairs={{0,64},{8,72},{16,80},{24,88},{32,96},{40,104},{48,112},{56,120},{... | collective-permute-start | bytes 1597448 | tf_op jit(solution)/shard_map/ppermute | solution.py:43
  34.0 18.9 %collective-permute-start.14 = (s16[1040,256]{1,0:T(8,128)(2,1)S(1)}, s16[1040,256]{1,0:T(8,128)(2,1)S(1)}, u32[]{:S(2)}, u32[]{:S(2)}) collective-permute-start(s16[1040,256]{1,0:T(8,128)(2,1)S(1)} %pack.2.refs_0_), channel_id=1, source_target_pairs={{0,96},{8,104},{16,112},{24,120},{32,0},{40,8},{48,16},{56,24},{64... | collective-permute-start | bytes 1597448 | tf_op jit(solution)/shard_map/ppermute | solution.py:43
  35.4 4.9 %collective-permute-start.6 = (s16[80,256]{1,0:T(8,128)(2,1)S(1)}, s16[80,256]{1,0:T(8,128)(2,1)S(1)}, u32[]{:S(2)}, u32[]{:S(2)}) collective-permute-start(s16[80,256]{1,0:T(8,128)(2,1)S(1)} %hold.1.a_ref), channel_id=1, source_target_pairs={{0,4},{2,6},{4,0},{6,2},{1,5},{3,7},{5,1},{7,3},{8,12},{10,14},{12... | collective-permute-start | bytes 122888 | tf_op jit(solution)/shard_map/ppermute | solution.py:33
  35.4 4.9 %collective-permute-start.7 = (s16[80,256]{1,0:T(8,128)(2,1)S(1)}, s16[80,256]{1,0:T(8,128)(2,1)S(1)}, u32[]{:S(2)}, u32[]{:S(2)}) collective-permute-start(s16[80,256]{1,0:T(8,128)(2,1)S(1)} %hold.1.a_ref), channel_id=1, source_target_pairs={{0,6},{2,0},{4,2},{6,4},{1,7},{3,1},{5,3},{7,5},{8,14},{10,8},{12,... | collective-permute-start | bytes 122888 | tf_op jit(solution)/shard_map/ppermute | solution.py:33
  40.8 19.2 %collective-permute-start.11 = (s16[272,256]{1,0:T(8,128)(2,1)S(1)}, s16[272,256]{1,0:T(8,128)(2,1)S(1)}, u32[]{:S(2)}, u32[]{:S(2)}) collective-permute-start(s16[272,256]{1,0:T(8,128)(2,1)S(1)} %stack.3.refs_0_), channel_id=1, source_target_pairs={{0,8},{8,16},{16,24},{24,0},{32,40},{40,48},{48,56},{56,32},{64,72... | collective-permute-start | bytes 417800 | tf_op jit(solution)/shard_map/ppermute | solution.py:43
  40.9 19.1 %collective-permute-start.12 = (s16[272,256]{1,0:T(8,128)(2,1)S(1)}, s16[272,256]{1,0:T(8,128)(2,1)S(1)}, u32[]{:S(2)}, u32[]{:S(2)}) collective-permute-start(s16[272,256]{1,0:T(8,128)(2,1)S(1)} %stack.3.refs_0_), channel_id=1, source_target_pairs={{0,16},{8,24},{16,0},{24,8},{32,48},{40,56},{48,32},{56,40},{64,80... | collective-permute-start | bytes 417800 | tf_op jit(solution)/shard_map/ppermute | solution.py:43
  44.1 15.9 %collective-permute-start.13 = (s16[272,256]{1,0:T(8,128)(2,1)S(1)}, s16[272,256]{1,0:T(8,128)(2,1)S(1)}, u32[]{:S(2)}, u32[]{:S(2)}) collective-permute-start(s16[272,256]{1,0:T(8,128)(2,1)S(1)} %stack.3.refs_0_), channel_id=1, source_target_pairs={{0,24},{8,0},{16,8},{24,16},{32,56},{40,32},{48,40},{56,48},{64,88... | collective-permute-start | bytes 417800 | tf_op jit(solution)/shard_map/ppermute | solution.py:43
  54.9 26.2 %collective-permute-start.20 = (s16[528,512]{1,0:T(8,128)(2,1)S(1)}, s16[528,512]{1,0:T(8,128)(2,1)S(1)}, u32[]{:S(2)}, u32[]{:S(2)}) collective-permute-start(s16[528,512]{1,0:T(8,128)(2,1)S(1)} %product.8.refs_4_), channel_id=1, source_target_pairs={{0,1},{1,0},{2,3},{3,2},{4,5},{5,4},{6,7},{7,6},{8,9},{9,8},{10,11... | collective-permute-start | bytes 1622024 | tf_op jit(solution)/shard_map/ppermute | solution.py:315
  60.1 16.3 %collective-permute-start.18 = (s16[1040,256]{1,0:T(8,128)(2,1)S(1)}, s16[1040,256]{1,0:T(8,128)(2,1)S(1)}, u32[]{:S(2)}, u32[]{:S(2)}) collective-permute-start(s16[1040,256]{1,0:T(8,128)(2,1)S(1)} %pack.3.refs_0_), channel_id=1, source_target_pairs={{0,32},{8,40},{16,48},{24,56},{32,64},{40,72},{48,80},{56,88},{64,... | collective-permute-start | bytes 1597448 | tf_op jit(solution)/shard_map/ppermute | solution.py:43
  60.1 16.2 %collective-permute-start.19 = (s16[1040,256]{1,0:T(8,128)(2,1)S(1)}, s16[1040,256]{1,0:T(8,128)(2,1)S(1)}, u32[]{:S(2)}, u32[]{:S(2)}) collective-permute-start(s16[1040,256]{1,0:T(8,128)(2,1)S(1)} %pack.3.refs_0_), channel_id=1, source_target_pairs={{0,64},{8,72},{16,80},{24,88},{32,96},{40,104},{48,112},{56,120},{... | collective-permute-start | bytes 1597448 | tf_op jit(solution)/shard_map/ppermute | solution.py:43
  61.5 17.8 %collective-permute-start.17 = (s16[1040,256]{1,0:T(8,128)(2,1)S(1)}, s16[1040,256]{1,0:T(8,128)(2,1)S(1)}, u32[]{:S(2)}, u32[]{:S(2)}) collective-permute-start(s16[1040,256]{1,0:T(8,128)(2,1)S(1)} %pack.3.refs_0_), channel_id=1, source_target_pairs={{0,96},{8,104},{16,112},{24,120},{32,0},{40,8},{48,16},{56,24},{64... | collective-permute-start | bytes 1597448 | tf_op jit(solution)/shard_map/ppermute | solution.py:43
  79.2 9.0 %copy-start.3 = (s32[512]{0:T(512)S(1)}, s32[512]{0:T(512)}, u32[]{:S(2)}) copy-start(s32[512]{0:T(512)} %param.7) | copy-start | bytes 6148
  82.4 15.3 %all-to-all-start = ((f32[64,4,128]{2,1,0:T(4,128)}), f32[64,4,128]{2,1,0:T(4,128)S(1)}, u32[]{:S(2)}, u32[]{:S(2)}) async-start(f32[64,4,128]{2,1,0:T(4,128)} %get-tuple-element.16), calls=%async_computation | async-start | bytes 262144 | tf_op jit(solution)/shard_map/all_to_all | solution.py:322
  97.9 1.3 %copy-start.2 = (f32[256]{0:T(256)}, f32[256]{0:T(256)S(1)}, u32[]{:S(2)}) copy-start(f32[256]{0:T(256)S(1)} %get-tuple-element.19) | copy-start | bytes 3076
  (2 other events, 1.6 us)
